TPU v7x, 128 devices: a whole 4x4x4 slice. The times are simulated.
128 devices in a mesh: pipe: 2 (over core), expert: 32 (over y, x, z_hi), tensor: 2 (over z_lo).
Axes of the slice: x: 4, y: 4, z: 4 (z_hi: 2, z_lo: 2; z = z_hi * 2 + z_lo), core: 2. Of those that a mesh axis runs over, the one named last changes fastest.
Arguments:
- tokens: bfloat16 [2, 4096, 1536], P(None, 'expert'), may hold values from -6 to 6
- cotangent: float32 [2, 4096, 1536], P(None, 'expert'), may hold values from -6 to 6
- routes: int32 [2, 2, 4096, 4], P('pipe', None, 'expert'), may hold values from 0 to 31, all different within a row; in each aligned block of 128 rows (0 to 127, 128 to 255, ..., all dimensions but the last counted through in order) at most 32 rows name the same one
- attn_gain: bfloat16 [2, 1536], P('pipe'), may hold values from 0.5 to 1.5
- w_query: bfloat16 [2, 1536, 1536], P('pipe', None, 'tensor'), may hold values from -0.15625 to 0.15625
- key_weight: bfloat16 [2, 1536, 256], P('pipe', None, 'tensor'), may hold values from -0.15625 to 0.15625
- value_weight: bfloat16 [2, 1536, 256], P('pipe', None, 'tensor'), may hold values from -0.15625 to 0.15625
- w_out: bfloat16 [2, 1536, 1536], P('pipe', 'tensor'), may hold values from -0.875 to 0.875
- moe_gain: bfloat16 [2, 1536], P('pipe'), may hold values from 0.5 to 1.5
- w_router: bfloat16 [2, 1536, 32], P('pipe'), may hold values from -0.076660156 to 0.076660156
- w_gate: bfloat16 [2, 32, 1536, 768], P('pipe', 'expert', None, 'tensor'), may hold values from -0.15625 to 0.15625
- w_up: bfloat16 [2, 32, 1536, 768], P('pipe', 'expert', None, 'tensor'), may hold values from -0.15625 to 0.15625
- w_down: bfloat16 [2, 32, 768, 1536], P('pipe', 'expert', 'tensor'), may hold values from -0.625 to 0.625
Outputs:
- layer_out: float32 [2, 2, 4096, 1536], P('pipe', None, 'expert')
- input_grads: float32 [2, 2, 4096, 1536], P('pipe', None, 'expert')
- grad_attn_gain: float32 [2, 1536], P('pipe')
- grad_query: float32 [2, 1536, 1536], P('pipe', None, 'tensor')
- grad_key: float32 [2, 1536, 256], P('pipe', None, 'tensor')
- grad_value: float32 [2, 1536, 256], P('pipe', None, 'tensor')
- grad_out: float32 [2, 1536, 1536], P('pipe', 'tensor')
- grad_moe_gain: float32 [2, 1536], P('pipe')
- grad_router: float32 [2, 1536, 32], P('pipe')
- grad_gate: float32 [2, 32, 1536, 768], P('pipe', 'expert', None, 'tensor')
- grad_up: float32 [2, 32, 1536, 768], P('pipe', 'expert', None, 'tensor')
- grad_down: float32 [2, 32, 768, 1536], P('pipe', 'expert', 'tensor')
Inputs may be any that keep to these rules, and one draw needn't show every extreme that they name: `routes`: each row names 4 different experts; among the 128 rows of one device in one layer and micro-batch (aligned blocks) no expert is named more than 32 times, and in some blocks one is named exactly 32 times.
All inputs are finite; a program needn't handle non-finite values.
Results may differ from a plain program's by a relative error of at most 0.025.
Values may be sent and summed in bfloat16 or wider, within the bound.
No kernel may reach another device: no remote copies, remote signals or barrier semaphores. Data moves between devices by JAX's collectives and lax.ppermute only.
A program may use at most 256 MiB of HBM per device.

v0:
```python
import jax
import jax.numpy as jnp
from jax import lax
from jax.sharding import PartitionSpec as P

HEAD_DIMENSION = 128


NORM_EPS = 1e-06
ROPE_BASE = 10000.0
EXACT = lax.Precision.HIGHEST


def from_behind(value, axis, steps):
    count = lax.axis_size(axis)
    leading, last = (max(0, -steps), min(count, count - steps))
    return lax.ppermute(value, axis, [(source, source + steps) for source in range(leading, last)])


def rotary_tables(sequence_length):
    half_size = HEAD_DIMENSION // 2
    frequency = ROPE_BASE ** (-(jnp.arange(half_size, dtype=jnp.float32) * 2.0) / HEAD_DIMENSION)
    angles = jnp.arange(sequence_length, dtype=jnp.float32)[:, None] * frequency[None, :]
    cosine = jnp.concatenate([jnp.cos(angles), jnp.cos(angles)], axis=1)
    sine_table = jnp.concatenate([jnp.sin(angles), jnp.sin(angles)], axis=1)
    return (cosine, sine_table)


def rotate_half(vector):
    half_size = vector.shape[-1] // 2
    return jnp.concatenate([-vector[..., half_size:], vector[..., :half_size]], axis=-1)


def rotary_turn(vector, cosine, sine_table):
    return vector * cosine + rotate_half(vector) * sine_table


def rotary_back(grad_in, cosine, sine_table):
    moved = grad_in * sine_table
    half_size = moved.shape[-1] // 2
    return grad_in * cosine + jnp.concatenate(
        [moved[..., half_size:], -moved[..., :half_size]], axis=-1
    )


def norm_rows(vector, gain_vec):
    row_scale = lax.rsqrt(jnp.mean(vector * vector, axis=-1, keepdims=True) + NORM_EPS)
    return (vector * row_scale * gain_vec, row_scale)


def norm_back(vector, row_scale, gain_vec, grad_in):
    scaled = grad_in * gain_vec
    grad_gain = jnp.sum(grad_in * vector * row_scale, axis=0)
    grad_vec = row_scale * scaled - vector * row_scale**3 * jnp.mean(
        scaled * vector, axis=-1, keepdims=True
    )
    return (grad_vec, grad_gain)


def dot_rows(left_mat, right_mat):
    return lax.dot_general(
        left_mat, right_mat, (((0,), (0,)), ((), ())), preferred_element_type=jnp.float32
    )


def dot_back(left_mat, right_mat):
    return lax.dot_general(
        left_mat, right_mat, (((1,), (1,)), ((), ())), preferred_element_type=jnp.float32
    )


def lower_mask(sequence_length):
    return jnp.arange(sequence_length)[:, None] >= jnp.arange(sequence_length)[None, :]


def slot_tables(route_ids, experts, capacity):
    row_count, pick_count = route_ids.shape
    onehot = (route_ids[:, :, None] == jnp.arange(experts, dtype=jnp.int32)[None, None, :]).astype(
        jnp.int32
    )
    flat_hot = onehot.reshape(row_count * pick_count, experts)
    before = jnp.cumsum(flat_hot, axis=0) - flat_hot
    slot_place = jnp.sum(before * flat_hot, axis=1).reshape(row_count, pick_count)
    target = route_ids * capacity + slot_place
    column = jnp.arange(experts * capacity, dtype=jnp.int32)
    select = target[:, :, None] == column[None, None, :]
    return (onehot, select)


def to_expert(arrived, local_count):
    source_count = arrived.shape[0] // local_count
    shaped = arrived.reshape(source_count, local_count, arrived.shape[1], arrived.shape[2])
    return shaped.transpose(1, 0, 2, 3).reshape(
        local_count, source_count * arrived.shape[1], arrived.shape[2]
    )


def from_expert(summed, local_count, capacity):
    source_count = summed.shape[1] // capacity
    shaped = summed.reshape(local_count, source_count, capacity, summed.shape[2])
    return shaped.transpose(1, 0, 2, 3).reshape(
        source_count * local_count, capacity, summed.shape[2]
    )


def attend_forward(source, params, cosine, sine_table):
    gain_a, w_query, key_weight, value_weight, w_out = params
    section_input = source.astype(jnp.float32)
    normed, scale_a = norm_rows(section_input, gain_a)
    normed_b = normed.astype(jnp.bfloat16)
    sequence_length = section_input.shape[0]
    kv_local = key_weight.shape[1] // HEAD_DIMENSION
    query_group_size = w_query.shape[1] // HEAD_DIMENSION // kv_local
    projected_queries = jnp.dot(normed_b, w_query, preferred_element_type=jnp.float32).reshape(
        sequence_length, kv_local, query_group_size, HEAD_DIMENSION
    )
    projected_queries = (
        rotary_turn(projected_queries, cosine[:, None, None, :], sine_table[:, None, None, :])
        * HEAD_DIMENSION ** (-0.5)
    ).astype(jnp.bfloat16)
    projected_keys = jnp.dot(normed_b, key_weight, preferred_element_type=jnp.float32).reshape(
        sequence_length, kv_local, HEAD_DIMENSION
    )
    projected_keys = rotary_turn(projected_keys, cosine[:, None, :], sine_table[:, None, :]).astype(
        jnp.bfloat16
    )
    projected_values = (
        jnp.dot(normed_b, value_weight, preferred_element_type=jnp.float32)
        .astype(jnp.bfloat16)
        .reshape(sequence_length, kv_local, HEAD_DIMENSION)
    )
    scores = jnp.einsum(
        "sghd,tgd->ghst", projected_queries, projected_keys, preferred_element_type=jnp.float32
    )
    scores = jnp.where(lower_mask(sequence_length), scores, -1e30)
    row_max = jnp.max(scores, axis=-1, keepdims=True)
    raised = jnp.exp(scores - row_max)
    row_total = jnp.sum(raised, axis=-1, keepdims=True)
    weights = raised / row_total
    log_total = row_max + jnp.log(row_total)
    attended = jnp.einsum(
        "ghst,tgd->sghd",
        weights.astype(jnp.bfloat16),
        projected_values,
        preferred_element_type=jnp.float32,
    )
    attended = attended.reshape(
        sequence_length, kv_local * query_group_size * HEAD_DIMENSION
    ).astype(jnp.bfloat16)
    branch = lax.psum(jnp.dot(attended, w_out, preferred_element_type=jnp.float32), "tensor")
    return (
        section_input + branch,
        (scale_a, projected_queries, projected_keys, projected_values, log_total, attended),
    )


def attend_backward(section_input, grad_in, params, saved, cosine, sine_table):
    gain_a, w_query, key_weight, value_weight, w_out = params
    scale_a, projected_queries, projected_keys, projected_values, log_total, attended = saved
    sequence_length = section_input.shape[0]
    kv_local = projected_keys.shape[1]
    query_group_size = projected_queries.shape[2]
    normed_b = (section_input * scale_a * gain_a).astype(jnp.bfloat16)
    grad_b = grad_in.astype(jnp.bfloat16)
    grad_wo = dot_rows(attended, grad_b)
    grad_att = (
        dot_back(grad_b, w_out)
        .astype(jnp.bfloat16)
        .reshape(sequence_length, kv_local, query_group_size, HEAD_DIMENSION)
    )
    scores = jnp.einsum(
        "sghd,tgd->ghst", projected_queries, projected_keys, preferred_element_type=jnp.float32
    )
    weights = jnp.where(
        lower_mask(sequence_length),
        jnp.exp(jnp.where(lower_mask(sequence_length), scores, -1e30) - log_total),
        0.0,
    )
    grad_weights = jnp.einsum(
        "sghd,tgd->ghst", grad_att, projected_values, preferred_element_type=jnp.float32
    )
    grad_scores = (
        weights * (grad_weights - jnp.sum(weights * grad_weights, axis=-1, keepdims=True))
    ).astype(jnp.bfloat16)
    grad_vals = jnp.einsum(
        "ghst,sghd->tgd", weights.astype(jnp.bfloat16), grad_att, preferred_element_type=jnp.float32
    )
    grad_vals = grad_vals.astype(jnp.bfloat16).reshape(sequence_length, kv_local * HEAD_DIMENSION)
    grad_query_r = jnp.einsum(
        "ghst,tgd->sghd", grad_scores, projected_keys, preferred_element_type=jnp.float32
    )
    grad_query_r = rotary_back(
        grad_query_r, cosine[:, None, None, :], sine_table[:, None, None, :]
    ) * HEAD_DIMENSION ** (-0.5)
    grad_query_r = grad_query_r.reshape(
        sequence_length, kv_local * query_group_size * HEAD_DIMENSION
    ).astype(jnp.bfloat16)
    grad_key_r = jnp.einsum(
        "ghst,sghd->tgd", grad_scores, projected_queries, preferred_element_type=jnp.float32
    )
    grad_key_r = (
        rotary_back(grad_key_r, cosine[:, None, :], sine_table[:, None, :])
        .reshape(sequence_length, kv_local * HEAD_DIMENSION)
        .astype(jnp.bfloat16)
    )
    grad_normed = (
        dot_back(grad_query_r, w_query)
        + dot_back(grad_key_r, key_weight)
        + dot_back(grad_vals, value_weight)
    )
    grad_normed = lax.psum(grad_normed, "tensor")
    grad_start, grad_gain = norm_back(section_input, scale_a, gain_a, grad_normed)
    grads_here = (
        grad_gain,
        dot_rows(normed_b, grad_query_r),
        dot_rows(normed_b, grad_key_r),
        dot_rows(normed_b, grad_vals),
        grad_wo,
    )
    return (grad_in + grad_start, grads_here)


def mix_forward(hidden, route_ids, params):
    gain_m, w_router, w_gate, w_up, w_down = params
    experts = w_router.shape[1]
    local_count = w_gate.shape[0]
    model_width = hidden.shape[1]
    capacity = 2 * route_ids.shape[1] * hidden.shape[0] // experts
    normed, scale_m = norm_rows(hidden, gain_m)
    normed_b = normed.astype(jnp.bfloat16)
    logits = jnp.dot(normed_b, w_router, preferred_element_type=jnp.float32)
    onehot, select = slot_tables(route_ids, experts, capacity)
    chosen = jnp.sum(onehot.astype(jnp.float32) * logits[:, None, :], axis=-1)
    gate_share = jax.nn.softmax(chosen, axis=-1)
    select_b = select.astype(jnp.bfloat16)
    outgoing = jnp.einsum("skj,sd->jd", select_b, normed_b, preferred_element_type=jnp.float32)
    outgoing = outgoing.astype(jnp.bfloat16).reshape(experts, capacity, model_width)
    arrived = lax.all_to_all(outgoing, "expert", split_axis=0, concat_axis=0, tiled=True)
    expert_rows = to_expert(arrived, local_count)
    gate_v = jnp.einsum("erd,edf->erf", expert_rows, w_gate, preferred_element_type=jnp.float32)
    up_v = jnp.einsum("erd,edf->erf", expert_rows, w_up, preferred_element_type=jnp.float32)
    hidden_act = (jax.nn.silu(gate_v) * up_v).astype(jnp.bfloat16)
    partial_value = jnp.einsum(
        "erf,efd->erd", hidden_act, w_down, preferred_element_type=jnp.float32
    )
    summed = lax.psum(partial_value, "tensor").astype(jnp.bfloat16)
    returned = lax.all_to_all(
        from_expert(summed, local_count, capacity),
        "expert",
        split_axis=0,
        concat_axis=0,
        tiled=True,
    )
    fetched = jnp.einsum(
        "skj,jd->skd",
        select_b,
        returned.reshape(experts * capacity, model_width),
        preferred_element_type=jnp.float32,
    )
    fetched = fetched.astype(jnp.bfloat16)
    result = hidden + jnp.sum(gate_share[:, :, None] * fetched.astype(jnp.float32), axis=1)
    return (result, (scale_m, gate_share, fetched, expert_rows, gate_v, up_v))


def mix_backward(hidden, route_ids, grad_in, params, saved):
    gain_m, w_router, w_gate, w_up, w_down = params
    scale_m, gate_share, fetched, expert_rows, gate_v, up_v = saved
    experts = w_router.shape[1]
    local_count = w_gate.shape[0]
    model_width = hidden.shape[1]
    capacity = 2 * route_ids.shape[1] * hidden.shape[0] // experts
    normed_b = (hidden * scale_m * gain_m).astype(jnp.bfloat16)
    onehot, select = slot_tables(route_ids, experts, capacity)
    select_b = select.astype(jnp.bfloat16)
    grad_gates = jnp.sum(grad_in[:, None, :] * fetched.astype(jnp.float32), axis=-1)
    grad_chosen = gate_share * (
        grad_gates - jnp.sum(gate_share * grad_gates, axis=-1, keepdims=True)
    )
    grad_logits = jnp.sum(onehot.astype(jnp.float32) * grad_chosen[:, :, None], axis=1)
    grad_slots = (gate_share[:, :, None] * grad_in[:, None, :]).astype(jnp.bfloat16)
    outgoing = jnp.einsum("skj,skd->jd", select_b, grad_slots, preferred_element_type=jnp.float32)
    outgoing = outgoing.astype(jnp.bfloat16).reshape(experts, capacity, model_width)
    arrived = lax.all_to_all(outgoing, "expert", split_axis=0, concat_axis=0, tiled=True)
    grad_rows = to_expert(arrived, local_count)
    sigmoid_g = jax.nn.sigmoid(gate_v)
    activated = gate_v * sigmoid_g
    hidden_act = (activated * up_v).astype(jnp.bfloat16)
    grad_act = jnp.einsum("erd,efd->erf", grad_rows, w_down, preferred_element_type=jnp.float32)
    grad_wd = jnp.einsum("erf,erd->efd", hidden_act, grad_rows, preferred_element_type=jnp.float32)
    grad_gate_v = (grad_act * up_v * sigmoid_g * (1.0 + gate_v * (1.0 - sigmoid_g))).astype(
        jnp.bfloat16
    )
    grad_up_v = (grad_act * activated).astype(jnp.bfloat16)
    grad_wg = jnp.einsum(
        "erd,erf->edf", expert_rows, grad_gate_v, preferred_element_type=jnp.float32
    )
    grad_wu = jnp.einsum("erd,erf->edf", expert_rows, grad_up_v, preferred_element_type=jnp.float32)
    grad_inputs = jnp.einsum(
        "erf,edf->erd", grad_gate_v, w_gate, preferred_element_type=jnp.float32
    )
    grad_inputs = grad_inputs + jnp.einsum(
        "erf,edf->erd", grad_up_v, w_up, preferred_element_type=jnp.float32
    )
    shared = lax.psum_scatter(grad_inputs, "tensor", scatter_dimension=2, tiled=True).astype(
        jnp.bfloat16
    )
    back_rows = lax.all_to_all(
        from_expert(shared, local_count, capacity),
        "expert",
        split_axis=0,
        concat_axis=0,
        tiled=True,
    )
    back_rows = lax.all_gather(back_rows, "tensor", axis=2, tiled=True)
    grad_normed = jnp.einsum(
        "skj,jd->sd",
        select_b,
        back_rows.reshape(experts * capacity, model_width),
        preferred_element_type=jnp.float32,
    )
    router_f = w_router.astype(jnp.float32)
    grad_normed = grad_normed + jnp.dot(grad_logits, router_f.T, precision=EXACT)
    grad_wr = jnp.dot(normed_b.astype(jnp.float32).T, grad_logits, precision=EXACT)
    grad_hidden, grad_gain = norm_back(hidden, scale_m, gain_m, grad_normed)
    return (grad_in + grad_hidden, (grad_gain, grad_wr, grad_wg, grad_wu, grad_wd))


def on_device(
    tokens,
    cotangent,
    routes,
    attn_gain,
    w_query,
    key_weight,
    value_weight,
    w_out,
    moe_gain,
    w_router,
    w_gate,
    w_up,
    w_down,
):
    section_index = lax.axis_index("pipe")
    micro_batch_count = tokens.shape[0]
    sequence_length = tokens.shape[1]
    cosine, sine_table = rotary_tables(sequence_length)
    attn_params = (
        attn_gain[0].astype(jnp.float32),
        w_query[0],
        key_weight[0],
        value_weight[0],
        w_out[0],
    )
    mix_params = (moe_gain[0].astype(jnp.float32), w_router[0], w_gate[0], w_up[0], w_down[0])
    incoming = jnp.zeros_like(tokens[0])
    out_rows = jnp.zeros(tokens.shape, jnp.float32)
    kept_state = None
    for step_index in range(micro_batch_count + 1):
        micro_index = step_index - section_index
        is_live = (micro_index >= 0) & (micro_index < micro_batch_count)
        slot_index = jnp.clip(micro_index, 0, micro_batch_count - 1)
        source = jnp.where(
            section_index == 0, tokens[min(step_index, micro_batch_count - 1)], incoming
        )
        hidden, attn_saved = attend_forward(source, attn_params, cosine, sine_table)
        result, mix_saved = mix_forward(hidden, routes[0][slot_index], mix_params)
        layer_result = result.astype(jnp.bfloat16)
        saved = (source, hidden, attn_saved, mix_saved)
        if kept_state is None:
            kept_state = jax.tree.map(
                lambda fresh: jnp.zeros((micro_batch_count,) + fresh.shape, fresh.dtype), saved
            )
        kept_state = jax.tree.map(
            lambda stored, fresh: stored.at[slot_index].set(
                jnp.where(is_live, fresh, stored[slot_index])
            ),
            kept_state,
            saved,
        )
        out_rows = out_rows.at[slot_index].set(jnp.where(is_live, result, out_rows[slot_index]))
        if step_index < micro_batch_count:
            incoming = from_behind(layer_result, "pipe", 1)
    returning = jnp.zeros_like(tokens[0])
    in_grads = jnp.zeros(tokens.shape, jnp.float32)
    grad_sums = None
    for step_index in range(micro_batch_count + 1):
        micro_index = step_index - 1 + section_index
        is_live = (micro_index >= 0) & (micro_index < micro_batch_count)
        slot_index = jnp.clip(micro_index, 0, micro_batch_count - 1)
        grad_top = jnp.where(
            section_index == 1,
            cotangent[min(step_index, micro_batch_count - 1)],
            returning.astype(jnp.float32),
        )
        source, hidden, attn_saved, mix_saved = jax.tree.map(
            lambda stored: stored[slot_index], kept_state
        )
        grad_hidden, mix_grads = mix_backward(
            hidden, routes[0][slot_index], grad_top, mix_params, mix_saved
        )
        grad_source, attn_grads = attend_backward(
            source.astype(jnp.float32), grad_hidden, attn_params, attn_saved, cosine, sine_table
        )
        fresh_grads = attn_grads + mix_grads
        if grad_sums is None:
            grad_sums = jax.tree.map(jnp.zeros_like, fresh_grads)
        grad_sums = jax.tree.map(
            lambda stored, fresh: stored + jnp.where(is_live, fresh, 0.0), grad_sums, fresh_grads
        )
        in_grads = in_grads.at[slot_index].set(
            jnp.where(is_live, grad_source, in_grads[slot_index])
        )
        if step_index < micro_batch_count:
            returning = from_behind(grad_source.astype(jnp.bfloat16), "pipe", -1)
    gain_a_g, query_g, key_g, value_g, out_g, gain_m_g, router_g, gate_g, up_g, down_g = grad_sums
    gain_a_g, query_g, key_g, value_g, out_g, gain_m_g, router_g = lax.psum(
        (gain_a_g, query_g, key_g, value_g, out_g, gain_m_g, router_g), "expert"
    )
    return (
        out_rows[None],
        in_grads[None],
        gain_a_g[None],
        query_g[None],
        key_g[None],
        value_g[None],
        out_g[None],
        gain_m_g[None],
        router_g[None],
        gate_g[None],
        up_g[None],
        down_g[None],
    )


def solution(mesh):
    return jax.shard_map(
        on_device,
        mesh=mesh,
        in_specs=(
            P(None, "expert", None),
            P(None, "expert", None),
            P("pipe", None, "expert", None),
            P("pipe", None),
            P("pipe", None, "tensor"),
            P("pipe", None, "tensor"),
            P("pipe", None, "tensor"),
            P("pipe", "tensor", None),
            P("pipe", None),
            P("pipe", None, None),
            P("pipe", "expert", None, "tensor"),
            P("pipe", "expert", None, "tensor"),
            P("pipe", "expert", "tensor", None),
        ),
        out_specs=(
            P("pipe", None, "expert", None),
            P("pipe", None, "expert", None),
            P("pipe", None),
            P("pipe", None, "tensor"),
            P("pipe", None, "tensor"),
            P("pipe", None, "tensor"),
            P("pipe", "tensor", None),
            P("pipe", None),
            P("pipe", None, None),
            P("pipe", "expert", None, "tensor"),
            P("pipe", "expert", None, "tensor"),
            P("pipe", "expert", "tensor", None),
        ),
        check_vma=False,
    )
```

profile of v0, /device:TPU:0, one launch (start us, length us, event | category | flops | bytes accessed | tf_op | source)
XLA Modules:
  0.0 2450.3 jit_solution(727651331128074581)
XLA Ops:
  38.5 39.9 %all-reduce.13.cloned.1.call-done = f32[128,1536]{1,0:T(8,128)} async-done(((f32[128,1536]{1,0:T(8,128)}), f32[128,1536]{1,0:T(8,128)}) %all-reduce.13.cloned.1.call-update) | async-done | bytes 786448 | tf_op jit(solution)/shard_map/psum | solution.py:150
  83.9 51.0 %all_to_all.60 = bf16[32,32,1536]{2,1,0:T(8,128)(2,1)S(1)} all-to-all(bf16[32,32,1536]{2,1,0:T(8,128)(2,1)S(1)} %bitcast.1399), channel_id=1, replica_groups=mesh['pipe'=2,'expert'=32,'tensor'=2] {'expert'}, dimensions={0} | all-to-all | bytes 6291456 | tf_op jit(solution)/shard_map/all_to_all | solution.py:238
  150.3 145.2 %all-reduce.26 = bf16[1,1024,1536]{2,1,0:T(8,128)(2,1)} all-reduce(f32[1,1024,1536]{2,1,0:T(8,128)} %convolution_bitcast_fusion.2), channel_id=1, replica_groups=mesh['pipe'=2,'expert'=32,'tensor'=2] {'tensor'}, use_global_device_ids=true, to_apply=%region_13.14 | all-reduce | flops 1572864 | bytes 9437184 | tf_op jit(solution)/shard_map/psum | solution.py:246
  295.5 4.9 all-to-all-start.1
  306.3 35.5 %all-to-all-done.1 = bf16[32,32,1536]{2,1,0:T(8,128)(2,1)} async-done(((bf16[32,32,1536]{2,1,0:T(8,128)(2,1)}), bf16[32,32,1536]{2,1,0:T(8,128)(2,1)}, u32[]{:S(2)}, u32[]{:S(2)}) %all-to-all-start.1) | async-done | bytes 3145760 | tf_op jit(solution)/shard_map/all_to_all | solution.py:247
  341.7 5.0 multiply_reduce_fusion.2
  391.3 26.3 %all-reduce.15.cloned.1.call-done = f32[128,1536]{1,0:T(8,128)} async-done(((f32[128,1536]{1,0:T(8,128)}), f32[128,1536]{1,0:T(8,128)}) %all-reduce.15.cloned.1.call-update) | async-done | bytes 786448 | tf_op jit(solution)/shard_map/psum | solution.py:150
  423.5 9.5 all-to-all-start.2
  436.8 41.4 %all-to-all-done.2 = bf16[32,32,1536]{2,1,0:T(8,128)(2,1)} async-done(((bf16[32,32,1536]{2,1,0:T(8,128)(2,1)}), bf16[32,32,1536]{2,1,0:T(8,128)(2,1)}, u32[]{:S(2)}, u32[]{:S(2)}) %all-to-all-start.2) | async-done | bytes 3145760 | tf_op jit(solution)/shard_map/all_to_all | solution.py:238
  478.2 6.9 fusion.130
  485.1 4.4 fusion.133
  491.3 4.4 convolution_bitcast_fusion.1
  495.7 144.8 %all-reduce.27 = bf16[1,1024,1536]{2,1,0:T(8,128)(2,1)} all-reduce(f32[1,1024,1536]{2,1,0:T(8,128)} %convolution_bitcast_fusion.1), channel_id=1, replica_groups=mesh['pipe'=2,'expert'=32,'tensor'=2] {'tensor'}, use_global_device_ids=true, to_apply=%region_28.29 | all-reduce | flops 1572864 | bytes 9437184 | tf_op jit(solution)/shard_map/psum | solution.py:246
  640.5 7.0 all-to-all-start.3
  651.4 37.9 %all-to-all-done.3 = bf16[32,32,1536]{2,1,0:T(8,128)(2,1)} async-done(((bf16[32,32,1536]{2,1,0:T(8,128)(2,1)}), bf16[32,32,1536]{2,1,0:T(8,128)(2,1)}, u32[]{:S(2)}, u32[]{:S(2)}) %all-to-all-start.3) | async-done | bytes 3145760 | tf_op jit(solution)/shard_map/all_to_all | solution.py:247
  689.4 5.0 multiply_reduce_fusion.1
  737.2 24.1 all-reduce.17.cloned.1.call-done
  768.0 9.5 all-to-all-start.4
  802.0 20.7 all-to-all-done.4
  822.7 6.8 fusion.129
  840.0 145.0 %all-reduce.28 = bf16[1,1024,1536]{2,1,0:T(8,128)(2,1)} all-reduce(f32[1,1024,1536]{2,1,0:T(8,128)} %convolution_bitcast_fusion), channel_id=1, replica_groups=mesh['pipe'=2,'expert'=32,'tensor'=2] {'tensor'}, use_global_device_ids=true, to_apply=%region_43.44 | all-reduce | flops 1572864 | bytes 9437184 | tf_op jit(solution)/shard_map/psum | solution.py:246
  985.0 6.9 all-to-all-start.5
  1006.5 27.3 %all-to-all-done.5 = bf16[32,32,1536]{2,1,0:T(8,128)(2,1)} async-done(((bf16[32,32,1536]{2,1,0:T(8,128)(2,1)}), bf16[32,32,1536]{2,1,0:T(8,128)(2,1)}, u32[]{:S(2)}, u32[]{:S(2)}) %all-to-all-start.5) | async-done | bytes 3145760 | tf_op jit(solution)/shard_map/all_to_all | solution.py:247
  1033.8 4.8 multiply_reduce_fusion
  1043.8 46.3 %all_to_all.61 = bf16[32,32,1536]{2,1,0:T(8,128)(2,1)S(1)} all-to-all(bf16[32,32,1536]{2,1,0:T(8,128)(2,1)S(1)} %bitcast.1427), channel_id=1, replica_groups=mesh['pipe'=2,'expert'=32,'tensor'=2] {'expert'}, dimensions={0} | all-to-all | bytes 6291456 | tf_op jit(solution)/shard_map/all_to_all | solution.py:283
  1094.3 4.5 add_bitcast_fusion.2
  1098.8 75.0 %reduce-scatter.4.cloned.1.call-done = f32[1,1024,768]{2,1,0:T(8,128)} async-done(((f32[1,1024,1536]{2,1,0:T(8,128)}), f32[1,1024,768]{2,1,0:T(8,128)}) %reduce-scatter.4.cloned.1.call-update) | async-done | bytes 3145744 | tf_op jit(solution)/shard_map/reduce_scatter | solution.py:304
  1177.0 9.5 all-to-all-start.7
  1200.5 11.0 all-to-all-done.7
  1231.4 23.7 all-gather.4.cloned.1.call-done
  1282.0 33.1 %all-reduce.19.cloned.1.call-done = f32[128,1536]{1,0:T(8,128)} async-done(((f32[128,1536]{1,0:T(8,128)}), f32[128,1536]{1,0:T(8,128)}) %all-reduce.19.cloned.1.call-update) | async-done | bytes 786448 | tf_op jit(solution)/shard_map/psum | solution.py:211
  1336.7 52.5 %all_to_all.62 = bf16[32,32,1536]{2,1,0:T(8,128)(2,1)S(1)} all-to-all(bf16[32,32,1536]{2,1,0:T(8,128)(2,1)S(1)} %bitcast.1428), channel_id=1, replica_groups=mesh['pipe'=2,'expert'=32,'tensor'=2] {'expert'}, dimensions={0} | all-to-all | bytes 6291456 | tf_op jit(solution)/shard_map/all_to_all | solution.py:283
  1393.4 4.5 add_bitcast_fusion.1
  1397.9 75.2 %reduce-scatter.6.cloned.1.call-done = f32[1,1024,768]{2,1,0:T(8,128)} async-done(((f32[1,1024,1536]{2,1,0:T(8,128)}), f32[1,1024,768]{2,1,0:T(8,128)}) %reduce-scatter.6.cloned.1.call-update) | async-done | bytes 3145744 | tf_op jit(solution)/shard_map/reduce_scatter | solution.py:304
  1475.2 34.2 %all_to_all.63 = bf16[32,32,768]{2,1,0:T(8,128)(2,1)} all-to-all(bf16[32,32,768]{2,1,0:T(8,128)(2,1)S(1)} %bitcast.1409), channel_id=1, replica_groups=mesh['pipe'=2,'expert'=32,'tensor'=2] {'expert'}, dimensions={0} | all-to-all | bytes 3145728 | tf_op jit(solution)/shard_map/all_to_all | solution.py:307
  1515.4 37.0 %all-gather.6.cloned.1.call-done = bf16[32,32,1536]{2,1,0:T(8,128)(2,1)} async-done(((bf16[32,32,768]{2,1,0:T(8,128)(2,1)}), bf16[32,32,1536]{2,1,0:T(8,128)(2,1)}) %all-gather.6.cloned.1.call-update) | async-done | bytes 3145744 | tf_op jit(solution)/shard_map/all_gather | solution.py:314
  1577.6 34.7 %all-reduce.21.cloned.1.call-done = f32[128,1536]{1,0:T(8,128)} async-done(((f32[128,1536]{1,0:T(8,128)}), f32[128,1536]{1,0:T(8,128)}) %all-reduce.21.cloned.1.call-update) | async-done | bytes 786448 | tf_op jit(solution)/shard_map/psum | solution.py:211
  1633.9 52.3 %all_to_all.64 = bf16[32,32,1536]{2,1,0:T(8,128)(2,1)S(1)} all-to-all(bf16[32,32,1536]{2,1,0:T(8,128)(2,1)S(1)} %bitcast.1429), channel_id=1, replica_groups=mesh['pipe'=2,'expert'=32,'tensor'=2] {'expert'}, dimensions={0} | all-to-all | bytes 6291456 | tf_op jit(solution)/shard_map/all_to_all | solution.py:283
  1690.3 4.5 add_bitcast_fusion
  1694.8 75.3 %reduce-scatter.8.cloned.1.call-done = f32[1,1024,768]{2,1,0:T(8,128)} async-done(((f32[1,1024,1536]{2,1,0:T(8,128)}), f32[1,1024,768]{2,1,0:T(8,128)}) %reduce-scatter.8.cloned.1.call-update) | async-done | bytes 3145744 | tf_op jit(solution)/shard_map/reduce_scatter | solution.py:304
  1773.3 9.5 all-to-all-start.11
  1789.4 18.4 all-to-all-done.11
  1834.6 16.7 all-gather.8.cloned.1.call-done
  1871.5 5.9 add_bitcast_fusion.3
  1880.1 5.8 add_bitcast_fusion.4
  1926.2 185.0 %all-reduce = (f32[1,1536]{1,0:T(1,128)}, f32[1,1536]{1,0:T(1,128)}) all-reduce(f32[1,1536]{1,0:T(1,128)S(1)} %broadcast_in_dim.154, f32[1,1536]{1,0:T(1,128)S(1)} %broadcast_in_dim.163), channel_id=1, replica_groups=mesh['pipe'=2,'expert'=32,'tensor'=2] {'expert'}, use_global_device_ids=true, to_apply=%region_93.94 | all-reduce | flops 3072 | bytes 24576 | tf_op jit(solution)/shard_map/psum | solution.py:416
  2114.9 318.9 %all-reduce.25.cloned.1.call-done = (f32[1,1536,768]{2,1,0:T(8,128)}, f32[1,1536,128]{2,1,0:T(8,128)}, f32[1,1536,128]{2,1,0:T(8,128)}, f32[1,768,1536]{2,1,0:T(8,128)}, f32[1,1536,32]{1,2,0:T(8,128)}) async-done(((f32[1,1536,768]{2,1,0:T(8,128)}, f32[1,1536,128]{2,1,0:T(8,128)}, f32[1,1536,128]{2,1,0:T(8,128)}, f32[1,768,1536]{2,1,0:T(8,128)}, f32[1,1536,32]{1,2,0:T(8,128)}), (f32[1,1536,768]{2,1,0:T(8,128)}, ...) | async-done | bytes 11206672 | tf_op jit(solution)/shard_map/psum | solution.py:416
  2433.7 5.0 copy.491
  (940 shorter events, 479.8 us)
Async XLA Ops:
  7.2 71.1 %all-reduce.13.cloned.1.call-start = ((), (), s32[]{:S(2)}) async-start(), calls=%async_computation.15 | async-start | bytes 1572864 | tf_op jit(solution)/shard_map/psum | solution.py:150
  7.3 366.1 %copy-start.137 = (pred[128,128]{0,1:T(8,128)(4,1)}, pred[128,128]{0,1:T(8,128)(4,1)S(1)}, u32[]{:S(2)}) copy-start(pred[128,128]{0,1:T(8,128)(4,1)S(1)} %iota_compare_fusion.30) | copy-start | bytes 49156
  11.9 359.8 %copy-start.72 = (f32[128,64]{1,0:T(8,128)}, f32[128,64]{1,0:T(8,128)S(1)}, u32[]{:S(2)}) copy-start(f32[128,64]{1,0:T(8,128)S(1)} %get-tuple-element.709) | copy-start | bytes 98308
  11.9 359.8 %copy-start.76 = (f32[128,64]{1,0:T(8,128)}, f32[128,64]{1,0:T(8,128)S(1)}, u32[]{:S(2)}) copy-start(f32[128,64]{1,0:T(8,128)S(1)} %get-tuple-element.710) | copy-start | bytes 98308
  17.2 345.8 %copy-start.55 = (f32[128,128]{0,1:T(8,128)}, f32[128,128]{0,1:T(8,128)S(1)}, u32[]{:S(2)}) copy-start(f32[128,128]{0,1:T(8,128)S(1)} %copy.284) | copy-start | bytes 196612
  35.3 47.3 %copy-start.197 = (s32[1,1,128,4]{2,3,1,0:T(4,128)}, s32[1,1,128,4]{2,3,1,0:T(4,128)S(1)}, u32[]{:S(2)}) copy-start(s32[1,1,128,4]{2,3,1,0:T(4,128)S(1)} %get-tuple-element.697) | copy-start | bytes 6148
  35.3 265.4 %copy-start.195 = (s32[1,1,128,4]{2,3,1,0:T(4,128)}, s32[1,1,128,4]{2,3,1,0:T(4,128)S(1)}, u32[]{:S(2)}) copy-start(s32[1,1,128,4]{2,3,1,0:T(4,128)S(1)} %get-tuple-element.696) | copy-start | bytes 6148
  37.5 45.3 %copy-start.219 = (s32[128,4]{0,1:T(4,128)}, s32[128,4]{0,1:T(4,128)S(1)}, u32[]{:S(2)}) copy-start(s32[128,4]{0,1:T(4,128)S(1)} %multiply_add_fusion.5) | copy-start | bytes 6148
  82.7 52.1 %copy-start.251 = (f32[128]{0:T(128)}, f32[128]{0:T(128)S(1)}, u32[]{:S(2)}) copy-start(f32[128]{0:T(128)S(1)} %multiply_reduce_fusion.5) | copy-start | bytes 1540
  82.8 52.1 %copy-start.237 = (f32[128]{0:T(128)}, f32[128]{0:T(128)S(1)}, u32[]{:S(2)}) copy-start(f32[128]{0:T(128)S(1)} %add_rsqrt_fusion.4) | copy-start | bytes 1540
  295.5 46.2 %all-to-all-start.1 = ((bf16[32,32,1536]{2,1,0:T(8,128)(2,1)}), bf16[32,32,1536]{2,1,0:T(8,128)(2,1)}, u32[]{:S(2)}, u32[]{:S(2)}) async-start(bf16[32,32,1536]{2,1,0:T(8,128)(2,1)} %bitcast.1405), calls=%async_computation.1 | async-start | bytes 6291456 | tf_op jit(solution)/shard_map/all_to_all | solution.py:247
  300.4 117.2 %all-reduce.15.cloned.1.call-start = ((), (), s32[]{:S(2)}) async-start(), calls=%async_computation.16 | async-start | bytes 1572864 | tf_op jit(solution)/shard_map/psum | solution.py:150
  347.8 5.5 collective-permute-start
  423.5 54.7 %all-to-all-start.2 = ((bf16[32,32,1536]{2,1,0:T(8,128)(2,1)}), bf16[32,32,1536]{2,1,0:T(8,128)(2,1)}, u32[]{:S(2)}, u32[]{:S(2)}) async-start(bf16[32,32,1536]{2,1,0:T(8,128)(2,1)} %bitcast.1398), calls=%async_computation.2 | async-start | bytes 6291456 | tf_op jit(solution)/shard_map/all_to_all | solution.py:238
  640.5 48.9 %copy-start.217 = (s32[128,4]{0,1:T(4,128)S(1)}, s32[128,4]{0,1:T(4,128)}, u32[]{:S(2)}) copy-start(s32[128,4]{0,1:T(4,128)} %copy-done.216) | copy-start | bytes 6148
  640.5 48.9 %all-to-all-start.3 = ((bf16[32,32,1536]{2,1,0:T(8,128)(2,1)}), bf16[32,32,1536]{2,1,0:T(8,128)(2,1)}, u32[]{:S(2)}, u32[]{:S(2)}) async-start(bf16[32,32,1536]{2,1,0:T(8,128)(2,1)} %bitcast.1404), calls=%async_computation.3 | async-start | bytes 6291456 | tf_op jit(solution)/shard_map/all_to_all | solution.py:247
  647.5 113.8 %all-reduce.17.cloned.1.call-start = ((), (), s32[]{:S(2)}) async-start(), calls=%async_computation.17 | async-start | bytes 1572864 | tf_op jit(solution)/shard_map/psum | solution.py:150
  651.4 43.1 %copy-start.175 = (f32[128,4]{0,1:T(4,128)}, f32[128,4]{0,1:T(4,128)S(1)}, u32[]{:S(2)}) copy-start(f32[128,4]{0,1:T(4,128)S(1)} %multiply_reduce_fusion.13) | copy-start | bytes 6148
  651.4 43.0 %copy-start.226 = (f32[128]{0:T(128)}, f32[128]{0:T(128)S(1)}, u32[]{:S(2)}) copy-start(f32[128]{0:T(128)S(1)} %reduce_max.57) | copy-start | bytes 1540
  651.4 43.0 %copy-start.234 = (f32[128]{0:T(128)}, f32[128]{0:T(128)S(1)}, u32[]{:S(2)}) copy-start(f32[128]{0:T(128)S(1)} %fusion.502) | copy-start | bytes 1540
  694.6 2.9 collective-permute-start.1
  768.0 54.7 %all-to-all-start.4 = ((bf16[32,32,1536]{2,1,0:T(8,128)(2,1)}), bf16[32,32,1536]{2,1,0:T(8,128)(2,1)}, u32[]{:S(2)}, u32[]{:S(2)}) async-start(bf16[32,32,1536]{2,1,0:T(8,128)(2,1)} %bitcast.1403), calls=%async_computation.4 | async-start | bytes 6291456 | tf_op jit(solution)/shard_map/all_to_all | solution.py:238
  985.0 48.9 %all-to-all-start.5 = ((bf16[32,32,1536]{2,1,0:T(8,128)(2,1)}), bf16[32,32,1536]{2,1,0:T(8,128)(2,1)}, u32[]{:S(2)}, u32[]{:S(2)}) async-start(bf16[32,32,1536]{2,1,0:T(8,128)(2,1)} %bitcast.1402), calls=%async_computation.5 | async-start | bytes 6291456 | tf_op jit(solution)/shard_map/all_to_all | solution.py:247
  991.8 182.0 %reduce-scatter.4.cloned.1.call-start = ((), (), s32[]{:S(2)}) async-start(), calls=%async_computation.18 | async-start | bytes 9437184 | tf_op jit(solution)/shard_map/reduce_scatter | solution.py:304
  1040.0 50.1 %copy-start.8 = (bf16[2,128,4,1536]{3,1,2,0:T(8,128)(2,1)}, bf16[2,128,4,1536]{3,1,2,0:T(8,128)(2,1)S(1)}, u32[]{:S(2)}) copy-start(bf16[2,128,4,1536]{3,1,2,0:T(8,128)(2,1)S(1)} %fusion.119) | copy-start | bytes 9437188
  1041.5 48.5 %copy-start.259 = (bf16[1,1,384,1536]{3,2,1,0:T(8,128)(2,1)S(1)}, bf16[1,1,384,1536]{3,2,1,0:T(8,128)(2,1)}, u32[]{:S(2)}) copy-start(bf16[1,1,384,1536]{3,2,1,0:T(8,128)(2,1)} %param.121) | copy-start | bytes 3538948
  1043.8 46.3 %copy-start.29 = (f32[2,1,1024,384]{3,2,1,0:T(8,128)S(1)}, f32[2,1,1024,384]{3,2,1,0:T(8,128)}, u32[]{:S(2)}) copy-start(f32[2,1,1024,384]{3,2,1,0:T(8,128)} %get-tuple-element.727) | copy-start | bytes 9437188
  1043.8 46.3 %copy-start.39 = (f32[2,1,1024,384]{3,2,1,0:T(8,128)S(1)}, f32[2,1,1024,384]{3,2,1,0:T(8,128)}, u32[]{:S(2)}) copy-start(f32[2,1,1024,384]{3,2,1,0:T(8,128)} %copy-done.38) | copy-start | bytes 9437188
  1177.0 34.5 %all-to-all-start.7 = ((bf16[32,32,768]{2,1,0:T(8,128)(2,1)}), bf16[32,32,768]{2,1,0:T(8,128)(2,1)}, u32[]{:S(2)}, u32[]{:S(2)}) async-start(bf16[32,32,768]{2,1,0:T(8,128)(2,1)} %bitcast.1408), calls=%async_computation.8 | async-start | bytes 3145728 | tf_op jit(solution)/shard_map/all_to_all | solution.py:307
  1186.5 68.6 %all-gather.4.cloned.1.call-start = ((), (), s32[]{:S(2)}) async-start(), calls=%async_computation.19 | async-start | bytes 4718592 | tf_op jit(solution)/shard_map/all_gather | solution.py:314
  1211.6 103.5 %all-reduce.19.cloned.1.call-start = ((), (), s32[]{:S(2)}) async-start(), calls=%async_computation.20 | async-start | bytes 1572864 | tf_op jit(solution)/shard_map/psum | solution.py:211
  1272.9 200.2 %reduce-scatter.6.cloned.1.call-start = ((), (), s32[]{:S(2)}) async-start(), calls=%async_computation.21 | async-start | bytes 9437184 | tf_op jit(solution)/shard_map/reduce_scatter | solution.py:304
  1319.8 10.6 collective-permute-start.2
  1334.5 54.8 %copy-start.260 = (bf16[1,1,384,1536]{3,2,1,0:T(8,128)(2,1)S(1)}, bf16[1,1,384,1536]{3,2,1,0:T(8,128)(2,1)}, u32[]{:S(2)}) copy-start(bf16[1,1,384,1536]{3,2,1,0:T(8,128)(2,1)} %param.121) | copy-start | bytes 3538948
  1336.7 52.5 %copy-start.30 = (f32[2,1,1024,384]{3,2,1,0:T(8,128)S(1)}, f32[2,1,1024,384]{3,2,1,0:T(8,128)}, u32[]{:S(2)}) copy-start(f32[2,1,1024,384]{3,2,1,0:T(8,128)} %get-tuple-element.727) | copy-start | bytes 9437188
  1336.7 52.5 %copy-start.40 = (f32[2,1,1024,384]{3,2,1,0:T(8,128)S(1)}, f32[2,1,1024,384]{3,2,1,0:T(8,128)}, u32[]{:S(2)}) copy-start(f32[2,1,1024,384]{3,2,1,0:T(8,128)} %copy-done.38) | copy-start | bytes 9437188
  1397.9 154.5 %all-gather.6.cloned.1.call-start = ((), (), s32[]{:S(2)}) async-start(), calls=%async_computation.22 | async-start | bytes 4718592 | tf_op jit(solution)/shard_map/all_gather | solution.py:314
  1509.5 102.9 %all-reduce.21.cloned.1.call-start = ((), (), s32[]{:S(2)}) async-start(), calls=%async_computation.23 | async-start | bytes 1572864 | tf_op jit(solution)/shard_map/psum | solution.py:211
  1570.2 199.9 %reduce-scatter.8.cloned.1.call-start = ((), (), s32[]{:S(2)}) async-start(), calls=%async_computation.24 | async-start | bytes 9437184 | tf_op jit(solution)/shard_map/reduce_scatter | solution.py:304
  1617.1 10.5 collective-permute-start.3
  1631.6 54.5 %copy-start.261 = (bf16[1,1,384,1536]{3,2,1,0:T(8,128)(2,1)S(1)}, bf16[1,1,384,1536]{3,2,1,0:T(8,128)(2,1)}, u32[]{:S(2)}) copy-start(bf16[1,1,384,1536]{3,2,1,0:T(8,128)(2,1)} %param.121) | copy-start | bytes 3538948
  1633.9 52.3 %copy-start.31 = (f32[2,1,1024,384]{3,2,1,0:T(8,128)S(1)}, f32[2,1,1024,384]{3,2,1,0:T(8,128)}, u32[]{:S(2)}) copy-start(f32[2,1,1024,384]{3,2,1,0:T(8,128)} %get-tuple-element.727) | copy-start | bytes 9437188
  1633.9 52.3 %copy-start.41 = (f32[2,1,1024,384]{3,2,1,0:T(8,128)S(1)}, f32[2,1,1024,384]{3,2,1,0:T(8,128)}, u32[]{:S(2)}) copy-start(f32[2,1,1024,384]{3,2,1,0:T(8,128)} %copy-done.38) | copy-start | bytes 9437188
  1773.3 34.5 %all-to-all-start.11 = ((bf16[32,32,768]{2,1,0:T(8,128)(2,1)}), bf16[32,32,768]{2,1,0:T(8,128)(2,1)}, u32[]{:S(2)}, u32[]{:S(2)}) async-start(bf16[32,32,768]{2,1,0:T(8,128)(2,1)} %bitcast.1407), calls=%async_computation.14 | async-start | bytes 3145728 | tf_op jit(solution)/shard_map/all_to_all | solution.py:307
  1782.8 68.5 %all-gather.8.cloned.1.call-start = ((), (), s32[]{:S(2)}) async-start(), calls=%async_computation.25 | async-start | bytes 4718592 | tf_op jit(solution)/shard_map/all_gather | solution.py:314
  1807.8 117.0 %all-reduce.23.cloned.1.call-start = ((), (), s32[]{:S(2)}) async-start(), calls=%async_computation.26 | async-start | bytes 1572864 | tf_op jit(solution)/shard_map/psum | solution.py:211
  1871.2 562.5 %all-reduce.25.cloned.1.call-start = ((), (), s32[]{:S(2)}) async-start(), calls=%async_computation.27 | async-start | bytes 22413312 | tf_op jit(solution)/shard_map/psum | solution.py:416
  1921.7 189.6 %copy-start.239 = (f32[128]{0:T(128)S(1)}, f32[128]{0:T(128)}, u32[]{:S(2)}) copy-start(f32[128]{0:T(128)} %get-tuple-element.618) | copy-start | bytes 1540
  (240 other events, 1102.2 us)
Sparse Core Ops, SparseCore 0:
  34.8 43.4 all-reduce.12
  377.5 40.0 all-reduce.14
  722.4 38.8 all-reduce.16
  1098.9 74.8 reduce-scatter.3
  1211.7 43.3 all-gather.3
  1273.0 41.9 all-reduce.18
  1398.0 75.0 reduce-scatter.5
  1509.6 42.7 all-gather.5
  1570.3 42.0 all-reduce.20
  1695.0 75.1 reduce-scatter.7
  1807.9 43.3 all-gather.7
  1871.3 42.0 all-reduce.22
  1917.1 516.5 all-reduce.24
where the time goes:
time: 2470 us; the launch traced here: 2450 us
  waiting for transfers between devices  972 us (39%)
  blocking collectives  856 us (35%)
  matrix products  226 us (9%)
  other arithmetic  189 us (8%)
  local copies, waits for them, and re-layouts  125 us (5%)
  starting transfers between devices  63.9 us (3%)
    psum x3, blocking collectives, mix_forward(): summed = lax.psum(partial_value, 'tensor').astype(jnp.bfloat16)  435 us
    psum x1, waiting for transfers between devices, on_device(): lax.psum((gain_a_g, query_g, key_g, value_g, out_g, gain_m_g, router_g),...  319 us
    reduce_scatter x3, waiting for transfers between devices, mix_backward(): lax.psum_scatter(grad_inputs, 'tensor', scatter_dimension=2, tiled=True)  226 us
    psum x1, blocking collectives, on_device(): lax.psum((gain_a_g, query_g, key_g, value_g, out_g, gain_m_g, router_g),...  185 us
    all_to_all x3, blocking collectives, mix_backward(): lax.all_to_all(outgoing, 'expert', split_axis=0, concat_axis=0, tiled=True)  151 us
    all_to_all x3, waiting for transfers between devices, mix_forward(): lax.all_to_all(from_expert(summed, local_count, capacity), 'expert', spli...  101 us
    psum x3, waiting for transfers between devices, attend_forward(): lax.psum(jnp.dot(attended, w_out, preferred_element_type=jnp.float32), 't...  90.3 us
    all_gather x3, waiting for transfers between devices, mix_backward(): back_rows = lax.all_gather(back_rows, 'tensor', axis=2, tiled=True)  77.3 us
  transfers between devices with their start and end apart: 24, of which 19 were waited for; matrix products, arithmetic and copies ran while one was open for 10% of the time, Pallas kernels for 0%

commit v1 on v0

v1 whole, which is shorter than its diff:
```python
import jax
import jax.numpy as jnp
from jax import lax
from jax.sharding import PartitionSpec as P

HEAD = 128
NORM_EPS = 1e-06
ROPE_BASE = 10000.0
BF16 = jnp.bfloat16
F32 = jnp.float32
SWAP = [(0, 1), (1, 0)]


def swap(value, axis):
    return lax.ppermute(value, axis, SWAP)


def expert_exchange(value):
    return lax.all_to_all(value, "expert", split_axis=0, concat_axis=0, tiled=True)


def mul(left, right, dims):
    return lax.dot_general(left, right, (dims, ((), ())), preferred_element_type=F32)


def mul_nn(left, right):
    return mul(left, right, ((1,), (0,)))


def mul_nt(left, right):
    return mul(left, right, ((1,), (1,)))


def mul_tn(left, right):
    return mul(left, right, ((0,), (0,)))


def rotary_tables(count):
    half = HEAD // 2
    frequency = ROPE_BASE ** (-(jnp.arange(half, dtype=F32) * 2.0) / HEAD)
    angles = jnp.arange(count, dtype=F32)[:, None] * frequency[None, :]
    cosine = jnp.concatenate([jnp.cos(angles), jnp.cos(angles)], axis=1)
    sine = jnp.concatenate([jnp.sin(angles), jnp.sin(angles)], axis=1)
    return cosine, sine


def turn(vector, cosine, sine):
    half = HEAD // 2
    moved = jnp.concatenate([-vector[..., half:], vector[..., :half]], axis=-1)
    return vector * cosine + moved * sine


def turn_back(grad, cosine, sine):
    half = HEAD // 2
    moved = grad * sine
    return grad * cosine + jnp.concatenate([moved[..., half:], -moved[..., :half]], axis=-1)


def row_scale_of(rows):
    return lax.rsqrt(jnp.mean(rows * rows, axis=-1, keepdims=True) + NORM_EPS)


def norm_back(rows, scale, gain, grad):
    scaled = grad * gain
    grad_gain = jnp.sum(grad * rows * scale, axis=0)
    grad_rows = scale * scaled - rows * scale**3 * jnp.mean(scaled * rows, axis=-1, keepdims=True)
    return grad_rows, grad_gain


def causal(count):
    return jnp.arange(count)[:, None] >= jnp.arange(count)[None, :]


def attend_forward(x, gain, wq, wk, wv, wo, cosine, sine):
    scale = row_scale_of(x)
    normed = (x * scale * gain).astype(BF16)
    count, heads = x.shape[0], wq.shape[1] // HEAD
    q = mul_nn(normed, wq).reshape(count, heads, HEAD)
    q = (turn(q, cosine[:, None], sine[:, None]) * HEAD**-0.5).astype(BF16)
    k = turn(mul_nn(normed, wk), cosine, sine).astype(BF16)
    v = mul_nn(normed, wv).astype(BF16)
    scores = jnp.einsum("shd,td->hst", q, k, preferred_element_type=F32)
    scores = jnp.where(causal(count), scores, -1e30)
    raised = jnp.exp(scores - jnp.max(scores, axis=-1, keepdims=True))
    weights = raised / jnp.sum(raised, axis=-1, keepdims=True)
    o = jnp.einsum("hst,td->shd", weights.astype(BF16), v, preferred_element_type=F32)
    o = o.reshape(count, heads * HEAD).astype(BF16)
    return mul_nn(o, wo).astype(BF16), (scale, normed, q, k, v, weights, o)


def attend_backward(dz, saved, wq, wk, wv, wo, cosine, sine):
    scale, normed, q, k, v, weights, o = saved
    count, heads = q.shape[0], q.shape[1]
    grad_out = mul_tn(o, dz)
    do = mul_nt(dz, wo).astype(BF16).reshape(count, heads, HEAD)
    dp = jnp.einsum("shd,td->hst", do, v, preferred_element_type=F32)
    ds = (weights * (dp - jnp.sum(weights * dp, axis=-1, keepdims=True))).astype(BF16)
    dv = jnp.einsum("hst,shd->td", weights.astype(BF16), do, preferred_element_type=F32).astype(BF16)
    dq = jnp.einsum("hst,td->shd", ds, k, preferred_element_type=F32)
    dq = (turn_back(dq, cosine[:, None], sine[:, None]) * HEAD**-0.5).astype(BF16)
    dq = dq.reshape(count, heads * HEAD)
    dk = jnp.einsum("hst,shd->td", ds, q, preferred_element_type=F32)
    dk = turn_back(dk, cosine, sine).astype(BF16)
    da = mul_nt(dq, wq) + mul_nt(dk, wk) + mul_nt(dv, wv)
    grads = (mul_tn(normed, dq), mul_tn(normed, dk), mul_tn(normed, dv), grad_out)
    return da.astype(BF16), grads


def slot_table(routes, experts, lanes, part):
    count = routes.shape[0]
    names = jnp.arange(experts, dtype=jnp.int32)
    hot = jnp.any(routes.T[:, None, :] == names[None, :, None], axis=0)
    before = (jnp.arange(count)[:, None] < jnp.arange(count)[None, :]).astype(BF16)
    rank = mul_nn(hot.astype(BF16), before).astype(jnp.int32)
    lane = jnp.arange(lanes, dtype=jnp.int32) + part * lanes
    chosen = hot[:, None, :] & (rank[:, None, :] == lane[None, :, None])
    return hot, chosen.reshape(experts * lanes, count).astype(BF16)


def gates_of(normed, w_router, hot):
    logits = mul(w_router, normed, ((0,), (1,)))
    logits = jnp.where(hot, logits, -1e30)
    raised = jnp.where(hot, jnp.exp(logits - jnp.max(logits, axis=0, keepdims=True)), 0.0)
    return raised / jnp.sum(raised, axis=0, keepdims=True)


def gated_table(table, gates):
    experts, count = gates.shape
    return (table.reshape(experts, -1, count) * gates[:, None, :].astype(BF16)).reshape(-1, count)


def spread(table, rows, experts):
    sent = mul_nn(table, rows).astype(BF16)
    return expert_exchange(sent.reshape(experts, -1, rows.shape[1])).reshape(-1, rows.shape[1])


def send_back(rows, experts):
    return expert_exchange(rows.reshape(experts, -1, rows.shape[1])).reshape(-1, rows.shape[1])


def experts_forward(rows, weights):
    total = 0.0
    for w_gate, w_up, w_down in weights:
        gate, up = mul_nn(rows, w_gate), mul_nn(rows, w_up)
        total = total + mul_nn((jax.nn.silu(gate) * up).astype(BF16), w_down)
    return total.astype(BF16)


def experts_backward(rows, grads, weights):
    total, out = 0.0, []
    for w_gate, w_up, w_down in weights:
        gate, up = mul_nn(rows, w_gate), mul_nn(rows, w_up)
        sig = jax.nn.sigmoid(gate)
        act = gate * sig
        hidden = (act * up).astype(BF16)
        grad_hidden = mul_nt(grads, w_down)
        grad_gate = (grad_hidden * up * sig * (1.0 + gate * (1.0 - sig))).astype(BF16)
        grad_up = (grad_hidden * act).astype(BF16)
        total = total + mul_nt(grad_gate, w_gate) + mul_nt(grad_up, w_up)
        out.append((mul_tn(rows, grad_gate), mul_tn(rows, grad_up), mul_tn(hidden, grads)))
    return total.astype(BF16), out


def place(index):
    return index // 8, (index // 2) % 4, index % 2


def index_of(y, x, z):
    return (y * 4 + x) * 2 + z


def partners(axis, flip):
    pairs = []
    for source in range(32):
        y, x, z = place(source)
        target = index_of(y ^ flip, x, z) if axis == "y" else index_of(y, x ^ flip, z)
        pairs.append((source, target))
    return pairs


def halving_orders():
    y, x, _ = place(lax.axis_index("expert"))
    xs = [(partners("x", 1), (x ^ (x >> 1)) & 1), (partners("x", 3), x >> 1)]
    ys = [(partners("y", 1), (y ^ (y >> 1)) & 1), (partners("y", 3), y >> 1)]
    return [xs + ys, xs[::-1] + ys[::-1], ys + xs, ys[::-1] + xs[::-1]]


def expert_sum(value):
    parts = list(value.reshape(4, value.shape[0] // 4, value.shape[1]))
    orders = halving_orders()
    for step in range(4):
        for i in range(4):
            pairs, bit = orders[i][step]
            halves = parts[i].reshape(2, parts[i].shape[0] // 2, parts[i].shape[1])
            give = lax.dynamic_index_in_dim(halves, 1 - bit, 0, keepdims=False)
            keep = lax.dynamic_index_in_dim(halves, bit, 0, keepdims=False)
            parts[i] = keep + lax.ppermute(give, "expert", pairs)
    across = [(source, source ^ 1) for source in range(32)]
    for i in range(4):
        parts[i] = parts[i] + lax.ppermute(parts[i], "expert", across)
    for step in (3, 2, 1, 0):
        for i in range(4):
            pairs, bit = orders[i][step]
            mine = parts[i]
            other = lax.ppermute(mine, "expert", pairs)
            parts[i] = jnp.where(
                bit == 0, jnp.concatenate([mine, other]), jnp.concatenate([other, mine])
            )
    return jnp.concatenate(parts)


def on_device(
    tokens,
    cotangent,
    routes,
    attn_gain,
    w_query,
    key_weight,
    value_weight,
    w_out,
    moe_gain,
    w_router,
    w_gate,
    w_up,
    w_down,
):
    core = lax.axis_index("pipe")
    part = lax.axis_index("tensor")
    first = core == 0
    experts = w_router.shape[2]
    count = tokens.shape[1]
    lanes = 2 * routes.shape[3] * count // experts // 2

    def layers(value):
        other = swap(value, "pipe")
        return jnp.where(first, value, other), jnp.where(first, other, value)

    def own_layer(zero, one):
        return jnp.where(first, zero, one)

    attn_gains = [v.astype(F32) for v in layers(attn_gain[0])]
    moe_gains = [v.astype(F32) for v in layers(moe_gain[0])]
    routers = layers(w_router[0])
    wqs, wks, wvs, wos = (layers(v[0]) for v in (w_query, key_weight, value_weight, w_out))
    own_half = (w_gate[0, 0], w_up[0, 0], w_down[0, 0])
    far_half = tuple(swap(v, "tensor") for v in own_half)
    near = [layers(v) for v in own_half]
    far = [layers(v) for v in far_half]
    ffs = [
        (tuple(v[layer] for v in near), tuple(v[layer] for v in far)) for layer in range(2)
    ]
    mine = lax.dynamic_index_in_dim(routes[0], core, 0, keepdims=False)
    give = lax.dynamic_index_in_dim(routes[0], 1 - core, 0, keepdims=False)
    got = swap(give, "pipe")
    picks = [jnp.where(first, mine, got), jnp.where(first, got, mine)]

    cosine, sine = rotary_tables(count)
    x = lax.dynamic_index_in_dim(tokens, core, 0, keepdims=False).astype(F32)
    top = lax.dynamic_index_in_dim(cotangent, core, 0, keepdims=False)

    kept, outs = [], []
    for layer in range(2):
        weights = (wqs[layer], wks[layer], wvs[layer], wos[layer])
        branch, saved = attend_forward(x, attn_gains[layer], *weights, cosine, sine)
        h = x + (branch.astype(F32) + swap(branch, "tensor").astype(F32))
        scale = row_scale_of(h)
        normed = (h * scale * moe_gains[layer]).astype(BF16)
        hot, table = slot_table(picks[layer], experts, lanes, part)
        gates = gates_of(normed, routers[layer], hot)
        gated = gated_table(table, gates)
        rows = spread(table, normed, experts)
        made = experts_forward(rows, ffs[layer])
        back = send_back(made, experts)
        share = mul_tn(gated, back).astype(BF16)
        y = h + (share.astype(F32) + swap(share, "tensor").astype(F32))
        outs.append(y)
        kept.append((x, saved, h, scale, normed, table, gates, gated, rows, back, weights))
        x = y.astype(BF16).astype(F32)

    grad = top
    attn_grads, ff_grads, in_grads = [None, None], [None, None], [None, None]
    for layer in (1, 0):
        x, saved, h, scale, normed, table, gates, gated, rows, back, weights = kept[layer]
        grad_b = grad.astype(BF16)
        seen = (mul_nt(back, grad_b) * table.astype(F32)).reshape(experts, lanes, count)
        grad_gates = jnp.sum(seen, axis=1)
        grad_gates = grad_gates + swap(grad_gates, "tensor")
        dlogits = gates * (grad_gates - jnp.sum(gates * grad_gates, axis=0, keepdims=True))
        dlogits = dlogits.astype(BF16)
        grad_rows = spread(gated, grad_b, experts)
        dx, ff_grads[layer] = experts_backward(rows, grad_rows, ffs[layer])
        dback = send_back(dx, experts)
        share = mul_tn(table, dback).astype(BF16)
        grad_normed = share.astype(F32) + swap(share, "tensor").astype(F32)
        grad_normed = grad_normed + mul(dlogits, routers[layer], ((0,), (1,)))
        grad_router = mul(normed, dlogits, ((0,), (1,)))
        grad_h, grad_moe_gain = norm_back(h, scale, moe_gains[layer], grad_normed)
        grad_h = grad + grad_h
        da, attn = attend_backward(grad_h.astype(BF16), saved, *weights, cosine, sine)
        da = da.astype(F32) + swap(da, "tensor").astype(F32)
        grad_x, grad_attn_gain = norm_back(x, saved[0], attn_gains[layer], da)
        grad = grad_h + grad_x
        in_grads[layer] = grad
        dq, dk, dv, dout = (v.astype(BF16) for v in attn)
        side = jnp.concatenate(
            [grad_router, grad_attn_gain[:, None], grad_moe_gain[:, None]], axis=1
        )
        side = jnp.pad(side, ((0, 0), (0, 128 - side.shape[1]))).astype(BF16)
        width = dout.shape[1] // 2
        dout = jnp.concatenate([dout[:, :width], dout[:, width:]], axis=0)
        attn_grads[layer] = jnp.concatenate([dq, dk, dv, dout, side], axis=1)
        grad = grad.astype(BF16).astype(F32)

    def both_parts(zero, one):
        sent = own_layer(one, zero).astype(BF16)
        return own_layer(zero, one).astype(F32) + swap(sent, "pipe").astype(F32)

    packed = both_parts(attn_grads[0], attn_grads[1]).astype(BF16)
    packed = expert_sum(packed).astype(F32)
    ff_out = []
    for i in range(3):
        near_sum = both_parts(ff_grads[0][0][i], ff_grads[1][0][i])
        far_sum = both_parts(ff_grads[0][1][i], ff_grads[1][1][i])
        ff_out.append(near_sum + swap(far_sum.astype(BF16), "tensor").astype(F32))

    def by_layer(zero, one):
        own, other = own_layer(zero, one), own_layer(one, zero)
        got = swap(other, "pipe")
        return jnp.where(first, jnp.stack([own, got]), jnp.stack([got, own]))

    q_width, kv_width = w_query.shape[2], key_weight.shape[2]
    a, b = q_width + kv_width, q_width + 2 * kv_width
    c = b + w_out.shape[2] // 2
    half = w_out.shape[1]
    grad_out = jnp.concatenate([packed[:half, b:c], packed[half:, b:c]], axis=1)
    side = packed[:, c:]
    return (
        by_layer(*outs)[None],
        by_layer(*in_grads)[None],
        side[:, experts][None],
        packed[:, :q_width][None],
        packed[:, q_width:a][None],
        packed[:, a:b][None],
        grad_out[None],
        side[:, experts + 1][None],
        side[:, :experts][None],
        ff_out[0][None, None],
        ff_out[1][None, None],
        ff_out[2][None, None],
    )


def solution(mesh):
    layered = P("pipe", None, "expert", None)
    by_expert = P("pipe", "expert", None, "tensor")
    columns = P("pipe", None, "tensor")
    rows = P("pipe", "tensor", None)
    down = P("pipe", "expert", "tensor", None)
    whole = P("pipe", None)
    router = P("pipe", None, None)
    tokens = P(None, "expert", None)
    return jax.shard_map(
        on_device,
        mesh=mesh,
        in_specs=(
            tokens,
            tokens,
            layered,
            whole,
            columns,
            columns,
            columns,
            rows,
            whole,
            router,
            by_expert,
            by_expert,
            down,
        ),
        out_specs=(
            layered,
            layered,
            whole,
            columns,
            columns,
            columns,
            rows,
            whole,
            router,
            by_expert,
            by_expert,
            down,
        ),
        check_vma=False,
    )
```

time: 2470 us -> 766 us (0.31)
  blocking collectives: 856 us -> 0 us
  waiting for transfers between devices: 972 us -> 338 us
  other arithmetic: 189 us -> 77.3 us
  local copies, waits for them, and re-layouts: 125 us -> 49.5 us
  matrix products: 226 us -> 171 us
  starting transfers between devices: 63.9 us -> 116 us
    psum x4 -> x0, blocking collectives: 620 us -> none  [the longest x3 435 us: mix_forward(): summed = lax.psum(partial_value, 'tensor').astype(jnp.bfloat16)]
    psum x7 -> x0, waiting for transfers between devices: 477 us -> none  [the longest x1 319 us: on_device(): lax.psum((gain_a_g, query_g, key_g, value_g, out_g, gain_m_g, router_g),...]
    ppermute x4 -> x75, waiting for transfers between devices: 0.03 us -> 240 us  [the longest x39 198 us: swap(): return lax.ppermute(value, axis, SWAP)]
    all_to_all x5 -> x0, blocking collectives: 236 us -> none  [the longest x3 151 us: mix_backward(): lax.all_to_all(outgoing, 'expert', split_axis=0, concat_axis=0, tiled=True)]
    reduce_scatter x3 -> x0, waiting for transfers between devices: 226 us -> none  [mix_backward(): lax.psum_scatter(grad_inputs, 'tensor', scatter_dimension=2, tiled=True)]
    all_to_all x7 -> x8, waiting for transfers between devices: 192 us -> 97.8 us  [expert_exchange(): lax.all_to_all(value, 'expert', split_axis=0, concat_axis=0, tiled=True)]
    all_gather x3 -> x0, waiting for transfers between devices: 77.3 us -> none  [mix_backward(): back_rows = lax.all_gather(back_rows, 'tensor', axis=2, tiled=True)]
    scatter x37 -> x0, other arithmetic: 65.2 us -> none  [the longest x31 57.5 us: on_device(): stored.at[slot_index].set(jnp.where(is_live, fresh, stored[slot_index]))]
  transfers between devices with their start and end apart: 24 -> 83, of which waited for: 19 -> 36; matrix products, arithmetic and copies ran while one was open for 10% -> 30% of each run, Pallas kernels for 0% -> 0%
where the time goes in v1:
time: 766 us; the launch traced here: 755 us
  waiting for transfers between devices  338 us (44%)
  matrix products  171 us (22%)
  starting transfers between devices  116 us (15%)
  other arithmetic  77.3 us (10%)
  local copies, waits for them, and re-layouts  49.5 us (6%)
    ppermute x39, waiting for transfers between devices, swap(): return lax.ppermute(value, axis, SWAP)  198 us
    dot_general x78, matrix products, mul(): lax.dot_general(left, right, (dims, ((), ())), preferred_element_type=F32)  156 us
    all_to_all x8, waiting for transfers between devices, expert_exchange(): lax.all_to_all(value, 'expert', split_axis=0, concat_axis=0, tiled=True)  97.8 us
    all_to_all x8, starting transfers between devices, expert_exchange(): lax.all_to_all(value, 'expert', split_axis=0, concat_axis=0, tiled=True)  48.3 us
    ppermute x39, starting transfers between devices, swap(): return lax.ppermute(value, axis, SWAP)  23.5 us
    ppermute x16, waiting for transfers between devices, expert_sum(): other = lax.ppermute(mine, 'expert', pairs)  22.8 us
    unnamed x420, local copies, waits for them, and re-layouts  20.3 us
    ppermute x16, starting transfers between devices, expert_sum(): other = lax.ppermute(mine, 'expert', pairs)  20.1 us
  transfers between devices with their start and end apart: 83, of which 36 were waited for; matrix products, arithmetic and copies ran while one was open for 30% of the time, Pallas kernels for 0%

profile of v1, /device:TPU:0, one launch (start us, length us, event | category | flops | bytes accessed | tf_op | source)
XLA Modules:
  0.0 755.5 jit_solution(16226097975987355804)
XLA Ops:
  2.6 4.6 copy.118
  29.0 24.7 %collective-permute-done.5 = bf16[128,1536]{1,0:T(8,128)(2,1)S(1)} collective-permute-done((bf16[128,1536]{1,0:T(8,128)(2,1)S(1)}, bf16[128,1536]{1,0:T(8,128)(2,1)S(1)}, u32[]{:S(2)}, u32[]{:S(2)}) %collective-permute-start.5) | collective-permute-done | bytes 393248 | tf_op jit(solution)/shard_map/ppermute | solution.py:15
  56.4 10.5 %all-to-all-start = ((bf16[32,16,1536]{2,1,0:T(8,128)(2,1)}), bf16[32,16,1536]{2,1,0:T(8,128)(2,1)S(1)}, u32[]{:S(2)}, u32[]{:S(2)}) async-start(bf16[32,16,1536]{2,1,0:T(8,128)(2,1)} %bitcast.582), calls=%async_computation | async-start | bytes 3145728 | tf_op jit(solution)/shard_map/all_to_all | solution.py:19
  69.5 42.2 %collective-permute-done.14 = bf16[1536,384]{1,0:T(8,128)(2,1)} collective-permute-done((bf16[1536,384]{1,0:T(8,128)(2,1)}, bf16[1536,384]{1,0:T(8,128)(2,1)}, u32[]{:S(2)}, u32[]{:S(2)}) %collective-permute-start.14) | collective-permute-done | bytes 1179680 | tf_op jit(solution)/shard_map/ppermute | solution.py:15
  112.2 24.0 %collective-permute-done.16 = bf16[384,1536]{1,0:T(8,128)(2,1)} collective-permute-done((bf16[384,1536]{1,0:T(8,128)(2,1)}, bf16[384,1536]{1,0:T(8,128)(2,1)}, u32[]{:S(2)}, u32[]{:S(2)}) %collective-permute-start.16) | collective-permute-done | bytes 1179680 | tf_op jit(solution)/shard_map/ppermute | solution.py:15
  147.4 3.6 fusion.6
  150.9 10.0 %all-to-all-start.1 = ((bf16[32,16,1536]{2,1,0:T(8,128)(2,1)}), bf16[32,16,1536]{2,1,0:T(8,128)(2,1)}, u32[]{:S(2)}, u32[]{:S(2)}) async-start(bf16[32,16,1536]{2,1,0:T(8,128)(2,1)} %bitcast.586), calls=%async_computation.1 | async-start | bytes 3145728 | tf_op jit(solution)/shard_map/all_to_all | solution.py:19
  160.9 3.7 collective-permute-start.7
  165.9 19.6 %all-to-all-done.1 = bf16[32,16,1536]{2,1,0:T(8,128)(2,1)} async-done(((bf16[32,16,1536]{2,1,0:T(8,128)(2,1)}), bf16[32,16,1536]{2,1,0:T(8,128)(2,1)}, u32[]{:S(2)}, u32[]{:S(2)}) %all-to-all-start.1) | async-done | bytes 1572896 | tf_op jit(solution)/shard_map/all_to_all | solution.py:19
  187.7 10.7 %collective-permute-done.18 = bf16[128,1536]{1,0:T(8,128)(2,1)S(1)} collective-permute-done((bf16[128,1536]{1,0:T(8,128)(2,1)S(1)}, bf16[128,1536]{1,0:T(8,128)(2,1)S(1)}, u32[]{:S(2)}, u32[]{:S(2)}) %collective-permute-start.18) | collective-permute-done | bytes 393248 | tf_op jit(solution)/shard_map/ppermute | solution.py:15
  210.3 8.9 %collective-permute-done.19 = bf16[128,1536]{1,0:T(8,128)(2,1)S(1)} collective-permute-done((bf16[128,1536]{1,0:T(8,128)(2,1)S(1)}, bf16[128,1536]{1,0:T(8,128)(2,1)S(1)}, u32[]{:S(2)}, u32[]{:S(2)}) %collective-permute-start.19) | collective-permute-done | bytes 393248 | tf_op jit(solution)/shard_map/ppermute | solution.py:15
  222.0 4.0 all-to-all-start.2
  232.3 16.3 %all-to-all-done.2 = bf16[32,16,1536]{2,1,0:T(8,128)(2,1)S(1)} async-done(((bf16[32,16,1536]{2,1,0:T(8,128)(2,1)}), bf16[32,16,1536]{2,1,0:T(8,128)(2,1)S(1)}, u32[]{:S(2)}, u32[]{:S(2)}) %all-to-all-start.2) | async-done | bytes 1572896 | tf_op jit(solution)/shard_map/all_to_all | solution.py:19
  248.6 4.9 all-to-all-start.4
  253.5 3.5 fusion.79
  260.1 14.8 %all-to-all-done.4 = bf16[32,16,1536]{2,1,0:T(8,128)(2,1)} async-done(((bf16[32,16,1536]{2,1,0:T(8,128)(2,1)}), bf16[32,16,1536]{2,1,0:T(8,128)(2,1)}, u32[]{:S(2)}, u32[]{:S(2)}) %all-to-all-start.4) | async-done | bytes 1572896 | tf_op jit(solution)/shard_map/all_to_all | solution.py:19
  292.7 3.5 fusion.8
  296.1 4.7 all-to-all-start.5
  303.7 3.4 fusion.7
  307.1 13.9 %all-to-all-done.5 = bf16[32,16,1536]{2,1,0:T(8,128)(2,1)} async-done(((bf16[32,16,1536]{2,1,0:T(8,128)(2,1)}), bf16[32,16,1536]{2,1,0:T(8,128)(2,1)}, u32[]{:S(2)}, u32[]{:S(2)}) %all-to-all-start.5) | async-done | bytes 1572896 | tf_op jit(solution)/shard_map/all_to_all | solution.py:19
  321.0 4.7 all-to-all-start.3
  330.6 16.7 %all-to-all-done.3 = bf16[32,16,1536]{2,1,0:T(8,128)(2,1)} async-done(((bf16[32,16,1536]{2,1,0:T(8,128)(2,1)}), bf16[32,16,1536]{2,1,0:T(8,128)(2,1)}, u32[]{:S(2)}, u32[]{:S(2)}) %all-to-all-start.3) | async-done | bytes 1572896 | tf_op jit(solution)/shard_map/all_to_all | solution.py:19
  392.8 4.7 all-to-all-start.6
  404.4 3.6 collective-permute-done.26
  409.5 6.4 all-to-all-done.6
  418.4 4.5 fusion.238
  422.9 4.1 select_convert_fusion
  440.8 3.5 fusion.9
  444.3 4.8 all-to-all-start.7
  449.1 4.1 select_convert_fusion.1
  464.8 10.1 %all-to-all-done.7 = bf16[32,16,1536]{2,1,0:T(8,128)(2,1)} async-done(((bf16[32,16,1536]{2,1,0:T(8,128)(2,1)}), bf16[32,16,1536]{2,1,0:T(8,128)(2,1)}, u32[]{:S(2)}, u32[]{:S(2)}) %all-to-all-start.7) | async-done | bytes 1572896 | tf_op jit(solution)/shard_map/all_to_all | solution.py:19
  480.9 7.5 collective-permute-done.25
  510.2 7.9 %collective-permute-done.27 = bf16[128,1536]{1,0:T(8,128)(2,1)S(1)} collective-permute-done((bf16[128,1536]{1,0:T(8,128)(2,1)S(1)}, bf16[128,1536]{1,0:T(8,128)(2,1)S(1)}, u32[]{:S(2)}, u32[]{:S(2)}) %collective-permute-start.27) | collective-permute-done | bytes 393248 | tf_op jit(solution)/shard_map/ppermute | solution.py:15
  519.4 7.9 %broadcast_select_fusion = bf16[1536,1920]{0,1:T(8,128)(2,1)} fusion(bf16[1536,1920]{0,1:T(8,128)(2,1)} %get-tuple-element.171, bf16[1536,1920]{0,1:T(8,128)(2,1)S(1)} %get-tuple-element.170, pred[]{:T(512)S(6)} %eq.106), kind=kLoop, calls=%fused_computation.4 | loop fusion | flops 2949120 | bytes 17694720 | tf_op jit(solution)/shard_map/jit(_where)/select_n | solution.py:239
  543.1 19.9 %collective-permute-done.74 = bf16[384,1536]{1,0:T(8,128)(2,1)S(1)} collective-permute-done((bf16[384,1536]{1,0:T(8,128)(2,1)S(1)}, bf16[384,1536]{1,0:T(8,128)(2,1)S(1)}, u32[]{:S(2)}, u32[]{:S(2)}) %collective-permute-start.74) | collective-permute-done | bytes 1179680 | tf_op jit(solution)/shard_map/ppermute | solution.py:15
  564.1 3.5 add_bitcast_fusion
  567.6 20.7 %collective-permute-done.71 = bf16[1536,384]{1,0:T(8,128)(2,1)S(1)} collective-permute-done((bf16[1536,384]{1,0:T(8,128)(2,1)S(1)}, bf16[1536,384]{1,0:T(8,128)(2,1)S(1)}, u32[]{:S(2)}, u32[]{:S(2)}) %collective-permute-start.71) | collective-permute-done | bytes 1179680 | tf_op jit(solution)/shard_map/ppermute | solution.py:15
  591.3 21.8 %collective-permute-done.68 = bf16[1536,384]{1,0:T(8,128)(2,1)S(1)} collective-permute-done((bf16[1536,384]{1,0:T(8,128)(2,1)S(1)}, bf16[1536,384]{1,0:T(8,128)(2,1)S(1)}, u32[]{:S(2)}, u32[]{:S(2)}) %collective-permute-start.68) | collective-permute-done | bytes 1179680 | tf_op jit(solution)/shard_map/ppermute | solution.py:15
  614.9 9.3 %add_convert_fusion = bf16[1536,1920]{0,1:T(8,128)(2,1)} fusion(bf16[1536,1920]{0,1:T(8,128)(2,1)} %collective-permute-done.29, bf16[1536,1920]{0,1:T(8,128)(2,1)} %copy-done.11, bf16[1536,1920]{0,1:T(8,128)(2,1)} %get-tuple-element.171, pred[]{:T(512)S(6)} %eq.106), kind=kLoop, calls=%fused_computation.2 | loop fusion | flops 14745600 | bytes 23592960 | tf_op jit(solution)/shard_map/convert_element_type | solution.py:318
  624.2 5.0 fusion.223
  646.2 4.2 collective-permute-done.30
  652.3 6.9 collective-permute-done.39
  669.1 3.6 collective-permute-done.49
  678.5 3.6 collective-permute-start.51
  711.5 4.9 collective-permute-done.37
  728.9 4.2 collective-permute-done.47
  734.0 3.8 collective-permute-done.65
  750.1 5.1 maximum_bitcast_fusion
  (779 shorter events, 313.1 us)
Async XLA Ops:
  2.0 13.1 %collective-permute-start = (bf16[1536]{0:T(1024)(128)(2,1)}, bf16[1536]{0:T(1024)(128)(2,1)}, u32[]{:S(2)}, u32[]{:S(2)}) collective-permute-start(bf16[1536]{0:T(1024)(128)(2,1)} %reduce), channel_id=1, source_target_pairs={{0,64},{64,0},{1,65},{65,1},{2,66},{66,2},{3,67},{67,3},{4,68},{68... | collective-permute-start | bytes 9224 | tf_op jit(solution)/shard_map/ppermute | solution.py:15
  2.0 14.5 %collective-permute-start.2 = (bf16[1536,128]{1,0:T(8,128)(2,1)}, bf16[1536,128]{1,0:T(8,128)(2,1)}, u32[]{:S(2)}, u32[]{:S(2)}) collective-permute-start(bf16[1536,128]{1,0:T(8,128)(2,1)} %bitcast.612), channel_id=1, source_target_pairs={{0,64},{64,0},{1,65},{65,1},{2,66},{66,2},{3,67},{67,3},{4,68},{68... | collective-permute-start | bytes 1179656 | tf_op jit(solution)/shard_map/ppermute | solution.py:15
  7.2 13.5 %collective-permute-start.3 = (bf16[1536,768]{0,1:T(8,128)(2,1)}, bf16[1536,768]{0,1:T(8,128)(2,1)}, u32[]{:S(2)}, u32[]{:S(2)}) collective-permute-start(bf16[1536,768]{0,1:T(8,128)(2,1)} %bitcast.579), channel_id=1, source_target_pairs={{0,64},{64,0},{1,65},{65,1},{2,66},{66,2},{3,67},{67,3},{4,68},{68... | collective-permute-start | bytes 7077896 | tf_op jit(solution)/shard_map/ppermute | solution.py:15
  7.2 12.4 %collective-permute-start.1 = (bf16[1536,128]{1,0:T(8,128)(2,1)}, bf16[1536,128]{1,0:T(8,128)(2,1)}, u32[]{:S(2)}, u32[]{:S(2)}) collective-permute-start(bf16[1536,128]{1,0:T(8,128)(2,1)} %bitcast.613), channel_id=1, source_target_pairs={{0,64},{64,0},{1,65},{65,1},{2,66},{66,2},{3,67},{67,3},{4,68},{68... | collective-permute-start | bytes 1179656 | tf_op jit(solution)/shard_map/ppermute | solution.py:15
  13.0 13.0 %collective-permute-start.4 = (bf16[768,1536]{1,0:T(8,128)(2,1)S(1)}, bf16[768,1536]{1,0:T(8,128)(2,1)}, u32[]{:S(2)}, u32[]{:S(2)}) collective-permute-start(bf16[768,1536]{1,0:T(8,128)(2,1)S(1)} %bitcast.577), channel_id=1, source_target_pairs={{0,64},{64,0},{1,65},{65,1},{2,66},{66,2},{3,67},{67,3},{4,68},{68... | collective-permute-start | bytes 7077896 | tf_op jit(solution)/shard_map/ppermute | solution.py:15
  15.0 12.7 %collective-permute-start.8 = (bf16[1536]{0:T(1024)(128)(2,1)}, bf16[1536]{0:T(1024)(128)(2,1)}, u32[]{:S(2)}, u32[]{:S(2)}) collective-permute-start(bf16[1536]{0:T(1024)(128)(2,1)} %reduce.1), channel_id=1, source_target_pairs={{0,64},{64,0},{1,65},{65,1},{2,66},{66,2},{3,67},{67,3},{4,68},{68... | collective-permute-start | bytes 9224 | tf_op jit(solution)/shard_map/ppermute | solution.py:15
  16.5 52.8 %collective-permute-start.12 = (bf16[1536,384]{1,0:T(8,128)(2,1)}, bf16[1536,384]{1,0:T(8,128)(2,1)}, u32[]{:S(2)}, u32[]{:S(2)}) collective-permute-start(bf16[1536,384]{1,0:T(8,128)(2,1)} %bitcast.596), channel_id=1, source_target_pairs={{0,1},{1,0},{2,3},{3,2},{4,5},{5,4},{6,7},{7,6},{8,9},{9,8},{10,11... | collective-permute-start | bytes 3538952 | tf_op jit(solution)/shard_map/ppermute | solution.py:15
  26.7 27.0 %collective-permute-start.5 = (bf16[128,1536]{1,0:T(8,128)(2,1)S(1)}, bf16[128,1536]{1,0:T(8,128)(2,1)S(1)}, u32[]{:S(2)}, u32[]{:S(2)}) collective-permute-start(bf16[128,1536]{1,0:T(8,128)(2,1)S(1)} %convolution_convert_fusion.13), channel_id=1, source_target_pairs={{0,1},{1,0},{2,3},{3,2},{4,5},{5,4},{6,7},{7,6},{8,9},{9,8},{10,11... | collective-permute-start | bytes 1179656 | tf_op jit(solution)/shard_map/ppermute | solution.py:15
  56.4 79.9 %all-to-all-start = ((bf16[32,16,1536]{2,1,0:T(8,128)(2,1)}), bf16[32,16,1536]{2,1,0:T(8,128)(2,1)S(1)}, u32[]{:S(2)}, u32[]{:S(2)}) async-start(bf16[32,16,1536]{2,1,0:T(8,128)(2,1)} %bitcast.582), calls=%async_computation | async-start | bytes 3145728 | tf_op jit(solution)/shard_map/all_to_all | solution.py:19
  66.9 44.8 %collective-permute-start.14 = (bf16[1536,384]{1,0:T(8,128)(2,1)}, bf16[1536,384]{1,0:T(8,128)(2,1)}, u32[]{:S(2)}, u32[]{:S(2)}) collective-permute-start(bf16[1536,384]{1,0:T(8,128)(2,1)} %bitcast.598), channel_id=1, source_target_pairs={{0,1},{1,0},{2,3},{3,2},{4,5},{5,4},{6,7},{7,6},{8,9},{9,8},{10,11... | collective-permute-start | bytes 3538952 | tf_op jit(solution)/shard_map/ppermute | solution.py:15
  68.0 43.7 %collective-permute-start.9 = (bf16[1536,384]{1,0:T(8,128)(2,1)}, bf16[1536,384]{1,0:T(8,128)(2,1)S(1)}, u32[]{:S(2)}, u32[]{:S(2)}) collective-permute-start(bf16[1536,384]{1,0:T(8,128)(2,1)} %bitcast.597), channel_id=1, source_target_pairs={{0,64},{64,0},{1,65},{65,1},{2,66},{66,2},{3,67},{67,3},{4,68},{68... | collective-permute-start | bytes 3538952 | tf_op jit(solution)/shard_map/ppermute | solution.py:15
  68.0 68.2 %collective-permute-start.16 = (bf16[384,1536]{1,0:T(8,128)(2,1)}, bf16[384,1536]{1,0:T(8,128)(2,1)}, u32[]{:S(2)}, u32[]{:S(2)}) collective-permute-start(bf16[384,1536]{1,0:T(8,128)(2,1)} %bitcast.600), channel_id=1, source_target_pairs={{0,1},{1,0},{2,3},{3,2},{4,5},{5,4},{6,7},{7,6},{8,9},{9,8},{10,11... | collective-permute-start | bytes 3538952 | tf_op jit(solution)/shard_map/ppermute | solution.py:15
  69.0 69.7 %collective-permute-start.10 = (bf16[1536,384]{1,0:T(8,128)(2,1)}, bf16[1536,384]{1,0:T(8,128)(2,1)}, u32[]{:S(2)}, u32[]{:S(2)}) collective-permute-start(bf16[1536,384]{1,0:T(8,128)(2,1)} %bitcast.599), channel_id=1, source_target_pairs={{0,64},{64,0},{1,65},{65,1},{2,66},{66,2},{3,67},{67,3},{4,68},{68... | collective-permute-start | bytes 3538952 | tf_op jit(solution)/shard_map/ppermute | solution.py:15
  69.2 71.4 %collective-permute-start.13 = (bf16[1536,384]{1,0:T(8,128)(2,1)}, bf16[1536,384]{1,0:T(8,128)(2,1)}, u32[]{:S(2)}, u32[]{:S(2)}) collective-permute-start(bf16[1536,384]{1,0:T(8,128)(2,1)} %collective-permute-done.12), channel_id=1, source_target_pairs={{0,64},{64,0},{1,65},{65,1},{2,66},{66,2},{3,67},{67,3},{4,68},{68... | collective-permute-start | bytes 3538952 | tf_op jit(solution)/shard_map/ppermute | solution.py:15
  111.7 31.4 %collective-permute-start.11 = (bf16[384,1536]{1,0:T(8,128)(2,1)}, bf16[384,1536]{1,0:T(8,128)(2,1)}, u32[]{:S(2)}, u32[]{:S(2)}) collective-permute-start(bf16[384,1536]{1,0:T(8,128)(2,1)} %bitcast.601), channel_id=1, source_target_pairs={{0,64},{64,0},{1,65},{65,1},{2,66},{66,2},{3,67},{67,3},{4,68},{68... | collective-permute-start | bytes 3538952 | tf_op jit(solution)/shard_map/ppermute | solution.py:15
  111.7 32.5 %collective-permute-start.15 = (bf16[1536,384]{1,0:T(8,128)(2,1)}, bf16[1536,384]{1,0:T(8,128)(2,1)}, u32[]{:S(2)}, u32[]{:S(2)}) collective-permute-start(bf16[1536,384]{1,0:T(8,128)(2,1)} %collective-permute-done.14), channel_id=1, source_target_pairs={{0,64},{64,0},{1,65},{65,1},{2,66},{66,2},{3,67},{67,3},{4,68},{68... | collective-permute-start | bytes 3538952 | tf_op jit(solution)/shard_map/ppermute | solution.py:15
  150.9 34.6 %all-to-all-start.1 = ((bf16[32,16,1536]{2,1,0:T(8,128)(2,1)}), bf16[32,16,1536]{2,1,0:T(8,128)(2,1)}, u32[]{:S(2)}, u32[]{:S(2)}) async-start(bf16[32,16,1536]{2,1,0:T(8,128)(2,1)} %bitcast.586), calls=%async_computation.1 | async-start | bytes 3145728 | tf_op jit(solution)/shard_map/all_to_all | solution.py:19
  222.0 26.6 %all-to-all-start.2 = ((bf16[32,16,1536]{2,1,0:T(8,128)(2,1)}), bf16[32,16,1536]{2,1,0:T(8,128)(2,1)S(1)}, u32[]{:S(2)}, u32[]{:S(2)}) async-start(bf16[32,16,1536]{2,1,0:T(8,128)(2,1)} %bitcast.583), calls=%async_computation.2 | async-start | bytes 3145728 | tf_op jit(solution)/shard_map/all_to_all | solution.py:19
  248.6 26.4 %all-to-all-start.4 = ((bf16[32,16,1536]{2,1,0:T(8,128)(2,1)}), bf16[32,16,1536]{2,1,0:T(8,128)(2,1)}, u32[]{:S(2)}, u32[]{:S(2)}) async-start(bf16[32,16,1536]{2,1,0:T(8,128)(2,1)} %bitcast.581), calls=%async_computation.4 | async-start | bytes 3145728 | tf_op jit(solution)/shard_map/all_to_all | solution.py:19
  296.1 24.8 %all-to-all-start.5 = ((bf16[32,16,1536]{2,1,0:T(8,128)(2,1)}), bf16[32,16,1536]{2,1,0:T(8,128)(2,1)}, u32[]{:S(2)}, u32[]{:S(2)}) async-start(bf16[32,16,1536]{2,1,0:T(8,128)(2,1)} %bitcast.587), calls=%async_computation.5 | async-start | bytes 3145728 | tf_op jit(solution)/shard_map/all_to_all | solution.py:19
  321.0 26.3 %all-to-all-start.3 = ((bf16[32,16,1536]{2,1,0:T(8,128)(2,1)}), bf16[32,16,1536]{2,1,0:T(8,128)(2,1)}, u32[]{:S(2)}, u32[]{:S(2)}) async-start(bf16[32,16,1536]{2,1,0:T(8,128)(2,1)} %bitcast.584), calls=%async_computation.3 | async-start | bytes 3145728 | tf_op jit(solution)/shard_map/all_to_all | solution.py:19
  330.0 25.7 %collective-permute-start.22 = (bf16[128,1536]{1,0:T(8,128)(2,1)}, bf16[128,1536]{1,0:T(8,128)(2,1)}, u32[]{:S(2)}, u32[]{:S(2)}) collective-permute-start(bf16[128,1536]{1,0:T(8,128)(2,1)} %fusion.16), channel_id=1, source_target_pairs={{0,1},{1,0},{2,3},{3,2},{4,5},{5,4},{6,7},{7,6},{8,9},{9,8},{10,11... | collective-permute-start | bytes 1179656 | tf_op jit(solution)/shard_map/ppermute | solution.py:15
  352.7 137.2 %collective-permute-start.20 = (bf16[128,1536]{1,0:T(8,128)(2,1)}, bf16[128,1536]{1,0:T(8,128)(2,1)}, u32[]{:S(2)}, u32[]{:S(2)}) collective-permute-start(bf16[128,1536]{1,0:T(8,128)(2,1)} %fusion.15), channel_id=1, source_target_pairs={{0,1},{1,0},{2,3},{3,2},{4,5},{5,4},{6,7},{7,6},{8,9},{9,8},{10,11... | collective-permute-start | bytes 1179656 | tf_op jit(solution)/shard_map/ppermute | solution.py:15
  392.8 23.2 %all-to-all-start.6 = ((bf16[32,16,1536]{2,1,0:T(8,128)(2,1)}), bf16[32,16,1536]{2,1,0:T(8,128)(2,1)}, u32[]{:S(2)}, u32[]{:S(2)}) async-start(bf16[32,16,1536]{2,1,0:T(8,128)(2,1)} %bitcast.580), calls=%async_computation.6 | async-start | bytes 3145728 | tf_op jit(solution)/shard_map/all_to_all | solution.py:19
  427.0 103.4 %collective-permute-start.73 = (bf16[384,1536]{1,0:T(8,128)(2,1)}, bf16[384,1536]{1,0:T(8,128)(2,1)}, u32[]{:S(2)}, u32[]{:S(2)}) collective-permute-start(bf16[384,1536]{1,0:T(8,128)(2,1)} %get-tuple-element.166), channel_id=1, source_target_pairs={{0,64},{64,0},{1,65},{65,1},{2,66},{66,2},{3,67},{67,3},{4,68},{68... | collective-permute-start | bytes 3538952 | tf_op jit(solution)/shard_map/ppermute | solution.py:15
  444.3 30.7 %all-to-all-start.7 = ((bf16[32,16,1536]{2,1,0:T(8,128)(2,1)}), bf16[32,16,1536]{2,1,0:T(8,128)(2,1)}, u32[]{:S(2)}, u32[]{:S(2)}) async-start(bf16[32,16,1536]{2,1,0:T(8,128)(2,1)} %bitcast.585), calls=%async_computation.7 | async-start | bytes 3145728 | tf_op jit(solution)/shard_map/all_to_all | solution.py:19
  453.2 89.7 %collective-permute-start.72 = (bf16[384,1536]{1,0:T(8,128)(2,1)}, bf16[384,1536]{1,0:T(8,128)(2,1)}, u32[]{:S(2)}, u32[]{:S(2)}) collective-permute-start(bf16[384,1536]{1,0:T(8,128)(2,1)} %get-tuple-element.168), channel_id=1, source_target_pairs={{0,64},{64,0},{1,65},{65,1},{2,66},{66,2},{3,67},{67,3},{4,68},{68... | collective-permute-start | bytes 3538952 | tf_op jit(solution)/shard_map/ppermute | solution.py:15
  458.4 75.7 %collective-permute-start.70 = (bf16[1536,384]{1,0:T(8,128)(2,1)}, bf16[1536,384]{1,0:T(8,128)(2,1)}, u32[]{:S(2)}, u32[]{:S(2)}) collective-permute-start(bf16[1536,384]{1,0:T(8,128)(2,1)} %get-tuple-element.162), channel_id=1, source_target_pairs={{0,64},{64,0},{1,65},{65,1},{2,66},{66,2},{3,67},{67,3},{4,68},{68... | collective-permute-start | bytes 3538952 | tf_op jit(solution)/shard_map/ppermute | solution.py:15
  488.4 79.2 %collective-permute-start.69 = (bf16[1536,384]{1,0:T(8,128)(2,1)}, bf16[1536,384]{1,0:T(8,128)(2,1)}, u32[]{:S(2)}, u32[]{:S(2)}) collective-permute-start(bf16[1536,384]{1,0:T(8,128)(2,1)} %get-tuple-element.164), channel_id=1, source_target_pairs={{0,64},{64,0},{1,65},{65,1},{2,66},{66,2},{3,67},{67,3},{4,68},{68... | collective-permute-start | bytes 3538952 | tf_op jit(solution)/shard_map/ppermute | solution.py:15
  527.3 87.6 %collective-permute-start.29 = (bf16[1536,1920]{0,1:T(8,128)(2,1)}, bf16[1536,1920]{0,1:T(8,128)(2,1)}, u32[]{:S(2)}, u32[]{:S(2)}) collective-permute-start(bf16[1536,1920]{0,1:T(8,128)(2,1)} %broadcast_select_fusion), channel_id=1, source_target_pairs={{0,64},{64,0},{1,65},{65,1},{2,66},{66,2},{3,67},{67,3},{4,68},{68... | collective-permute-start | bytes 17694728 | tf_op jit(solution)/shard_map/ppermute | solution.py:15
  534.1 28.8 %collective-permute-start.74 = (bf16[384,1536]{1,0:T(8,128)(2,1)S(1)}, bf16[384,1536]{1,0:T(8,128)(2,1)S(1)}, u32[]{:S(2)}, u32[]{:S(2)}) collective-permute-start(bf16[384,1536]{1,0:T(8,128)(2,1)S(1)} %add_convert_fusion.1), channel_id=1, source_target_pairs={{0,1},{1,0},{2,3},{3,2},{4,5},{5,4},{6,7},{7,6},{8,9},{9,8},{10,11... | collective-permute-start | bytes 3538952 | tf_op jit(solution)/shard_map/ppermute | solution.py:15
  538.6 49.7 %collective-permute-start.71 = (bf16[1536,384]{1,0:T(8,128)(2,1)S(1)}, bf16[1536,384]{1,0:T(8,128)(2,1)S(1)}, u32[]{:S(2)}, u32[]{:S(2)}) collective-permute-start(bf16[1536,384]{1,0:T(8,128)(2,1)S(1)} %add_convert_fusion.2), channel_id=1, source_target_pairs={{0,1},{1,0},{2,3},{3,2},{4,5},{5,4},{6,7},{7,6},{8,9},{9,8},{10,11... | collective-permute-start | bytes 3538952 | tf_op jit(solution)/shard_map/ppermute | solution.py:15
  542.9 48.4 %collective-permute-start.66 = (bf16[1536,384]{1,0:T(8,128)(2,1)S(1)}, bf16[1536,384]{1,0:T(8,128)(2,1)S(1)}, u32[]{:S(2)}, u32[]{:S(2)}) collective-permute-start(bf16[1536,384]{1,0:T(8,128)(2,1)S(1)} %get-tuple-element.160), channel_id=1, source_target_pairs={{0,64},{64,0},{1,65},{65,1},{2,66},{66,2},{3,67},{67,3},{4,68},{68... | collective-permute-start | bytes 3538952 | tf_op jit(solution)/shard_map/ppermute | solution.py:15
  563.0 50.1 %collective-permute-start.68 = (bf16[1536,384]{1,0:T(8,128)(2,1)S(1)}, bf16[1536,384]{1,0:T(8,128)(2,1)S(1)}, u32[]{:S(2)}, u32[]{:S(2)}) collective-permute-start(bf16[1536,384]{1,0:T(8,128)(2,1)S(1)} %add_convert_fusion.3), channel_id=1, source_target_pairs={{0,1},{1,0},{2,3},{3,2},{4,5},{5,4},{6,7},{7,6},{8,9},{9,8},{10,11... | collective-permute-start | bytes 3538952 | tf_op jit(solution)/shard_map/ppermute | solution.py:15
  567.6 65.5 %collective-permute-start.21 = (f32[128,1536]{1,0:T(8,128)}, f32[128,1536]{1,0:T(8,128)}, u32[]{:S(2)}, u32[]{:S(2)}) collective-permute-start(f32[128,1536]{1,0:T(8,128)} %get-tuple-element.79), channel_id=1, source_target_pairs={{0,64},{64,0},{1,65},{65,1},{2,66},{66,2},{3,67},{67,3},{4,68},{68... | collective-permute-start | bytes 2359304 | tf_op jit(solution)/shard_map/ppermute | solution.py:15
  588.3 102.9 %collective-permute-start.28 = (f32[128,1536]{1,0:T(8,128)}, f32[128,1536]{1,0:T(8,128)}, u32[]{:S(2)}, u32[]{:S(2)}) collective-permute-start(f32[128,1536]{1,0:T(8,128)} %get-tuple-element.77), channel_id=1, source_target_pairs={{0,64},{64,0},{1,65},{65,1},{2,66},{66,2},{3,67},{67,3},{4,68},{68... | collective-permute-start | bytes 2359304 | tf_op jit(solution)/shard_map/ppermute | solution.py:15
  632.0 18.4 %collective-permute-start.30 = (bf16[192,1920]{1,0:T(8,128)(2,1)}, bf16[192,1920]{1,0:T(8,128)(2,1)}, u32[]{:S(2)}, u32[]{:S(2)}) collective-permute-start(bf16[192,1920]{1,0:T(8,128)(2,1)} %dynamic-slice_bitcast_fusion.3), channel_id=1, source_target_pairs={{0,4},{2,6},{4,0},{6,2},{8,12},{10,14},{12,8},{14,10},{16,20},{18,... | collective-permute-start | bytes 2211848 | tf_op jit(solution)/shard_map/ppermute | solution.py:197
  638.3 21.0 %collective-permute-start.39 = (bf16[192,1920]{1,0:T(8,128)(2,1)}, bf16[192,1920]{1,0:T(8,128)(2,1)}, u32[]{:S(2)}, u32[]{:S(2)}) collective-permute-start(bf16[192,1920]{1,0:T(8,128)(2,1)} %dynamic-slice_bitcast_fusion.2), channel_id=1, source_target_pairs={{0,12},{2,14},{4,8},{6,10},{8,4},{10,6},{12,0},{14,2},{16,28},{18,... | collective-permute-start | bytes 2211848 | tf_op jit(solution)/shard_map/ppermute | solution.py:197
  641.6 18.9 %collective-permute-start.48 = (bf16[192,1920]{1,0:T(8,128)(2,1)}, bf16[192,1920]{1,0:T(8,128)(2,1)}, u32[]{:S(2)}, u32[]{:S(2)}) collective-permute-start(bf16[192,1920]{1,0:T(8,128)(2,1)} %dynamic-slice_bitcast_fusion.1), channel_id=1, source_target_pairs={{0,16},{2,18},{4,20},{6,22},{8,24},{10,26},{12,28},{14,30},{16,0},... | collective-permute-start | bytes 2211848 | tf_op jit(solution)/shard_map/ppermute | solution.py:197
  644.3 18.6 %collective-permute-start.57 = (bf16[192,1920]{1,0:T(8,128)(2,1)S(1)}, bf16[192,1920]{1,0:T(8,128)(2,1)S(1)}, u32[]{:S(2)}, u32[]{:S(2)}) collective-permute-start(bf16[192,1920]{1,0:T(8,128)(2,1)S(1)} %dynamic-slice_bitcast_fusion), channel_id=1, source_target_pairs={{0,48},{2,50},{4,52},{6,54},{8,56},{10,58},{12,60},{14,62},{16,32}... | collective-permute-start | bytes 2211848 | tf_op jit(solution)/shard_map/ppermute | solution.py:197
  651.6 13.7 %collective-permute-start.31 = (bf16[96,1920]{1,0:T(8,128)(2,1)S(1)}, bf16[96,1920]{1,0:T(8,128)(2,1)S(1)}, u32[]{:S(2)}, u32[]{:S(2)}) collective-permute-start(bf16[96,1920]{1,0:T(8,128)(2,1)S(1)} %dynamic-slice_bitcast_fusion.7), channel_id=1, source_target_pairs={{0,12},{2,14},{4,8},{6,10},{8,4},{10,6},{12,0},{14,2},{16,28},{18,... | collective-permute-start | bytes 1105928 | tf_op jit(solution)/shard_map/ppermute | solution.py:197
  702.6 14.0 %collective-permute-start.63 = (bf16[48,1920]{1,0:T(8,128)(2,1)S(1)}, bf16[48,1920]{1,0:T(8,128)(2,1)S(1)}, u32[]{:S(2)}, u32[]{:S(2)}) collective-permute-start(bf16[48,1920]{1,0:T(8,128)(2,1)S(1)} %maximum_select_fusion.17), channel_id=1, source_target_pairs={{0,12},{2,14},{4,8},{6,10},{8,4},{10,6},{12,0},{14,2},{16,28},{18,... | collective-permute-start | bytes 552968 | tf_op jit(solution)/shard_map/ppermute | solution.py:205
  703.9 12.5 %collective-permute-start.37 = (bf16[96,1920]{1,0:T(8,128)(2,1)S(1)}, bf16[96,1920]{1,0:T(8,128)(2,1)S(1)}, u32[]{:S(2)}, u32[]{:S(2)}) collective-permute-start(bf16[96,1920]{1,0:T(8,128)(2,1)S(1)} %maximum_select_fusion.10), channel_id=1, source_target_pairs={{0,12},{2,14},{4,8},{6,10},{8,4},{10,6},{12,0},{14,2},{16,28},{18,... | collective-permute-start | bytes 1105928 | tf_op jit(solution)/shard_map/ppermute | solution.py:205
  709.4 11.8 %collective-permute-start.55 = (bf16[96,1920]{1,0:T(8,128)(2,1)S(1)}, bf16[96,1920]{1,0:T(8,128)(2,1)S(1)}, u32[]{:S(2)}, u32[]{:S(2)}) collective-permute-start(bf16[96,1920]{1,0:T(8,128)(2,1)S(1)} %maximum_select_fusion.12), channel_id=1, source_target_pairs={{0,48},{2,50},{4,52},{6,54},{8,56},{10,58},{12,60},{14,62},{16,32}... | collective-permute-start | bytes 1105928 | tf_op jit(solution)/shard_map/ppermute | solution.py:205
  716.6 11.8 %collective-permute-start.38 = (bf16[192,1920]{1,0:T(8,128)(2,1)S(1)}, bf16[192,1920]{1,0:T(8,128)(2,1)S(1)}, u32[]{:S(2)}, u32[]{:S(2)}) collective-permute-start(bf16[192,1920]{1,0:T(8,128)(2,1)S(1)} %maximum_select_fusion.6), channel_id=1, source_target_pairs={{0,4},{2,6},{4,0},{6,2},{8,12},{10,14},{12,8},{14,10},{16,20},{18,... | collective-permute-start | bytes 2211848 | tf_op jit(solution)/shard_map/ppermute | solution.py:205
  720.4 12.8 %collective-permute-start.47 = (bf16[192,1920]{1,0:T(8,128)(2,1)S(1)}, bf16[192,1920]{1,0:T(8,128)(2,1)S(1)}, u32[]{:S(2)}, u32[]{:S(2)}) collective-permute-start(bf16[192,1920]{1,0:T(8,128)(2,1)S(1)} %maximum_select_fusion.7), channel_id=1, source_target_pairs={{0,12},{2,14},{4,8},{6,10},{8,4},{10,6},{12,0},{14,2},{16,28},{18,... | collective-permute-start | bytes 2211848 | tf_op jit(solution)/shard_map/ppermute | solution.py:205
  721.3 12.2 %collective-permute-start.56 = (bf16[192,1920]{1,0:T(8,128)(2,1)S(1)}, bf16[192,1920]{1,0:T(8,128)(2,1)S(1)}, u32[]{:S(2)}, u32[]{:S(2)}) collective-permute-start(bf16[192,1920]{1,0:T(8,128)(2,1)S(1)} %maximum_select_fusion.8), channel_id=1, source_target_pairs={{0,16},{2,18},{4,20},{6,22},{8,24},{10,26},{12,28},{14,30},{16,0},... | collective-permute-start | bytes 2211848 | tf_op jit(solution)/shard_map/ppermute | solution.py:205
  724.8 13.0 %collective-permute-start.65 = (bf16[192,1920]{1,0:T(8,128)(2,1)S(1)}, bf16[192,1920]{1,0:T(8,128)(2,1)S(1)}, u32[]{:S(2)}, u32[]{:S(2)}) collective-permute-start(bf16[192,1920]{1,0:T(8,128)(2,1)S(1)} %maximum_select_fusion.9), channel_id=1, source_target_pairs={{0,48},{2,50},{4,52},{6,54},{8,56},{10,58},{12,60},{14,62},{16,32}... | collective-permute-start | bytes 2211848 | tf_op jit(solution)/shard_map/ppermute | solution.py:205
  (244 other events, 1613.6 us)

commit v2 on v1

v2 whole, which is shorter than its diff:
```python
import jax
import jax.numpy as jnp
from jax import lax
from jax.experimental import pallas as pl
from jax.experimental.pallas import tpu as pltpu
from jax.sharding import PartitionSpec as P

HEAD = 128
NORM_EPS = 1e-06
ROPE_BASE = 10000.0
BF16 = jnp.bfloat16
F32 = jnp.float32
SWAP = [(0, 1), (1, 0)]
VMEM_LIMIT = 52 * 1024 * 1024


def swap(value, axis):
    return lax.ppermute(value, axis, SWAP)


def slot_groups(experts):
    return [[e * 2 + ((e % 2) ^ s) for e in range(experts)] for s in range(2)]


def expert_exchange(value):
    return lax.all_to_all(
        value,
        ("expert", "tensor"),
        split_axis=0,
        concat_axis=0,
        axis_index_groups=slot_groups(value.shape[0]),
        tiled=True,
    )


def plane_groups(level):
    groups = []
    for z in range(2):
        for i in range(4):
            along_y = [(y * 4 + i) * 2 + z for y in range(4)]
            along_x = [(i * 4 + x) * 2 + z for x in range(4)]
            zero, one = (along_y, along_x) if level == 0 else (along_x, along_y)
            groups += [zero, [32 + e for e in one]]
    return groups


def mul(left, right, dims):
    return lax.dot_general(left, right, (dims, ((), ())), preferred_element_type=F32)


def mul_nn(left, right):
    return mul(left, right, ((1,), (0,)))


def mul_nt(left, right):
    return mul(left, right, ((1,), (1,)))


def mul_tn(left, right):
    return mul(left, right, ((0,), (0,)))


VMEM = pl.BlockSpec(memory_space=pltpu.VMEM)
SMEM = pl.BlockSpec(memory_space=pltpu.SMEM)
ANY = pl.BlockSpec(memory_space=pl.ANY)


def call(body, outs, in_specs, scratch, operands, name, spaces=None):
    return pl.pallas_call(
        body,
        out_shape=[jax.ShapeDtypeStruct(shape, kind) for shape, kind in outs],
        in_specs=in_specs,
        out_specs=spaces or [VMEM] * len(outs),
        scratch_shapes=scratch,
        compiler_params=pltpu.CompilerParams(vmem_limit_bytes=VMEM_LIMIT),
        cost_estimate=pl.CostEstimate(flops=1024, bytes_accessed=1024, transcendentals=0),
        name=name,
    )(*operands)


def fetch(own, mine, theirs, target, sem):
    @pl.when(own == 1)
    def _():
        pltpu.make_async_copy(mine, target, sem).start()

    @pl.when(own != 1)
    def _():
        pltpu.make_async_copy(theirs, target, sem).start()


def arrive(mine, target, sem):
    pltpu.make_async_copy(mine, target, sem).wait()


def rotary_tables(count):
    half = HEAD // 2
    frequency = ROPE_BASE ** (-(jnp.arange(half, dtype=F32) * 2.0) / HEAD)
    angles = jnp.arange(count, dtype=F32)[:, None] * frequency[None, :]
    cosine = jnp.concatenate([jnp.cos(angles), jnp.cos(angles)], axis=1)
    sine = jnp.concatenate([-jnp.sin(angles), jnp.sin(angles)], axis=1)
    return cosine, sine


def turn(vector, cosine, sine):
    return vector * cosine + pltpu.roll(vector, HEAD // 2, 1) * sine


def turn_back(grad, cosine, sine):
    return grad * cosine - pltpu.roll(grad, HEAD // 2, 1) * sine


def row_scale_of(rows):
    return lax.rsqrt(jnp.mean(rows * rows, axis=-1, keepdims=True) + NORM_EPS)


def norm_back(rows, scale, gain, grad):
    scaled = grad * gain
    return scale * scaled - rows * (scale * scale * scale) * jnp.mean(
        scaled * rows, axis=-1, keepdims=True
    )


def attention_weights(q, k):
    count = q.shape[0]
    scores = mul_nt(q, k)
    row = lax.broadcasted_iota(jnp.int32, (count, count), 0)
    column = lax.broadcasted_iota(jnp.int32, (count, count), 1)
    scores = jnp.where(row >= column, scores, -1e30)
    raised = jnp.exp(scores - jnp.max(scores, axis=-1, keepdims=True))
    return raised / jnp.sum(raised, axis=-1, keepdims=True)


def head_of(index):
    return slice(index * HEAD, (index + 1) * HEAD)


def attend_body(own, x_ref, h_ref, a_ref, b_ref, gain, cos, sin, refs, outs, scratch):
    (wq, wq_r, wk, wk_r, wv, wv_r, wo, wo_r) = refs
    (qkv_s, wo_s, sems) = scratch
    (branch, q_o, kv_o, o_o, x_o, y_o) = outs
    mine = own[0]
    width = wo.shape[0]
    heads = width // HEAD
    kv_at = width + HEAD
    moves = [
        (wq, wq_r, qkv_s.at[:, :width]),
        (wk, wk_r, qkv_s.at[:, width:kv_at]),
        (wv, wv_r, qkv_s.at[:, kv_at:]),
        (wo, wo_r, wo_s),
    ]
    for i, (a, b, target) in enumerate(moves):
        fetch(mine, a, b, target, sems.at[i])
    if h_ref is None:
        x = x_ref[...].astype(F32)
    else:
        y = h_ref[...] + (a_ref[...].astype(F32) + b_ref[...].astype(F32))
        y_o[...] = y
        x_o[...] = y.astype(BF16)
        x = y.astype(BF16).astype(F32)
    normed = (x * row_scale_of(x) * gain[...]).astype(BF16)
    cosine, sine = cos[...], sin[...]
    for i in range(3):
        arrive(moves[i][0], moves[i][2], sems.at[i])
    made = mul_nn(normed, qkv_s[...])
    k = turn(made[:, width : width + HEAD], cosine, sine).astype(BF16)
    v = made[:, width + HEAD :].astype(BF16)
    kv_o[:, :HEAD] = k
    kv_o[:, HEAD:] = v
    for i in range(heads):
        q = (turn(made[:, head_of(i)], cosine, sine) * HEAD**-0.5).astype(BF16)
        q_o[:, head_of(i)] = q
        weights = attention_weights(q, k)
        o_o[:, head_of(i)] = mul_nn(weights.astype(BF16), v).astype(BF16)
    arrive(wo, wo_s, sems.at[3])
    branch[...] = mul_nn(o_o[...], wo_s[...]).astype(BF16)


def attend_forward(own, source, gain, cosine, sine, weights):
    later = isinstance(source, tuple)
    count = cosine.shape[0]
    width, model = weights[6].shape

    def body(own_ref, *refs):
        if later:
            h_ref, a_ref, b_ref, gain_ref, cos, sin = refs[:6]
            x_ref, rest = None, refs[6:]
        else:
            x_ref, gain_ref, cos, sin = refs[:4]
            h_ref, a_ref, b_ref, rest = None, None, None, refs[4:]
        ws, rest = rest[:8], rest[8:]
        outs, scratch = (rest[:6], rest[6:]) if later else (rest[:4] + (None, None), rest[4:])
        attend_body(
            own_ref, x_ref, h_ref, a_ref, b_ref, gain_ref, cos, sin, ws, outs, scratch
        )

    outs = [
        ((count, model), BF16),
        ((count, width), BF16),
        ((count, 2 * HEAD), BF16),
        ((count, width), BF16),
    ]
    if later:
        outs += [((count, model), BF16), ((count, model), F32)]
    values = source if later else (source,)
    return call(
        body,
        outs,
        [SMEM] + [VMEM] * (len(values) + 3) + [ANY] * 8,
        [
            pltpu.VMEM((model, width + 2 * HEAD), BF16),
            pltpu.VMEM((width, model), BF16),
            pltpu.SemaphoreType.DMA((4,)),
        ],
        (own, *values, gain, cosine, sine, *weights),
        "attend_forward",
    )


def hot_of(routes_ref, experts):
    count = routes_ref.shape[1]
    names = lax.broadcasted_iota(jnp.int32, (experts, count), 0)
    hot = routes_ref[0:1, :] == names
    for pick in range(1, routes_ref.shape[0]):
        hot = hot | (routes_ref[pick : pick + 1, :] == names)
    return hot


def slot_tables(lane, routes, top, experts, lanes):
    count, model = top.shape
    slots = experts * lanes

    def body(lane_ref, first_ref, second_ref, top_ref, first_o, second_o, rows_o):
        row = lax.broadcasted_iota(jnp.int32, (count, count), 0)
        column = lax.broadcasted_iota(jnp.int32, (count, count), 1)
        before = jnp.where(row < column, 1.0, 0.0).astype(BF16)
        place = lax.broadcasted_iota(jnp.int32, (lanes, count), 0).astype(F32)
        start = (lane_ref[0] * lanes).astype(F32)
        for routes_ref, out in ((first_ref, first_o), (second_ref, second_o)):
            hot = hot_of(routes_ref, experts)
            rank = mul_nn(jnp.where(hot, 1.0, 0.0).astype(BF16), before)
            rank = jnp.where(hot, rank, -1.0) - start
            for e in range(experts):
                chosen = jnp.where(rank[e : e + 1, :] == place, 1.0, 0.0)
                out[e * lanes : (e + 1) * lanes, :] = chosen.astype(BF16)
        rows_o[...] = mul_nn(second_o[...], top_ref[...].astype(BF16)).astype(BF16)

    return call(
        body,
        [((slots, count), BF16), ((slots, count), BF16), ((slots, model), BF16)],
        [SMEM] + [VMEM] * 3,
        [],
        (lane, *routes, top),
        "slot_tables",
    )


def pair_columns(value, count):
    high = value.astype(BF16).astype(F32)
    lanes = lax.broadcasted_iota(jnp.int32, (count, HEAD), 1)
    both = jnp.where(lanes == 0, high, jnp.where(lanes == 1, value - high, 0.0))
    return both.astype(BF16)


def dispatch(table, routes, x, own, received, gain, router, lanes, with_gates):
    count, model = x.shape
    experts = router.shape[0]
    slots = experts * lanes
    wide = model + HEAD if with_gates else model

    def body(table_ref, routes_ref, x_ref, a_ref, b_ref, gain_ref, router_ref, *outs):
        h_o, rows_o, gated_o, gates_o = outs
        h = x_ref[...].astype(F32) + (a_ref[...].astype(F32) + b_ref[...].astype(F32))
        h_o[...] = h
        normed = (h * row_scale_of(h) * gain_ref[...]).astype(BF16)
        rows_o[:, :model] = mul_nn(table_ref[...], normed).astype(BF16)
        hot = hot_of(routes_ref, experts)
        logits = jnp.where(hot, mul_nt(router_ref[...], normed), -1e30)
        raised = jnp.where(hot, jnp.exp(logits - jnp.max(logits, axis=0, keepdims=True)), 0.0)
        gates = raised / jnp.sum(raised, axis=0, keepdims=True)
        gates_o[...] = gates
        for e in range(experts):
            spot = slice(e * lanes, (e + 1) * lanes)
            gated = table_ref[spot, :].astype(F32) * gates[e : e + 1, :]
            gated_o[spot, :] = gated.astype(BF16)
            if with_gates:
                total = jnp.sum(gated, axis=1, keepdims=True)
                rows_o[spot, model:] = pair_columns(total, lanes)

    return call(
        body,
        [
            ((count, model), F32),
            ((slots, wide), BF16),
            ((slots, count), BF16),
            ((experts, count), F32),
        ],
        [VMEM] * 7,
        [],
        (table, routes, x, own, received, gain, router),
        "dispatch",
    )


def collect(table, back, experts):
    slots, count = table.shape
    lanes = slots // experts
    model = back.shape[1] - HEAD

    def body(table_ref, back_ref, share_o, seen_s):
        share_o[:, :model] = mul_tn(table_ref[...], back_ref[:, :model]).astype(BF16)
        value = back_ref[:, model:].astype(F32)
        value = value[:, 0:1] + value[:, 1:2]
        seen_s[...] = jnp.zeros_like(seen_s)
        for e in range(experts):
            spot = slice(e * lanes, (e + 1) * lanes)
            part = table_ref[spot, :].astype(F32) * value[spot, :]
            seen_s[e : e + 1, :] = jnp.sum(part, axis=0, keepdims=True)
        seen = seen_s[:experts, :]
        high = seen.astype(BF16).astype(F32)
        seen_s[experts : 2 * experts, :] = seen - high
        seen_s[:experts, :] = high
        share_o[:, model:] = seen_s[...].T.astype(BF16)

    return call(
        body,
        [((count, model + HEAD), BF16)],
        [VMEM] * 2,
        [pltpu.VMEM((HEAD, count), F32)],
        (table, back),
        "collect",
    )[0]


def turn_over(grad, x, own, received, gain, table, gated, back, experts):
    slots, count = table.shape
    lanes = slots // experts
    model = x.shape[1]

    def body(g_ref, x_ref, a_ref, b_ref, gain_ref, table_ref, gated_ref, back_ref, *outs):
        grad_o, low_o, rows_o, seen_o = outs
        x_v = x_ref[...].astype(F32)
        da = a_ref[...].astype(F32) + b_ref[...].astype(F32)
        total = g_ref[...] + norm_back(x_v, row_scale_of(x_v), gain_ref[...], da)
        grad_o[...] = total
        low = total.astype(BF16)
        low_o[...] = low
        rows_o[...] = mul_nn(gated_ref[...], low).astype(BF16)
        seen = mul_nt(back_ref[...], low) * table_ref[...].astype(F32)
        for e in range(experts):
            spot = slice(e * lanes, (e + 1) * lanes)
            seen_o[e : e + 1, :] = jnp.sum(seen[spot, :], axis=0, keepdims=True)

    return call(
        body,
        [
            ((count, model), F32),
            ((count, model), BF16),
            ((slots, model), BF16),
            ((experts, count), F32),
        ],
        [VMEM] * 8,
        [],
        (grad, x, own, received, gain, table, gated, back),
        "turn_over",
    )


def expert_moves(sources, wgu, wd, half):
    hidden = 2 * half
    targets = (wgu.at[:, :half], wgu.at[:, hidden : hidden + half], wd.at[:half, :])
    targets += (wgu.at[:, half:hidden], wgu.at[:, hidden + half :], wd.at[half:, :])
    return [(sources[i], sources[i + 3], t) for i, t in zip((0, 1, 2, 6, 7, 8), targets)]


def experts_forward(own, rows, weights):
    slots, model = rows.shape
    half = weights[0].shape[1]
    hidden = 2 * half
    tile = 256

    def body(own_ref, x_ref, *refs):
        sources, (y_o, wgu, wd, h_s, sems) = refs[:12], refs[12:]
        moves = expert_moves(sources, wgu, wd, half)
        for i in (0, 1, 3, 4, 2, 5):
            fetch(own_ref[0], moves[i][0], moves[i][1], moves[i][2], sems.at[i])
        for i in (0, 1, 3, 4):
            arrive(moves[i][0], moves[i][2], sems.at[i])

        def step(c, carry):
            at = pl.multiple_of(c * tile, tile)
            gate = mul_nn(x_ref[...], wgu[:, pl.ds(at, tile)])
            up = mul_nn(x_ref[...], wgu[:, pl.ds(at + hidden, tile)])
            act = gate / (1.0 + jnp.exp(-gate))
            h_s[:, pl.ds(at, tile)] = (act * up).astype(BF16)
            return carry

        lax.fori_loop(0, hidden // tile, step, 0)
        for i in (2, 5):
            arrive(moves[i][0], moves[i][2], sems.at[i])

        def finish(c, carry):
            spot = pl.ds(pl.multiple_of(c * tile, tile), tile)
            y_o[:, spot] = mul_nn(h_s[...], wd[:, spot]).astype(BF16)
            return carry

        lax.fori_loop(0, model // tile, finish, 0)

    return call(
        body,
        [((slots, model), BF16)],
        [SMEM, VMEM] + [ANY] * 12,
        [
            pltpu.VMEM((model, 2 * hidden), BF16),
            pltpu.VMEM((hidden, model), BF16),
            pltpu.VMEM((slots, hidden), BF16),
            pltpu.SemaphoreType.DMA((6,)),
        ],
        (own, rows, *weights),
        "experts_forward",
    )[0]


def experts_backward(own, rows, grads, weights):
    slots, wide = rows.shape
    model, half = weights[0].shape
    hidden = 2 * half
    gated = wide > model
    tile = 256

    def body(own_ref, x_ref, g_ref, *refs):
        sources, refs = refs[:12], refs[12:]
        dx_o, h_o, dgu_o, wgu, wd, sems = refs[:6]
        moves = expert_moves(sources, wgu, wd, half)
        for i in (0, 1, 3, 4, 2, 5):
            fetch(own_ref[0], moves[i][0], moves[i][1], moves[i][2], sems.at[i])
        if gated:
            scale = x_ref[:, model:].astype(F32)
            scale = scale[:, 0:1] + scale[:, 1:2]
            seen_s = refs[6]
            seen_s[...] = jnp.zeros_like(seen_s)
        for i in range(6):
            arrive(moves[i][0], moves[i][2], sems.at[i])

        def step(c, carry):
            at = pl.multiple_of(c * tile, tile)
            spot, later = pl.ds(at, tile), pl.ds(at + hidden, tile)
            gate = mul_nn(x_ref[:, :model], wgu[:, spot])
            up = mul_nn(x_ref[:, :model], wgu[:, later])
            sig = 1.0 / (1.0 + jnp.exp(-gate))
            act = gate * sig
            made = act * up
            h_o[:, spot] = made.astype(BF16)
            grad_hidden = mul_nt(g_ref[...], wd[spot, :])
            if gated:
                seen = made * grad_hidden
                seen_s[...] += seen[:, :HEAD] + seen[:, HEAD:]
                grad_hidden = grad_hidden * scale
            dgu_o[:, spot] = (grad_hidden * up * sig * (1.0 + gate * (1.0 - sig))).astype(BF16)
            dgu_o[:, later] = (grad_hidden * act).astype(BF16)
            return carry

        lax.fori_loop(0, hidden // tile, step, 0)

        def finish(c, carry):
            spot = pl.ds(pl.multiple_of(c * tile, tile), tile)
            dx_o[:, spot] = mul_nt(dgu_o[...], wgu[spot, :]).astype(BF16)
            return carry

        lax.fori_loop(0, model // tile, finish, 0)
        if gated:
            total = jnp.sum(seen_s[...], axis=1, keepdims=True)
            dx_o[:, model:] = pair_columns(total, slots)

    return call(
        body,
        [((slots, wide), BF16), ((slots, hidden), BF16), ((slots, 2 * hidden), BF16)],
        [SMEM, VMEM, VMEM] + [ANY] * 12,
        [
            pltpu.VMEM((model, 2 * hidden), BF16),
            pltpu.VMEM((hidden, model), BF16),
            pltpu.SemaphoreType.DMA((6,)),
        ]
        + ([pltpu.VMEM((slots, HEAD), F32)] if gated else []),
        (own, rows, grads, *weights),
        "experts_backward",
    )


def experts_grads(own, rows, grads, hidden_rows, dgu, weights):
    slots, wide = rows.shape
    model, half = weights[0].shape
    hidden = 2 * half
    blocks = model // half
    gated = wide > model
    tile = 256

    def body(own_ref, x_ref, g_ref, h_ref, dgu_ref, *refs):
        sources, refs = refs[:4], refs[4:]
        near_o, far_o, refs = refs[0], refs[1], refs[2:]
        if gated:
            y_o, xt_s, dy_s, wd, sems = refs
            moves = [
                (sources[0], sources[1], wd.at[:half, :]),
                (sources[2], sources[3], wd.at[half:, :]),
            ]
            for i, (a, b, target) in enumerate(moves):
                fetch(own_ref[0], a, b, target, sems.at[i])
            scale = x_ref[:, model:].astype(F32)
            scale = scale[:, 0:1] + scale[:, 1:2]
            dy_s[...] = (g_ref[...].astype(F32) * scale).astype(BF16)
        else:
            (xt_s,), dy_s = refs, g_ref
        for i in range(model // tile):
            xt_s[i * tile : (i + 1) * tile, :] = x_ref[:, i * tile : (i + 1) * tile].T
        if gated:
            for i, (a, b, target) in enumerate(moves):
                arrive(a, target, sems.at[i])

        def step(c, carry):
            spot = pl.ds(pl.multiple_of(c * tile, tile), tile)
            made = mul_nn(xt_s[spot, :], dgu_ref[...]).astype(BF16)
            near_o[spot, :half] = made[:, :half]
            far_o[spot, :half] = made[:, half:hidden]
            near_o[spot, half:hidden] = made[:, hidden : hidden + half]
            far_o[spot, half:hidden] = made[:, hidden + half :]
            if gated:
                y_o[:, spot] = mul_nn(h_ref[...], wd[:, spot]).astype(BF16)
            return carry

        lax.fori_loop(0, model // tile, step, 0)
        down = tile // 2
        for i in range(hidden // down):
            made = mul_tn(h_ref[:, i * down : (i + 1) * down], dy_s[...]).astype(BF16)
            low = i * down
            out, low = (near_o, low) if low < half else (far_o, low - half)
            for j in range(blocks):
                at = j * half + low
                out[at : at + down, hidden:] = made[:, j * half : (j + 1) * half]

    outs = [((model, 3 * half), BF16)] * 2
    scratch = [pltpu.VMEM((model, slots), BF16)]
    if gated:
        outs = outs + [((slots, model), BF16)]
        scratch += [
            pltpu.VMEM((slots, model), BF16),
            pltpu.VMEM((hidden, model), BF16),
            pltpu.SemaphoreType.DMA((2,)),
        ]
    return call(
        body,
        outs,
        [SMEM] + [VMEM] * 4 + [ANY] * 4,
        scratch,
        (own, rows, grads, hidden_rows, dgu, *[weights[i] for i in (2, 5, 8, 11)]),
        "experts_grads",
    )


def attend_backward(
    own, grad, h, x, shares, gates, seen, router, moe_gain, attn_gain, kept, cosine, sine, weights
):
    count, model = h.shape
    width = weights[6].shape[0]
    heads = width // HEAD
    experts = router.shape[0]
    kv_at, out_at = width + HEAD, width + 2 * HEAD
    riding = len(seen) == 0

    def body(own_ref, *refs):
        (g_ref, h_ref, x_ref, a_ref, b_ref, gates_ref) = refs[:6]
        refs = refs[6:]
        if riding:
            tail = a_ref[:, model:].astype(F32) + b_ref[:, model:].astype(F32)
            tail = tail.T
            grad_gates = tail[:experts, :] + tail[experts : 2 * experts, :]
        else:
            grad_gates = refs[0][...] + refs[1][...]
            refs = refs[2:]
        (router_ref, mgain_ref, again_ref, q_ref, kv_ref, cos, sin) = refs[:7]
        (wq, wq_r, wk, wk_r, wv, wv_r, wo, wo_r) = refs[7:15]
        (dqkv_o, da_o, gh_o, dlogits_o, gains_o) = refs[15:20]
        (qkv_s, wo_s, sems) = refs[20:]
        mine = own_ref[0]
        moves = [
            (wo, wo_r, wo_s),
            (wq, wq_r, qkv_s.at[:, :width]),
            (wk, wk_r, qkv_s.at[:, width:kv_at]),
            (wv, wv_r, qkv_s.at[:, kv_at:]),
        ]
        for i, (a, b, target) in enumerate(moves):
            fetch(mine, a, b, target, sems.at[i])
        gates_v = gates_ref[...]
        dlogits = gates_v * (grad_gates - jnp.sum(gates_v * grad_gates, axis=0, keepdims=True))
        dlogits = dlogits.astype(BF16)
        dlogits_o[...] = dlogits
        dn = a_ref[:, :model].astype(F32) + b_ref[:, :model].astype(F32)
        dn = dn + mul_tn(dlogits, router_ref[...])
        hv = h_ref[...]
        scale = row_scale_of(hv)
        gh = g_ref[...].astype(F32) + norm_back(hv, scale, mgain_ref[...], dn)
        gh_o[...] = gh
        moe_part = jnp.sum(dn * hv * scale, axis=0, keepdims=True)
        dz = gh.astype(BF16)
        arrive(wo, wo_s, sems.at[0])
        do = mul_nt(dz, wo_s[...]).astype(BF16)
        cosine_v, sine_v = cos[...], sin[...]
        k, v = kv_ref[:, :HEAD], kv_ref[:, HEAD:]
        dk, dv = 0.0, 0.0
        for i in range(heads):
            q = q_ref[:, head_of(i)]
            p = attention_weights(q, k)
            do_i = do[:, head_of(i)]
            dp = mul_nt(do_i, v)
            ds = (p * (dp - jnp.sum(p * dp, axis=-1, keepdims=True))).astype(BF16)
            dv = dv + mul_tn(p.astype(BF16), do_i)
            dk = dk + mul_tn(ds, q)
            dq = turn_back(mul_nn(ds, k), cosine_v, sine_v) * HEAD**-0.5
            dqkv_o[:, head_of(i)] = dq.astype(BF16)
        dqkv_o[:, width:kv_at] = turn_back(dk, cosine_v, sine_v).astype(BF16)
        dqkv_o[:, kv_at:] = dv.astype(BF16)
        for i in range(1, 4):
            arrive(moves[i][0], moves[i][2], sems.at[i])
        da = mul_nt(dqkv_o[...], qkv_s[...])
        da_o[...] = da.astype(BF16)
        xv = x_ref[...].astype(F32)
        attn_part = jnp.sum(da * xv * row_scale_of(xv), axis=0, keepdims=True)
        lane = lax.broadcasted_iota(jnp.int32, (16, model), 0)
        total = jnp.zeros((16, model), F32)
        for i, value in enumerate((attn_part, moe_part)):
            high = value.astype(BF16).astype(F32)
            total = jnp.where(lane == 2 * i, high, total)
            total = jnp.where(lane == 2 * i + 1, value - high, total)
        gains_o[...] = total.astype(BF16)

    q, kv, _ = kept
    operands = (own, grad, h, x, *shares, gates, *seen, router, moe_gain, attn_gain)
    operands += (q, kv, cosine, sine)
    return call(
        body,
        [
            ((count, out_at), BF16),
            ((count, model), BF16),
            ((count, model), F32),
            ((experts, count), BF16),
            ((16, model), BF16),
        ],
        [SMEM] + [VMEM] * (len(operands) - 1) + [ANY] * 8,
        [
            pltpu.VMEM((model, out_at), BF16),
            pltpu.VMEM((width, model), BF16),
            pltpu.SemaphoreType.DMA((4,)),
        ],
        (*operands, *weights),
        "attend_backward",
    )


def attend_grads(own, x, h, grad_h, o, dqkv, dlogits, gains, attn_gain, moe_gain):
    count, model = h.shape
    width, out_at = o.shape[1], dqkv.shape[1]
    experts = dlogits.shape[0]
    side_at = out_at + model // 2
    tile = 256
    parts = model // tile // 2

    def body(own_ref, x_ref, h_ref, gh_ref, o_ref, dqkv_ref, dl_ref, gains_ref, again, mgain, *rest):
        keep_o, give_o, left_s, pack_s, sems = rest
        xv = x_ref[...].astype(F32)
        normed = (xv * row_scale_of(xv) * again[...]).astype(BF16)
        for i in range(model // tile):
            left_s[i * tile : (i + 1) * tile, :] = normed[:, i * tile : (i + 1) * tile].T
        hv = h_ref[...]
        normed_m = (hv * row_scale_of(hv) * mgain[...]).astype(BF16)
        dz = gh_ref[...].astype(BF16)
        row = lax.broadcasted_iota(jnp.int32, (experts, HEAD), 0)
        column = lax.broadcasted_iota(jnp.int32, (experts, HEAD), 1)
        spread_logits = mul_tn(dl_ref[...], jnp.where(row == column, 1.0, 0.0).astype(BF16))
        spread_logits = spread_logits.astype(BF16)
        row = lax.broadcasted_iota(jnp.int32, (16, HEAD), 0)
        column = lax.broadcasted_iota(jnp.int32, (16, HEAD), 1)
        hit = (column == experts + row // 2) & (row < 4)
        marks = jnp.where(hit, 1.0, 0.0).astype(BF16)

        def step(c, carry):
            spot = pl.ds(pl.multiple_of(c * tile, tile), tile)
            target = pl.ds(pl.multiple_of(lax.rem(c, parts) * tile, tile), tile)
            made = mul_nn(left_s[spot, :], dqkv_ref[...]).astype(BF16)
            pack_s[lax.div(c, parts), target, :out_at] = made
            return carry

        lax.fori_loop(0, model // tile, step, 0)
        for i in range(width // HEAD):
            made = mul_tn(o_ref[:, head_of(i)], dz).astype(BF16)
            spot = slice(i * HEAD, (i + 1) * HEAD)
            pack_s[0, spot, out_at:side_at] = made[:, : model // 2]
            pack_s[1, spot, out_at:side_at] = made[:, model // 2 :]
        for i in range(model // tile):
            spot = slice(i * tile, (i + 1) * tile)
            total = mul_tn(normed_m[:, spot], spread_logits) + mul_tn(gains_ref[:, spot], marks)
            at = (i % parts) * tile
            pack_s[i // parts, at : at + tile, side_at:] = total.astype(BF16)
        kept = 1 - own_ref[0]
        copies = [
            pltpu.make_async_copy(pack_s.at[kept], keep_o, sems.at[0]),
            pltpu.make_async_copy(pack_s.at[1 - kept], give_o, sems.at[1]),
        ]
        for copy in copies:
            copy.start()
        for copy in copies:
            copy.wait()

    return call(
        body,
        [((model // 2, side_at + HEAD), BF16)] * 2,
        [SMEM] + [VMEM] * 9,
        [
            pltpu.VMEM((model, count), BF16),
            pltpu.VMEM((2, model // 2, side_at + HEAD), BF16),
            pltpu.SemaphoreType.DMA((2,)),
        ],
        (own, x, h, grad_h, o, dqkv, dlogits, gains, attn_gain, moe_gain),
        "attend_grads",
        [ANY, ANY],
    )


def ff_total(core, zero, one):
    model, wide = zero[0].shape
    half = wide // 3
    blocks = model // half
    pieces = len(zero) - 2
    rows = model // pieces
    count = len(zero)

    def body(core_ref, *refs):
        ins, outs, (held, sems) = refs[: 2 * count], refs[2 * count : 2 * count + 3], refs[-2:]
        targets = [held.at[0], held.at[1]]
        targets += [held.at[2, i * rows : (i + 1) * rows] for i in range(pieces)]
        for i, target in enumerate(targets):
            fetch(core_ref[0], ins[count + i], ins[i], target, sems.at[i])
        for i, target in enumerate(targets):
            arrive(ins[i], target, sems.at[i])

        def total(rows, columns):
            return (
                held[0, rows, columns].astype(F32)
                + held[1, rows, columns].astype(F32)
                + held[2, rows, columns].astype(F32)
            )

        for i in range(blocks):
            spot = slice(i * half, (i + 1) * half)
            outs[0][spot, :] = total(spot, slice(0, half))
            outs[1][spot, :] = total(spot, slice(half, 2 * half))
            outs[2][:, spot] = total(spot, slice(2 * half, wide))

    return call(
        body,
        [((model, half), F32), ((model, half), F32), ((half, model), F32)],
        [SMEM] + [ANY] * (2 * count),
        [pltpu.VMEM((3, model, wide), BF16), pltpu.SemaphoreType.DMA((count,))],
        (core, *zero, *one),
        "ff_total",
    )


def attn_total(core, zero, one, width, model):
    rows, wide = zero[0].shape
    out_at = width + 2 * HEAD
    side_at = out_at + model // 2

    def body(core_ref, *refs):
        ins, outs, (held, sems) = refs[:4], refs[4:9], refs[9:]
        for i in range(2):
            fetch(core_ref[0], ins[2 + i], ins[i], held.at[i], sems.at[i])
        query, key, value, out, side = outs
        for i in range(2):
            arrive(ins[i], held.at[i], sems.at[i])
            spot = slice(i * rows, (i + 1) * rows)
            query[spot, :] = held[i, :, :width].astype(F32)
            key[spot, :] = held[i, :, width : width + HEAD].astype(F32)
            value[spot, :] = held[i, :, width + HEAD : out_at].astype(F32)
            out[:, i * (model // 2) : (i + 1) * (model // 2)] = held[i, :, out_at:side_at].astype(F32)
            side[spot, :] = held[i, :, side_at:].astype(F32)

    return call(
        body,
        [
            ((model, width), F32),
            ((model, HEAD), F32),
            ((model, HEAD), F32),
            ((width, model), F32),
            ((model, wide - side_at), F32),
        ],
        [SMEM] + [ANY] * 4,
        [pltpu.VMEM((2, rows, wide), BF16), pltpu.SemaphoreType.DMA((2,))],
        (core, *zero, *one),
        "attn_total",
    )


def exchange_rows(rows, experts):
    return expert_exchange(rows.reshape(experts, -1, rows.shape[1])).reshape(-1, rows.shape[1])


def plane_exchange(value, level):
    return lax.all_to_all(
        value,
        ("pipe", "expert"),
        split_axis=0,
        concat_axis=0,
        axis_index_groups=plane_groups(level),
        tiled=True,
    )


def plane_sum(value, level):
    rows, wide = value.shape
    arrived = plane_exchange(value.reshape(4, rows // 4, wide), level)
    return jnp.sum(arrived.astype(F32), axis=0).astype(BF16)


def plane_copy(piece, level):
    rows, wide = piece.shape
    spread = jnp.broadcast_to(piece[None], (4, rows, wide))
    return plane_exchange(spread, level).reshape(4 * rows, wide)


def plane_gather(piece, level):
    return lax.all_gather(
        piece, ("pipe", "expert"), axis=0, axis_index_groups=plane_groups(level), tiled=True
    )


def across_planes(piece):
    return piece + lax.ppermute(piece, "expert", [(e, e ^ 1) for e in range(32)])


def after(value, *others):
    return lax.optimization_barrier((value, *others))[0]


def on_device(
    tokens,
    cotangent,
    routes,
    attn_gain,
    w_query,
    key_weight,
    value_weight,
    w_out,
    moe_gain,
    w_router,
    w_gate,
    w_up,
    w_down,
):
    core = lax.axis_index("pipe")
    part = lax.axis_index("tensor")
    first = core == 0
    experts = w_router.shape[2]
    count, model = tokens.shape[1], tokens.shape[2]
    lanes = 2 * routes.shape[3] * count // experts // 2
    lane = (part ^ (lax.axis_index("expert") % 2)).astype(jnp.int32).reshape(1)
    owns = [(core == layer).astype(jnp.int32).reshape(1) for layer in range(2)]

    mine = lax.dynamic_index_in_dim(routes[0], core, 0, keepdims=False)
    give = lax.dynamic_index_in_dim(routes[0], 1 - core, 0, keepdims=False)
    got = swap(give, "pipe")
    picks = [jnp.where(first, mine, got).T, jnp.where(first, got, mine).T]
    half = w_gate.shape[3]
    width = w_out.shape[1]
    mine_w = (w_query[0], key_weight[0], value_weight[0], w_out[0])
    attn_weights = [v for w in mine_w for v in (w, swap(w, "pipe"))]
    small = jnp.concatenate([w_router[0].T, attn_gain, moe_gain], axis=0)
    small_r = swap(small, "pipe")
    smalls = jnp.where(first, small, small_r), jnp.where(first, small_r, small)
    routers = [v[:experts] for v in smalls]
    attn_gains = [v[experts : experts + 1].astype(F32) for v in smalls]
    moe_gains = [v[experts + 1 :].astype(F32) for v in smalls]

    def over(value, layer):
        return lax.ppermute(value, "pipe", [(1 - layer, layer)])

    def across(value, layer):
        pairs = [(2 * layer, 2 * layer + 1), (2 * layer + 1, 2 * layer)]
        return lax.ppermute(value, ("pipe", "tensor"), pairs)

    cosine, sine = rotary_tables(count)
    x_0 = lax.dynamic_index_in_dim(tokens, core, 0, keepdims=False)
    top = lax.dynamic_index_in_dim(cotangent, core, 0, keepdims=False)
    near = (w_gate[0, 0], w_up[0, 0], w_down[0, 0])
    far_0 = [across(near[0], 0)]

    table_0, table_1, top_rows = slot_tables(lane, picks, top, experts, lanes)
    x_0 = after(x_0, table_0)
    branch, *kept_0 = attend_forward(owns[0], x_0, attn_gains[0], cosine, sine, attn_weights)
    branch_r = swap(after(branch, far_0[0]), "tensor")
    far_0 += [across(after(w, branch_r), 0) for w in near[1:]]
    h_0, rows, gated_0, gates_0 = dispatch(
        table_0, picks[0], x_0, branch, branch_r, moe_gains[0], routers[0], lanes, False
    )
    rows_0 = exchange_rows(rows, experts)
    near_r = [swap(after(w, branch_r), "pipe") for w in near]
    far_0r = [over(w, 1) for w in far_0]
    rows_0 = after(rows_0, *near_r, *far_0r)
    far_1 = [across(after(w, rows_0), 1) for w in near[:2]]
    ff_0 = (*near, *near_r, *far_0, *far_0r)
    back_0 = exchange_rows(experts_forward(owns[0], rows_0, ff_0), experts)
    share = after(mul_tn(gated_0, back_0).astype(BF16), *far_1)
    share_r = swap(share, "tensor")
    top_rows = exchange_rows(after(top_rows, share), experts)
    far_1r = [over(after(w, share_r), 0) for w in far_1]

    branch, *kept_1, x_1, y_0 = attend_forward(
        owns[1], (h_0, share, share_r), attn_gains[1], cosine, sine, attn_weights
    )
    branch_r = swap(branch, "tensor")
    far_1 += [across(after(near[2], branch_r), 1)]
    far_1r += [over(far_1[2], 0)]
    h_1, rows, gated_1, gates_1 = dispatch(
        table_1, picks[1], x_1, branch, branch_r, moe_gains[1], routers[1], lanes, True
    )
    rows_1 = exchange_rows(after(rows, top_rows), experts)
    ff_1 = (*near, *near_r, *far_1, *far_1r)
    dx, made, dgu = experts_backward(owns[1], rows_1, top_rows, ff_1)
    dx = exchange_rows(dx, experts)
    near_1, far_g1, out_rows = experts_grads(owns[1], rows_1, top_rows, made, dgu, ff_1)
    dx = after(dx, near_1)
    pieces = model // 3

    def far_pieces(mine, theirs):
        return [
            mine[i : i + pieces] + theirs[i : i + pieces] for i in range(0, model, pieces)
        ]

    share = collect(table_1, dx, experts)
    share_r = swap(share, "tensor")
    back_1 = exchange_rows(after(out_rows, share), experts)
    near_1r, far_r = over(after(near_1, share), 1), over(after(far_g1, share), 1)
    dqkv, da, grad_h, dlogits, gains = attend_backward(
        owns[1], top, h_1, x_1, (share, share_r), gates_1, (),
        routers[1], moe_gains[1], attn_gains[1], kept_1, cosine, sine, attn_weights,
    )
    da_r = swap(after(da, near_1r, far_r), "tensor")
    far_sum = far_pieces(far_g1, far_r)
    keep, give = attend_grads(
        owns[1], x_1, h_1, grad_h, kept_1[2], dqkv, dlogits, gains, attn_gains[1], moe_gains[1]
    )
    grad_1, grad, rows, seen = turn_over(
        grad_h, x_1, da, after(da_r, back_1, keep), attn_gains[1], table_0, gated_0, back_0,
        experts,
    )

    seen_r = swap(seen, "tensor")
    grad_rows = exchange_rows(rows, experts)
    far_z = [across(after(far_sum[0], rows), 1)]
    half_1 = keep + swap(after(give, rows), "pipe")
    share = mul_tn(gated_1, back_1).astype(BF16)
    share_r = swap(after(share, rows), "tensor")
    grad_rows = after(grad_rows, half_1, share_r, seen_r, far_z[0])
    y_1 = h_1 + (share.astype(F32) + share_r.astype(F32))
    far_z += [across(after(far_sum[1], grad_rows), 1)]
    dx, made, dgu = experts_backward(owns[0], rows_0, grad_rows, ff_0)
    far_z += [across(after(far_sum[2], dx), 1)]
    ff_grads_1 = (near_1, near_1r, *far_z)
    dx = exchange_rows(after(dx, far_z[1]), experts)
    near_0, far_g0 = experts_grads(owns[0], rows_0, grad_rows, made, dgu, ff_0)
    dx = after(dx, near_0, far_z[2])
    share = mul_tn(table_0, dx).astype(BF16)
    share_r = swap(share, "tensor")
    level_1 = plane_sum(after(half_1, share), 0)
    near_0r, far_r = over(after(near_0, share), 0), over(after(far_g0, share), 0)
    dqkv, da, grad_h, dlogits, gains = attend_backward(
        owns[0], grad, h_0, x_0, (share, share_r), gates_0, (seen, seen_r),
        routers[0], moe_gains[0], attn_gains[0], kept_0, cosine, sine, attn_weights,
    )
    da_r = swap(after(da, near_0r, far_r), "tensor")
    keep, give = attend_grads(
        owns[0], x_0, h_0, grad_h, kept_0[2], after(dqkv, level_1), dlogits, gains,
        attn_gains[0], moe_gains[0],
    )
    far_sum = far_pieces(far_g0, far_r)

    half_0 = after(keep, *far_sum) + swap(give, "pipe")
    far_z = [across(after(far_sum[0], half_0), 0)]
    level_0 = plane_sum(half_0, 0)
    level = after(jnp.concatenate([level_0, level_1], axis=1), far_z[0], da_r)
    wide = level_0.shape[1]
    piece = across_planes(plane_sum(level, 1))
    far_z += [across(after(v, piece), 0) for v in far_sum[1:]]
    part = plane_copy(piece, 1)
    da = da.astype(F32) + da_r.astype(F32)
    x_f = x_0.astype(F32)
    grad_0 = grad_h + norm_back(x_f, row_scale_of(x_f), attn_gains[0], da)
    ff_grads_0 = (near_0, near_0r, *far_z)

    def by_layer(zero, one):
        own, other = jnp.where(first, zero, one), jnp.where(first, one, zero)
        got = swap(other, "pipe")
        return got, jnp.where(first, jnp.stack([own, got]), jnp.stack([got, own]))

    got_y, layer_out = by_layer(y_0, y_1)
    got_g, input_grads = by_layer(grad_0, grad_1)
    part = after(part, got_y, got_g)
    sum_0 = plane_copy(part[:, :wide], 0)
    sum_1 = plane_gather(part[:, wide:], 0)
    core_v = core.astype(jnp.int32).reshape(1)
    gate_g, up_g, down_g = ff_total(core_v, ff_grads_0, ff_grads_1)
    over_0, over_1 = over(after(sum_0, gate_g), 0), over(sum_1, 1)
    query_g, key_g, value_g, out_g, side = attn_total(
        core_v, (sum_0, over_0), (sum_1, over_1), width, model
    )
    at = wide - HEAD + experts
    attn_part = jnp.concatenate(
        [
            jnp.where(first, zero[:, at], one[:, at]).astype(F32)
            for zero, one in ((sum_0, sum_1), (over_0, over_1))
        ]
    )
    attn_part = attn_part + swap(attn_part, "tensor")
    return (
        layer_out[None],
        input_grads[None],
        attn_part[None],
        query_g[None],
        key_g[None],
        value_g[None],
        out_g[None],
        side[:, experts + 1][None],
        side[:, :experts][None],
        gate_g[None, None],
        up_g[None, None],
        down_g[None, None],
    )


def solution(mesh):
    layered = P("pipe", None, "expert", None)
    by_expert = P("pipe", "expert", None, "tensor")
    columns = P("pipe", None, "tensor")
    rows = P("pipe", "tensor", None)
    down = P("pipe", "expert", "tensor", None)
    whole = P("pipe", None)
    router = P("pipe", None, None)
    tokens = P(None, "expert", None)
    return jax.shard_map(
        on_device,
        mesh=mesh,
        in_specs=(
            tokens,
            tokens,
            layered,
            whole,
            columns,
            columns,
            columns,
            rows,
            whole,
            router,
            by_expert,
            by_expert,
            down,
        ),
        out_specs=(
            layered,
            layered,
            whole,
            columns,
            columns,
            columns,
            rows,
            whole,
            router,
            by_expert,
            by_expert,
            down,
        ),
        check_vma=False,
    )
```

time: 766 us -> 580 us (0.76)
  matrix products: 171 us -> 5.4 us
  waiting for transfers between devices: 338 us -> 188 us
  Pallas kernels: 0 us -> 130 us
  starting transfers between devices: 116 us -> 160 us
  other arithmetic: 77.3 us -> 42.4 us
  local copies, waits for them, and re-layouts: 49.5 us -> 28.5 us
  between operations: 4.08 us -> 15.9 us
    ppermute x39 -> x23, waiting for transfers between devices: 198 us -> 45.1 us  [swap(): return lax.ppermute(value, axis, SWAP)]
    dot_general x78 -> x3, matrix products: 156 us -> 5.4 us  [mul(): lax.dot_general(left, right, (dims, ((), ())), preferred_element_type=F32)]
    pallas_call x0 -> x18, Pallas kernels: none -> 130 us  [call(): pl.pallas_call(body, out_shape=[jax.ShapeDtypeStruct(shape, kind) for sha...]
    all_to_all x8 -> x13, starting transfers between devices: 48.3 us -> 76.1 us  [the longest x8 55 us: expert_exchange(): lax.all_to_all(value, ('expert', 'tensor'), split_axis=0, concat_axis=0,...]
    ppermute x36 -> x25, starting transfers between devices: 43.8 us -> 64.7 us  [the longest x12 31.8 us: over(): return lax.ppermute(value, 'pipe', [(1 - layer, layer)])]
    convert_element_type x22 -> x3, other arithmetic: 18.5 us -> 0.78 us  [the longest x1 0.76 us: on_device(): attn_gains = [v[experts:experts + 1].astype(F32) for v in smalls]]
    broadcast_in_dim x6 -> x0, other arithmetic: 15.6 us -> none  [the longest x1 5.09 us: on_device(): grad_out[None]]
    another operation x6 -> x0, local copies, waits for them, and re-layouts: 12.7 us -> none  [the longest x5 12.1 us: expert_sum(): parts = list(value.reshape(4, value.shape[0] // 4, value.shape[1]))]
  transfers between devices with their start and end apart: 83 -> 62, of which waited for: 36 -> 28; matrix products, arithmetic and copies ran while one was open for 30% -> 9% of each run, Pallas kernels for 0% -> 16%
where the time goes in v2:
time: 580 us; the launch traced here: 570 us
  waiting for transfers between devices  188 us (32%)
  starting transfers between devices  160 us (28%)
  Pallas kernels  130 us (22%)
  other arithmetic  42.4 us (7%)
  local copies, waits for them, and re-layouts  28.5 us (5%)
  between operations  15.9 us (3%)
    pallas_call x18, Pallas kernels, call(): pl.pallas_call(body, out_shape=[jax.ShapeDtypeStruct(shape, kind) for sha...  130 us
    all_to_all x8, starting transfers between devices, expert_exchange(): lax.all_to_all(value, ('expert', 'tensor'), split_axis=0, concat_axis=0,...  55 us
    all_to_all x8, waiting for transfers between devices, expert_exchange(): lax.all_to_all(value, ('expert', 'tensor'), split_axis=0, concat_axis=0,...  49.9 us
    ppermute x23, waiting for transfers between devices, swap(): return lax.ppermute(value, axis, SWAP)  45.1 us
    all_to_all x5, waiting for transfers between devices, plane_exchange(): lax.all_to_all(value, ('pipe', 'expert'), split_axis=0, concat_axis=0, ax...  38.9 us
    ppermute x12, waiting for transfers between devices, across(): return lax.ppermute(value, ('pipe', 'tensor'), pairs)  35.2 us
    ppermute x12, starting transfers between devices, over(): return lax.ppermute(value, 'pipe', [(1 - layer, layer)])  31.8 us
    ppermute x12, starting transfers between devices, across(): return lax.ppermute(value, ('pipe', 'tensor'), pairs)  27.7 us
  transfers between devices with their start and end apart: 62, of which 28 were waited for; matrix products, arithmetic and copies ran while one was open for 9% of the time, Pallas kernels for 16%

profile of v2, /device:TPU:0, one launch (start us, length us, event | category | flops | bytes accessed | tf_op | source)
XLA Modules:
  0.0 569.8 jit_solution(14675427028524827454)
XLA Ops:
  21.2 4.8 attend_forward.2
  33.8 4.8 collective-permute-done.7.b_ref
  47.3 9.9 %all-to-all-start = ((bf16[32,16,1536]{2,1,0:T(8,128)(2,1)}), bf16[32,16,1536]{2,1,0:T(8,128)(2,1)}, u32[]{:S(2)}, u32[]{:S(2)}) async-start(bf16[32,16,1536]{2,1,0:T(8,128)(2,1)} %bitcast.120), calls=%async_computation | async-start | bytes 3145728 | tf_op jit(solution)/shard_map/all_to_all | solution.py:26
  61.2 8.4 %collective-permute-done.14.refs_8_.refs_2_ = bf16[384,1536]{1,0:T(8,128)(2,1)} collective-permute-done((bf16[384,1536]{1,0:T(8,128)(2,1)S(1)}, bf16[384,1536]{1,0:T(8,128)(2,1)}, u32[]{:S(2)}, u32[]{:S(2)}) %collective-permute-start.14) | collective-permute-done | bytes 1179680 | tf_op jit(solution)/shard_map/ppermute | solution.py:887
  75.7 10.0 %experts_forward.1 = bf16[512,1536]{1,0:T(8,128)(2,1)} custom-call(s32[1]{0:T(128)} %bitcast.8.own_ref, bf16[512,1536]{1,0:T(8,128)(2,1)} %bitcast.17.x_ref, bf16[1536,384]{1,0:T(8,128)(2,1)S(1)} %bitcast.83, bf16[1536,384]{1,0:T(8,128)(2,1)} %bitcast.18.refs_1_, bf16[384,1536]{1,0:T(8,128)(2,1)} %bitcast.73, bf16[1536,384]{1,0:T(8,128)(2,1)} %copy-done.64, ...), custom_call_target="tpu_custom_call" | custom-call | flops 1024 | bytes 1024 | tf_op jit(solution)/shard_map/experts_forward/pallas_call | solution.py:69
  85.7 7.8 %all-to-all-start.1 = ((bf16[32,16,1536]{2,1,0:T(8,128)(2,1)}), bf16[32,16,1536]{2,1,0:T(8,128)(2,1)}, u32[]{:S(2)}, u32[]{:S(2)}) async-start(bf16[32,16,1536]{2,1,0:T(8,128)(2,1)} %bitcast.112), calls=%async_computation.1 | async-start | bytes 3145728 | tf_op jit(solution)/shard_map/all_to_all | solution.py:26
  95.9 23.1 %all-to-all-done.1 = bf16[32,16,1536]{2,1,0:T(8,128)(2,1)} async-done(((bf16[32,16,1536]{2,1,0:T(8,128)(2,1)}), bf16[32,16,1536]{2,1,0:T(8,128)(2,1)}, u32[]{:S(2)}, u32[]{:S(2)}) %all-to-all-start.1) | async-done | bytes 1572896 | tf_op jit(solution)/shard_map/all_to_all | solution.py:26
  121.8 5.2 all-to-all-start.2
  127.0 4.3 collective-permute-done.18.refs_2_
  131.3 6.7 %attend_forward.3 = (bf16[128,1536]{1,0:T(8,128)(2,1)S(1)}, bf16[128,768]{1,0:T(8,128)(2,1)S(1)}, bf16[128,256]{1,0:T(8,128)(2,1)S(1)}, bf16[128,768]{1,0:T(8,12...) custom-call(s32[1]{0:T(128)} %bitcast.own_ref, f32[128,1536]{1,0:T(8,128)} %get-tuple-element.114.refs_0_.refs_1_.h_ref, ...), custom_call_target="tpu_custom_call" | custom-call | flops 1024 | bytes 1024 | tf_op jit(solution)/shard_map/attend_forward/pallas_call | solution.py:69
  139.4 7.8 %collective-permute-done.19.b_ref = bf16[128,1536]{1,0:T(8,128)(2,1)S(1)} collective-permute-done((bf16[128,1536]{1,0:T(8,128)(2,1)S(1)}, bf16[128,1536]{1,0:T(8,128)(2,1)S(1)}, u32[]{:S(2)}, u32[]{:S(2)}) %collective-permute-start.19) | collective-permute-done | bytes 393248 | tf_op jit(solution)/shard_map/ppermute | solution.py:18
  153.9 5.9 %all-to-all-start.3 = ((bf16[32,16,1664]{2,1,0:T(8,128)(2,1)}), bf16[32,16,1664]{2,1,0:T(8,128)(2,1)}, u32[]{:S(2)}, u32[]{:S(2)}) async-start(bf16[32,16,1664]{2,1,0:T(8,128)(2,1)} %bitcast.115), calls=%async_computation.3 | async-start | bytes 3407872 | tf_op jit(solution)/shard_map/all_to_all | solution.py:26
  163.7 8.9 %collective-permute-done.21.refs_9_ = bf16[1536,384]{1,0:T(8,128)(2,1)S(1)} collective-permute-done((bf16[1536,384]{1,0:T(8,128)(2,1)}, bf16[1536,384]{1,0:T(8,128)(2,1)S(1)}, u32[]{:S(2)}, u32[]{:S(2)}) %collective-permute-start.21) | collective-permute-done | bytes 1179680 | tf_op jit(solution)/shard_map/ppermute | solution.py:883
  179.9 14.4 %experts_backward.2 = (bf16[512,1664]{1,0:T(8,128)(2,1)}, bf16[512,768]{1,0:T(8,128)(2,1)S(1)}, bf16[512,1536]{1,0:T(8,128)(2,1)}) custom-call(s32[1]{0:T(128)} %bitcast.own_ref, bf16[512,1664]{1,0:T(8,128)(2,1)} %bitcast.25.x_ref, bf16[512,1536]{1,0:T(8,128)(2,1)} %bitcast.23.g_ref, bf16[1536,384]{1,0:T(8,128)(2,1)S(1)} %bitcast.85, ...), custom_call_target="tpu_custom_call" | custom-call | flops 1024 | bytes 1024 | tf_op jit(solution)/shard_map/experts_backward/pallas_call | solution.py:69
  194.4 6.5 %all-to-all-start.4 = ((bf16[32,16,1664]{2,1,0:T(8,128)(2,1)}), bf16[32,16,1664]{2,1,0:T(8,128)(2,1)}, u32[]{:S(2)}, u32[]{:S(2)}) async-start(bf16[32,16,1664]{2,1,0:T(8,128)(2,1)} %bitcast.116), calls=%async_computation.4 | async-start | bytes 3407872 | tf_op jit(solution)/shard_map/all_to_all | solution.py:26
  200.9 13.3 %experts_grads.2 = (bf16[1536,1152]{1,0:T(8,128)(2,1)}, bf16[1536,1152]{1,0:T(8,128)(2,1)}, bf16[512,1536]{1,0:T(8,128)(2,1)}) custom-call(s32[1]{0:T(128)} %bitcast.own_ref, bf16[512,1664]{1,0:T(8,128)(2,1)} %bitcast.25.x_ref, bf16[512,1536]{1,0:T(8,128)(2,1)} %bitcast.23.g_ref, bf16[512,768]{1,0:T(8,128)(2,1)S(1)} %get-tuple-element.137.h_ref, ...), custom_call_target="tpu_custom_call" | custom-call | flops 1024 | bytes 1024 | tf_op jit(solution)/shard_map/experts_grads/pallas_call | solution.py:69
  214.1 10.1 %all-to-all-done.4 = bf16[32,16,1664]{2,1,0:T(8,128)(2,1)} async-done(((bf16[32,16,1664]{2,1,0:T(8,128)(2,1)}), bf16[32,16,1664]{2,1,0:T(8,128)(2,1)}, u32[]{:S(2)}, u32[]{:S(2)}) %all-to-all-start.4) | async-done | bytes 1703968 | tf_op jit(solution)/shard_map/all_to_all | solution.py:26
  226.1 8.1 %collective-permute-start.25 = (bf16[1536,1152]{1,0:T(8,128)(2,1)}, bf16[1536,1152]{1,0:T(8,128)(2,1)}, u32[]{:S(2)}, u32[]{:S(2)}) collective-permute-start(bf16[1536,1152]{1,0:T(8,128)(2,1)} %get-tuple-element.149.refs_5_), channel_id=1, source_target_pairs={{0,64},{1,65},{2,66},{3,67},{4,68},{5,69},{6,70},{7,71},{8,72},{9,... | collective-permute-start | bytes 10616840 | tf_op jit(solution)/shard_map/ppermute | solution.py:883
  237.4 4.8 all-to-all-start.5
  242.4 8.1 %collective-permute-done.24.refs_4_ = bf16[128,1664]{1,0:T(8,128)(2,1)S(1)} collective-permute-done((bf16[128,1664]{1,0:T(8,128)(2,1)S(1)}, bf16[128,1664]{1,0:T(8,128)(2,1)S(1)}, u32[]{:S(2)}, u32[]{:S(2)}) %collective-permute-start.24) | collective-permute-done | bytes 426016 | tf_op jit(solution)/shard_map/ppermute | solution.py:18
  252.9 8.7 %attend_backward.2 = (bf16[128,1024]{1,0:T(8,128)(2,1)S(1)}, bf16[128,1536]{1,0:T(8,128)(2,1)}, f32[128,1536]{1,0:T(8,128)}, bf16[32,128]{1,0:T(8,128)(2,1)S(1)}, bf16[16,1536]{1,0:T(8,128)(2,1)S(1)}) custom-call(s32[1]{0:T(128)} %bitcast.own_ref, f32[128,1536]{1,0:T(8,128)} %copy-done.10, f32[128,1536]{1,0:T(8,128)} %get-tuple-element.128.refs_1_.h_ref, ...), custom_call_target="tpu_custom_call" | custom-call | flops 1024 | bytes 1024 | tf_op jit(solution)/shard_map/attend_backward/pallas_call | solution.py:69
  261.8 6.8 %attend_grads.2 = (bf16[768,1920]{1,0:T(8,128)(2,1)}, bf16[768,1920]{1,0:T(8,128)(2,1)}) custom-call(s32[1]{0:T(128)} %bitcast.own_ref, bf16[128,1536]{1,0:T(8,128)(2,1)S(1)} %copy-done.15, f32[128,1536]{1,0:T(8,128)S(1)} %copy-done.11, f32[128,1536]{1,0:T(8,128)} %get-tuple-element.147.gh_ref.g_ref, bf16[128,768]{1,0:T(8,128)(2,1)S(1)} %copy-done.46, ...), custom_call_target="tpu_custom_call" | custom-call | flops 1024 | bytes 1024 | tf_op jit(solution)/shard_map/attend_grads/pallas_call | solution.py:69
  274.6 9.5 %all-to-all-start.6 = ((bf16[32,16,1536]{2,1,0:T(8,128)(2,1)}), bf16[32,16,1536]{2,1,0:T(8,128)(2,1)}, u32[]{:S(2)}, u32[]{:S(2)}) async-start(bf16[32,16,1536]{2,1,0:T(8,128)(2,1)} %bitcast.119), calls=%async_computation.6 | async-start | bytes 3145728 | tf_op jit(solution)/shard_map/all_to_all | solution.py:26
  284.2 4.6 slice_add_fusion.3
  298.5 6.2 %collective-permute-done.31.refs_7_ = f32[32,128]{1,0:T(8,128)S(1)} collective-permute-done((f32[32,128]{1,0:T(8,128)S(1)}, f32[32,128]{1,0:T(8,128)S(1)}, u32[]{:S(2)}, u32[]{:S(2)}) %collective-permute-start.31) | collective-permute-done | bytes 16416 | tf_op jit(solution)/shard_map/ppermute | solution.py:18
  305.5 4.2 all-to-all-done.6
  310.4 13.8 %experts_backward.3 = (bf16[512,1536]{1,0:T(8,128)(2,1)}, bf16[512,768]{1,0:T(8,128)(2,1)S(1)}, bf16[512,1536]{1,0:T(8,128)(2,1)}) custom-call(s32[1]{0:T(128)} %bitcast.8.own_ref, bf16[512,1536]{1,0:T(8,128)(2,1)} %bitcast.17.x_ref, bf16[512,1536]{1,0:T(8,128)(2,1)} %bitcast.33.g_ref, bf16[1536,384]{1,0:T(8,128)(2,1)S(1)} %bitcast.86, ...), custom_call_target="tpu_custom_call" | custom-call | flops 1024 | bytes 1024 | tf_op jit(solution)/shard_map/experts_backward/pallas_call | solution.py:69
  326.2 5.5 all-to-all-start.7
  333.6 10.3 %experts_grads.3 = (bf16[1536,1152]{1,0:T(8,128)(2,1)}, bf16[1536,1152]{1,0:T(8,128)(2,1)}) custom-call(s32[1]{0:T(128)} %bitcast.8.own_ref, bf16[512,1536]{1,0:T(8,128)(2,1)} %bitcast.17.x_ref, bf16[512,1536]{1,0:T(8,128)(2,1)} %bitcast.33.g_ref, bf16[512,768]{1,0:T(8,128)(2,1)S(1)} %copy-done.32, bf16[512,1536]{1,0:T(8,128)(2,1)} %get-tuple-element.171.dgu_ref, ...), custom_call_target="tpu_custom_call" | custom-call | flops 1024 | bytes 1024 | tf_op jit(solution)/shard_map/experts_grads/pallas_call | solution.py:69
  343.9 5.9 %all-to-all-done.7 = bf16[32,16,1536]{2,1,0:T(8,128)(2,1)} async-done(((bf16[32,16,1536]{2,1,0:T(8,128)(2,1)}), bf16[32,16,1536]{2,1,0:T(8,128)(2,1)}, u32[]{:S(2)}, u32[]{:S(2)}) %all-to-all-start.7) | async-done | bytes 1572896 | tf_op jit(solution)/shard_map/all_to_all | solution.py:26
  351.7 4.7 all-to-all-start.8
  357.8 7.8 %collective-permute-done.35.refs_4_ = bf16[128,1536]{1,0:T(8,128)(2,1)S(1)} collective-permute-done((bf16[128,1536]{1,0:T(8,128)(2,1)S(1)}, bf16[128,1536]{1,0:T(8,128)(2,1)S(1)}, u32[]{:S(2)}, u32[]{:S(2)}) %collective-permute-start.35) | collective-permute-done | bytes 393248 | tf_op jit(solution)/shard_map/ppermute | solution.py:18
  366.4 7.7 %attend_backward.3 = (bf16[128,1024]{1,0:T(8,128)(2,1)S(1)}, bf16[128,1536]{1,0:T(8,128)(2,1)S(1)}, f32[128,1536]{1,0:T(8,128)}, bf16[32,128]{1,0:T(8,128)(2,1)S(1)}, bf16[16,1536]{1,0:T(8,128)(2,1)S(1)}) custom-call(s32[1]{0:T(128)} %bitcast.8.own_ref, bf16[128,1536]{1,0:T(8,128)(2,1)S(1)} %copy-done.38, ...), custom_call_target="tpu_custom_call" | custom-call | flops 1024 | bytes 1024 | tf_op jit(solution)/shard_map/attend_backward/pallas_call | solution.py:69
  380.9 6.8 %attend_grads.3 = (bf16[768,1920]{1,0:T(8,128)(2,1)}, bf16[768,1920]{1,0:T(8,128)(2,1)}) custom-call(s32[1]{0:T(128)} %bitcast.8.own_ref, bf16[128,1536]{1,0:T(8,128)(2,1)S(1)} %copy-done.7, f32[128,1536]{1,0:T(8,128)S(1)} %copy-done.9, f32[128,1536]{1,0:T(8,128)} %get-tuple-element.178.gh_ref, bf16[128,768]{1,0:T(8,128)(2,1)S(1)} %copy-done.42, ...), custom_call_target="tpu_custom_call" | custom-call | flops 1024 | bytes 1024 | tf_op jit(solution)/shard_map/attend_grads/pallas_call | solution.py:69
  387.7 10.3 %collective-permute-start.40 = (bf16[768,1920]{1,0:T(8,128)(2,1)}, bf16[768,1920]{1,0:T(8,128)(2,1)S(1)}, u32[]{:S(2)}, u32[]{:S(2)}) collective-permute-start(bf16[768,1920]{1,0:T(8,128)(2,1)} %get-tuple-element.193), channel_id=1, source_target_pairs={{0,64},{64,0},{1,65},{65,1},{2,66},{66,2},{3,67},{67,3},{4,68},{68... | collective-permute-start | bytes 8847368 | tf_op jit(solution)/shard_map/ppermute | solution.py:18
  399.2 5.1 slice_add_fusion
  406.7 4.6 all-to-all-start.9
  415.3 17.1 %all-to-all-done.9 = bf16[4,192,1920]{2,1,0:T(8,128)(2,1)} async-done(((bf16[4,192,1920]{2,1,0:T(8,128)(2,1)}), bf16[4,192,1920]{2,1,0:T(8,128)(2,1)}, u32[]{:S(2)}, u32[]{:S(2)}) %all-to-all-start.9) | async-done | bytes 2949152 | tf_op jit(solution)/shard_map/all_to_all | solution.py:807
  438.0 4.3 all-to-all-start.10
  445.3 10.3 %all-to-all-done.10 = bf16[4,48,3840]{2,1,0:T(8,128)(2,1)} async-done(((bf16[4,48,3840]{2,1,0:T(8,128)(2,1)}), bf16[4,48,3840]{2,1,0:T(8,128)(2,1)}, u32[]{:S(2)}, u32[]{:S(2)}) %all-to-all-start.10) | async-done | bytes 1474592 | tf_op jit(solution)/shard_map/all_to_all | solution.py:807
  457.2 5.2 collective-permute-start.42
  462.4 8.1 %collective-permute-done.42 = bf16[48,3840]{1,0:T(8,128)(2,1)S(1)} collective-permute-done((bf16[48,3840]{1,0:T(8,128)(2,1)S(1)}, bf16[48,3840]{1,0:T(8,128)(2,1)S(1)}, u32[]{:S(2)}, u32[]{:S(2)}) %collective-permute-start.42) | collective-permute-done | bytes 368672 | tf_op jit(solution)/shard_map/ppermute | solution.py:836
  480.5 8.1 %all-to-all-done.11 = bf16[4,48,3840]{2,1,0:T(8,128)(2,1)S(1)} async-done(((bf16[4,48,3840]{2,1,0:T(8,128)(2,1)}), bf16[4,48,3840]{2,1,0:T(8,128)(2,1)S(1)}, u32[]{:S(2)}, u32[]{:S(2)}) %all-to-all-start.11) | async-done | bytes 1474592 | tf_op jit(solution)/shard_map/all_to_all | solution.py:807
  501.0 12.4 %collective-permute-done.43.refs_3_ = bf16[512,1152]{1,0:T(8,128)(2,1)S(1)} collective-permute-done((bf16[512,1152]{1,0:T(8,128)(2,1)}, bf16[512,1152]{1,0:T(8,128)(2,1)S(1)}, u32[]{:S(2)}, u32[]{:S(2)}) %collective-permute-start.43) | collective-permute-done | bytes 1179680 | tf_op jit(solution)/shard_map/ppermute | solution.py:887
  513.4 12.6 %collective-permute-done.44.refs_4_ = bf16[512,1152]{1,0:T(8,128)(2,1)S(1)} collective-permute-done((bf16[512,1152]{1,0:T(8,128)(2,1)}, bf16[512,1152]{1,0:T(8,128)(2,1)S(1)}, u32[]{:S(2)}, u32[]{:S(2)}) %collective-permute-start.44) | collective-permute-done | bytes 1179680 | tf_op jit(solution)/shard_map/ppermute | solution.py:887
  527.1 7.5 %ff_total.1 = (f32[1536,384]{1,0:T(8,128)}, f32[1536,384]{1,0:T(8,128)}, f32[384,1536]{1,0:T(8,128)}) custom-call(s32[1]{0:T(128)} %bitcast.43.core_ref, bf16[1536,1152]{1,0:T(8,128)(2,1)} %get-tuple-element.180.refs_0_, bf16[1536,1152]{1,0:T(8,128)(2,1)} %collective-permute-done.36.refs_1_, bf16[512,1152]{1,0:T(8,128)(2,1)} %collective-permute-done.41.refs_2_, ...), custom_call_target="tpu_custom_call" | custom-call | flops 1024 | bytes 1024 | tf_op jit(solution)/shard_map/ff_total/pallas_call | solution.py:69
  535.9 4.8 collective-permute-start.46
  549.7 7.0 %attn_total.1 = (f32[1536,768]{1,0:T(8,128)}, f32[1536,128]{1,0:T(8,128)}, f32[1536,128]{1,0:T(8,128)}, f32[768,1536]{1,0:T(8,128)}, f32[1536,128]{1,0:T(8,128)S(1)}) custom-call(s32[1]{0:T(128)} %bitcast.43.core_ref, bf16[768,1920]{1,0:T(8,128)(2,1)} %bitcast.104, bf16[768,1920]{1,0:T(8,128)(2,1)} %collective-permute-done.45.refs_1_, ...), custom_call_target="tpu_custom_call" | custom-call | flops 1024 | bytes 1024 | tf_op jit(solution)/shard_map/attn_total/pallas_call | solution.py:69
  (328 shorter events, 161.1 us)
Async XLA Ops:
  7.2 13.1 %collective-permute-start.2 = (bf16[1536,768]{1,0:T(8,128)(2,1)}, bf16[1536,768]{1,0:T(8,128)(2,1)}, u32[]{:S(2)}, u32[]{:S(2)}) collective-permute-start(bf16[1536,768]{1,0:T(8,128)(2,1)} %bitcast.92), channel_id=1, source_target_pairs={{0,64},{64,0},{1,65},{65,1},{2,66},{66,2},{3,67},{67,3},{4,68},{68... | collective-permute-start | bytes 7077896 | tf_op jit(solution)/shard_map/ppermute | solution.py:18
  7.3 13.0 %collective-permute-start.5 = (bf16[768,1536]{1,0:T(8,128)(2,1)}, bf16[768,1536]{1,0:T(8,128)(2,1)}, u32[]{:S(2)}, u32[]{:S(2)}) collective-permute-start(bf16[768,1536]{1,0:T(8,128)(2,1)} %bitcast.97), channel_id=1, source_target_pairs={{0,64},{64,0},{1,65},{65,1},{2,66},{66,2},{3,67},{67,3},{4,68},{68... | collective-permute-start | bytes 7077896 | tf_op jit(solution)/shard_map/ppermute | solution.py:18
  10.6 18.4 %collective-permute-start.6 = (bf16[1536,384]{1,0:T(8,128)(2,1)}, bf16[1536,384]{1,0:T(8,128)(2,1)}, u32[]{:S(2)}, u32[]{:S(2)}) collective-permute-start(bf16[1536,384]{1,0:T(8,128)(2,1)} %bitcast.81), channel_id=1, source_target_pairs={{0,1},{1,0},{2,3},{3,2},{4,5},{5,4},{6,7},{7,6},{8,9},{9,8},{10,11... | collective-permute-start | bytes 3538952 | tf_op jit(solution)/shard_map/ppermute | solution.py:887
  31.4 26.4 %collective-permute-start.11 = (bf16[1536,384]{1,0:T(8,128)(2,1)}, bf16[1536,384]{1,0:T(8,128)(2,1)}, u32[]{:S(2)}, u32[]{:S(2)}) collective-permute-start(bf16[1536,384]{1,0:T(8,128)(2,1)} %collective-permute-done.6.refs_6_), channel_id=1, source_target_pairs={{0,64},{1,65},{2,66},{3,67},{4,68},{5,69},{6,70},{7,71},{8,72},{9,... | collective-permute-start | bytes 3538952 | tf_op jit(solution)/shard_map/ppermute | solution.py:883
  38.6 19.3 %collective-permute-start.12 = (bf16[1536,384]{1,0:T(8,128)(2,1)}, bf16[1536,384]{1,0:T(8,128)(2,1)}, u32[]{:S(2)}, u32[]{:S(2)}) collective-permute-start(bf16[1536,384]{1,0:T(8,128)(2,1)} %bitcast.18.refs_1_), channel_id=1, source_target_pairs={{0,1},{1,0},{2,3},{3,2},{4,5},{5,4},{6,7},{7,6},{8,9},{9,8},{10,11... | collective-permute-start | bytes 3538952 | tf_op jit(solution)/shard_map/ppermute | solution.py:887
  41.3 28.4 %collective-permute-start.14 = (bf16[384,1536]{1,0:T(8,128)(2,1)S(1)}, bf16[384,1536]{1,0:T(8,128)(2,1)}, u32[]{:S(2)}, u32[]{:S(2)}) collective-permute-start(bf16[384,1536]{1,0:T(8,128)(2,1)S(1)} %bitcast.76), channel_id=1, source_target_pairs={{0,1},{1,0},{2,3},{3,2},{4,5},{5,4},{6,7},{7,6},{8,9},{9,8},{10,11... | collective-permute-start | bytes 3538952 | tf_op jit(solution)/shard_map/ppermute | solution.py:887
  47.3 28.4 %all-to-all-start = ((bf16[32,16,1536]{2,1,0:T(8,128)(2,1)}), bf16[32,16,1536]{2,1,0:T(8,128)(2,1)}, u32[]{:S(2)}, u32[]{:S(2)}) async-start(bf16[32,16,1536]{2,1,0:T(8,128)(2,1)} %bitcast.120), calls=%async_computation | async-start | bytes 3145728 | tf_op jit(solution)/shard_map/all_to_all | solution.py:26
  57.2 15.8 %collective-permute-start.9 = (bf16[1536,384]{1,0:T(8,128)(2,1)}, bf16[1536,384]{1,0:T(8,128)(2,1)}, u32[]{:S(2)}, u32[]{:S(2)}) collective-permute-start(bf16[1536,384]{1,0:T(8,128)(2,1)} %bitcast.18.refs_1_), channel_id=1, source_target_pairs={{0,64},{64,0},{1,65},{65,1},{2,66},{66,2},{3,67},{67,3},{4,68},{68... | collective-permute-start | bytes 3538952 | tf_op jit(solution)/shard_map/ppermute | solution.py:18
  57.3 14.7 %collective-permute-start.8 = (bf16[1536,384]{1,0:T(8,128)(2,1)S(1)}, bf16[1536,384]{1,0:T(8,128)(2,1)S(1)}, u32[]{:S(2)}, u32[]{:S(2)}) collective-permute-start(bf16[1536,384]{1,0:T(8,128)(2,1)S(1)} %bitcast.82), channel_id=1, source_target_pairs={{0,64},{64,0},{1,65},{65,1},{2,66},{66,2},{3,67},{67,3},{4,68},{68... | collective-permute-start | bytes 3538952 | tf_op jit(solution)/shard_map/ppermute | solution.py:18
  57.8 15.2 %collective-permute-start.10 = (bf16[384,1536]{1,0:T(8,128)(2,1)S(1)}, bf16[384,1536]{1,0:T(8,128)(2,1)}, u32[]{:S(2)}, u32[]{:S(2)}) collective-permute-start(bf16[384,1536]{1,0:T(8,128)(2,1)S(1)} %bitcast.77), channel_id=1, source_target_pairs={{0,64},{64,0},{1,65},{65,1},{2,66},{66,2},{3,67},{67,3},{4,68},{68... | collective-permute-start | bytes 3538952 | tf_op jit(solution)/shard_map/ppermute | solution.py:18
  57.9 17.8 %collective-permute-start.13 = (bf16[1536,384]{1,0:T(8,128)(2,1)}, bf16[1536,384]{1,0:T(8,128)(2,1)}, u32[]{:S(2)}, u32[]{:S(2)}) collective-permute-start(bf16[1536,384]{1,0:T(8,128)(2,1)} %collective-permute-done.12.refs_7_), channel_id=1, source_target_pairs={{0,64},{1,65},{2,66},{3,67},{4,68},{5,69},{6,70},{7,71},{8,72},{9,... | collective-permute-start | bytes 3538952 | tf_op jit(solution)/shard_map/ppermute | solution.py:883
  85.7 33.3 %all-to-all-start.1 = ((bf16[32,16,1536]{2,1,0:T(8,128)(2,1)}), bf16[32,16,1536]{2,1,0:T(8,128)(2,1)}, u32[]{:S(2)}, u32[]{:S(2)}) async-start(bf16[32,16,1536]{2,1,0:T(8,128)(2,1)} %bitcast.112), calls=%async_computation.1 | async-start | bytes 3145728 | tf_op jit(solution)/shard_map/all_to_all | solution.py:26
  93.5 27.3 %collective-permute-start.16 = (bf16[1536,384]{1,0:T(8,128)(2,1)S(1)}, bf16[1536,384]{1,0:T(8,128)(2,1)S(1)}, u32[]{:S(2)}, u32[]{:S(2)}) collective-permute-start(bf16[1536,384]{1,0:T(8,128)(2,1)S(1)} %bitcast.84), channel_id=1, source_target_pairs={{64,65},{65,64},{66,67},{67,66},{68,69},{69,68},{70,71},{71,70},{7... | collective-permute-start | bytes 3538952 | tf_op jit(solution)/shard_map/ppermute | solution.py:887
  94.2 26.6 %collective-permute-start.17 = (bf16[1536,384]{1,0:T(8,128)(2,1)}, bf16[1536,384]{1,0:T(8,128)(2,1)}, u32[]{:S(2)}, u32[]{:S(2)}) collective-permute-start(bf16[1536,384]{1,0:T(8,128)(2,1)} %bitcast.18.refs_1_), channel_id=1, source_target_pairs={{64,65},{65,64},{66,67},{67,66},{68,69},{69,68},{70,71},{71,70},{7... | collective-permute-start | bytes 3538952 | tf_op jit(solution)/shard_map/ppermute | solution.py:887
  121.8 32.1 %all-to-all-start.2 = ((bf16[32,16,1536]{2,1,0:T(8,128)(2,1)}), bf16[32,16,1536]{2,1,0:T(8,128)(2,1)}, u32[]{:S(2)}, u32[]{:S(2)}) async-start(bf16[32,16,1536]{2,1,0:T(8,128)(2,1)} %bitcast.117), calls=%async_computation.2 | async-start | bytes 3145728 | tf_op jit(solution)/shard_map/all_to_all | solution.py:26
  147.1 15.2 %collective-permute-start.20 = (bf16[384,1536]{1,0:T(8,128)(2,1)S(1)}, bf16[384,1536]{1,0:T(8,128)(2,1)}, u32[]{:S(2)}, u32[]{:S(2)}) collective-permute-start(bf16[384,1536]{1,0:T(8,128)(2,1)S(1)} %bitcast.78), channel_id=1, source_target_pairs={{64,65},{65,64},{66,67},{67,66},{68,69},{69,68},{70,71},{71,70},{7... | collective-permute-start | bytes 3538952 | tf_op jit(solution)/shard_map/ppermute | solution.py:887
  153.9 26.0 %all-to-all-start.3 = ((bf16[32,16,1664]{2,1,0:T(8,128)(2,1)}), bf16[32,16,1664]{2,1,0:T(8,128)(2,1)}, u32[]{:S(2)}, u32[]{:S(2)}) async-start(bf16[32,16,1664]{2,1,0:T(8,128)(2,1)} %bitcast.115), calls=%async_computation.3 | async-start | bytes 3407872 | tf_op jit(solution)/shard_map/all_to_all | solution.py:26
  159.8 12.8 %collective-permute-start.21 = (bf16[1536,384]{1,0:T(8,128)(2,1)}, bf16[1536,384]{1,0:T(8,128)(2,1)S(1)}, u32[]{:S(2)}, u32[]{:S(2)}) collective-permute-start(bf16[1536,384]{1,0:T(8,128)(2,1)} %copy-done.78), channel_id=1, source_target_pairs={{64,0},{65,1},{66,2},{67,3},{68,4},{69,5},{70,6},{71,7},{72,8},{73... | collective-permute-start | bytes 3538952 | tf_op jit(solution)/shard_map/ppermute | solution.py:883
  161.1 13.2 %collective-permute-start.22 = (bf16[1536,384]{1,0:T(8,128)(2,1)}, bf16[1536,384]{1,0:T(8,128)(2,1)S(1)}, u32[]{:S(2)}, u32[]{:S(2)}) collective-permute-start(bf16[1536,384]{1,0:T(8,128)(2,1)} %collective-permute-done.17.refs_7_), channel_id=1, source_target_pairs={{64,0},{65,1},{66,2},{67,3},{68,4},{69,5},{70,6},{71,7},{72,8},{73... | collective-permute-start | bytes 3538952 | tf_op jit(solution)/shard_map/ppermute | solution.py:883
  162.4 13.6 %collective-permute-start.23 = (bf16[384,1536]{1,0:T(8,128)(2,1)}, bf16[384,1536]{1,0:T(8,128)(2,1)S(1)}, u32[]{:S(2)}, u32[]{:S(2)}) collective-permute-start(bf16[384,1536]{1,0:T(8,128)(2,1)} %collective-permute-done.20.refs_8_.refs_2_), channel_id=1, source_target_pairs={{64,0},{65,1},{66,2},{67,3},{68,4},{69,5},{70,6},{71,7},{72,8},{73... | collective-permute-start | bytes 3538952 | tf_op jit(solution)/shard_map/ppermute | solution.py:883
  194.4 29.9 %all-to-all-start.4 = ((bf16[32,16,1664]{2,1,0:T(8,128)(2,1)}), bf16[32,16,1664]{2,1,0:T(8,128)(2,1)}, u32[]{:S(2)}, u32[]{:S(2)}) async-start(bf16[32,16,1664]{2,1,0:T(8,128)(2,1)} %bitcast.116), calls=%async_computation.4 | async-start | bytes 3407872 | tf_op jit(solution)/shard_map/all_to_all | solution.py:26
  226.1 35.5 %collective-permute-start.25 = (bf16[1536,1152]{1,0:T(8,128)(2,1)}, bf16[1536,1152]{1,0:T(8,128)(2,1)}, u32[]{:S(2)}, u32[]{:S(2)}) collective-permute-start(bf16[1536,1152]{1,0:T(8,128)(2,1)} %get-tuple-element.149.refs_5_), channel_id=1, source_target_pairs={{0,64},{1,65},{2,66},{3,67},{4,68},{5,69},{6,70},{7,71},{8,72},{9,... | collective-permute-start | bytes 10616840 | tf_op jit(solution)/shard_map/ppermute | solution.py:883
  234.3 27.4 %collective-permute-start.26 = (bf16[1536,1152]{1,0:T(8,128)(2,1)}, bf16[1536,1152]{1,0:T(8,128)(2,1)}, u32[]{:S(2)}, u32[]{:S(2)}) collective-permute-start(bf16[1536,1152]{1,0:T(8,128)(2,1)} %get-tuple-element.151), channel_id=1, source_target_pairs={{0,64},{1,65},{2,66},{3,67},{4,68},{5,69},{6,70},{7,71},{8,72},{9,... | collective-permute-start | bytes 10616840 | tf_op jit(solution)/shard_map/ppermute | solution.py:883
  237.4 31.2 %all-to-all-start.5 = ((bf16[32,16,1536]{2,1,0:T(8,128)(2,1)}), bf16[32,16,1536]{2,1,0:T(8,128)(2,1)}, u32[]{:S(2)}, u32[]{:S(2)}) async-start(bf16[32,16,1536]{2,1,0:T(8,128)(2,1)} %bitcast.118), calls=%async_computation.5 | async-start | bytes 3145728 | tf_op jit(solution)/shard_map/all_to_all | solution.py:26
  274.6 19.8 %collective-permute-start.30 = (bf16[768,1920]{1,0:T(8,128)(2,1)}, bf16[768,1920]{1,0:T(8,128)(2,1)}, u32[]{:S(2)}, u32[]{:S(2)}) collective-permute-start(bf16[768,1920]{1,0:T(8,128)(2,1)} %get-tuple-element.163), channel_id=1, source_target_pairs={{0,64},{64,0},{1,65},{65,1},{2,66},{66,2},{3,67},{67,3},{4,68},{68... | collective-permute-start | bytes 8847368 | tf_op jit(solution)/shard_map/ppermute | solution.py:18
  274.6 35.1 %all-to-all-start.6 = ((bf16[32,16,1536]{2,1,0:T(8,128)(2,1)}), bf16[32,16,1536]{2,1,0:T(8,128)(2,1)}, u32[]{:S(2)}, u32[]{:S(2)}) async-start(bf16[32,16,1536]{2,1,0:T(8,128)(2,1)} %bitcast.119), calls=%async_computation.6 | async-start | bytes 3145728 | tf_op jit(solution)/shard_map/all_to_all | solution.py:26
  288.7 16.7 %collective-permute-start.32 = (bf16[512,1152]{1,0:T(8,128)(2,1)S(1)}, bf16[512,1152]{1,0:T(8,128)(2,1)}, u32[]{:S(2)}, u32[]{:S(2)}) collective-permute-start(bf16[512,1152]{1,0:T(8,128)(2,1)S(1)} %get-tuple-element.165), channel_id=1, source_target_pairs={{64,65},{65,64},{66,67},{67,66},{68,69},{69,68},{70,71},{71,70},{7... | collective-permute-start | bytes 3538952 | tf_op jit(solution)/shard_map/ppermute | solution.py:887
  292.2 12.5 %collective-permute-start.28 = (bf16[128,1536]{1,0:T(8,128)(2,1)S(1)}, bf16[128,1536]{1,0:T(8,128)(2,1)S(1)}, u32[]{:S(2)}, u32[]{:S(2)}) collective-permute-start(bf16[128,1536]{1,0:T(8,128)(2,1)S(1)} %convolution_convert_fusion.1), channel_id=1, source_target_pairs={{0,1},{1,0},{2,3},{3,2},{4,5},{5,4},{6,7},{7,6},{8,9},{9,8},{10,11... | collective-permute-start | bytes 1179656 | tf_op jit(solution)/shard_map/ppermute | solution.py:18
  309.7 15.5 %collective-permute-start.33 = (bf16[512,1152]{1,0:T(8,128)(2,1)S(1)}, bf16[512,1152]{1,0:T(8,128)(2,1)S(1)}, u32[]{:S(2)}, u32[]{:S(2)}) collective-permute-start(bf16[512,1152]{1,0:T(8,128)(2,1)S(1)} %get-tuple-element.168), channel_id=1, source_target_pairs={{64,65},{65,64},{66,67},{67,66},{68,69},{69,68},{70,71},{71,70},{7... | collective-permute-start | bytes 3538952 | tf_op jit(solution)/shard_map/ppermute | solution.py:887
  326.2 23.6 %all-to-all-start.7 = ((bf16[32,16,1536]{2,1,0:T(8,128)(2,1)}), bf16[32,16,1536]{2,1,0:T(8,128)(2,1)}, u32[]{:S(2)}, u32[]{:S(2)}) async-start(bf16[32,16,1536]{2,1,0:T(8,128)(2,1)} %bitcast.121), calls=%async_computation.7 | async-start | bytes 3145728 | tf_op jit(solution)/shard_map/all_to_all | solution.py:26
  331.6 12.2 %collective-permute-start.34 = (bf16[512,1152]{1,0:T(8,128)(2,1)}, bf16[512,1152]{1,0:T(8,128)(2,1)}, u32[]{:S(2)}, u32[]{:S(2)}) collective-permute-start(bf16[512,1152]{1,0:T(8,128)(2,1)} %get-tuple-element.173), channel_id=1, source_target_pairs={{64,65},{65,64},{66,67},{67,66},{68,69},{69,68},{70,71},{71,70},{7... | collective-permute-start | bytes 3538952 | tf_op jit(solution)/shard_map/ppermute | solution.py:887
  351.7 25.9 %all-to-all-start.8 = ((bf16[4,192,1920]{2,1,0:T(8,128)(2,1)}), bf16[4,192,1920]{2,1,0:T(8,128)(2,1)}, u32[]{:S(2)}, u32[]{:S(2)}) async-start(bf16[4,192,1920]{2,1,0:T(8,128)(2,1)} %bitcast.105), calls=%async_computation.8 | async-start | bytes 5898240 | tf_op jit(solution)/shard_map/all_to_all | solution.py:807
  356.4 42.8 %collective-permute-start.37 = (bf16[1536,1152]{1,0:T(8,128)(2,1)}, bf16[1536,1152]{1,0:T(8,128)(2,1)}, u32[]{:S(2)}, u32[]{:S(2)}) collective-permute-start(bf16[1536,1152]{1,0:T(8,128)(2,1)} %get-tuple-element.182), channel_id=1, source_target_pairs={{64,0},{65,1},{66,2},{67,3},{68,4},{69,5},{70,6},{71,7},{72,8},{73... | collective-permute-start | bytes 10616840 | tf_op jit(solution)/shard_map/ppermute | solution.py:883
  387.7 16.7 %collective-permute-start.40 = (bf16[768,1920]{1,0:T(8,128)(2,1)}, bf16[768,1920]{1,0:T(8,128)(2,1)S(1)}, u32[]{:S(2)}, u32[]{:S(2)}) collective-permute-start(bf16[768,1920]{1,0:T(8,128)(2,1)} %get-tuple-element.193), channel_id=1, source_target_pairs={{0,64},{64,0},{1,65},{65,1},{2,66},{66,2},{3,67},{67,3},{4,68},{68... | collective-permute-start | bytes 8847368 | tf_op jit(solution)/shard_map/ppermute | solution.py:18
  397.9 17.1 %collective-permute-start.36 = (bf16[1536,1152]{1,0:T(8,128)(2,1)}, bf16[1536,1152]{1,0:T(8,128)(2,1)}, u32[]{:S(2)}, u32[]{:S(2)}) collective-permute-start(bf16[1536,1152]{1,0:T(8,128)(2,1)} %get-tuple-element.180.refs_0_), channel_id=1, source_target_pairs={{64,0},{65,1},{66,2},{67,3},{68,4},{69,5},{70,6},{71,7},{72,8},{73... | collective-permute-start | bytes 10616840 | tf_op jit(solution)/shard_map/ppermute | solution.py:883
  406.7 25.7 %all-to-all-start.9 = ((bf16[4,192,1920]{2,1,0:T(8,128)(2,1)}), bf16[4,192,1920]{2,1,0:T(8,128)(2,1)}, u32[]{:S(2)}, u32[]{:S(2)}) async-start(bf16[4,192,1920]{2,1,0:T(8,128)(2,1)} %bitcast.106), calls=%async_computation.9 | async-start | bytes 5898240 | tf_op jit(solution)/shard_map/all_to_all | solution.py:807
  411.3 26.7 %collective-permute-start.41 = (bf16[512,1152]{1,0:T(8,128)(2,1)}, bf16[512,1152]{1,0:T(8,128)(2,1)}, u32[]{:S(2)}, u32[]{:S(2)}) collective-permute-start(bf16[512,1152]{1,0:T(8,128)(2,1)} %get-tuple-element.194), channel_id=1, source_target_pairs={{0,1},{1,0},{2,3},{3,2},{4,5},{5,4},{6,7},{7,6},{8,9},{9,8},{10,11... | collective-permute-start | bytes 3538952 | tf_op jit(solution)/shard_map/ppermute | solution.py:887
  415.0 23.0 %collective-permute-start.38 = (bf16[128,1536]{1,0:T(8,128)(2,1)S(1)}, bf16[128,1536]{1,0:T(8,128)(2,1)S(1)}, u32[]{:S(2)}, u32[]{:S(2)}) collective-permute-start(bf16[128,1536]{1,0:T(8,128)(2,1)S(1)} %get-tuple-element.183), channel_id=1, source_target_pairs={{0,1},{1,0},{2,3},{3,2},{4,5},{5,4},{6,7},{7,6},{8,9},{9,8},{10,11... | collective-permute-start | bytes 1179656 | tf_op jit(solution)/shard_map/ppermute | solution.py:18
  438.0 17.6 %all-to-all-start.10 = ((bf16[4,48,3840]{2,1,0:T(8,128)(2,1)}), bf16[4,48,3840]{2,1,0:T(8,128)(2,1)}, u32[]{:S(2)}, u32[]{:S(2)}) async-start(bf16[4,48,3840]{2,1,0:T(8,128)(2,1)} %bitcast.114), calls=%async_computation.10 | async-start | bytes 2949120 | tf_op jit(solution)/shard_map/all_to_all | solution.py:807
  444.5 33.6 %collective-permute-start.29 = (f32[128,1536]{1,0:T(8,128)}, f32[128,1536]{1,0:T(8,128)}, u32[]{:S(2)}, u32[]{:S(2)}) collective-permute-start(f32[128,1536]{1,0:T(8,128)} %get-tuple-element.255), channel_id=1, source_target_pairs={{0,64},{64,0},{1,65},{65,1},{2,66},{66,2},{3,67},{67,3},{4,68},{68... | collective-permute-start | bytes 2359304 | tf_op jit(solution)/shard_map/ppermute | solution.py:18
  457.2 13.3 %collective-permute-start.42 = (bf16[48,3840]{1,0:T(8,128)(2,1)S(1)}, bf16[48,3840]{1,0:T(8,128)(2,1)S(1)}, u32[]{:S(2)}, u32[]{:S(2)}) collective-permute-start(bf16[48,3840]{1,0:T(8,128)(2,1)S(1)} %reduce_sum.58), channel_id=1, source_target_pairs={{0,2},{2,0},{4,6},{6,4},{8,10},{10,8},{12,14},{14,12},{16,18},{18,... | collective-permute-start | bytes 1105928 | tf_op jit(solution)/shard_map/ppermute | solution.py:836
  471.8 16.8 %all-to-all-start.11 = ((bf16[4,48,3840]{2,1,0:T(8,128)(2,1)}), bf16[4,48,3840]{2,1,0:T(8,128)(2,1)S(1)}, u32[]{:S(2)}, u32[]{:S(2)}) async-start(bf16[4,48,3840]{2,1,0:T(8,128)(2,1)} %broadcast_in_dim.22), calls=%async_computation.11 | async-start | bytes 2949120 | tf_op jit(solution)/shard_map/all_to_all | solution.py:807
  475.5 60.4 %all-gather.2.cloned.1.call-start = ((), (), s32[]{:S(2)}) async-start(), calls=%async_computation.13 | async-start | bytes 3686400 | tf_op jit(solution)/shard_map/all_gather | solution.py:830
  491.4 43.1 %all-to-all-start.12 = ((bf16[4,192,1920]{2,1,0:T(8,128)(2,1)}), bf16[4,192,1920]{2,1,0:T(8,128)(2,1)S(1)}, u32[]{:S(2)}, u32[]{:S(2)}) async-start(bf16[4,192,1920]{2,1,0:T(8,128)(2,1)} %broadcast_in_dim.46), calls=%async_computation.12 | async-start | bytes 5898240 | tf_op jit(solution)/shard_map/all_to_all | solution.py:807
  495.1 18.3 %collective-permute-start.43 = (bf16[512,1152]{1,0:T(8,128)(2,1)}, bf16[512,1152]{1,0:T(8,128)(2,1)S(1)}, u32[]{:S(2)}, u32[]{:S(2)}) collective-permute-start(bf16[512,1152]{1,0:T(8,128)(2,1)} %get-tuple-element.197), channel_id=1, source_target_pairs={{0,1},{1,0},{2,3},{3,2},{4,5},{5,4},{6,7},{7,6},{8,9},{9,8},{10,11... | collective-permute-start | bytes 3538952 | tf_op jit(solution)/shard_map/ppermute | solution.py:887
  497.9 28.2 %collective-permute-start.44 = (bf16[512,1152]{1,0:T(8,128)(2,1)}, bf16[512,1152]{1,0:T(8,128)(2,1)S(1)}, u32[]{:S(2)}, u32[]{:S(2)}) collective-permute-start(bf16[512,1152]{1,0:T(8,128)(2,1)} %get-tuple-element.198), channel_id=1, source_target_pairs={{0,1},{1,0},{2,3},{3,2},{4,5},{5,4},{6,7},{7,6},{8,9},{9,8},{10,11... | collective-permute-start | bytes 3538952 | tf_op jit(solution)/shard_map/ppermute | solution.py:887
  534.6 13.5 %collective-permute-start.45 = (bf16[768,1920]{1,0:T(8,128)(2,1)S(1)}, bf16[768,1920]{1,0:T(8,128)(2,1)}, u32[]{:S(2)}, u32[]{:S(2)}) collective-permute-start(bf16[768,1920]{1,0:T(8,128)(2,1)S(1)} %bitcast.102), channel_id=1, source_target_pairs={{64,0},{65,1},{66,2},{67,3},{68,4},{69,5},{70,6},{71,7},{72,8},{73... | collective-permute-start | bytes 8847368 | tf_op jit(solution)/shard_map/ppermute | solution.py:883
  535.9 12.2 %collective-permute-start.46 = (bf16[768,1920]{1,0:T(8,128)(2,1)}, bf16[768,1920]{1,0:T(8,128)(2,1)S(1)}, u32[]{:S(2)}, u32[]{:S(2)}) collective-permute-start(bf16[768,1920]{1,0:T(8,128)(2,1)} %all-gather.2.cloned.1.call-done.refs_2_), channel_id=1, source_target_pairs={{0,64},{1,65},{2,66},{3,67},{4,68},{5,69},{6,70},{7,71},{8,72},{9,... | collective-permute-start | bytes 8847368 | tf_op jit(solution)/shard_map/ppermute | solution.py:883
  (108 other events, 939.1 us)
Sparse Core Ops, SparseCore 0:
  489.7 35.7 all-gather.1

commit v3 on v2

--- a/solution.py
+++ b/solution.py
@@ -35,12 +35,18 @@
 
 def plane_groups(level):
     groups = []
-    for z in range(2):
+    if level < 2:
+        for z in range(2):
+            for i in range(4):
+                along_y = [(y * 4 + i) * 2 + z for y in range(4)]
+                along_x = [(i * 4 + x) * 2 + z for x in range(4)]
+                zero, one = (along_y, along_x) if level == 0 else (along_x, along_y)
+                groups += [zero, [32 + e for e in one]]
+    else:
         for i in range(4):
-            along_y = [(y * 4 + i) * 2 + z for y in range(4)]
-            along_x = [(i * 4 + x) * 2 + z for x in range(4)]
-            zero, one = (along_y, along_x) if level == 0 else (along_x, along_y)
-            groups += [zero, [32 + e for e in one]]
+            along_x = [(i * 4 + x) * 2 + z for x in range(4) for z in range(2)]
+            along_y = [(y * 4 + i) * 2 + z for y in range(4) for z in range(2)]
+            groups += [along_x, [32 + e for e in along_y]]
     return groups
 
 
@@ -379,17 +385,25 @@
     tile = 256
 
     def body(own_ref, x_ref, *refs):
-        sources, (y_o, wgu, wd, h_s, sems) = refs[:12], refs[12:]
+        sources, (y_o, x_s, wgu, wd, h_s, sems) = refs[:12], refs[12:]
         moves = expert_moves(sources, wgu, wd, half)
+        arrival = pltpu.make_async_copy(x_ref, x_s, sems.at[6])
+        arrival.start()
         for i in (0, 1, 3, 4, 2, 5):
             fetch(own_ref[0], moves[i][0], moves[i][1], moves[i][2], sems.at[i])
-        for i in (0, 1, 3, 4):
+        arrival.wait()
+        for i in (0, 1):
             arrive(moves[i][0], moves[i][2], sems.at[i])
 
         def step(c, carry):
+            @pl.when(c == 1)
+            def _():
+                for i in (3, 4):
+                    arrive(moves[i][0], moves[i][2], sems.at[i])
+
             at = pl.multiple_of(c * tile, tile)
-            gate = mul_nn(x_ref[...], wgu[:, pl.ds(at, tile)])
-            up = mul_nn(x_ref[...], wgu[:, pl.ds(at + hidden, tile)])
+            gate = mul_nn(x_s[...], wgu[:, pl.ds(at, tile)])
+            up = mul_nn(x_s[...], wgu[:, pl.ds(at + hidden, tile)])
             act = gate / (1.0 + jnp.exp(-gate))
             h_s[:, pl.ds(at, tile)] = (act * up).astype(BF16)
             return carry
@@ -408,12 +422,13 @@
     return call(
         body,
         [((slots, model), BF16)],
-        [SMEM, VMEM] + [ANY] * 12,
+        [SMEM] + [ANY] * 13,
         [
+            pltpu.VMEM((slots, model), BF16),
             pltpu.VMEM((model, 2 * hidden), BF16),
             pltpu.VMEM((hidden, model), BF16),
             pltpu.VMEM((slots, hidden), BF16),
-            pltpu.SemaphoreType.DMA((6,)),
+            pltpu.SemaphoreType.DMA((7,)),
         ],
         (own, rows, *weights),
         "experts_forward",
@@ -429,60 +444,88 @@
 
     def body(own_ref, x_ref, g_ref, *refs):
         sources, refs = refs[:12], refs[12:]
-        dx_o, h_o, dgu_o, wgu, wd, sems = refs[:6]
+        dx_o, h_o, dgu_o, x_s, g_s, h_s, dgu_s, wgu, wd, sems = refs[:10]
         moves = expert_moves(sources, wgu, wd, half)
-        for i in (0, 1, 3, 4, 2, 5):
+        arrivals = [
+            pltpu.make_async_copy(x_ref, x_s, sems.at[6]),
+            pltpu.make_async_copy(g_ref, g_s, sems.at[7]),
+        ]
+        leaving = [
+            pltpu.make_async_copy(h_s, h_o, sems.at[8]),
+            pltpu.make_async_copy(dgu_s, dgu_o, sems.at[9]),
+        ]
+        arrivals[0].start()
+        for i in (0, 1, 2, 3, 4, 5):
             fetch(own_ref[0], moves[i][0], moves[i][1], moves[i][2], sems.at[i])
+            if i == 1:
+                arrivals[1].start()
+        arrivals[0].wait()
         if gated:
-            scale = x_ref[:, model:].astype(F32)
+            scale = x_s[:, model:].astype(F32)
             scale = scale[:, 0:1] + scale[:, 1:2]
-            seen_s = refs[6]
+            seen_s = refs[10]
             seen_s[...] = jnp.zeros_like(seen_s)
-        for i in range(6):
+        for i in (0, 1):
             arrive(moves[i][0], moves[i][2], sems.at[i])
+        arrivals[1].wait()
+        arrive(moves[2][0], moves[2][2], sems.at[2])
 
         def step(c, carry):
+            @pl.when(c == 1)
+            def _():
+                for i in (3, 4, 5):
+                    arrive(moves[i][0], moves[i][2], sems.at[i])
+
             at = pl.multiple_of(c * tile, tile)
             spot, later = pl.ds(at, tile), pl.ds(at + hidden, tile)
-            gate = mul_nn(x_ref[:, :model], wgu[:, spot])
-            up = mul_nn(x_ref[:, :model], wgu[:, later])
+            gate = mul_nn(x_s[:, :model], wgu[:, spot])
+            up = mul_nn(x_s[:, :model], wgu[:, later])
             sig = 1.0 / (1.0 + jnp.exp(-gate))
             act = gate * sig
             made = act * up
-            h_o[:, spot] = made.astype(BF16)
-            grad_hidden = mul_nt(g_ref[...], wd[spot, :])
+            h_s[:, spot] = made.astype(BF16)
+            grad_hidden = mul_nt(g_s[...], wd[spot, :])
             if gated:
                 seen = made * grad_hidden
                 seen_s[...] += seen[:, :HEAD] + seen[:, HEAD:]
                 grad_hidden = grad_hidden * scale
-            dgu_o[:, spot] = (grad_hidden * up * sig * (1.0 + gate * (1.0 - sig))).astype(BF16)
-            dgu_o[:, later] = (grad_hidden * act).astype(BF16)
+            dgu_s[:, spot] = (grad_hidden * up * sig * (1.0 + gate * (1.0 - sig))).astype(BF16)
+            dgu_s[:, later] = (grad_hidden * act).astype(BF16)
             return carry
 
         lax.fori_loop(0, hidden // tile, step, 0)
+        for copy in leaving:
+            copy.start()
 
         def finish(c, carry):
             spot = pl.ds(pl.multiple_of(c * tile, tile), tile)
-            dx_o[:, spot] = mul_nt(dgu_o[...], wgu[spot, :]).astype(BF16)
+            dx_o[:, spot] = mul_nt(dgu_s[...], wgu[spot, :]).astype(BF16)
             return carry
 
         lax.fori_loop(0, model // tile, finish, 0)
         if gated:
             total = jnp.sum(seen_s[...], axis=1, keepdims=True)
             dx_o[:, model:] = pair_columns(total, slots)
+        for copy in leaving:
+            copy.wait()
 
     return call(
         body,
         [((slots, wide), BF16), ((slots, hidden), BF16), ((slots, 2 * hidden), BF16)],
-        [SMEM, VMEM, VMEM] + [ANY] * 12,
+        [SMEM] + [ANY] * 14,
         [
+            pltpu.VMEM((slots, wide), BF16),
+            pltpu.VMEM((slots, model), BF16),
+            pltpu.VMEM((slots, hidden), BF16),
+            pltpu.VMEM((slots, 2 * hidden), BF16),
             pltpu.VMEM((model, 2 * hidden), BF16),
             pltpu.VMEM((hidden, model), BF16),
-            pltpu.SemaphoreType.DMA((6,)),
+            pltpu.SemaphoreType.DMA((10,)),
         ]
         + ([pltpu.VMEM((slots, HEAD), F32)] if gated else []),
         (own, rows, grads, *weights),
         "experts_backward",
+        [VMEM, ANY, ANY],
     )
 
 
@@ -496,7 +539,7 @@
 
     def body(own_ref, x_ref, g_ref, h_ref, dgu_ref, *refs):
         sources, refs = refs[:4], refs[4:]
-        near_o, far_o, refs = refs[0], refs[1], refs[2:]
+        both_o, refs = refs[0], refs[1:]
         if gated:
             y_o, xt_s, dy_s, wd, sems = refs
             moves = [
@@ -519,10 +562,10 @@
         def step(c, carry):
             spot = pl.ds(pl.multiple_of(c * tile, tile), tile)
             made = mul_nn(xt_s[spot, :], dgu_ref[...]).astype(BF16)
-            near_o[spot, :half] = made[:, :half]
-            far_o[spot, :half] = made[:, half:hidden]
-            near_o[spot, half:hidden] = made[:, hidden : hidden + half]
-            far_o[spot, half:hidden] = made[:, hidden + half :]
+            both_o[0, spot, :half] = made[:, :half]
+            both_o[1, spot, :half] = made[:, half:hidden]
+            both_o[0, spot, half:hidden] = made[:, hidden : hidden + half]
+            both_o[1, spot, half:hidden] = made[:, hidden + half :]
             if gated:
                 y_o[:, spot] = mul_nn(h_ref[...], wd[:, spot]).astype(BF16)
             return carry
@@ -532,12 +575,12 @@
         for i in range(hidden // down):
             made = mul_tn(h_ref[:, i * down : (i + 1) * down], dy_s[...]).astype(BF16)
             low = i * down
-            out, low = (near_o, low) if low < half else (far_o, low - half)
+            side, low = (0, low) if low < half else (1, low - half)
             for j in range(blocks):
                 at = j * half + low
-                out[at : at + down, hidden:] = made[:, j * half : (j + 1) * half]
-
-    outs = [((model, 3 * half), BF16)] * 2
+                both_o[side, at : at + down, hidden:] = made[:, j * half : (j + 1) * half]
+
+    outs = [((2, model, 3 * half), BF16)]
     scratch = [pltpu.VMEM((model, slots), BF16)]
     if gated:
         outs = outs + [((slots, model), BF16)]
@@ -655,7 +698,7 @@
     )
 
 
-def attend_grads(own, x, h, grad_h, o, dqkv, dlogits, gains, attn_gain, moe_gain):
+def attend_grads(own, x, h, grad_h, o, dqkv, dlogits, gains, gains_r, attn_gain, moe_gain):
     count, model = h.shape
     width, out_at = o.shape[1], dqkv.shape[1]
     experts = dlogits.shape[0]
@@ -663,7 +706,8 @@
     tile = 256
     parts = model // tile // 2
 
-    def body(own_ref, x_ref, h_ref, gh_ref, o_ref, dqkv_ref, dl_ref, gains_ref, again, mgain, *rest):
+    def body(own_ref, x_ref, h_ref, gh_ref, o_ref, dqkv_ref, dl_ref, *rest):
+        gains_ref, far_ref, again, mgain, *rest = rest
         keep_o, give_o, left_s, pack_s, sems = rest
         xv = x_ref[...].astype(F32)
         normed = (xv * row_scale_of(xv) * again[...]).astype(BF16)
@@ -680,6 +724,7 @@
         column = lax.broadcasted_iota(jnp.int32, (16, HEAD), 1)
         hit = (column == experts + row // 2) & (row < 4)
         marks = jnp.where(hit, 1.0, 0.0).astype(BF16)
+        far_marks = jnp.where(hit & (row < 2), 1.0, 0.0).astype(BF16)
 
         def step(c, carry):
             spot = pl.ds(pl.multiple_of(c * tile, tile), tile)
@@ -696,7 +741,9 @@
             pack_s[1, spot, out_at:side_at] = made[:, model // 2 :]
         for i in range(model // tile):
             spot = slice(i * tile, (i + 1) * tile)
-            total = mul_tn(normed_m[:, spot], spread_logits) + mul_tn(gains_ref[:, spot], marks)
+            total = mul_tn(normed_m[:, spot], spread_logits)
+            total = total + mul_tn(gains_ref[:, spot], marks)
+            total = total + mul_tn(far_ref[:, spot], far_marks)
             at = (i % parts) * tile
             pack_s[i // parts, at : at + tile, side_at:] = total.astype(BF16)
         kept = 1 - own_ref[0]
@@ -712,34 +759,46 @@
     return call(
         body,
         [((model // 2, side_at + HEAD), BF16)] * 2,
-        [SMEM] + [VMEM] * 9,
+        [SMEM] + [VMEM] * 10,
         [
             pltpu.VMEM((model, count), BF16),
             pltpu.VMEM((2, model // 2, side_at + HEAD), BF16),
             pltpu.SemaphoreType.DMA((2,)),
         ],
-        (own, x, h, grad_h, o, dqkv, dlogits, gains, attn_gain, moe_gain),
+        (own, x, h, grad_h, o, dqkv, dlogits, gains, gains_r, attn_gain, moe_gain),
         "attend_grads",
         [ANY, ANY],
     )
 
 
 def ff_total(core, zero, one):
-    model, wide = zero[0].shape
+    _, model, wide = zero[0].shape
     half = wide // 3
     blocks = model // half
-    pieces = len(zero) - 2
-    rows = model // pieces
-    count = len(zero)
+
+    def parts(refs):
+        return [refs[0].at[0], refs[1].at[0], *refs[2:]]
 
     def body(core_ref, *refs):
-        ins, outs, (held, sems) = refs[: 2 * count], refs[2 * count : 2 * count + 3], refs[-2:]
-        targets = [held.at[0], held.at[1]]
-        targets += [held.at[2, i * rows : (i + 1) * rows] for i in range(pieces)]
-        for i, target in enumerate(targets):
-            fetch(core_ref[0], ins[count + i], ins[i], target, sems.at[i])
-        for i, target in enumerate(targets):
-            arrive(ins[i], target, sems.at[i])
+        first, second = parts(refs[: len(zero)]), parts(refs[len(zero) : len(zero) + len(one)])
+        outs, (held, sems) = refs[-5:-2], refs[-2:]
+
+        def moves(sources):
+            targets, low = [held.at[0], held.at[1]], 0
+            for ref in sources[2:]:
+                targets.append(held.at[2, low : low + ref.shape[0]])
+                low += ref.shape[0]
+            pairs = enumerate(zip(sources, targets))
+            return [pltpu.make_async_copy(a, b, sems.at[i]) for i, (a, b) in pairs]
+
+        for number, sources in ((0, first), (1, second)):
+
+            @pl.when(core_ref[0] == number)
+            def _(sources=sources):
+                for copy in moves(sources):
+                    copy.start()
+                for copy in moves(sources):
+                    copy.wait()
 
         def total(rows, columns):
             return (
@@ -757,23 +816,36 @@
     return call(
         body,
         [((model, half), F32), ((model, half), F32), ((half, model), F32)],
-        [SMEM] + [ANY] * (2 * count),
-        [pltpu.VMEM((3, model, wide), BF16), pltpu.SemaphoreType.DMA((count,))],
+        [SMEM] + [ANY] * (len(zero) + len(one)),
+        [pltpu.VMEM((3, model, wide), BF16), pltpu.SemaphoreType.DMA((4,))],
         (core, *zero, *one),
         "ff_total",
     )
 
 
-def attn_total(core, zero, one, width, model):
+def attn_total(core, zero, one, width, model, experts):
     rows, wide = zero[0].shape
     out_at = width + 2 * HEAD
     side_at = out_at + model // 2
 
     def body(core_ref, *refs):
-        ins, outs, (held, sems) = refs[:4], refs[4:9], refs[9:]
-        for i in range(2):
-            fetch(core_ref[0], ins[2 + i], ins[i], held.at[i], sems.at[i])
-        query, key, value, out, side = outs
+        ins, outs, (held, sems) = refs[:4], refs[4:11], refs[11:]
+        fetch(core_ref[0], ins[3], ins[1], held.at[1], sems.at[1])
+        piece = rows // 16
+
+        @pl.when(core_ref[0] == 1)
+        def _():
+            for y in range(4):
+                for x in range(4):
+                    source = ins[2].at[(y * 4 + x) * piece : (y * 4 + x + 1) * piece]
+                    target = held.at[0, (x * 4 + y) * piece : (x * 4 + y + 1) * piece]
+                    pltpu.make_async_copy(source, target, sems.at[0]).start()
+
+        @pl.when(core_ref[0] != 1)
+        def _():
+            pltpu.make_async_copy(ins[0], held.at[0], sems.at[0]).start()
+
+        query, key, value, out, router, attn, moe = outs
         for i in range(2):
             arrive(ins[i], held.at[i], sems.at[i])
             spot = slice(i * rows, (i + 1) * rows)
@@ -781,7 +853,12 @@
             key[spot, :] = held[i, :, width : width + HEAD].astype(F32)
             value[spot, :] = held[i, :, width + HEAD : out_at].astype(F32)
             out[:, i * (model // 2) : (i + 1) * (model // 2)] = held[i, :, out_at:side_at].astype(F32)
-            side[spot, :] = held[i, :, side_at:].astype(F32)
+            for j in range(0, rows, HEAD):
+                side = held[i, j : j + HEAD, side_at:].astype(F32).T
+                at = slice(i * rows + j, i * rows + j + HEAD)
+                router[:, at] = side[:experts, :]
+                attn[:, at] = side[experts : experts + 1, :]
+                moe[:, at] = side[experts + 1 : experts + 2, :]
 
     return call(
         body,
@@ -790,7 +867,9 @@
             ((model, HEAD), F32),
             ((model, HEAD), F32),
             ((width, model), F32),
-            ((model, wide - side_at), F32),
+            ((experts, model), F32),
+            ((1, model), F32),
+            ((1, model), F32),
         ],
         [SMEM] + [ANY] * 4,
         [pltpu.VMEM((2, rows, wide), BF16), pltpu.SemaphoreType.DMA((2,))],
@@ -814,21 +893,35 @@
     )
 
 
-def plane_sum(value, level):
+def plane_sum(value, level, *others):
     rows, wide = value.shape
-    arrived = plane_exchange(value.reshape(4, rows // 4, wide), level)
-    return jnp.sum(arrived.astype(F32), axis=0).astype(BF16)
+    count = len(plane_groups(level)[0])
+    arrived = plane_exchange(value.reshape(count, rows // count, wide), level)
+    return jnp.sum(after(arrived, *others).astype(F32), axis=0).astype(BF16)
 
 
 def plane_copy(piece, level):
     rows, wide = piece.shape
-    spread = jnp.broadcast_to(piece[None], (4, rows, wide))
-    return plane_exchange(spread, level).reshape(4 * rows, wide)
-
-
-def plane_gather(piece, level):
+    count = len(plane_groups(level)[0])
+    spread = jnp.broadcast_to(piece[None], (count, rows, wide))
+    return plane_exchange(spread, level).reshape(count * rows, wide)
+
+
+def gather_plane(piece):
+    plane = [[(y * 4 + x) * 2 + z for y in range(4) for x in range(4)] for z in range(2)]
+    groups = plane + [[32 + e for e in group] for group in plane]
     return lax.all_gather(
-        piece, ("pipe", "expert"), axis=0, axis_index_groups=plane_groups(level), tiled=True
+        piece, ("pipe", "expert"), axis=0, axis_index_groups=groups, tiled=True
+    )
+
+
+def background_sum(value, level):
+    return lax.psum_scatter(
+        value,
+        ("pipe", "expert"),
+        scatter_dimension=0,
+        axis_index_groups=plane_groups(level),
+        tiled=True,
     )
 
 
@@ -886,6 +979,11 @@
         pairs = [(2 * layer, 2 * layer + 1), (2 * layer + 1, 2 * layer)]
         return lax.ppermute(value, ("pipe", "tensor"), pairs)
 
+    def by_layer(zero, one):
+        own, other = jnp.where(first, zero, one), jnp.where(first, one, zero)
+        got = swap(other, "pipe")
+        return got, jnp.where(first, jnp.stack([own, got]), jnp.stack([got, own]))
+
     cosine, sine = rotary_tables(count)
     x_0 = lax.dynamic_index_in_dim(tokens, core, 0, keepdims=False)
     top = lax.dynamic_index_in_dim(cotangent, core, 0, keepdims=False)
@@ -925,110 +1023,88 @@
     ff_1 = (*near, *near_r, *far_1, *far_1r)
     dx, made, dgu = experts_backward(owns[1], rows_1, top_rows, ff_1)
     dx = exchange_rows(dx, experts)
-    near_1, far_g1, out_rows = experts_grads(owns[1], rows_1, top_rows, made, dgu, ff_1)
-    dx = after(dx, near_1)
-    pieces = model // 3
-
-    def far_pieces(mine, theirs):
-        return [
-            mine[i : i + pieces] + theirs[i : i + pieces] for i in range(0, model, pieces)
-        ]
-
+    both_1, out_rows = experts_grads(owns[1], rows_1, top_rows, made, dgu, ff_1)
+    dx = after(dx, both_1)
     share = collect(table_1, dx, experts)
     share_r = swap(share, "tensor")
     back_1 = exchange_rows(after(out_rows, share), experts)
-    near_1r, far_r = over(after(near_1, share), 1), over(after(far_g1, share), 1)
+    both_1r = over(after(both_1, share), 1)
     dqkv, da, grad_h, dlogits, gains = attend_backward(
         owns[1], top, h_1, x_1, (share, share_r), gates_1, (),
         routers[1], moe_gains[1], attn_gains[1], kept_1, cosine, sine, attn_weights,
     )
-    da_r = swap(after(da, near_1r, far_r), "tensor")
-    far_sum = far_pieces(far_g1, far_r)
+    da_r = swap(after(da, both_1r), "tensor")
+    far_sum = both_1[1] + both_1r[1]
+    gains_r = swap(gains, "tensor")
+    grad_1, grad, rows, seen = turn_over(
+        grad_h, x_1, da, after(da_r, back_1, far_sum, gains_r), attn_gains[1], table_0, gated_0, back_0,
+        experts,
+    )
+
+    grad_rows = exchange_rows(rows, experts)
+    far_z = across(after(far_sum, da_r), 1)
+    ff_grads_1 = (both_1, both_1r, far_z)
     keep, give = attend_grads(
-        owns[1], x_1, h_1, grad_h, kept_1[2], dqkv, dlogits, gains, attn_gains[1], moe_gains[1]
-    )
-    grad_1, grad, rows, seen = turn_over(
-        grad_h, x_1, da, after(da_r, back_1, keep), attn_gains[1], table_0, gated_0, back_0,
-        experts,
-    )
-
+        owns[1], x_1, h_1, grad_h, kept_1[2], dqkv, dlogits, gains, gains_r,
+        attn_gains[1], moe_gains[1],
+    )
     seen_r = swap(seen, "tensor")
-    grad_rows = exchange_rows(rows, experts)
-    far_z = [across(after(far_sum[0], rows), 1)]
-    half_1 = keep + swap(after(give, rows), "pipe")
-    share = mul_tn(gated_1, back_1).astype(BF16)
-    share_r = swap(after(share, rows), "tensor")
-    grad_rows = after(grad_rows, half_1, share_r, seen_r, far_z[0])
-    y_1 = h_1 + (share.astype(F32) + share_r.astype(F32))
-    far_z += [across(after(far_sum[1], grad_rows), 1)]
+    grad_rows = after(grad_rows, keep)
     dx, made, dgu = experts_backward(owns[0], rows_0, grad_rows, ff_0)
-    far_z += [across(after(far_sum[2], dx), 1)]
-    ff_grads_1 = (near_1, near_1r, *far_z)
-    dx = exchange_rows(after(dx, far_z[1]), experts)
-    near_0, far_g0 = experts_grads(owns[0], rows_0, grad_rows, made, dgu, ff_0)
-    dx = after(dx, near_0, far_z[2])
+    half_1 = keep + swap(after(give, dx), "pipe")
+    level_1 = background_sum(half_1, 0)
+    late = mul_tn(gated_1, after(back_1, dx)).astype(BF16)
+    dx = exchange_rows(dx, experts)
+    (both_0,) = experts_grads(owns[0], rows_0, grad_rows, made, dgu, ff_0)
+    late_r = swap(late, "tensor")
+    y_1 = h_1 + (late.astype(F32) + late_r.astype(F32))
+    dx = after(dx, both_0, late_r, far_z, half_1, seen_r)
     share = mul_tn(table_0, dx).astype(BF16)
     share_r = swap(share, "tensor")
-    level_1 = plane_sum(after(half_1, share), 0)
-    near_0r, far_r = over(after(near_0, share), 0), over(after(far_g0, share), 0)
+    level_1 = background_sum(after(level_1, dx), 1)
+    both_0r = over(after(both_0, share), 0)
     dqkv, da, grad_h, dlogits, gains = attend_backward(
         owns[0], grad, h_0, x_0, (share, share_r), gates_0, (seen, seen_r),
         routers[0], moe_gains[0], attn_gains[0], kept_0, cosine, sine, attn_weights,
     )
-    da_r = swap(after(da, near_0r, far_r), "tensor")
+    gains_r = swap(gains, "tensor")
     keep, give = attend_grads(
-        owns[0], x_0, h_0, grad_h, kept_0[2], after(dqkv, level_1), dlogits, gains,
+        owns[0], x_0, h_0, grad_h, kept_0[2], dqkv, dlogits, gains, gains_r,
         attn_gains[0], moe_gains[0],
     )
-    far_sum = far_pieces(far_g0, far_r)
-
+
+    cuts = ((0, model * 2 // 3), (model * 2 // 3, model))
+    far_sum = [both_0[1, a:b] + both_0r[1, a:b] for a, b in cuts]
     half_0 = after(keep, *far_sum) + swap(give, "pipe")
-    far_z = [across(after(far_sum[0], half_0), 0)]
-    level_0 = plane_sum(half_0, 0)
-    level = after(jnp.concatenate([level_0, level_1], axis=1), far_z[0], da_r)
-    wide = level_0.shape[1]
-    piece = across_planes(plane_sum(level, 1))
-    far_z += [across(after(v, piece), 0) for v in far_sum[1:]]
-    part = plane_copy(piece, 1)
-    da = da.astype(F32) + da_r.astype(F32)
+    da_r = swap(after(da, half_0), "tensor")
+    got_y, layer_out = by_layer(y_0, after(y_1, keep))
+    level_0 = plane_sum(half_0, 0, da_r, got_y)
+    piece_1 = across_planes(after(level_1, level_0))
+    sum_1 = gather_plane(piece_1)
+    part = plane_copy(plane_sum(level_0, 2), 2)
+    far_z = [across(after(v, part), 0) for v in far_sum]
+    da = da.astype(F32) + after(da_r, part).astype(F32)
     x_f = x_0.astype(F32)
     grad_0 = grad_h + norm_back(x_f, row_scale_of(x_f), attn_gains[0], da)
-    ff_grads_0 = (near_0, near_0r, *far_z)
-
-    def by_layer(zero, one):
-        own, other = jnp.where(first, zero, one), jnp.where(first, one, zero)
-        got = swap(other, "pipe")
-        return got, jnp.where(first, jnp.stack([own, got]), jnp.stack([got, own]))
-
-    got_y, layer_out = by_layer(y_0, y_1)
     got_g, input_grads = by_layer(grad_0, grad_1)
-    part = after(part, got_y, got_g)
-    sum_0 = plane_copy(part[:, :wide], 0)
-    sum_1 = plane_gather(part[:, wide:], 0)
+    ff_grads_0 = (both_0, both_0r, *far_z)
+    sum_0 = after(plane_copy(part, 0), far_z[0])
     core_v = core.astype(jnp.int32).reshape(1)
-    gate_g, up_g, down_g = ff_total(core_v, ff_grads_0, ff_grads_1)
-    over_0, over_1 = over(after(sum_0, gate_g), 0), over(sum_1, 1)
-    query_g, key_g, value_g, out_g, side = attn_total(
-        core_v, (sum_0, over_0), (sum_1, over_1), width, model
-    )
-    at = wide - HEAD + experts
-    attn_part = jnp.concatenate(
-        [
-            jnp.where(first, zero[:, at], one[:, at]).astype(F32)
-            for zero, one in ((sum_0, sum_1), (over_0, over_1))
-        ]
-    )
-    attn_part = attn_part + swap(attn_part, "tensor")
+    over_0, over_1 = over(after(sum_0, got_g), 0), over(sum_1, 1)
+    query_g, key_g, value_g, out_g, router_g, attn_g, moe_g = attn_total(
+        core_v, (sum_0, over_0), (sum_1, over_1), width, model, experts
+    )
+    gate_g, up_g, down_g = ff_total(after(core_v, moe_g), ff_grads_0, ff_grads_1)
     return (
         layer_out[None],
         input_grads[None],
-        attn_part[None],
+        attn_g,
         query_g[None],
         key_g[None],
         value_g[None],
         out_g[None],
-        side[:, experts + 1][None],
-        side[:, :experts][None],
+        moe_g,
+        router_g.T[None],
         gate_g[None, None],
         up_g[None, None],
         down_g[None, None],

time: 580 us -> 528 us (0.910)
  starting transfers between devices: 160 us -> 125 us
  waiting for transfers between devices: 188 us -> 159 us
  blocking collectives: 0 us -> 28.9 us
  local copies, waits for them, and re-layouts: 28.5 us -> 20.7 us
  other arithmetic: 42.4 us -> 35.8 us
    all_to_all x0 -> x2, blocking collectives: none -> 28.9 us  [plane_exchange(): lax.all_to_all(value, ('pipe', 'expert'), split_axis=0, concat_axis=0, ax...]
    ppermute x12 -> x9, waiting for transfers between devices: 35.2 us -> 12.2 us  [across(): return lax.ppermute(value, ('pipe', 'tensor'), pairs)]
    all_to_all x5 -> x2, waiting for transfers between devices: 38.9 us -> 26.5 us  [plane_exchange(): lax.all_to_all(value, ('pipe', 'expert'), split_axis=0, concat_axis=0, ax...]
    all_to_all x5 -> x2, starting transfers between devices: 21 us -> 9.52 us  [plane_exchange(): lax.all_to_all(value, ('pipe', 'expert'), split_axis=0, concat_axis=0, ax...]
    all_to_all x8, waiting for transfers between devices: 49.9 us -> 58.1 us  [expert_exchange(): lax.all_to_all(value, ('expert', 'tensor'), split_axis=0, concat_axis=0,...]
    ppermute x23 -> x24, starting transfers between devices: 19.1 us -> 12.7 us  [swap(): return lax.ppermute(value, axis, SWAP)]
    ppermute x12 -> x9, starting transfers between devices: 27.7 us -> 22.7 us  [across(): return lax.ppermute(value, ('pipe', 'tensor'), pairs)]
    unnamed x189 -> x172, local copies, waits for them, and re-layouts: 21 us -> 17.1 us
  transfers between devices with their start and end apart: 62 -> 57, of which waited for: 28 -> 25; matrix products, arithmetic and copies ran while one was open for 9% -> 8% of each run, Pallas kernels for 16% -> 18%
where the time goes in v3:
time: 528 us; the launch traced here: 517 us
  waiting for transfers between devices  159 us (30%)
  Pallas kernels  126 us (24%)
  starting transfers between devices  125 us (24%)
  other arithmetic  35.8 us (7%)
  blocking collectives  28.9 us (5%)
  local copies, waits for them, and re-layouts  20.7 us (4%)
  between operations  15.4 us (3%)
  matrix products  6.3 us (1%)
    pallas_call x18, Pallas kernels, call(): pl.pallas_call(body, out_shape=[jax.ShapeDtypeStruct(shape, kind) for sha...  126 us
    all_to_all x8, waiting for transfers between devices, expert_exchange(): lax.all_to_all(value, ('expert', 'tensor'), split_axis=0, concat_axis=0,...  58.1 us
    all_to_all x8, starting transfers between devices, expert_exchange(): lax.all_to_all(value, ('expert', 'tensor'), split_axis=0, concat_axis=0,...  51.4 us
    ppermute x24, waiting for transfers between devices, swap(): return lax.ppermute(value, axis, SWAP)  44.4 us
    all_to_all x2, blocking collectives, plane_exchange(): lax.all_to_all(value, ('pipe', 'expert'), split_axis=0, concat_axis=0, ax...  28.9 us
    ppermute x10, starting transfers between devices, over(): return lax.ppermute(value, 'pipe', [(1 - layer, layer)])  28.4 us
    all_to_all x2, waiting for transfers between devices, plane_exchange(): lax.all_to_all(value, ('pipe', 'expert'), split_axis=0, concat_axis=0, ax...  26.5 us
    ppermute x9, starting transfers between devices, across(): return lax.ppermute(value, ('pipe', 'tensor'), pairs)  22.7 us
  transfers between devices with their start and end apart: 57, of which 25 were waited for; matrix products, arithmetic and copies ran while one was open for 8% of the time, Pallas kernels for 18%

profile of v3, /device:TPU:0, one launch (start us, length us, event | category | flops | bytes accessed | tf_op | source)
XLA Modules:
  0.0 517.5 jit_solution(4451445864974337934)
XLA Ops:
  10.6 3.9 collective-permute-start.6
  21.2 4.8 attend_forward.2
  33.7 5.0 collective-permute-done.7.b_ref
  47.4 9.8 %all-to-all-start = ((bf16[32,16,1536]{2,1,0:T(8,128)(2,1)}), bf16[32,16,1536]{2,1,0:T(8,128)(2,1)}, u32[]{:S(2)}, u32[]{:S(2)}) async-start(bf16[32,16,1536]{2,1,0:T(8,128)(2,1)} %bitcast.124), calls=%async_computation | async-start | bytes 3145728 | tf_op jit(solution)/shard_map/all_to_all | solution.py:26
  61.3 8.4 %collective-permute-done.14.refs_8_.refs_2_ = bf16[384,1536]{1,0:T(8,128)(2,1)} collective-permute-done((bf16[384,1536]{1,0:T(8,128)(2,1)S(1)}, bf16[384,1536]{1,0:T(8,128)(2,1)}, u32[]{:S(2)}, u32[]{:S(2)}) %collective-permute-start.14) | collective-permute-done | bytes 1179680 | tf_op jit(solution)/shard_map/ppermute | solution.py:980
  75.8 8.2 %experts_forward.1 = bf16[512,1536]{1,0:T(8,128)(2,1)} custom-call(s32[1]{0:T(128)} %bitcast.8.own_ref, bf16[512,1536]{1,0:T(8,128)(2,1)} %bitcast.17.x_ref, bf16[1536,384]{1,0:T(8,128)(2,1)S(1)} %bitcast.89, bf16[1536,384]{1,0:T(8,128)(2,1)} %bitcast.18.refs_1_, bf16[384,1536]{1,0:T(8,128)(2,1)} %bitcast.79, bf16[1536,384]{1,0:T(8,128)(2,1)} %copy-done.59, ...), custom_call_target="tpu_custom_call" | custom-call | flops 1024 | bytes 1024 | tf_op jit(solution)/shard_map/experts_forward/pallas_call | solution.py:75
  84.0 7.7 %all-to-all-start.1 = ((bf16[32,16,1536]{2,1,0:T(8,128)(2,1)}), bf16[32,16,1536]{2,1,0:T(8,128)(2,1)}, u32[]{:S(2)}, u32[]{:S(2)}) async-start(bf16[32,16,1536]{2,1,0:T(8,128)(2,1)} %bitcast.116), calls=%async_computation.1 | async-start | bytes 3145728 | tf_op jit(solution)/shard_map/all_to_all | solution.py:26
  94.2 23.2 %all-to-all-done.1 = bf16[32,16,1536]{2,1,0:T(8,128)(2,1)} async-done(((bf16[32,16,1536]{2,1,0:T(8,128)(2,1)}), bf16[32,16,1536]{2,1,0:T(8,128)(2,1)}, u32[]{:S(2)}, u32[]{:S(2)}) %all-to-all-start.1) | async-done | bytes 1572896 | tf_op jit(solution)/shard_map/all_to_all | solution.py:26
  120.2 5.2 all-to-all-start.2
  125.4 4.2 collective-permute-done.18.refs_2_
  130.4 6.7 %attend_forward.3 = (bf16[128,1536]{1,0:T(8,128)(2,1)S(1)}, bf16[128,768]{1,0:T(8,128)(2,1)S(1)}, bf16[128,256]{1,0:T(8,128)(2,1)S(1)}, bf16[128,768]{1,0:T(8,12...) custom-call(s32[1]{0:T(128)} %bitcast.own_ref, f32[128,1536]{1,0:T(8,128)} %get-tuple-element.110.refs_0_.refs_1_.h_ref, ...), custom_call_target="tpu_custom_call" | custom-call | flops 1024 | bytes 1024 | tf_op jit(solution)/shard_map/attend_forward/pallas_call | solution.py:75
  139.1 7.8 %collective-permute-done.19.b_ref = bf16[128,1536]{1,0:T(8,128)(2,1)S(1)} collective-permute-done((bf16[128,1536]{1,0:T(8,128)(2,1)S(1)}, bf16[128,1536]{1,0:T(8,128)(2,1)S(1)}, u32[]{:S(2)}, u32[]{:S(2)}) %collective-permute-start.19) | collective-permute-done | bytes 393248 | tf_op jit(solution)/shard_map/ppermute | solution.py:18
  151.7 5.8 %all-to-all-start.3 = ((bf16[32,16,1664]{2,1,0:T(8,128)(2,1)}), bf16[32,16,1664]{2,1,0:T(8,128)(2,1)}, u32[]{:S(2)}, u32[]{:S(2)}) async-start(bf16[32,16,1664]{2,1,0:T(8,128)(2,1)} %bitcast.119), calls=%async_computation.3 | async-start | bytes 3407872 | tf_op jit(solution)/shard_map/all_to_all | solution.py:26
  161.4 8.9 %collective-permute-done.21.refs_9_ = bf16[1536,384]{1,0:T(8,128)(2,1)S(1)} collective-permute-done((bf16[1536,384]{1,0:T(8,128)(2,1)}, bf16[1536,384]{1,0:T(8,128)(2,1)S(1)}, u32[]{:S(2)}, u32[]{:S(2)}) %collective-permute-start.21) | collective-permute-done | bytes 1179680 | tf_op jit(solution)/shard_map/ppermute | solution.py:976
  173.6 4.0 all-to-all-done.3
  177.6 12.6 %experts_backward.2 = (bf16[512,1664]{1,0:T(8,128)(2,1)}, bf16[512,768]{1,0:T(8,128)(2,1)S(1)}, bf16[512,1536]{1,0:T(8,128)(2,1)}) custom-call(s32[1]{0:T(128)} %bitcast.own_ref, bf16[512,1664]{1,0:T(8,128)(2,1)} %bitcast.25.x_ref, bf16[512,1536]{1,0:T(8,128)(2,1)} %bitcast.23.g_ref, bf16[1536,384]{1,0:T(8,128)(2,1)S(1)} %bitcast.91, ...), custom_call_target="tpu_custom_call" | custom-call | flops 1024 | bytes 1024 | tf_op jit(solution)/shard_map/experts_backward/pallas_call | solution.py:75
  191.0 6.4 %all-to-all-start.4 = ((bf16[32,16,1664]{2,1,0:T(8,128)(2,1)}), bf16[32,16,1664]{2,1,0:T(8,128)(2,1)}, u32[]{:S(2)}, u32[]{:S(2)}) async-start(bf16[32,16,1664]{2,1,0:T(8,128)(2,1)} %bitcast.120), calls=%async_computation.4 | async-start | bytes 3407872 | tf_op jit(solution)/shard_map/all_to_all | solution.py:26
  198.6 13.3 %experts_grads.2 = (bf16[2,1536,1152]{2,1,0:T(8,128)(2,1)}, bf16[512,1536]{1,0:T(8,128)(2,1)}) custom-call(s32[1]{0:T(128)} %bitcast.own_ref, bf16[512,1664]{1,0:T(8,128)(2,1)} %bitcast.25.x_ref, bf16[512,1536]{1,0:T(8,128)(2,1)} %bitcast.23.g_ref, bf16[512,768]{1,0:T(8,128)(2,1)S(1)} %copy-done.30, bf16[512,1536]{1,0:T(8,128)(2,1)} %get-tuple-element.134.dgu_ref, ...), custom_call_target="tpu_custom_call" | custom-call | flops 1024 | bytes 1024 | tf_op jit(solution)/shard_map/experts_grads/pallas_call | solution.py:75
  211.9 9.0 %all-to-all-done.4 = bf16[32,16,1664]{2,1,0:T(8,128)(2,1)} async-done(((bf16[32,16,1664]{2,1,0:T(8,128)(2,1)}), bf16[32,16,1664]{2,1,0:T(8,128)(2,1)}, u32[]{:S(2)}, u32[]{:S(2)}) %all-to-all-start.4) | async-done | bytes 1703968 | tf_op jit(solution)/shard_map/all_to_all | solution.py:26
  222.7 9.1 %collective-permute-start.25 = (bf16[2,1536,1152]{2,1,0:T(8,128)(2,1)}, bf16[2,1536,1152]{2,1,0:T(8,128)(2,1)}, u32[]{:S(2)}, u32[]{:S(2)}) collective-permute-start(bf16[2,1536,1152]{2,1,0:T(8,128)(2,1)} %get-tuple-element.145.refs_4_), channel_id=1, source_target_pairs={{0,64},{1,65},{2,66},{3,67},{4,68},{5,69},{6,70},{7,71},{8,72},{9,... | collective-permute-start | bytes 21233672 | tf_op jit(solution)/shard_map/ppermute | solution.py:976
  231.8 4.8 all-to-all-start.5
  241.0 9.0 %attend_backward.2 = (bf16[128,1024]{1,0:T(8,128)(2,1)S(1)}, bf16[128,1536]{1,0:T(8,128)(2,1)S(1)}, f32[128,1536]{1,0:T(8,128)}, bf16[32,128]{1,0:T(8,128)(2,1)S(1)}, bf16[16,1536]{1,0:T(8,128)(2,1)S(1)}) custom-call(s32[1]{0:T(128)} %bitcast.own_ref, f32[128,1536]{1,0:T(8,128)} %copy-done.10, f32[128,1536]{1,0:T(8,128)} %get-tuple-element.124.refs_1_.h_ref, ...), custom_call_target="tpu_custom_call" | custom-call | flops 1024 | bytes 1024 | tf_op jit(solution)/shard_map/attend_backward/pallas_call | solution.py:75
  252.1 4.2 fusion
  258.6 4.0 turn_over.1
  263.4 6.9 %all-to-all-start.6 = ((bf16[32,16,1536]{2,1,0:T(8,128)(2,1)}), bf16[32,16,1536]{2,1,0:T(8,128)(2,1)}, u32[]{:S(2)}, u32[]{:S(2)}) async-start(bf16[32,16,1536]{2,1,0:T(8,128)(2,1)} %bitcast.125), calls=%async_computation.6 | async-start | bytes 3145728 | tf_op jit(solution)/shard_map/all_to_all | solution.py:26
  272.7 7.0 %attend_grads.2 = (bf16[768,1920]{1,0:T(8,128)(2,1)}, bf16[768,1920]{1,0:T(8,128)(2,1)}) custom-call(s32[1]{0:T(128)} %bitcast.own_ref, bf16[128,1536]{1,0:T(8,128)(2,1)S(1)} %copy-done.15, f32[128,1536]{1,0:T(8,128)S(1)} %copy-done.11, f32[128,1536]{1,0:T(8,128)} %get-tuple-element.143.g_ref.gh_ref, bf16[128,768]{1,0:T(8,128)(2,1)S(1)} %copy-done.44, ...), custom_call_target="tpu_custom_call" | custom-call | flops 1024 | bytes 1024 | tf_op jit(solution)/shard_map/attend_grads/pallas_call | solution.py:75
  279.7 11.0 %all-to-all-done.6 = bf16[32,16,1536]{2,1,0:T(8,128)(2,1)} async-done(((bf16[32,16,1536]{2,1,0:T(8,128)(2,1)}), bf16[32,16,1536]{2,1,0:T(8,128)(2,1)}, u32[]{:S(2)}, u32[]{:S(2)}) %all-to-all-start.6) | async-done | bytes 1572896 | tf_op jit(solution)/shard_map/all_to_all | solution.py:26
  290.6 11.8 %experts_backward.3 = (bf16[512,1536]{1,0:T(8,128)(2,1)}, bf16[512,768]{1,0:T(8,128)(2,1)S(1)}, bf16[512,1536]{1,0:T(8,128)(2,1)}) custom-call(s32[1]{0:T(128)} %bitcast.8.own_ref, bf16[512,1536]{1,0:T(8,128)(2,1)} %bitcast.17.x_ref, bf16[512,1536]{1,0:T(8,128)(2,1)} %bitcast.32.g_ref, bf16[1536,384]{1,0:T(8,128)(2,1)S(1)} %bitcast.92, ...), custom_call_target="tpu_custom_call" | custom-call | flops 1024 | bytes 1024 | tf_op jit(solution)/shard_map/experts_backward/pallas_call | solution.py:75
  303.4 4.8 all-to-all-start.7
  313.2 10.7 %experts_grads.3.refs_0_ = bf16[2,1536,1152]{2,1,0:T(8,128)(2,1)} custom-call(s32[1]{0:T(128)} %bitcast.8.own_ref, bf16[512,1536]{1,0:T(8,128)(2,1)} %bitcast.17.x_ref, bf16[512,1536]{1,0:T(8,128)(2,1)} %bitcast.32.g_ref, bf16[512,768]{1,0:T(8,128)(2,1)S(1)} %copy-done.28, bf16[512,1536]{1,0:T(8,128)(2,1)} %get-tuple-element.159.dgu_ref, ...), custom_call_target="tpu_custom_call" | custom-call | flops 1024 | bytes 1024 | tf_op jit(solution)/shard_map/experts_grads/pallas_call | solution.py:75
  324.0 4.3 add.80
  328.3 5.9 %all-to-all-done.7 = bf16[32,16,1536]{2,1,0:T(8,128)(2,1)} async-done(((bf16[32,16,1536]{2,1,0:T(8,128)(2,1)}), bf16[32,16,1536]{2,1,0:T(8,128)(2,1)}, u32[]{:S(2)}, u32[]{:S(2)}) %all-to-all-start.7) | async-done | bytes 1572896 | tf_op jit(solution)/shard_map/all_to_all | solution.py:26
  337.6 8.8 %collective-permute-done.32.refs_4_ = bf16[128,1536]{1,0:T(8,128)(2,1)S(1)} collective-permute-done((bf16[128,1536]{1,0:T(8,128)(2,1)S(1)}, bf16[128,1536]{1,0:T(8,128)(2,1)S(1)}, u32[]{:S(2)}, u32[]{:S(2)}) %collective-permute-start.32) | collective-permute-done | bytes 393248 | tf_op jit(solution)/shard_map/ppermute | solution.py:18
  347.3 7.8 %attend_backward.3 = (bf16[128,1024]{1,0:T(8,128)(2,1)S(1)}, bf16[128,1536]{1,0:T(8,128)(2,1)S(1)}, f32[128,1536]{1,0:T(8,128)}, bf16[32,128]{1,0:T(8,128)(2,1)S(1)}, bf16[16,1536]{1,0:T(8,128)(2,1)S(1)}) custom-call(s32[1]{0:T(128)} %bitcast.8.own_ref, bf16[128,1536]{1,0:T(8,128)(2,1)S(1)} %copy-done.36, ...), custom_call_target="tpu_custom_call" | custom-call | flops 1024 | bytes 1024 | tf_op jit(solution)/shard_map/attend_backward/pallas_call | solution.py:75
  355.3 3.9 collective-permute-done.33.rest_1_
  359.3 7.0 %attend_grads.3 = (bf16[768,1920]{1,0:T(8,128)(2,1)}, bf16[768,1920]{1,0:T(8,128)(2,1)}) custom-call(s32[1]{0:T(128)} %bitcast.8.own_ref, bf16[128,1536]{1,0:T(8,128)(2,1)S(1)} %copy-done.7, f32[128,1536]{1,0:T(8,128)S(1)} %copy-done.9, f32[128,1536]{1,0:T(8,128)} %get-tuple-element.168.gh_ref, bf16[128,768]{1,0:T(8,128)(2,1)S(1)} %copy-done.40, ...), custom_call_target="tpu_custom_call" | custom-call | flops 1024 | bytes 1024 | tf_op jit(solution)/shard_map/attend_grads/pallas_call | solution.py:75
  371.9 4.2 fusion.1
  378.4 4.8 all-to-all-start.8
  388.9 9.1 %collective-permute-done.37 = bf16[128,1536]{1,0:T(8,128)(2,1)S(1)} collective-permute-done((bf16[128,1536]{1,0:T(8,128)(2,1)S(1)}, bf16[128,1536]{1,0:T(8,128)(2,1)S(1)}, u32[]{:S(2)}, u32[]{:S(2)}) %collective-permute-start.37) | collective-permute-done | bytes 393248 | tf_op jit(solution)/shard_map/ppermute | solution.py:18
  398.0 9.1 %all-to-all-done.8 = bf16[4,192,1920]{2,1,0:T(8,128)(2,1)} async-done(((bf16[4,192,1920]{2,1,0:T(8,128)(2,1)}), bf16[4,192,1920]{2,1,0:T(8,128)(2,1)}, u32[]{:S(2)}, u32[]{:S(2)}) %all-to-all-start.8) | async-done | bytes 2949152 | tf_op jit(solution)/shard_map/all_to_all | solution.py:886
  409.9 7.1 %collective-permute-done.41 = bf16[48,1920]{1,0:T(8,128)(2,1)S(1)} collective-permute-done((bf16[48,1920]{1,0:T(8,128)(2,1)}, bf16[48,1920]{1,0:T(8,128)(2,1)S(1)}, u32[]{:S(2)}, u32[]{:S(2)}) %collective-permute-start.41) | collective-permute-done | bytes 184352 | tf_op jit(solution)/shard_map/ppermute | solution.py:929
  418.7 14.5 %all_to_all.60 = bf16[8,24,1920]{2,1,0:T(8,128)(2,1)S(1)} all-to-all(bf16[8,24,1920]{2,1,0:T(8,128)(2,1)S(1)} %bitcast.118), channel_id=1, replica_groups={{0,2,4,6,8,10,12,14},{64,66,80,82,96,98,112,114},{16,18,20,22,24,26,28,..., dimensions={0} | all-to-all | bytes 1474560 | tf_op jit(solution)/shard_map/all_to_all | solution.py:886
  433.4 14.4 %all_to_all.61 = bf16[8,24,1920]{2,1,0:T(8,128)(2,1)S(1)} all-to-all(bf16[8,24,1920]{2,1,0:T(8,128)(2,1)S(1)} %broadcast_in_dim.20), channel_id=1, replica_groups={{0,2,4,6,8,10,12,14},{64,66,80,82,96,98,112,114},{16,18,20,22,24,26,28,..., dimensions={0} | all-to-all | bytes 1474560 | tf_op jit(solution)/shard_map/all_to_all | solution.py:886
  452.9 4.8 all-to-all-start.11
  461.4 17.4 %all-to-all-done.11 = bf16[4,192,1920]{2,1,0:T(8,128)(2,1)} async-done(((bf16[4,192,1920]{2,1,0:T(8,128)(2,1)}), bf16[4,192,1920]{2,1,0:T(8,128)(2,1)}, u32[]{:S(2)}, u32[]{:S(2)}) %all-to-all-start.11) | async-done | bytes 2949152 | tf_op jit(solution)/shard_map/all_to_all | solution.py:886
  480.2 4.8 collective-permute-start.42
  493.8 7.4 %attn_total.1 = (f32[1536,768]{1,0:T(8,128)}, f32[1536,128]{1,0:T(8,128)}, f32[1536,128]{1,0:T(8,128)}, f32[768,1536]{1,0:T(8,128)}, f32[32,1536]{1,0:T(8,128)}, /*index=5*/f32[1,1536]{1,0:T(1,128)}, f32[1,1536]{1,0:T(1,128)}) custom-call(s32[1]{0:T(128)} %bitcast.44.core_ref, bf16[768,1920]{1,0:T(8,128)(2,1)} %bitcast.45.refs_0_, ...), custom_call_target="tpu_custom_call" | custom-call | flops 1024 | bytes 1024 | tf_op jit(solution)/shard_map/attn_total/pallas_call | solution.py:75
  503.3 7.2 %ff_total.1 = (f32[1536,384]{1,0:T(8,128)}, f32[1536,384]{1,0:T(8,128)}, f32[384,1536]{1,0:T(8,128)}) custom-call(s32[1]{0:T(128)} %bitcast.44.core_ref, bf16[2,1536,1152]{2,1,0:T(8,128)(2,1)} %experts_grads.3.refs_0_, bf16[2,1536,1152]{2,1,0:T(8,128)(2,1)} %collective-permute-done.35.refs_1_, bf16[1024,1152]{1,0:T(8,128)(2,1)} %collective-permute-done.39.refs_2_, ...), custom_call_target="tpu_custom_call" | custom-call | flops 1024 | bytes 1024 | tf_op jit(solution)/shard_map/ff_total/pallas_call | solution.py:75
  (297 shorter events, 121.5 us)
Async XLA Ops:
  7.2 13.1 %collective-permute-start.2 = (bf16[1536,768]{1,0:T(8,128)(2,1)}, bf16[1536,768]{1,0:T(8,128)(2,1)}, u32[]{:S(2)}, u32[]{:S(2)}) collective-permute-start(bf16[1536,768]{1,0:T(8,128)(2,1)} %bitcast.98), channel_id=1, source_target_pairs={{0,64},{64,0},{1,65},{65,1},{2,66},{66,2},{3,67},{67,3},{4,68},{68... | collective-permute-start | bytes 7077896 | tf_op jit(solution)/shard_map/ppermute | solution.py:18
  7.3 13.0 %collective-permute-start.5 = (bf16[768,1536]{1,0:T(8,128)(2,1)}, bf16[768,1536]{1,0:T(8,128)(2,1)}, u32[]{:S(2)}, u32[]{:S(2)}) collective-permute-start(bf16[768,1536]{1,0:T(8,128)(2,1)} %bitcast.103), channel_id=1, source_target_pairs={{0,64},{64,0},{1,65},{65,1},{2,66},{66,2},{3,67},{67,3},{4,68},{68... | collective-permute-start | bytes 7077896 | tf_op jit(solution)/shard_map/ppermute | solution.py:18
  10.2 7.9 %collective-permute-start.1 = (bf16[34,1536]{1,0:T(8,128)(2,1)}, bf16[34,1536]{1,0:T(8,128)(2,1)}, u32[]{:S(2)}, u32[]{:S(2)}) collective-permute-start(bf16[34,1536]{1,0:T(8,128)(2,1)} %pad_maximum_fusion), channel_id=1, source_target_pairs={{0,64},{64,0},{1,65},{65,1},{2,66},{66,2},{3,67},{67,3},{4,68},{68... | collective-permute-start | bytes 313352 | tf_op jit(solution)/shard_map/ppermute | solution.py:18
  10.6 18.4 %collective-permute-start.6 = (bf16[1536,384]{1,0:T(8,128)(2,1)}, bf16[1536,384]{1,0:T(8,128)(2,1)}, u32[]{:S(2)}, u32[]{:S(2)}) collective-permute-start(bf16[1536,384]{1,0:T(8,128)(2,1)} %bitcast.87), channel_id=1, source_target_pairs={{0,1},{1,0},{2,3},{3,2},{4,5},{5,4},{6,7},{7,6},{8,9},{9,8},{10,11... | collective-permute-start | bytes 3538952 | tf_op jit(solution)/shard_map/ppermute | solution.py:980
  29.0 9.6 %collective-permute-start.7 = (bf16[128,1536]{1,0:T(8,128)(2,1)S(1)}, bf16[128,1536]{1,0:T(8,128)(2,1)S(1)}, u32[]{:S(2)}, u32[]{:S(2)}) collective-permute-start(bf16[128,1536]{1,0:T(8,128)(2,1)S(1)} %get-tuple-element.109.a_ref), channel_id=1, source_target_pairs={{0,1},{1,0},{2,3},{3,2},{4,5},{5,4},{6,7},{7,6},{8,9},{9,8},{10,11... | collective-permute-start | bytes 1179656 | tf_op jit(solution)/shard_map/ppermute | solution.py:18
  31.4 26.4 %collective-permute-start.11 = (bf16[1536,384]{1,0:T(8,128)(2,1)}, bf16[1536,384]{1,0:T(8,128)(2,1)}, u32[]{:S(2)}, u32[]{:S(2)}) collective-permute-start(bf16[1536,384]{1,0:T(8,128)(2,1)} %collective-permute-done.6.refs_6_), channel_id=1, source_target_pairs={{0,64},{1,65},{2,66},{3,67},{4,68},{5,69},{6,70},{7,71},{8,72},{9,... | collective-permute-start | bytes 3538952 | tf_op jit(solution)/shard_map/ppermute | solution.py:976
  38.6 19.3 %collective-permute-start.12 = (bf16[1536,384]{1,0:T(8,128)(2,1)}, bf16[1536,384]{1,0:T(8,128)(2,1)}, u32[]{:S(2)}, u32[]{:S(2)}) collective-permute-start(bf16[1536,384]{1,0:T(8,128)(2,1)} %bitcast.18.refs_1_), channel_id=1, source_target_pairs={{0,1},{1,0},{2,3},{3,2},{4,5},{5,4},{6,7},{7,6},{8,9},{9,8},{10,11... | collective-permute-start | bytes 3538952 | tf_op jit(solution)/shard_map/ppermute | solution.py:980
  41.3 28.4 %collective-permute-start.14 = (bf16[384,1536]{1,0:T(8,128)(2,1)S(1)}, bf16[384,1536]{1,0:T(8,128)(2,1)}, u32[]{:S(2)}, u32[]{:S(2)}) collective-permute-start(bf16[384,1536]{1,0:T(8,128)(2,1)S(1)} %bitcast.82), channel_id=1, source_target_pairs={{0,1},{1,0},{2,3},{3,2},{4,5},{5,4},{6,7},{7,6},{8,9},{9,8},{10,11... | collective-permute-start | bytes 3538952 | tf_op jit(solution)/shard_map/ppermute | solution.py:980
  47.4 28.4 %all-to-all-start = ((bf16[32,16,1536]{2,1,0:T(8,128)(2,1)}), bf16[32,16,1536]{2,1,0:T(8,128)(2,1)}, u32[]{:S(2)}, u32[]{:S(2)}) async-start(bf16[32,16,1536]{2,1,0:T(8,128)(2,1)} %bitcast.124), calls=%async_computation | async-start | bytes 3145728 | tf_op jit(solution)/shard_map/all_to_all | solution.py:26
  57.2 15.8 %collective-permute-start.9 = (bf16[1536,384]{1,0:T(8,128)(2,1)}, bf16[1536,384]{1,0:T(8,128)(2,1)}, u32[]{:S(2)}, u32[]{:S(2)}) collective-permute-start(bf16[1536,384]{1,0:T(8,128)(2,1)} %bitcast.18.refs_1_), channel_id=1, source_target_pairs={{0,64},{64,0},{1,65},{65,1},{2,66},{66,2},{3,67},{67,3},{4,68},{68... | collective-permute-start | bytes 3538952 | tf_op jit(solution)/shard_map/ppermute | solution.py:18
  57.3 14.7 %collective-permute-start.8 = (bf16[1536,384]{1,0:T(8,128)(2,1)S(1)}, bf16[1536,384]{1,0:T(8,128)(2,1)S(1)}, u32[]{:S(2)}, u32[]{:S(2)}) collective-permute-start(bf16[1536,384]{1,0:T(8,128)(2,1)S(1)} %bitcast.88), channel_id=1, source_target_pairs={{0,64},{64,0},{1,65},{65,1},{2,66},{66,2},{3,67},{67,3},{4,68},{68... | collective-permute-start | bytes 3538952 | tf_op jit(solution)/shard_map/ppermute | solution.py:18
  57.8 15.2 %collective-permute-start.10 = (bf16[384,1536]{1,0:T(8,128)(2,1)S(1)}, bf16[384,1536]{1,0:T(8,128)(2,1)}, u32[]{:S(2)}, u32[]{:S(2)}) collective-permute-start(bf16[384,1536]{1,0:T(8,128)(2,1)S(1)} %bitcast.83), channel_id=1, source_target_pairs={{0,64},{64,0},{1,65},{65,1},{2,66},{66,2},{3,67},{67,3},{4,68},{68... | collective-permute-start | bytes 3538952 | tf_op jit(solution)/shard_map/ppermute | solution.py:18
  57.9 17.9 %collective-permute-start.13 = (bf16[1536,384]{1,0:T(8,128)(2,1)}, bf16[1536,384]{1,0:T(8,128)(2,1)}, u32[]{:S(2)}, u32[]{:S(2)}) collective-permute-start(bf16[1536,384]{1,0:T(8,128)(2,1)} %collective-permute-done.12.refs_7_), channel_id=1, source_target_pairs={{0,64},{1,65},{2,66},{3,67},{4,68},{5,69},{6,70},{7,71},{8,72},{9,... | collective-permute-start | bytes 3538952 | tf_op jit(solution)/shard_map/ppermute | solution.py:976
  84.0 33.3 %all-to-all-start.1 = ((bf16[32,16,1536]{2,1,0:T(8,128)(2,1)}), bf16[32,16,1536]{2,1,0:T(8,128)(2,1)}, u32[]{:S(2)}, u32[]{:S(2)}) async-start(bf16[32,16,1536]{2,1,0:T(8,128)(2,1)} %bitcast.116), calls=%async_computation.1 | async-start | bytes 3145728 | tf_op jit(solution)/shard_map/all_to_all | solution.py:26
  91.7 27.4 %collective-permute-start.16 = (bf16[1536,384]{1,0:T(8,128)(2,1)S(1)}, bf16[1536,384]{1,0:T(8,128)(2,1)S(1)}, u32[]{:S(2)}, u32[]{:S(2)}) collective-permute-start(bf16[1536,384]{1,0:T(8,128)(2,1)S(1)} %bitcast.90), channel_id=1, source_target_pairs={{64,65},{65,64},{66,67},{67,66},{68,69},{69,68},{70,71},{71,70},{7... | collective-permute-start | bytes 3538952 | tf_op jit(solution)/shard_map/ppermute | solution.py:980
  92.5 26.7 %collective-permute-start.17 = (bf16[1536,384]{1,0:T(8,128)(2,1)}, bf16[1536,384]{1,0:T(8,128)(2,1)}, u32[]{:S(2)}, u32[]{:S(2)}) collective-permute-start(bf16[1536,384]{1,0:T(8,128)(2,1)} %bitcast.18.refs_1_), channel_id=1, source_target_pairs={{64,65},{65,64},{66,67},{67,66},{68,69},{69,68},{70,71},{71,70},{7... | collective-permute-start | bytes 3538952 | tf_op jit(solution)/shard_map/ppermute | solution.py:980
  119.2 10.4 %collective-permute-start.18 = (bf16[128,1536]{1,0:T(8,128)(2,1)S(1)}, bf16[128,1536]{1,0:T(8,128)(2,1)S(1)}, u32[]{:S(2)}, u32[]{:S(2)}) collective-permute-start(bf16[128,1536]{1,0:T(8,128)(2,1)S(1)} %convolution_convert_fusion.2.refs_1_), channel_id=1, source_target_pairs={{0,1},{1,0},{2,3},{3,2},{4,5},{5,4},{6,7},{7,6},{8,9},{9,8},{10,11... | collective-permute-start | bytes 1179656 | tf_op jit(solution)/shard_map/ppermute | solution.py:18
  120.2 30.8 %all-to-all-start.2 = ((bf16[32,16,1536]{2,1,0:T(8,128)(2,1)}), bf16[32,16,1536]{2,1,0:T(8,128)(2,1)}, u32[]{:S(2)}, u32[]{:S(2)}) async-start(bf16[32,16,1536]{2,1,0:T(8,128)(2,1)} %bitcast.121), calls=%async_computation.2 | async-start | bytes 3145728 | tf_op jit(solution)/shard_map/all_to_all | solution.py:26
  146.9 13.2 %collective-permute-start.20 = (bf16[384,1536]{1,0:T(8,128)(2,1)S(1)}, bf16[384,1536]{1,0:T(8,128)(2,1)}, u32[]{:S(2)}, u32[]{:S(2)}) collective-permute-start(bf16[384,1536]{1,0:T(8,128)(2,1)S(1)} %bitcast.84), channel_id=1, source_target_pairs={{64,65},{65,64},{66,67},{67,66},{68,69},{69,68},{70,71},{71,70},{7... | collective-permute-start | bytes 3538952 | tf_op jit(solution)/shard_map/ppermute | solution.py:980
  151.7 25.9 %all-to-all-start.3 = ((bf16[32,16,1664]{2,1,0:T(8,128)(2,1)}), bf16[32,16,1664]{2,1,0:T(8,128)(2,1)}, u32[]{:S(2)}, u32[]{:S(2)}) async-start(bf16[32,16,1664]{2,1,0:T(8,128)(2,1)} %bitcast.119), calls=%async_computation.3 | async-start | bytes 3407872 | tf_op jit(solution)/shard_map/all_to_all | solution.py:26
  157.5 12.8 %collective-permute-start.21 = (bf16[1536,384]{1,0:T(8,128)(2,1)}, bf16[1536,384]{1,0:T(8,128)(2,1)S(1)}, u32[]{:S(2)}, u32[]{:S(2)}) collective-permute-start(bf16[1536,384]{1,0:T(8,128)(2,1)} %copy-done.70), channel_id=1, source_target_pairs={{64,0},{65,1},{66,2},{67,3},{68,4},{69,5},{70,6},{71,7},{72,8},{73... | collective-permute-start | bytes 3538952 | tf_op jit(solution)/shard_map/ppermute | solution.py:976
  158.8 13.2 %collective-permute-start.22 = (bf16[1536,384]{1,0:T(8,128)(2,1)}, bf16[1536,384]{1,0:T(8,128)(2,1)S(1)}, u32[]{:S(2)}, u32[]{:S(2)}) collective-permute-start(bf16[1536,384]{1,0:T(8,128)(2,1)} %collective-permute-done.17.refs_7_), channel_id=1, source_target_pairs={{64,0},{65,1},{66,2},{67,3},{68,4},{69,5},{70,6},{71,7},{72,8},{73... | collective-permute-start | bytes 3538952 | tf_op jit(solution)/shard_map/ppermute | solution.py:976
  160.1 13.5 %collective-permute-start.23 = (bf16[384,1536]{1,0:T(8,128)(2,1)}, bf16[384,1536]{1,0:T(8,128)(2,1)S(1)}, u32[]{:S(2)}, u32[]{:S(2)}) collective-permute-start(bf16[384,1536]{1,0:T(8,128)(2,1)} %collective-permute-done.20.refs_8_.refs_2_), channel_id=1, source_target_pairs={{64,0},{65,1},{66,2},{67,3},{68,4},{69,5},{70,6},{71,7},{72,8},{73... | collective-permute-start | bytes 3538952 | tf_op jit(solution)/shard_map/ppermute | solution.py:976
  191.0 29.8 %all-to-all-start.4 = ((bf16[32,16,1664]{2,1,0:T(8,128)(2,1)}), bf16[32,16,1664]{2,1,0:T(8,128)(2,1)}, u32[]{:S(2)}, u32[]{:S(2)}) async-start(bf16[32,16,1664]{2,1,0:T(8,128)(2,1)} %bitcast.120), calls=%async_computation.4 | async-start | bytes 3407872 | tf_op jit(solution)/shard_map/all_to_all | solution.py:26
  222.7 27.6 %collective-permute-start.25 = (bf16[2,1536,1152]{2,1,0:T(8,128)(2,1)}, bf16[2,1536,1152]{2,1,0:T(8,128)(2,1)}, u32[]{:S(2)}, u32[]{:S(2)}) collective-permute-start(bf16[2,1536,1152]{2,1,0:T(8,128)(2,1)} %get-tuple-element.145.refs_4_), channel_id=1, source_target_pairs={{0,64},{1,65},{2,66},{3,67},{4,68},{5,69},{6,70},{7,71},{8,72},{9,... | collective-permute-start | bytes 21233672 | tf_op jit(solution)/shard_map/ppermute | solution.py:976
  231.8 8.4 %collective-permute-start.24 = (bf16[128,1664]{1,0:T(8,128)(2,1)S(1)}, bf16[128,1664]{1,0:T(8,128)(2,1)S(1)}, u32[]{:S(2)}, u32[]{:S(2)}) collective-permute-start(bf16[128,1664]{1,0:T(8,128)(2,1)S(1)} %collect.1.refs_3_), channel_id=1, source_target_pairs={{0,1},{1,0},{2,3},{3,2},{4,5},{5,4},{6,7},{7,6},{8,9},{9,8},{10,11... | collective-permute-start | bytes 1277960 | tf_op jit(solution)/shard_map/ppermute | solution.py:18
  231.8 26.8 %all-to-all-start.5 = ((bf16[32,16,1536]{2,1,0:T(8,128)(2,1)}), bf16[32,16,1536]{2,1,0:T(8,128)(2,1)}, u32[]{:S(2)}, u32[]{:S(2)}) async-start(bf16[32,16,1536]{2,1,0:T(8,128)(2,1)} %bitcast.122), calls=%async_computation.5 | async-start | bytes 3145728 | tf_op jit(solution)/shard_map/all_to_all | solution.py:26
  250.4 8.2 %collective-permute-start.26 = (bf16[128,1536]{1,0:T(8,128)(2,1)S(1)}, bf16[128,1536]{1,0:T(8,128)(2,1)S(1)}, u32[]{:S(2)}, u32[]{:S(2)}) collective-permute-start(bf16[128,1536]{1,0:T(8,128)(2,1)S(1)} %get-tuple-element.146.a_ref), channel_id=1, source_target_pairs={{0,1},{1,0},{2,3},{3,2},{4,5},{5,4},{6,7},{7,6},{8,9},{9,8},{10,11... | collective-permute-start | bytes 1179656 | tf_op jit(solution)/shard_map/ppermute | solution.py:18
  263.4 27.3 %all-to-all-start.6 = ((bf16[32,16,1536]{2,1,0:T(8,128)(2,1)}), bf16[32,16,1536]{2,1,0:T(8,128)(2,1)}, u32[]{:S(2)}, u32[]{:S(2)}) async-start(bf16[32,16,1536]{2,1,0:T(8,128)(2,1)} %bitcast.125), calls=%async_computation.6 | async-start | bytes 3145728 | tf_op jit(solution)/shard_map/all_to_all | solution.py:26
  270.3 63.9 %collective-permute-start.29 = (bf16[1536,1152]{1,0:T(8,128)(2,1)}, bf16[1536,1152]{1,0:T(8,128)(2,1)}, u32[]{:S(2)}, u32[]{:S(2)}) collective-permute-start(bf16[1536,1152]{1,0:T(8,128)(2,1)} %fusion), channel_id=1, source_target_pairs={{64,65},{65,64},{66,67},{67,66},{68,69},{69,68},{70,71},{71,70},{7... | collective-permute-start | bytes 10616840 | tf_op jit(solution)/shard_map/ppermute | solution.py:980
  303.4 20.6 %collective-permute-start.30 = (bf16[768,1920]{1,0:T(8,128)(2,1)}, bf16[768,1920]{1,0:T(8,128)(2,1)}, u32[]{:S(2)}, u32[]{:S(2)}) collective-permute-start(bf16[768,1920]{1,0:T(8,128)(2,1)} %get-tuple-element.162), channel_id=1, source_target_pairs={{0,64},{64,0},{1,65},{65,1},{2,66},{66,2},{3,67},{67,3},{4,68},{68... | collective-permute-start | bytes 8847368 | tf_op jit(solution)/shard_map/ppermute | solution.py:18
  303.4 30.8 %all-to-all-start.7 = ((bf16[32,16,1536]{2,1,0:T(8,128)(2,1)}), bf16[32,16,1536]{2,1,0:T(8,128)(2,1)}, u32[]{:S(2)}, u32[]{:S(2)}) async-start(bf16[32,16,1536]{2,1,0:T(8,128)(2,1)} %bitcast.123), calls=%async_computation.7 | async-start | bytes 3145728 | tf_op jit(solution)/shard_map/all_to_all | solution.py:26
  308.3 75.0 %reduce-scatter.3.cloned.1.call-start = ((), (), s32[]{:S(2)}) async-start(), calls=%async_computation.14 | async-start | bytes 3686400 | tf_op jit(solution)/shard_map/reduce_scatter | solution.py:919
  311.0 17.3 %collective-permute-start.28 = (bf16[128,1536]{1,0:T(8,128)(2,1)}, bf16[128,1536]{1,0:T(8,128)(2,1)S(1)}, u32[]{:S(2)}, u32[]{:S(2)}) collective-permute-start(bf16[128,1536]{1,0:T(8,128)(2,1)} %convolution_convert_fusion.1), channel_id=1, source_target_pairs={{0,1},{1,0},{2,3},{3,2},{4,5},{5,4},{6,7},{7,6},{8,9},{9,8},{10,11... | collective-permute-start | bytes 1179656 | tf_op jit(solution)/shard_map/ppermute | solution.py:18
  311.0 17.3 %collective-permute-start.31 = (f32[32,128]{1,0:T(8,128)S(1)}, f32[32,128]{1,0:T(8,128)S(1)}, u32[]{:S(2)}, u32[]{:S(2)}) collective-permute-start(f32[32,128]{1,0:T(8,128)S(1)} %get-tuple-element.163.refs_6_), channel_id=1, source_target_pairs={{0,1},{1,0},{2,3},{3,2},{4,5},{5,4},{6,7},{7,6},{8,9},{9,8},{10,11... | collective-permute-start | bytes 49160 | tf_op jit(solution)/shard_map/ppermute | solution.py:18
  336.1 33.0 %collective-permute-start.35 = (bf16[2,1536,1152]{2,1,0:T(8,128)(2,1)}, bf16[2,1536,1152]{2,1,0:T(8,128)(2,1)}, u32[]{:S(2)}, u32[]{:S(2)}) collective-permute-start(bf16[2,1536,1152]{2,1,0:T(8,128)(2,1)} %experts_grads.3.refs_0_), channel_id=1, source_target_pairs={{64,0},{65,1},{66,2},{67,3},{68,4},{69,5},{70,6},{71,7},{72,8},{73... | collective-permute-start | bytes 21233672 | tf_op jit(solution)/shard_map/ppermute | solution.py:976
  337.5 8.9 %collective-permute-start.32 = (bf16[128,1536]{1,0:T(8,128)(2,1)S(1)}, bf16[128,1536]{1,0:T(8,128)(2,1)S(1)}, u32[]{:S(2)}, u32[]{:S(2)}) collective-permute-start(bf16[128,1536]{1,0:T(8,128)(2,1)S(1)} %convolution_convert_fusion.refs_3_), channel_id=1, source_target_pairs={{0,1},{1,0},{2,3},{3,2},{4,5},{5,4},{6,7},{7,6},{8,9},{9,8},{10,11... | collective-permute-start | bytes 1179656 | tf_op jit(solution)/shard_map/ppermute | solution.py:18
  366.3 9.8 %collective-permute-start.36 = (bf16[768,1920]{1,0:T(8,128)(2,1)}, bf16[768,1920]{1,0:T(8,128)(2,1)S(1)}, u32[]{:S(2)}, u32[]{:S(2)}) collective-permute-start(bf16[768,1920]{1,0:T(8,128)(2,1)} %get-tuple-element.178), channel_id=1, source_target_pairs={{0,64},{64,0},{1,65},{65,1},{2,66},{66,2},{3,67},{67,3},{4,68},{68... | collective-permute-start | bytes 8847368 | tf_op jit(solution)/shard_map/ppermute | solution.py:18
  378.4 28.7 %all-to-all-start.8 = ((bf16[4,192,1920]{2,1,0:T(8,128)(2,1)}), bf16[4,192,1920]{2,1,0:T(8,128)(2,1)}, u32[]{:S(2)}, u32[]{:S(2)}) async-start(bf16[4,192,1920]{2,1,0:T(8,128)(2,1)} %bitcast.110), calls=%async_computation.8 | async-start | bytes 5898240 | tf_op jit(solution)/shard_map/all_to_all | solution.py:886
  383.2 26.5 %reduce-scatter.5.cloned.1.call-start = ((), (), s32[]{:S(2)}) async-start(), calls=%async_computation.15 | async-start | bytes 921600 | tf_op jit(solution)/shard_map/reduce_scatter | solution.py:919
  383.9 96.2 %all-gather.2.cloned.1.call-start = ((), (), s32[]{:S(2)}) async-start(), calls=%async_computation.16 | async-start | bytes 3133440 | tf_op jit(solution)/shard_map/all_gather | solution.py:913
  386.5 11.5 %collective-permute-start.37 = (bf16[128,1536]{1,0:T(8,128)(2,1)S(1)}, bf16[128,1536]{1,0:T(8,128)(2,1)S(1)}, u32[]{:S(2)}, u32[]{:S(2)}) collective-permute-start(bf16[128,1536]{1,0:T(8,128)(2,1)S(1)} %get-tuple-element.179), channel_id=1, source_target_pairs={{0,1},{1,0},{2,3},{3,2},{4,5},{5,4},{6,7},{7,6},{8,9},{9,8},{10,11... | collective-permute-start | bytes 1179656 | tf_op jit(solution)/shard_map/ppermute | solution.py:18
  447.8 31.0 %collective-permute-start.39 = (bf16[1024,1152]{1,0:T(8,128)(2,1)}, bf16[1024,1152]{1,0:T(8,128)(2,1)}, u32[]{:S(2)}, u32[]{:S(2)}) collective-permute-start(bf16[1024,1152]{1,0:T(8,128)(2,1)} %fusion.1), channel_id=1, source_target_pairs={{0,1},{1,0},{2,3},{3,2},{4,5},{5,4},{6,7},{7,6},{8,9},{9,8},{10,11... | collective-permute-start | bytes 7077896 | tf_op jit(solution)/shard_map/ppermute | solution.py:980
  452.9 25.9 %all-to-all-start.11 = ((bf16[4,192,1920]{2,1,0:T(8,128)(2,1)}), bf16[4,192,1920]{2,1,0:T(8,128)(2,1)}, u32[]{:S(2)}, u32[]{:S(2)}) async-start(bf16[4,192,1920]{2,1,0:T(8,128)(2,1)} %broadcast_in_dim.42), calls=%async_computation.11 | async-start | bytes 5898240 | tf_op jit(solution)/shard_map/all_to_all | solution.py:886
  461.4 17.5 %collective-permute-start.38 = (f32[128,1536]{1,0:T(8,128)}, f32[128,1536]{1,0:T(8,128)S(1)}, u32[]{:S(2)}, u32[]{:S(2)}) collective-permute-start(f32[128,1536]{1,0:T(8,128)} %get-tuple-element.203), channel_id=1, source_target_pairs={{0,64},{64,0},{1,65},{65,1},{2,66},{66,2},{3,67},{67,3},{4,68},{68... | collective-permute-start | bytes 2359304 | tf_op jit(solution)/shard_map/ppermute | solution.py:18
  478.9 13.3 %collective-permute-start.40 = (bf16[768,1920]{1,0:T(8,128)(2,1)}, bf16[768,1920]{1,0:T(8,128)(2,1)}, u32[]{:S(2)}, u32[]{:S(2)}) collective-permute-start(bf16[768,1920]{1,0:T(8,128)(2,1)} %bitcast.45.refs_0_), channel_id=1, source_target_pairs={{64,0},{65,1},{66,2},{67,3},{68,4},{69,5},{70,6},{71,7},{72,8},{73... | collective-permute-start | bytes 8847368 | tf_op jit(solution)/shard_map/ppermute | solution.py:976
  480.2 12.0 %collective-permute-start.42 = (bf16[768,1920]{1,0:T(8,128)(2,1)}, bf16[768,1920]{1,0:T(8,128)(2,1)S(1)}, u32[]{:S(2)}, u32[]{:S(2)}) collective-permute-start(bf16[768,1920]{1,0:T(8,128)(2,1)} %all-gather.2.cloned.1.call-done.refs_2_), channel_id=1, source_target_pairs={{0,64},{1,65},{2,66},{3,67},{4,68},{5,69},{6,70},{7,71},{8,72},{9,... | collective-permute-start | bytes 8847368 | tf_op jit(solution)/shard_map/ppermute | solution.py:976
  485.0 18.3 %collective-permute-start.43 = (bf16[512,1152]{1,0:T(8,128)(2,1)}, bf16[512,1152]{1,0:T(8,128)(2,1)S(1)}, u32[]{:S(2)}, u32[]{:S(2)}) collective-permute-start(bf16[512,1152]{1,0:T(8,128)(2,1)} %fusion.2), channel_id=1, source_target_pairs={{0,1},{1,0},{2,3},{3,2},{4,5},{5,4},{6,7},{7,6},{8,9},{9,8},{10,11... | collective-permute-start | bytes 3538952 | tf_op jit(solution)/shard_map/ppermute | solution.py:980
  (95 other events, 897.1 us)
Sparse Core Ops, SparseCore 0:
  337.6 26.1 reduce-scatter.2
  386.6 22.0 reduce-scatter.4
  418.8 46.8 all-gather.1

commit v4 on v3

--- a/solution.py
+++ b/solution.py
@@ -69,15 +69,17 @@
 VMEM = pl.BlockSpec(memory_space=pltpu.VMEM)
 SMEM = pl.BlockSpec(memory_space=pltpu.SMEM)
 ANY = pl.BlockSpec(memory_space=pl.ANY)
-
-
-def call(body, outs, in_specs, scratch, operands, name, spaces=None):
+HBM = pl.BlockSpec(memory_space=pltpu.HBM)
+
+
+def call(body, outs, in_specs, scratch, operands, name, spaces=None, aliases=None):
     return pl.pallas_call(
         body,
         out_shape=[jax.ShapeDtypeStruct(shape, kind) for shape, kind in outs],
         in_specs=in_specs,
         out_specs=spaces or [VMEM] * len(outs),
         scratch_shapes=scratch,
+        input_output_aliases=aliases or {},
         compiler_params=pltpu.CompilerParams(vmem_limit_bytes=VMEM_LIMIT),
         cost_estimate=pl.CostEstimate(flops=1024, bytes_accessed=1024, transcendentals=0),
         name=name,
@@ -337,13 +339,11 @@
     )[0]
 
 
-def turn_over(grad, x, own, received, gain, table, gated, back, experts):
-    slots, count = table.shape
-    lanes = slots // experts
+def turn_over(grad, x, own, received, gain, gated):
+    slots, count = gated.shape
     model = x.shape[1]
 
-    def body(g_ref, x_ref, a_ref, b_ref, gain_ref, table_ref, gated_ref, back_ref, *outs):
-        grad_o, low_o, rows_o, seen_o = outs
+    def body(g_ref, x_ref, a_ref, b_ref, gain_ref, gated_ref, grad_o, low_o, rows_o):
         x_v = x_ref[...].astype(F32)
         da = a_ref[...].astype(F32) + b_ref[...].astype(F32)
         total = g_ref[...] + norm_back(x_v, row_scale_of(x_v), gain_ref[...], da)
@@ -351,23 +351,43 @@
         low = total.astype(BF16)
         low_o[...] = low
         rows_o[...] = mul_nn(gated_ref[...], low).astype(BF16)
-        seen = mul_nt(back_ref[...], low) * table_ref[...].astype(F32)
+
+    return call(
+        body,
+        [((count, model), F32), ((count, model), BF16), ((slots, model), BF16)],
+        [VMEM] * 6,
+        [],
+        (grad, x, own, received, gain, gated),
+        "turn_over",
+    )
+
+
+def gates_seen(back, low, table, experts):
+    slots, count = table.shape
+    lanes = slots // experts
+
+    def body(back_ref, low_ref, table_ref, seen_o):
+        seen = mul_nt(back_ref[...], low_ref[...]) * table_ref[...].astype(F32)
         for e in range(experts):
             spot = slice(e * lanes, (e + 1) * lanes)
             seen_o[e : e + 1, :] = jnp.sum(seen[spot, :], axis=0, keepdims=True)
 
     return call(
-        body,
-        [
-            ((count, model), F32),
-            ((count, model), BF16),
-            ((slots, model), BF16),
-            ((experts, count), F32),
-        ],
-        [VMEM] * 8,
-        [],
-        (grad, x, own, received, gain, table, gated, back),
-        "turn_over",
+        body, [((experts, count), F32)], [VMEM] * 3, [], (back, low, table), "gates_seen"
+    )[0]
+
+
+def expert_sources(refs, half):
+    if len(refs) == 12:
+        return refs
+    far, far_r = refs[6], refs[8]
+    columns = (slice(0, half), slice(half, 2 * half))
+    return (
+        *refs[:6],
+        *[far.at[:, spot] for spot in columns],
+        refs[7],
+        *[far_r.at[:, spot] for spot in columns],
+        refs[9],
     )
 
 
@@ -443,7 +463,7 @@
     tile = 256
 
     def body(own_ref, x_ref, g_ref, *refs):
-        sources, refs = refs[:12], refs[12:]
+        sources, refs = expert_sources(refs[: len(weights)], half), refs[len(weights) :]
         dx_o, h_o, dgu_o, x_s, g_s, h_s, dgu_s, wgu, wd, sems = refs[:10]
         moves = expert_moves(sources, wgu, wd, half)
         arrivals = [
@@ -512,7 +532,7 @@
     return call(
         body,
         [((slots, wide), BF16), ((slots, hidden), BF16), ((slots, 2 * hidden), BF16)],
-        [SMEM] + [ANY] * 14,
+        [SMEM] + [ANY] * (2 + len(weights)),
         [
             pltpu.VMEM((slots, wide), BF16),
             pltpu.VMEM((slots, model), BF16),
@@ -537,9 +557,19 @@
     gated = wide > model
     tile = 256
 
-    def body(own_ref, x_ref, g_ref, h_ref, dgu_ref, *refs):
+    def body(own_ref, x_in, g_in, h_in, dgu_in, *refs):
         sources, refs = refs[:4], refs[4:]
         both_o, refs = refs[0], refs[1:]
+        x_ref, g_ref, h_ref, dgu_ref, load = refs[-5:]
+        refs = refs[:-5]
+        loads = [
+            pltpu.make_async_copy(a, b, load.at[i])
+            for i, (a, b) in enumerate(
+                ((x_in, x_ref), (dgu_in, dgu_ref), (g_in, g_ref), (h_in, h_ref))
+            )
+        ]
+        for copy in loads:
+            copy.start()
         if gated:
             y_o, xt_s, dy_s, wd, sems = refs
             moves = [
@@ -548,14 +578,18 @@
             ]
             for i, (a, b, target) in enumerate(moves):
                 fetch(own_ref[0], a, b, target, sems.at[i])
+            loads[0].wait()
             scale = x_ref[:, model:].astype(F32)
             scale = scale[:, 0:1] + scale[:, 1:2]
-            dy_s[...] = (g_ref[...].astype(F32) * scale).astype(BF16)
         else:
             (xt_s,), dy_s = refs, g_ref
+            loads[0].wait()
         for i in range(model // tile):
             xt_s[i * tile : (i + 1) * tile, :] = x_ref[:, i * tile : (i + 1) * tile].T
+        for copy in loads[1:]:
+            copy.wait()
         if gated:
+            dy_s[...] = (g_ref[...].astype(F32) * scale).astype(BF16)
             for i, (a, b, target) in enumerate(moves):
                 arrive(a, target, sems.at[i])
 
@@ -589,12 +623,19 @@
             pltpu.VMEM((hidden, model), BF16),
             pltpu.SemaphoreType.DMA((2,)),
         ]
+    scratch += [
+        pltpu.VMEM((slots, wide), BF16),
+        pltpu.VMEM((slots, model), BF16),
+        pltpu.VMEM((slots, hidden), BF16),
+        pltpu.VMEM((slots, 2 * hidden), BF16),
+        pltpu.SemaphoreType.DMA((4,)),
+    ]
     return call(
         body,
         outs,
-        [SMEM] + [VMEM] * 4 + [ANY] * 4,
+        [SMEM] + [ANY] * 8,
         scratch,
-        (own, rows, grads, hidden_rows, dgu, *[weights[i] for i in (2, 5, 8, 11)]),
+        (own, rows, grads, hidden_rows, dgu, *[weights[i] for i in (2, 5, -(len(weights) // 6) - 2, -1)]),
         "experts_grads",
     )
 
@@ -771,94 +812,130 @@
     )
 
 
-def ff_total(core, zero, one):
+def move_all(pairs, sems, first):
+    copies = [pltpu.make_async_copy(a, b, sems.at[first + i]) for i, (a, b) in enumerate(pairs)]
+    for copy in copies:
+        copy.start()
+    return copies
+
+
+def ff_total(core, which, zero, one, done):
     _, model, wide = zero[0].shape
     half = wide // 3
-    blocks = model // half
-
-    def parts(refs):
-        return [refs[0].at[0], refs[1].at[0], *refs[2:]]
+    rows = model // 2
+    low = which * rows
+    pieces = rows // half
+
+    given = len(zero) + len(one)
 
     def body(core_ref, *refs):
-        first, second = parts(refs[: len(zero)]), parts(refs[len(zero) : len(zero) + len(one)])
-        outs, (held, sems) = refs[-5:-2], refs[-2:]
-
-        def moves(sources):
-            targets, low = [held.at[0], held.at[1]], 0
-            for ref in sources[2:]:
-                targets.append(held.at[2, low : low + ref.shape[0]])
-                low += ref.shape[0]
-            pairs = enumerate(zip(sources, targets))
-            return [pltpu.make_async_copy(a, b, sems.at[i]) for i, (a, b) in pairs]
-
-        for number, sources in ((0, first), (1, second)):
+        ins = (refs[: len(zero)], refs[len(zero) : given])
+        outs = refs[given + len(done) : given + len(done) + 3]
+        held, gate_s, up_s, down_s, sems = refs[given + len(done) + 3 :]
+        spot = slice(low, low + rows)
+        for number in range(2):
+            near, near_r = ins[number][:2]
+            pairs = [(near.at[0, spot], held.at[0]), (near_r.at[0, spot], held.at[1])]
+            start = 0
+            for z in ins[number][2:]:
+                stop = start + z.shape[0]
+                a, b = max(start, low), min(stop, low + rows)
+                if a < b:
+                    pairs.append((z.at[a - start : b - start], held.at[2, a - low : b - low]))
+                start = stop
 
             @pl.when(core_ref[0] == number)
-            def _(sources=sources):
-                for copy in moves(sources):
-                    copy.start()
-                for copy in moves(sources):
+            def _(pairs=pairs):
+                for copy in move_all(pairs, sems, 0):
                     copy.wait()
 
-        def total(rows, columns):
+        def total(at, columns):
             return (
-                held[0, rows, columns].astype(F32)
-                + held[1, rows, columns].astype(F32)
-                + held[2, rows, columns].astype(F32)
+                held[0, at, columns].astype(F32)
+                + held[1, at, columns].astype(F32)
+                + held[2, at, columns].astype(F32)
             )
 
-        for i in range(blocks):
-            spot = slice(i * half, (i + 1) * half)
-            outs[0][spot, :] = total(spot, slice(0, half))
-            outs[1][spot, :] = total(spot, slice(half, 2 * half))
-            outs[2][:, spot] = total(spot, slice(2 * half, wide))
+        gate_s[...] = total(slice(0, rows), slice(0, half))
+        up_s[...] = total(slice(0, rows), slice(half, 2 * half))
+        for i in range(pieces):
+            at = slice(i * half, (i + 1) * half)
+            down_s[:, at] = total(at, slice(2 * half, wide))
+        pairs = (
+            (gate_s, outs[0].at[spot]),
+            (up_s, outs[1].at[spot]),
+            (down_s, outs[2].at[:, spot]),
+        )
+        for copy in move_all(pairs, sems, 4):
+            copy.wait()
 
     return call(
         body,
         [((model, half), F32), ((model, half), F32), ((half, model), F32)],
-        [SMEM] + [ANY] * (len(zero) + len(one)),
-        [pltpu.VMEM((3, model, wide), BF16), pltpu.SemaphoreType.DMA((4,))],
-        (core, *zero, *one),
+        [SMEM] + [HBM] * (given + len(done)),
+        [
+            pltpu.VMEM((3, rows, wide), BF16),
+            pltpu.VMEM((rows, half), F32),
+            pltpu.VMEM((rows, half), F32),
+            pltpu.VMEM((half, rows), F32),
+            pltpu.SemaphoreType.DMA((7,)),
+        ],
+        (core, *zero, *one, *done),
         "ff_total",
-    )
-
-
-def attn_total(core, zero, one, width, model, experts):
-    rows, wide = zero[0].shape
+        [HBM] * 3,
+        {1 + given + i: i for i in range(len(done))},
+    )
+
+
+def attn_total(core, which, zero, one, done, width, model, experts):
+    rows, wide = zero.shape
     out_at = width + 2 * HEAD
     side_at = out_at + model // 2
-
-    def body(core_ref, *refs):
-        ins, outs, (held, sems) = refs[:4], refs[4:11], refs[11:]
-        fetch(core_ref[0], ins[3], ins[1], held.at[1], sems.at[1])
+    mixed = which == 0
+
+    def body(core_ref, zero_ref, one_ref, *refs):
+        outs = refs[len(done) : len(done) + 7]
+        held, query, key, value, out, router, gains, sems = refs[len(done) + 7 :]
         piece = rows // 16
 
         @pl.when(core_ref[0] == 1)
         def _():
-            for y in range(4):
-                for x in range(4):
-                    source = ins[2].at[(y * 4 + x) * piece : (y * 4 + x + 1) * piece]
-                    target = held.at[0, (x * 4 + y) * piece : (x * 4 + y + 1) * piece]
-                    pltpu.make_async_copy(source, target, sems.at[0]).start()
+            if mixed:
+                for y in range(4):
+                    for x in range(4):
+                        source = one_ref.at[(y * 4 + x) * piece : (y * 4 + x + 1) * piece]
+                        target = held.at[(x * 4 + y) * piece : (x * 4 + y + 1) * piece]
+                        pltpu.make_async_copy(source, target, sems.at[0]).start()
+            else:
+                pltpu.make_async_copy(one_ref, held, sems.at[0]).start()
 
         @pl.when(core_ref[0] != 1)
         def _():
-            pltpu.make_async_copy(ins[0], held.at[0], sems.at[0]).start()
-
-        query, key, value, out, router, attn, moe = outs
-        for i in range(2):
-            arrive(ins[i], held.at[i], sems.at[i])
-            spot = slice(i * rows, (i + 1) * rows)
-            query[spot, :] = held[i, :, :width].astype(F32)
-            key[spot, :] = held[i, :, width : width + HEAD].astype(F32)
-            value[spot, :] = held[i, :, width + HEAD : out_at].astype(F32)
-            out[:, i * (model // 2) : (i + 1) * (model // 2)] = held[i, :, out_at:side_at].astype(F32)
-            for j in range(0, rows, HEAD):
-                side = held[i, j : j + HEAD, side_at:].astype(F32).T
-                at = slice(i * rows + j, i * rows + j + HEAD)
-                router[:, at] = side[:experts, :]
-                attn[:, at] = side[experts : experts + 1, :]
-                moe[:, at] = side[experts + 1 : experts + 2, :]
+            pltpu.make_async_copy(zero_ref, held, sems.at[0]).start()
+
+        pltpu.make_async_copy(zero_ref, held, sems.at[0]).wait()
+        spot = slice(which * rows, (which + 1) * rows)
+        query[...] = held[:, :width].astype(F32)
+        copies = move_all([(query, outs[0].at[spot])], sems, 1)
+        out[...] = held[:, out_at:side_at].astype(F32)
+        copies += move_all([(out, outs[3].at[:, spot])], sems, 2)
+        key[...] = held[:, width : width + HEAD].astype(F32)
+        value[...] = held[:, width + HEAD : out_at].astype(F32)
+        for j in range(0, rows, HEAD):
+            side = held[j : j + HEAD, side_at:].astype(F32).T
+            at = slice(j, j + HEAD)
+            router[:, at] = side[:experts, :]
+            gains[:, at] = side[experts : experts + 8, :]
+        pairs = (
+            (key, outs[1].at[spot]),
+            (value, outs[2].at[spot]),
+            (router, outs[4].at[:, spot]),
+            (gains.at[0:1], outs[5].at[:, spot]),
+            (gains.at[1:2], outs[6].at[:, spot]),
+        )
+        copies += move_all(pairs, sems, 3)
+        for copy in copies:
+            copy.wait()
 
     return call(
         body,
@@ -871,10 +948,21 @@
             ((1, model), F32),
             ((1, model), F32),
         ],
-        [SMEM] + [ANY] * 4,
-        [pltpu.VMEM((2, rows, wide), BF16), pltpu.SemaphoreType.DMA((2,))],
-        (core, *zero, *one),
+        [SMEM] + [HBM] * (2 + len(done)),
+        [
+            pltpu.VMEM((rows, wide), BF16),
+            pltpu.VMEM((rows, width), F32),
+            pltpu.VMEM((rows, HEAD), F32),
+            pltpu.VMEM((rows, HEAD), F32),
+            pltpu.VMEM((width, model // 2), F32),
+            pltpu.VMEM((experts, rows), F32),
+            pltpu.VMEM((8, rows), F32),
+            pltpu.SemaphoreType.DMA((8,)),
+        ],
+        (core, zero, one, *done),
         "attn_total",
+        [HBM] * 7,
+        {3 + i: i for i in range(len(done))},
     )
 
 
@@ -1002,7 +1090,8 @@
     near_r = [swap(after(w, branch_r), "pipe") for w in near]
     far_0r = [over(w, 1) for w in far_0]
     rows_0 = after(rows_0, *near_r, *far_0r)
-    far_1 = [across(after(w, rows_0), 1) for w in near[:2]]
+    pair = jnp.concatenate(near[:2], axis=1)
+    far_1 = [across(after(pair, rows_0), 1)]
     ff_0 = (*near, *near_r, *far_0, *far_0r)
     back_0 = exchange_rows(experts_forward(owns[0], rows_0, ff_0), experts)
     share = after(mul_tn(gated_0, back_0).astype(BF16), *far_1)
@@ -1015,7 +1104,7 @@
     )
     branch_r = swap(branch, "tensor")
     far_1 += [across(after(near[2], branch_r), 1)]
-    far_1r += [over(far_1[2], 0)]
+    far_1r += [over(far_1[1], 0)]
     h_1, rows, gated_1, gates_1 = dispatch(
         table_1, picks[1], x_1, branch, branch_r, moe_gains[1], routers[1], lanes, True
     )
@@ -1036,9 +1125,8 @@
     da_r = swap(after(da, both_1r), "tensor")
     far_sum = both_1[1] + both_1r[1]
     gains_r = swap(gains, "tensor")
-    grad_1, grad, rows, seen = turn_over(
-        grad_h, x_1, da, after(da_r, back_1, far_sum, gains_r), attn_gains[1], table_0, gated_0, back_0,
-        experts,
+    grad_1, grad, rows = turn_over(
+        grad_h, x_1, da, after(da_r, back_1, far_sum, gains_r), attn_gains[1], gated_0
     )
 
     grad_rows = exchange_rows(rows, experts)
@@ -1048,8 +1136,9 @@
         owns[1], x_1, h_1, grad_h, kept_1[2], dqkv, dlogits, gains, gains_r,
         attn_gains[1], moe_gains[1],
     )
+    seen = gates_seen(back_0, after(grad, rows), table_0, experts)
     seen_r = swap(seen, "tensor")
-    grad_rows = after(grad_rows, keep)
+    grad_rows = after(grad_rows, keep, seen)
     dx, made, dgu = experts_backward(owns[0], rows_0, grad_rows, ff_0)
     half_1 = keep + swap(after(give, dx), "pipe")
     level_1 = background_sum(half_1, 0)
@@ -1087,14 +1176,21 @@
     x_f = x_0.astype(F32)
     grad_0 = grad_h + norm_back(x_f, row_scale_of(x_f), attn_gains[0], da)
     got_g, input_grads = by_layer(grad_0, grad_1)
-    ff_grads_0 = (both_0, both_0r, *far_z)
     sum_0 = after(plane_copy(part, 0), far_z[0])
     core_v = core.astype(jnp.int32).reshape(1)
-    over_0, over_1 = over(after(sum_0, got_g), 0), over(sum_1, 1)
-    query_g, key_g, value_g, out_g, router_g, attn_g, moe_g = attn_total(
-        core_v, (sum_0, over_0), (sum_1, over_1), width, model, experts
-    )
-    gate_g, up_g, down_g = ff_total(after(core_v, moe_g), ff_grads_0, ff_grads_1)
+    over_0 = over(after(sum_0, got_g), 0)
+    sizes = (width, model, experts)
+    attn_g = attn_total(core_v, 0, sum_0, sum_1, (), *sizes)
+    over_1 = over(after(sum_1, far_z[1], attn_g[0]), 1)
+    ff_g = ff_total(
+        after(core_v, attn_g[0]), 0, (both_0, both_0r, far_z[0]), ff_grads_1, ()
+    )
+    over_0, over_1 = after(over_0, ff_g[0]), after(over_1, ff_g[0])
+    attn_g = attn_total(core_v, 1, over_0, over_1, attn_g, *sizes)
+    query_g, key_g, value_g, out_g, router_g, attn_g, moe_g = attn_g
+    gate_g, up_g, down_g = ff_total(
+        after(core_v, moe_g), 1, (both_0, both_0r, *far_z), ff_grads_1, ff_g
+    )
     return (
         layer_out[None],
         input_grads[None],

time: 528 us -> 525 us (level)
  starting transfers between devices: 125 us -> 117 us
    ppermute x10 -> x9, starting transfers between devices: 28.4 us -> 18.9 us  [over(): return lax.ppermute(value, 'pipe', [(1 - layer, layer)])]
    all_to_all x8, waiting for transfers between devices: 58.1 us -> 65.8 us  [expert_exchange(): lax.all_to_all(value, ('expert', 'tensor'), split_axis=0, concat_axis=0,...]
    ppermute x10 -> x9, waiting for transfers between devices: 10.2 us -> 4.53 us  [over(): return lax.ppermute(value, 'pipe', [(1 - layer, layer)])]
    ppermute x9 -> x8, waiting for transfers between devices: 12.2 us -> 16.6 us  [across(): return lax.ppermute(value, ('pipe', 'tensor'), pairs)]
    pallas_call x18 -> x21, Pallas kernels: 126 us -> 129 us  [call(): pl.pallas_call(body, out_shape=[jax.ShapeDtypeStruct(shape, kind) for sha...]
    ppermute x9 -> x8, starting transfers between devices: 22.7 us -> 22 us  [across(): return lax.ppermute(value, ('pipe', 'tensor'), pairs)]
  transfers between devices with their start and end apart: 57 -> 55, of which waited for: 25 -> 22; matrix products, arithmetic and copies ran while one was open for 8% -> 9% of each run, Pallas kernels for 18% -> 20%
where the time goes in v4:
time: 525 us; the launch traced here: 515 us
  waiting for transfers between devices  163 us (31%)
  Pallas kernels  129 us (25%)
  starting transfers between devices  117 us (22%)
  other arithmetic  37.6 us (7%)
  blocking collectives  29 us (6%)
  local copies, waits for them, and re-layouts  17.9 us (3%)
  between operations  15.6 us (3%)
  matrix products  6.32 us (1%)
    pallas_call x21, Pallas kernels, call(): pl.pallas_call(body, out_shape=[jax.ShapeDtypeStruct(shape, kind) for sha...  129 us
    all_to_all x8, waiting for transfers between devices, expert_exchange(): lax.all_to_all(value, ('expert', 'tensor'), split_axis=0, concat_axis=0,...  65.8 us
    all_to_all x8, starting transfers between devices, expert_exchange(): lax.all_to_all(value, ('expert', 'tensor'), split_axis=0, concat_axis=0,...  53.4 us
    ppermute x24, waiting for transfers between devices, swap(): return lax.ppermute(value, axis, SWAP)  44.6 us
    all_to_all x2, blocking collectives, plane_exchange(): lax.all_to_all(value, ('pipe', 'expert'), split_axis=0, concat_axis=0, ax...  29 us
    all_to_all x2, waiting for transfers between devices, plane_exchange(): lax.all_to_all(value, ('pipe', 'expert'), split_axis=0, concat_axis=0, ax...  23.5 us
    ppermute x8, starting transfers between devices, across(): return lax.ppermute(value, ('pipe', 'tensor'), pairs)  22 us
    ppermute x9, starting transfers between devices, over(): return lax.ppermute(value, 'pipe', [(1 - layer, layer)])  18.9 us
  transfers between devices with their start and end apart: 55, of which 22 were waited for; matrix products, arithmetic and copies ran while one was open for 9% of the time, Pallas kernels for 20%

profile of v4, /device:TPU:0, one launch (start us, length us, event | category | flops | bytes accessed | tf_op | source)
XLA Modules:
  0.0 515.2 jit_solution(15885206270581941524)
XLA Ops:
  10.6 3.9 collective-permute-start.6
  21.2 4.8 attend_forward.2
  33.7 4.9 collective-permute-done.7.b_ref
  47.4 9.8 %all-to-all-start = ((bf16[32,16,1536]{2,1,0:T(8,128)(2,1)}), bf16[32,16,1536]{2,1,0:T(8,128)(2,1)}, u32[]{:S(2)}, u32[]{:S(2)}) async-start(bf16[32,16,1536]{2,1,0:T(8,128)(2,1)} %bitcast.129), calls=%async_computation | async-start | bytes 3145728 | tf_op jit(solution)/shard_map/all_to_all | solution.py:26
  61.3 8.4 %collective-permute-done.14.refs_8_.refs_2_ = bf16[384,1536]{1,0:T(8,128)(2,1)} collective-permute-done((bf16[384,1536]{1,0:T(8,128)(2,1)S(1)}, bf16[384,1536]{1,0:T(8,128)(2,1)}, u32[]{:S(2)}, u32[]{:S(2)}) %collective-permute-start.14) | collective-permute-done | bytes 1179680 | tf_op jit(solution)/shard_map/ppermute | solution.py:1068
  78.1 8.2 %experts_forward.1 = bf16[512,1536]{1,0:T(8,128)(2,1)} custom-call(s32[1]{0:T(128)} %bitcast.8.own_ref, bf16[512,1536]{1,0:T(8,128)(2,1)} %bitcast.17.x_ref.x_in, bf16[1536,384]{1,0:T(8,128)(2,1)S(1)} %bitcast.90, bf16[1536,384]{1,0:T(8,128)(2,1)} %bitcast.18.refs_1_, bf16[384,1536]{1,0:T(8,128)(2,1)} %bitcast.79, bf16[1536,384]{1,0:T(8,128)(2,1)} %copy-done.60, ...), custom_call_target="tpu_custom_call" | custom-call | flops 1024 | bytes 1024 | tf_op jit(solution)/shard_map/experts_forward/pallas_call | solution.py:76
  86.3 9.7 %all-to-all-start.1 = ((bf16[32,16,1536]{2,1,0:T(8,128)(2,1)}), bf16[32,16,1536]{2,1,0:T(8,128)(2,1)}, u32[]{:S(2)}, u32[]{:S(2)}) async-start(bf16[32,16,1536]{2,1,0:T(8,128)(2,1)} %bitcast.116), calls=%async_computation.1 | async-start | bytes 3145728 | tf_op jit(solution)/shard_map/all_to_all | solution.py:26
  96.0 24.2 %all-to-all-done.1 = bf16[32,16,1536]{2,1,0:T(8,128)(2,1)} async-done(((bf16[32,16,1536]{2,1,0:T(8,128)(2,1)}), bf16[32,16,1536]{2,1,0:T(8,128)(2,1)}, u32[]{:S(2)}, u32[]{:S(2)}) %all-to-all-start.1) | async-done | bytes 1572896 | tf_op jit(solution)/shard_map/all_to_all | solution.py:26
  122.2 5.3 %all-to-all-start.2 = ((bf16[32,16,1536]{2,1,0:T(8,128)(2,1)}), bf16[32,16,1536]{2,1,0:T(8,128)(2,1)}, u32[]{:S(2)}, u32[]{:S(2)}) async-start(bf16[32,16,1536]{2,1,0:T(8,128)(2,1)} %bitcast.126), calls=%async_computation.2 | async-start | bytes 3145728 | tf_op jit(solution)/shard_map/all_to_all | solution.py:26
  132.1 6.7 %attend_forward.3 = (bf16[128,1536]{1,0:T(8,128)(2,1)S(1)}, bf16[128,768]{1,0:T(8,128)(2,1)S(1)}, bf16[128,256]{1,0:T(8,128)(2,1)S(1)}, bf16[128,768]{1,0:T(8,12...) custom-call(s32[1]{0:T(128)} %bitcast.own_ref, f32[128,1536]{1,0:T(8,128)} %get-tuple-element.122.refs_0_.refs_1_.h_ref, ...), custom_call_target="tpu_custom_call" | custom-call | flops 1024 | bytes 1024 | tf_op jit(solution)/shard_map/attend_forward/pallas_call | solution.py:76
  142.3 6.6 %collective-permute-done.18.b_ref = bf16[128,1536]{1,0:T(8,128)(2,1)S(1)} collective-permute-done((bf16[128,1536]{1,0:T(8,128)(2,1)S(1)}, bf16[128,1536]{1,0:T(8,128)(2,1)S(1)}, u32[]{:S(2)}, u32[]{:S(2)}) %collective-permute-start.18) | collective-permute-done | bytes 393248 | tf_op jit(solution)/shard_map/ppermute | solution.py:18
  153.8 6.6 %all-to-all-start.3 = ((bf16[32,16,1664]{2,1,0:T(8,128)(2,1)}), bf16[32,16,1664]{2,1,0:T(8,128)(2,1)}, u32[]{:S(2)}, u32[]{:S(2)}) async-start(bf16[32,16,1664]{2,1,0:T(8,128)(2,1)} %bitcast.124), calls=%async_computation.3 | async-start | bytes 3407872 | tf_op jit(solution)/shard_map/all_to_all | solution.py:26
  161.7 4.5 collective-permute-done.21.refs_9_.refs_3_
  166.2 19.3 %all-to-all-done.3 = bf16[32,16,1664]{2,1,0:T(8,128)(2,1)} async-done(((bf16[32,16,1664]{2,1,0:T(8,128)(2,1)}), bf16[32,16,1664]{2,1,0:T(8,128)(2,1)}, u32[]{:S(2)}, u32[]{:S(2)}) %all-to-all-start.3) | async-done | bytes 1703968 | tf_op jit(solution)/shard_map/all_to_all | solution.py:26
  185.5 12.5 %experts_backward.2 = (bf16[512,1664]{1,0:T(8,128)(2,1)}, bf16[512,768]{1,0:T(8,128)(2,1)S(1)}, bf16[512,1536]{1,0:T(8,128)(2,1)}) custom-call(s32[1]{0:T(128)} %bitcast.own_ref, bf16[512,1664]{1,0:T(8,128)(2,1)} %bitcast.25.x_ref.x_in, bf16[512,1536]{1,0:T(8,128)(2,1)} %bitcast.23.g_ref.g_in, bf16[1536,384]{1,0:T(8,128)(2,1)S(1)} %bitcast.91, ...), custom_call_target="tpu_custom_call" | custom-call | flops 1024 | bytes 1024 | tf_op jit(solution)/shard_map/experts_backward/pallas_call | solution.py:76
  198.9 4.8 all-to-all-start.4
  204.9 12.2 %experts_grads.2 = (bf16[2,1536,1152]{2,1,0:T(8,128)(2,1)}, bf16[512,1536]{1,0:T(8,128)(2,1)}) custom-call(s32[1]{0:T(128)} %bitcast.own_ref, bf16[512,1664]{1,0:T(8,128)(2,1)} %bitcast.25.x_ref.x_in, bf16[512,1536]{1,0:T(8,128)(2,1)} %bitcast.23.g_ref.g_in, bf16[512,768]{1,0:T(8,128)(2,1)S(1)} %copy-done.31, bf16[512,1536]{1,0:T(8,128)(2,1)} %get-tuple-element.144.dgu_in, ...), custom_call_target="tpu_custom_call" | custom-call | flops 1024 | bytes 1024 | tf_op jit(solution)/shard_map/experts_grads/pallas_call | solution.py:76
  217.1 10.6 %all-to-all-done.4 = bf16[32,16,1664]{2,1,0:T(8,128)(2,1)} async-done(((bf16[32,16,1664]{2,1,0:T(8,128)(2,1)}), bf16[32,16,1664]{2,1,0:T(8,128)(2,1)}, u32[]{:S(2)}, u32[]{:S(2)}) %all-to-all-start.4) | async-done | bytes 1703968 | tf_op jit(solution)/shard_map/all_to_all | solution.py:26
  229.6 4.2 collective-permute-start.23
  233.8 4.8 all-to-all-start.5
  242.7 9.0 %attend_backward.2 = (bf16[128,1024]{1,0:T(8,128)(2,1)S(1)}, bf16[128,1536]{1,0:T(8,128)(2,1)S(1)}, f32[128,1536]{1,0:T(8,128)}, bf16[32,128]{1,0:T(8,128)(2,1)S(1)}, bf16[16,1536]{1,0:T(8,128)(2,1)S(1)}) custom-call(s32[1]{0:T(128)} %bitcast.own_ref, f32[128,1536]{1,0:T(8,128)} %copy-done.10, f32[128,1536]{1,0:T(8,128)} %get-tuple-element.135.refs_1_.h_ref, ...), custom_call_target="tpu_custom_call" | custom-call | flops 1024 | bytes 1024 | tf_op jit(solution)/shard_map/attend_backward/pallas_call | solution.py:76
  253.8 4.2 fusion
  263.4 7.3 %all-to-all-start.6 = ((bf16[32,16,1536]{2,1,0:T(8,128)(2,1)}), bf16[32,16,1536]{2,1,0:T(8,128)(2,1)}, u32[]{:S(2)}, u32[]{:S(2)}) async-start(bf16[32,16,1536]{2,1,0:T(8,128)(2,1)} %bitcast.130), calls=%async_computation.6 | async-start | bytes 3145728 | tf_op jit(solution)/shard_map/all_to_all | solution.py:26
  273.4 6.9 %attend_grads.2 = (bf16[768,1920]{1,0:T(8,128)(2,1)}, bf16[768,1920]{1,0:T(8,128)(2,1)}) custom-call(s32[1]{0:T(128)} %bitcast.own_ref, bf16[128,1536]{1,0:T(8,128)(2,1)S(1)} %copy-done.15, f32[128,1536]{1,0:T(8,128)S(1)} %copy-done.11, f32[128,1536]{1,0:T(8,128)} %get-tuple-element.153.g_ref.gh_ref, bf16[128,768]{1,0:T(8,128)(2,1)S(1)} %copy-done.43, ...), custom_call_target="tpu_custom_call" | custom-call | flops 1024 | bytes 1024 | tf_op jit(solution)/shard_map/attend_grads/pallas_call | solution.py:76
  282.9 5.5 %all-to-all-done.6 = bf16[32,16,1536]{2,1,0:T(8,128)(2,1)} async-done(((bf16[32,16,1536]{2,1,0:T(8,128)(2,1)}), bf16[32,16,1536]{2,1,0:T(8,128)(2,1)}, u32[]{:S(2)}, u32[]{:S(2)}) %all-to-all-start.6) | async-done | bytes 1572896 | tf_op jit(solution)/shard_map/all_to_all | solution.py:26
  288.4 11.8 %experts_backward.3 = (bf16[512,1536]{1,0:T(8,128)(2,1)}, bf16[512,768]{1,0:T(8,128)(2,1)S(1)}, bf16[512,1536]{1,0:T(8,128)(2,1)}) custom-call(s32[1]{0:T(128)} %bitcast.8.own_ref, bf16[512,1536]{1,0:T(8,128)(2,1)} %bitcast.17.x_ref.x_in, bf16[512,1536]{1,0:T(8,128)(2,1)} %bitcast.32.g_ref.g_in, bf16[1536,384]{1,0:T(8,128)(2,1)S(1)} %bitcast.92, ...), custom_call_target="tpu_custom_call" | custom-call | flops 1024 | bytes 1024 | tf_op jit(solution)/shard_map/experts_backward/pallas_call | solution.py:76
  301.1 4.8 all-to-all-start.7
  311.0 10.3 %experts_grads.3.refs_0_ = bf16[2,1536,1152]{2,1,0:T(8,128)(2,1)} custom-call(s32[1]{0:T(128)} %bitcast.8.own_ref, bf16[512,1536]{1,0:T(8,128)(2,1)} %bitcast.17.x_ref.x_in, bf16[512,1536]{1,0:T(8,128)(2,1)} %bitcast.32.g_ref.g_in, bf16[512,768]{1,0:T(8,128)(2,1)S(1)} %copy-done.29, bf16[512,1536]{1,0:T(8,128)(2,1)} %get-tuple-element.170.dgu_in, ...), custom_call_target="tpu_custom_call" | custom-call | flops 1024 | bytes 1024 | tf_op jit(solution)/shard_map/experts_grads/pallas_call | solution.py:76
  321.4 4.3 add.80
  325.6 6.3 %all-to-all-done.7 = bf16[32,16,1536]{2,1,0:T(8,128)(2,1)} async-done(((bf16[32,16,1536]{2,1,0:T(8,128)(2,1)}), bf16[32,16,1536]{2,1,0:T(8,128)(2,1)}, u32[]{:S(2)}, u32[]{:S(2)}) %all-to-all-start.7) | async-done | bytes 1572896 | tf_op jit(solution)/shard_map/all_to_all | solution.py:26
  335.4 8.8 %collective-permute-done.30.refs_4_ = bf16[128,1536]{1,0:T(8,128)(2,1)S(1)} collective-permute-done((bf16[128,1536]{1,0:T(8,128)(2,1)S(1)}, bf16[128,1536]{1,0:T(8,128)(2,1)S(1)}, u32[]{:S(2)}, u32[]{:S(2)}) %collective-permute-start.30) | collective-permute-done | bytes 393248 | tf_op jit(solution)/shard_map/ppermute | solution.py:18
  345.0 7.9 %attend_backward.3 = (bf16[128,1024]{1,0:T(8,128)(2,1)S(1)}, bf16[128,1536]{1,0:T(8,128)(2,1)S(1)}, f32[128,1536]{1,0:T(8,128)}, bf16[32,128]{1,0:T(8,128)(2,1)S(1)}, bf16[16,1536]{1,0:T(8,128)(2,1)S(1)}) custom-call(s32[1]{0:T(128)} %bitcast.8.own_ref, bf16[128,1536]{1,0:T(8,128)(2,1)S(1)} %get-tuple-element.165.low_ref.refs_0_, ...), custom_call_target="tpu_custom_call" | custom-call | flops 1024 | bytes 1024 | tf_op jit(solution)/shard_map/attend_backward/pallas_call | solution.py:76
  353.1 4.0 collective-permute-done.31.rest_1_
  357.1 7.0 %attend_grads.3 = (bf16[768,1920]{1,0:T(8,128)(2,1)}, bf16[768,1920]{1,0:T(8,128)(2,1)}) custom-call(s32[1]{0:T(128)} %bitcast.8.own_ref, bf16[128,1536]{1,0:T(8,128)(2,1)S(1)} %copy-done.7, f32[128,1536]{1,0:T(8,128)S(1)} %copy-done.9, f32[128,1536]{1,0:T(8,128)} %get-tuple-element.178.gh_ref, bf16[128,768]{1,0:T(8,128)(2,1)S(1)} %copy-done.39, ...), custom_call_target="tpu_custom_call" | custom-call | flops 1024 | bytes 1024 | tf_op jit(solution)/shard_map/attend_grads/pallas_call | solution.py:76
  369.6 4.2 fusion.1
  376.2 4.6 all-to-all-start.8
  386.4 9.3 %collective-permute-done.35 = bf16[128,1536]{1,0:T(8,128)(2,1)S(1)} collective-permute-done((bf16[128,1536]{1,0:T(8,128)(2,1)S(1)}, bf16[128,1536]{1,0:T(8,128)(2,1)S(1)}, u32[]{:S(2)}, u32[]{:S(2)}) %collective-permute-start.35) | collective-permute-done | bytes 393248 | tf_op jit(solution)/shard_map/ppermute | solution.py:18
  395.7 9.0 %all-to-all-done.8 = bf16[4,192,1920]{2,1,0:T(8,128)(2,1)} async-done(((bf16[4,192,1920]{2,1,0:T(8,128)(2,1)}), bf16[4,192,1920]{2,1,0:T(8,128)(2,1)}, u32[]{:S(2)}, u32[]{:S(2)}) %all-to-all-start.8) | async-done | bytes 2949152 | tf_op jit(solution)/shard_map/all_to_all | solution.py:974
  407.5 7.1 %collective-permute-done.39 = bf16[48,1920]{1,0:T(8,128)(2,1)S(1)} collective-permute-done((bf16[48,1920]{1,0:T(8,128)(2,1)}, bf16[48,1920]{1,0:T(8,128)(2,1)S(1)}, u32[]{:S(2)}, u32[]{:S(2)}) %collective-permute-start.39) | collective-permute-done | bytes 184352 | tf_op jit(solution)/shard_map/ppermute | solution.py:1017
  416.3 14.5 %all_to_all.60 = bf16[8,24,1920]{2,1,0:T(8,128)(2,1)S(1)} all-to-all(bf16[8,24,1920]{2,1,0:T(8,128)(2,1)S(1)} %bitcast.120), channel_id=1, replica_groups={{0,2,4,6,8,10,12,14},{64,66,80,82,96,98,112,114},{16,18,20,22,24,26,28,..., dimensions={0} | all-to-all | bytes 1474560 | tf_op jit(solution)/shard_map/all_to_all | solution.py:974
  431.0 14.4 %all_to_all.61 = bf16[8,24,1920]{2,1,0:T(8,128)(2,1)S(1)} all-to-all(bf16[8,24,1920]{2,1,0:T(8,128)(2,1)S(1)} %broadcast_in_dim.20), channel_id=1, replica_groups={{0,2,4,6,8,10,12,14},{64,66,80,82,96,98,112,114},{16,18,20,22,24,26,28,..., dimensions={0} | all-to-all | bytes 1474560 | tf_op jit(solution)/shard_map/all_to_all | solution.py:974
  450.5 4.8 all-to-all-start.11
  461.9 14.5 %all-to-all-done.11 = bf16[4,192,1920]{2,1,0:T(8,128)(2,1)} async-done(((bf16[4,192,1920]{2,1,0:T(8,128)(2,1)}), bf16[4,192,1920]{2,1,0:T(8,128)(2,1)}, u32[]{:S(2)}, u32[]{:S(2)}) %all-to-all-start.11) | async-done | bytes 2949152 | tf_op jit(solution)/shard_map/all_to_all | solution.py:974
  477.8 4.7 attn_total.2
  482.5 6.5 %collective-permute-done.40.refs_3_ = bf16[512,1152]{1,0:T(8,128)(2,1)S(1)} collective-permute-done((bf16[512,1152]{1,0:T(8,128)(2,1)}, bf16[512,1152]{1,0:T(8,128)(2,1)S(1)}, u32[]{:S(2)}, u32[]{:S(2)}) %collective-permute-start.40) | collective-permute-done | bytes 1179680 | tf_op jit(solution)/shard_map/ppermute | solution.py:1068
  493.1 4.6 ff_total.2
  499.4 4.5 attn_total.3
  503.9 4.3 ff_total.3
  (297 shorter events, 122.4 us)
Async XLA Ops:
  7.2 13.1 %collective-permute-start.2 = (bf16[1536,768]{1,0:T(8,128)(2,1)}, bf16[1536,768]{1,0:T(8,128)(2,1)}, u32[]{:S(2)}, u32[]{:S(2)}) collective-permute-start(bf16[1536,768]{1,0:T(8,128)(2,1)} %bitcast.100), channel_id=1, source_target_pairs={{0,64},{64,0},{1,65},{65,1},{2,66},{66,2},{3,67},{67,3},{4,68},{68... | collective-permute-start | bytes 7077896 | tf_op jit(solution)/shard_map/ppermute | solution.py:18
  7.3 13.0 %collective-permute-start.5 = (bf16[768,1536]{1,0:T(8,128)(2,1)}, bf16[768,1536]{1,0:T(8,128)(2,1)}, u32[]{:S(2)}, u32[]{:S(2)}) collective-permute-start(bf16[768,1536]{1,0:T(8,128)(2,1)} %bitcast.105), channel_id=1, source_target_pairs={{0,64},{64,0},{1,65},{65,1},{2,66},{66,2},{3,67},{67,3},{4,68},{68... | collective-permute-start | bytes 7077896 | tf_op jit(solution)/shard_map/ppermute | solution.py:18
  8.5 7.7 %collective-permute-start = (s32[128,4]{0,1:T(4,128)S(1)}, s32[128,4]{0,1:T(4,128)S(1)}, u32[]{:S(2)}, u32[]{:S(2)}) collective-permute-start(s32[128,4]{0,1:T(4,128)S(1)} %dynamic-slice_bitcast_fusion.2), channel_id=1, source_target_pairs={{0,64},{64,0},{1,65},{65,1},{2,66},{66,2},{3,67},{67,3},{4,68},{68... | collective-permute-start | bytes 6152 | tf_op jit(solution)/shard_map/ppermute | solution.py:18
  10.2 7.9 %collective-permute-start.1 = (bf16[34,1536]{1,0:T(8,128)(2,1)}, bf16[34,1536]{1,0:T(8,128)(2,1)}, u32[]{:S(2)}, u32[]{:S(2)}) collective-permute-start(bf16[34,1536]{1,0:T(8,128)(2,1)} %pad_maximum_fusion.1), channel_id=1, source_target_pairs={{0,64},{64,0},{1,65},{65,1},{2,66},{66,2},{3,67},{67,3},{4,68},{68... | collective-permute-start | bytes 313352 | tf_op jit(solution)/shard_map/ppermute | solution.py:18
  10.6 18.4 %collective-permute-start.6 = (bf16[1536,384]{1,0:T(8,128)(2,1)}, bf16[1536,384]{1,0:T(8,128)(2,1)}, u32[]{:S(2)}, u32[]{:S(2)}) collective-permute-start(bf16[1536,384]{1,0:T(8,128)(2,1)} %bitcast.87), channel_id=1, source_target_pairs={{0,1},{1,0},{2,3},{3,2},{4,5},{5,4},{6,7},{7,6},{8,9},{9,8},{10,11... | collective-permute-start | bytes 3538952 | tf_op jit(solution)/shard_map/ppermute | solution.py:1068
  29.0 9.6 %collective-permute-start.7 = (bf16[128,1536]{1,0:T(8,128)(2,1)S(1)}, bf16[128,1536]{1,0:T(8,128)(2,1)S(1)}, u32[]{:S(2)}, u32[]{:S(2)}) collective-permute-start(bf16[128,1536]{1,0:T(8,128)(2,1)S(1)} %get-tuple-element.121.a_ref), channel_id=1, source_target_pairs={{0,1},{1,0},{2,3},{3,2},{4,5},{5,4},{6,7},{7,6},{8,9},{9,8},{10,11... | collective-permute-start | bytes 1179656 | tf_op jit(solution)/shard_map/ppermute | solution.py:18
  31.4 26.4 %collective-permute-start.11 = (bf16[1536,384]{1,0:T(8,128)(2,1)}, bf16[1536,384]{1,0:T(8,128)(2,1)}, u32[]{:S(2)}, u32[]{:S(2)}) collective-permute-start(bf16[1536,384]{1,0:T(8,128)(2,1)} %collective-permute-done.6.refs_6_), channel_id=1, source_target_pairs={{0,64},{1,65},{2,66},{3,67},{4,68},{5,69},{6,70},{7,71},{8,72},{9,... | collective-permute-start | bytes 3538952 | tf_op jit(solution)/shard_map/ppermute | solution.py:1064
  38.6 19.3 %collective-permute-start.12 = (bf16[1536,384]{1,0:T(8,128)(2,1)}, bf16[1536,384]{1,0:T(8,128)(2,1)}, u32[]{:S(2)}, u32[]{:S(2)}) collective-permute-start(bf16[1536,384]{1,0:T(8,128)(2,1)} %bitcast.18.refs_1_), channel_id=1, source_target_pairs={{0,1},{1,0},{2,3},{3,2},{4,5},{5,4},{6,7},{7,6},{8,9},{9,8},{10,11... | collective-permute-start | bytes 3538952 | tf_op jit(solution)/shard_map/ppermute | solution.py:1068
  41.3 28.4 %collective-permute-start.14 = (bf16[384,1536]{1,0:T(8,128)(2,1)S(1)}, bf16[384,1536]{1,0:T(8,128)(2,1)}, u32[]{:S(2)}, u32[]{:S(2)}) collective-permute-start(bf16[384,1536]{1,0:T(8,128)(2,1)S(1)} %bitcast.82), channel_id=1, source_target_pairs={{0,1},{1,0},{2,3},{3,2},{4,5},{5,4},{6,7},{7,6},{8,9},{9,8},{10,11... | collective-permute-start | bytes 3538952 | tf_op jit(solution)/shard_map/ppermute | solution.py:1068
  47.4 28.5 %all-to-all-start = ((bf16[32,16,1536]{2,1,0:T(8,128)(2,1)}), bf16[32,16,1536]{2,1,0:T(8,128)(2,1)}, u32[]{:S(2)}, u32[]{:S(2)}) async-start(bf16[32,16,1536]{2,1,0:T(8,128)(2,1)} %bitcast.129), calls=%async_computation | async-start | bytes 3145728 | tf_op jit(solution)/shard_map/all_to_all | solution.py:26
  57.2 18.7 %collective-permute-start.9 = (bf16[1536,384]{1,0:T(8,128)(2,1)}, bf16[1536,384]{1,0:T(8,128)(2,1)}, u32[]{:S(2)}, u32[]{:S(2)}) collective-permute-start(bf16[1536,384]{1,0:T(8,128)(2,1)} %bitcast.18.refs_1_), channel_id=1, source_target_pairs={{0,64},{64,0},{1,65},{65,1},{2,66},{66,2},{3,67},{67,3},{4,68},{68... | collective-permute-start | bytes 3538952 | tf_op jit(solution)/shard_map/ppermute | solution.py:18
  57.3 17.6 %collective-permute-start.8 = (bf16[1536,384]{1,0:T(8,128)(2,1)S(1)}, bf16[1536,384]{1,0:T(8,128)(2,1)S(1)}, u32[]{:S(2)}, u32[]{:S(2)}) collective-permute-start(bf16[1536,384]{1,0:T(8,128)(2,1)S(1)} %bitcast.88), channel_id=1, source_target_pairs={{0,64},{64,0},{1,65},{65,1},{2,66},{66,2},{3,67},{67,3},{4,68},{68... | collective-permute-start | bytes 3538952 | tf_op jit(solution)/shard_map/ppermute | solution.py:18
  57.8 18.1 %collective-permute-start.10 = (bf16[384,1536]{1,0:T(8,128)(2,1)S(1)}, bf16[384,1536]{1,0:T(8,128)(2,1)}, u32[]{:S(2)}, u32[]{:S(2)}) collective-permute-start(bf16[384,1536]{1,0:T(8,128)(2,1)S(1)} %bitcast.83), channel_id=1, source_target_pairs={{0,64},{64,0},{1,65},{65,1},{2,66},{66,2},{3,67},{67,3},{4,68},{68... | collective-permute-start | bytes 3538952 | tf_op jit(solution)/shard_map/ppermute | solution.py:18
  57.9 18.0 %collective-permute-start.13 = (bf16[1536,384]{1,0:T(8,128)(2,1)}, bf16[1536,384]{1,0:T(8,128)(2,1)}, u32[]{:S(2)}, u32[]{:S(2)}) collective-permute-start(bf16[1536,384]{1,0:T(8,128)(2,1)} %collective-permute-done.12.refs_7_), channel_id=1, source_target_pairs={{0,64},{1,65},{2,66},{3,67},{4,68},{5,69},{6,70},{7,71},{8,72},{9,... | collective-permute-start | bytes 3538952 | tf_op jit(solution)/shard_map/ppermute | solution.py:1064
  75.9 46.1 %collective-permute-start.16 = (bf16[1536,768]{1,0:T(8,128)(2,1)}, bf16[1536,768]{1,0:T(8,128)(2,1)}, u32[]{:S(2)}, u32[]{:S(2)}) collective-permute-start(bf16[1536,768]{1,0:T(8,128)(2,1)} %pad_maximum_fusion), channel_id=1, source_target_pairs={{64,65},{65,64},{66,67},{67,66},{68,69},{69,68},{70,71},{71,70},{7... | collective-permute-start | bytes 7077896 | tf_op jit(solution)/shard_map/ppermute | solution.py:1068
  86.3 33.9 %all-to-all-start.1 = ((bf16[32,16,1536]{2,1,0:T(8,128)(2,1)}), bf16[32,16,1536]{2,1,0:T(8,128)(2,1)}, u32[]{:S(2)}, u32[]{:S(2)}) async-start(bf16[32,16,1536]{2,1,0:T(8,128)(2,1)} %bitcast.116), calls=%async_computation.1 | async-start | bytes 3145728 | tf_op jit(solution)/shard_map/all_to_all | solution.py:26
  122.1 9.2 %collective-permute-start.17 = (bf16[128,1536]{1,0:T(8,128)(2,1)S(1)}, bf16[128,1536]{1,0:T(8,128)(2,1)S(1)}, u32[]{:S(2)}, u32[]{:S(2)}) collective-permute-start(bf16[128,1536]{1,0:T(8,128)(2,1)S(1)} %convolution_convert_fusion.2.refs_1_), channel_id=1, source_target_pairs={{0,1},{1,0},{2,3},{3,2},{4,5},{5,4},{6,7},{7,6},{8,9},{9,8},{10,11... | collective-permute-start | bytes 1179656 | tf_op jit(solution)/shard_map/ppermute | solution.py:18
  122.2 30.9 %all-to-all-start.2 = ((bf16[32,16,1536]{2,1,0:T(8,128)(2,1)}), bf16[32,16,1536]{2,1,0:T(8,128)(2,1)}, u32[]{:S(2)}, u32[]{:S(2)}) async-start(bf16[32,16,1536]{2,1,0:T(8,128)(2,1)} %bitcast.126), calls=%async_computation.2 | async-start | bytes 3145728 | tf_op jit(solution)/shard_map/all_to_all | solution.py:26
  140.8 8.2 %collective-permute-start.18 = (bf16[128,1536]{1,0:T(8,128)(2,1)S(1)}, bf16[128,1536]{1,0:T(8,128)(2,1)S(1)}, u32[]{:S(2)}, u32[]{:S(2)}) collective-permute-start(bf16[128,1536]{1,0:T(8,128)(2,1)S(1)} %get-tuple-element.134.a_ref), channel_id=1, source_target_pairs={{0,1},{1,0},{2,3},{3,2},{4,5},{5,4},{6,7},{7,6},{8,9},{9,8},{10,11... | collective-permute-start | bytes 1179656 | tf_op jit(solution)/shard_map/ppermute | solution.py:18
  141.0 20.7 %collective-permute-start.20 = (bf16[1536,768]{1,0:T(8,128)(2,1)}, bf16[1536,768]{1,0:T(8,128)(2,1)}, u32[]{:S(2)}, u32[]{:S(2)}) collective-permute-start(bf16[1536,768]{1,0:T(8,128)(2,1)} %collective-permute-done.16.refs_6_), channel_id=1, source_target_pairs={{64,0},{65,1},{66,2},{67,3},{68,4},{69,5},{70,6},{71,7},{72,8},{73... | collective-permute-start | bytes 7077896 | tf_op jit(solution)/shard_map/ppermute | solution.py:1064
  149.0 11.4 %collective-permute-start.19 = (bf16[384,1536]{1,0:T(8,128)(2,1)S(1)}, bf16[384,1536]{1,0:T(8,128)(2,1)}, u32[]{:S(2)}, u32[]{:S(2)}) collective-permute-start(bf16[384,1536]{1,0:T(8,128)(2,1)S(1)} %bitcast.84), channel_id=1, source_target_pairs={{64,65},{65,64},{66,67},{67,66},{68,69},{69,68},{70,71},{71,70},{7... | collective-permute-start | bytes 3538952 | tf_op jit(solution)/shard_map/ppermute | solution.py:1068
  153.8 31.8 %all-to-all-start.3 = ((bf16[32,16,1664]{2,1,0:T(8,128)(2,1)}), bf16[32,16,1664]{2,1,0:T(8,128)(2,1)}, u32[]{:S(2)}, u32[]{:S(2)}) async-start(bf16[32,16,1664]{2,1,0:T(8,128)(2,1)} %bitcast.124), calls=%async_computation.3 | async-start | bytes 3407872 | tf_op jit(solution)/shard_map/all_to_all | solution.py:26
  198.9 28.8 %all-to-all-start.4 = ((bf16[32,16,1664]{2,1,0:T(8,128)(2,1)}), bf16[32,16,1664]{2,1,0:T(8,128)(2,1)}, u32[]{:S(2)}, u32[]{:S(2)}) async-start(bf16[32,16,1664]{2,1,0:T(8,128)(2,1)} %bitcast.125), calls=%async_computation.4 | async-start | bytes 3407872 | tf_op jit(solution)/shard_map/all_to_all | solution.py:26
  229.6 22.2 %collective-permute-start.23 = (bf16[2,1536,1152]{2,1,0:T(8,128)(2,1)}, bf16[2,1536,1152]{2,1,0:T(8,128)(2,1)}, u32[]{:S(2)}, u32[]{:S(2)}) collective-permute-start(bf16[2,1536,1152]{2,1,0:T(8,128)(2,1)} %get-tuple-element.155.refs_3_.refs_4_), channel_id=1, source_target_pairs={{0,64},{1,65},{2,66},{3,67},{4,68},{5,69},{6,70},{7,71},{8,72},{9,... | collective-permute-start | bytes 21233672 | tf_op jit(solution)/shard_map/ppermute | solution.py:1064
  233.8 8.1 %collective-permute-start.22 = (bf16[128,1664]{1,0:T(8,128)(2,1)S(1)}, bf16[128,1664]{1,0:T(8,128)(2,1)S(1)}, u32[]{:S(2)}, u32[]{:S(2)}) collective-permute-start(bf16[128,1664]{1,0:T(8,128)(2,1)S(1)} %collect.1.refs_3_), channel_id=1, source_target_pairs={{0,1},{1,0},{2,3},{3,2},{4,5},{5,4},{6,7},{7,6},{8,9},{9,8},{10,11... | collective-permute-start | bytes 1277960 | tf_op jit(solution)/shard_map/ppermute | solution.py:18
  233.8 24.2 %all-to-all-start.5 = ((bf16[32,16,1536]{2,1,0:T(8,128)(2,1)}), bf16[32,16,1536]{2,1,0:T(8,128)(2,1)}, u32[]{:S(2)}, u32[]{:S(2)}) async-start(bf16[32,16,1536]{2,1,0:T(8,128)(2,1)} %bitcast.127), calls=%async_computation.5 | async-start | bytes 3145728 | tf_op jit(solution)/shard_map/all_to_all | solution.py:26
  251.8 8.3 %collective-permute-start.24 = (bf16[128,1536]{1,0:T(8,128)(2,1)S(1)}, bf16[128,1536]{1,0:T(8,128)(2,1)S(1)}, u32[]{:S(2)}, u32[]{:S(2)}) collective-permute-start(bf16[128,1536]{1,0:T(8,128)(2,1)S(1)} %get-tuple-element.156.a_ref), channel_id=1, source_target_pairs={{0,1},{1,0},{2,3},{3,2},{4,5},{5,4},{6,7},{7,6},{8,9},{9,8},{10,11... | collective-permute-start | bytes 1179656 | tf_op jit(solution)/shard_map/ppermute | solution.py:18
  263.4 25.0 %all-to-all-start.6 = ((bf16[32,16,1536]{2,1,0:T(8,128)(2,1)}), bf16[32,16,1536]{2,1,0:T(8,128)(2,1)}, u32[]{:S(2)}, u32[]{:S(2)}) async-start(bf16[32,16,1536]{2,1,0:T(8,128)(2,1)} %bitcast.130), calls=%async_computation.6 | async-start | bytes 3145728 | tf_op jit(solution)/shard_map/all_to_all | solution.py:26
  270.7 61.2 %collective-permute-start.27 = (bf16[1536,1152]{1,0:T(8,128)(2,1)}, bf16[1536,1152]{1,0:T(8,128)(2,1)}, u32[]{:S(2)}, u32[]{:S(2)}) collective-permute-start(bf16[1536,1152]{1,0:T(8,128)(2,1)} %fusion), channel_id=1, source_target_pairs={{64,65},{65,64},{66,67},{67,66},{68,69},{69,68},{70,71},{71,70},{7... | collective-permute-start | bytes 10616840 | tf_op jit(solution)/shard_map/ppermute | solution.py:1068
  301.1 20.2 %collective-permute-start.28 = (bf16[768,1920]{1,0:T(8,128)(2,1)}, bf16[768,1920]{1,0:T(8,128)(2,1)}, u32[]{:S(2)}, u32[]{:S(2)}) collective-permute-start(bf16[768,1920]{1,0:T(8,128)(2,1)} %get-tuple-element.173), channel_id=1, source_target_pairs={{0,64},{64,0},{1,65},{65,1},{2,66},{66,2},{3,67},{67,3},{4,68},{68... | collective-permute-start | bytes 8847368 | tf_op jit(solution)/shard_map/ppermute | solution.py:18
  301.1 30.8 %all-to-all-start.7 = ((bf16[32,16,1536]{2,1,0:T(8,128)(2,1)}), bf16[32,16,1536]{2,1,0:T(8,128)(2,1)}, u32[]{:S(2)}, u32[]{:S(2)}) async-start(bf16[32,16,1536]{2,1,0:T(8,128)(2,1)} %bitcast.128), calls=%async_computation.7 | async-start | bytes 3145728 | tf_op jit(solution)/shard_map/all_to_all | solution.py:26
  306.0 74.8 %reduce-scatter.3.cloned.1.call-start = ((), (), s32[]{:S(2)}) async-start(), calls=%async_computation.14 | async-start | bytes 3686400 | tf_op jit(solution)/shard_map/reduce_scatter | solution.py:1007
  308.8 16.8 %collective-permute-start.26 = (bf16[128,1536]{1,0:T(8,128)(2,1)}, bf16[128,1536]{1,0:T(8,128)(2,1)}, u32[]{:S(2)}, u32[]{:S(2)}) collective-permute-start(bf16[128,1536]{1,0:T(8,128)(2,1)} %convolution_convert_fusion.1), channel_id=1, source_target_pairs={{0,1},{1,0},{2,3},{3,2},{4,5},{5,4},{6,7},{7,6},{8,9},{9,8},{10,11... | collective-permute-start | bytes 1179656 | tf_op jit(solution)/shard_map/ppermute | solution.py:18
  308.8 16.8 %collective-permute-start.29 = (f32[32,128]{1,0:T(8,128)S(1)}, f32[32,128]{1,0:T(8,128)S(1)}, u32[]{:S(2)}, u32[]{:S(2)}) collective-permute-start(f32[32,128]{1,0:T(8,128)S(1)} %copy-done.55), channel_id=1, source_target_pairs={{0,1},{1,0},{2,3},{3,2},{4,5},{5,4},{6,7},{7,6},{8,9},{9,8},{10,11... | collective-permute-start | bytes 49160 | tf_op jit(solution)/shard_map/ppermute | solution.py:18
  333.8 33.0 %collective-permute-start.33 = (bf16[2,1536,1152]{2,1,0:T(8,128)(2,1)}, bf16[2,1536,1152]{2,1,0:T(8,128)(2,1)}, u32[]{:S(2)}, u32[]{:S(2)}) collective-permute-start(bf16[2,1536,1152]{2,1,0:T(8,128)(2,1)} %experts_grads.3.refs_0_), channel_id=1, source_target_pairs={{64,0},{65,1},{66,2},{67,3},{68,4},{69,5},{70,6},{71,7},{72,8},{73... | collective-permute-start | bytes 21233672 | tf_op jit(solution)/shard_map/ppermute | solution.py:1064
  335.3 8.9 %collective-permute-start.30 = (bf16[128,1536]{1,0:T(8,128)(2,1)S(1)}, bf16[128,1536]{1,0:T(8,128)(2,1)S(1)}, u32[]{:S(2)}, u32[]{:S(2)}) collective-permute-start(bf16[128,1536]{1,0:T(8,128)(2,1)S(1)} %convolution_convert_fusion.refs_3_), channel_id=1, source_target_pairs={{0,1},{1,0},{2,3},{3,2},{4,5},{5,4},{6,7},{7,6},{8,9},{9,8},{10,11... | collective-permute-start | bytes 1179656 | tf_op jit(solution)/shard_map/ppermute | solution.py:18
  364.0 9.8 %collective-permute-start.34 = (bf16[768,1920]{1,0:T(8,128)(2,1)}, bf16[768,1920]{1,0:T(8,128)(2,1)S(1)}, u32[]{:S(2)}, u32[]{:S(2)}) collective-permute-start(bf16[768,1920]{1,0:T(8,128)(2,1)} %get-tuple-element.188), channel_id=1, source_target_pairs={{0,64},{64,0},{1,65},{65,1},{2,66},{66,2},{3,67},{67,3},{4,68},{68... | collective-permute-start | bytes 8847368 | tf_op jit(solution)/shard_map/ppermute | solution.py:18
  376.2 28.5 %all-to-all-start.8 = ((bf16[4,192,1920]{2,1,0:T(8,128)(2,1)}), bf16[4,192,1920]{2,1,0:T(8,128)(2,1)}, u32[]{:S(2)}, u32[]{:S(2)}) async-start(bf16[4,192,1920]{2,1,0:T(8,128)(2,1)} %bitcast.110), calls=%async_computation.8 | async-start | bytes 5898240 | tf_op jit(solution)/shard_map/all_to_all | solution.py:974
  380.8 26.5 %reduce-scatter.5.cloned.1.call-start = ((), (), s32[]{:S(2)}) async-start(), calls=%async_computation.15 | async-start | bytes 921600 | tf_op jit(solution)/shard_map/reduce_scatter | solution.py:1007
  381.5 96.3 %all-gather.2.cloned.1.call-start = ((), (), s32[]{:S(2)}) async-start(), calls=%async_computation.16 | async-start | bytes 3133440 | tf_op jit(solution)/shard_map/all_gather | solution.py:1001
  384.2 11.5 %collective-permute-start.35 = (bf16[128,1536]{1,0:T(8,128)(2,1)S(1)}, bf16[128,1536]{1,0:T(8,128)(2,1)S(1)}, u32[]{:S(2)}, u32[]{:S(2)}) collective-permute-start(bf16[128,1536]{1,0:T(8,128)(2,1)S(1)} %get-tuple-element.189), channel_id=1, source_target_pairs={{0,1},{1,0},{2,3},{3,2},{4,5},{5,4},{6,7},{7,6},{8,9},{9,8},{10,11... | collective-permute-start | bytes 1179656 | tf_op jit(solution)/shard_map/ppermute | solution.py:18
  407.3 7.3 %collective-permute-start.39 = (bf16[48,1920]{1,0:T(8,128)(2,1)}, bf16[48,1920]{1,0:T(8,128)(2,1)S(1)}, u32[]{:S(2)}, u32[]{:S(2)}) collective-permute-start(bf16[48,1920]{1,0:T(8,128)(2,1)} %reduce-scatter.5.cloned.1.call-done), channel_id=1, source_target_pairs={{0,2},{2,0},{4,6},{6,4},{8,10},{10,8},{12,14},{14,12},{16,18},{18,... | collective-permute-start | bytes 552968 | tf_op jit(solution)/shard_map/ppermute | solution.py:1017
  445.4 31.0 %collective-permute-start.37 = (bf16[1024,1152]{1,0:T(8,128)(2,1)}, bf16[1024,1152]{1,0:T(8,128)(2,1)}, u32[]{:S(2)}, u32[]{:S(2)}) collective-permute-start(bf16[1024,1152]{1,0:T(8,128)(2,1)} %fusion.1), channel_id=1, source_target_pairs={{0,1},{1,0},{2,3},{3,2},{4,5},{5,4},{6,7},{7,6},{8,9},{9,8},{10,11... | collective-permute-start | bytes 7077896 | tf_op jit(solution)/shard_map/ppermute | solution.py:1068
  450.5 25.9 %all-to-all-start.11 = ((bf16[4,192,1920]{2,1,0:T(8,128)(2,1)}), bf16[4,192,1920]{2,1,0:T(8,128)(2,1)}, u32[]{:S(2)}, u32[]{:S(2)}) async-start(bf16[4,192,1920]{2,1,0:T(8,128)(2,1)} %broadcast_in_dim.42), calls=%async_computation.11 | async-start | bytes 5898240 | tf_op jit(solution)/shard_map/all_to_all | solution.py:974
  456.1 32.9 %collective-permute-start.40 = (bf16[512,1152]{1,0:T(8,128)(2,1)}, bf16[512,1152]{1,0:T(8,128)(2,1)S(1)}, u32[]{:S(2)}, u32[]{:S(2)}) collective-permute-start(bf16[512,1152]{1,0:T(8,128)(2,1)} %fusion.2), channel_id=1, source_target_pairs={{0,1},{1,0},{2,3},{3,2},{4,5},{5,4},{6,7},{7,6},{8,9},{9,8},{10,11... | collective-permute-start | bytes 3538952 | tf_op jit(solution)/shard_map/ppermute | solution.py:1068
  461.9 14.6 %collective-permute-start.36 = (f32[128,1536]{1,0:T(8,128)}, f32[128,1536]{1,0:T(8,128)S(1)}, u32[]{:S(2)}, u32[]{:S(2)}) collective-permute-start(f32[128,1536]{1,0:T(8,128)} %get-tuple-element.227), channel_id=1, source_target_pairs={{0,64},{64,0},{1,65},{65,1},{2,66},{66,2},{3,67},{67,3},{4,68},{68... | collective-permute-start | bytes 2359304 | tf_op jit(solution)/shard_map/ppermute | solution.py:18
  476.5 21.2 %collective-permute-start.38 = (bf16[768,1920]{1,0:T(8,128)(2,1)}, bf16[768,1920]{1,0:T(8,128)(2,1)}, u32[]{:S(2)}, u32[]{:S(2)}) collective-permute-start(bf16[768,1920]{1,0:T(8,128)(2,1)} %bitcast.45.zero_ref), channel_id=1, source_target_pairs={{64,0},{65,1},{66,2},{67,3},{68,4},{69,5},{70,6},{71,7},{72,8},{73... | collective-permute-start | bytes 8847368 | tf_op jit(solution)/shard_map/ppermute | solution.py:1064
  489.0 8.7 %collective-permute-start.41 = (bf16[768,1920]{1,0:T(8,128)(2,1)S(1)}, bf16[768,1920]{1,0:T(8,128)(2,1)S(1)}, u32[]{:S(2)}, u32[]{:S(2)}) collective-permute-start(bf16[768,1920]{1,0:T(8,128)(2,1)S(1)} %copy-done.66), channel_id=1, source_target_pairs={{0,64},{1,65},{2,66},{3,67},{4,68},{5,69},{6,70},{7,71},{8,72},{9,... | collective-permute-start | bytes 8847368 | tf_op jit(solution)/shard_map/ppermute | solution.py:1064
  (93 other events, 916.6 us)
Sparse Core Ops, SparseCore 0:
  335.4 26.1 reduce-scatter.2
  384.2 22.1 reduce-scatter.4
  416.4 47.4 all-gather.1

commit v5 on v4

--- a/solution.py
+++ b/solution.py
@@ -1162,7 +1162,7 @@
         attn_gains[0], moe_gains[0],
     )
 
-    cuts = ((0, model * 2 // 3), (model * 2 // 3, model))
+    cuts = ((0, model * 5 // 6), (model * 5 // 6, model))
     far_sum = [both_0[1, a:b] + both_0r[1, a:b] for a, b in cuts]
     half_0 = after(keep, *far_sum) + swap(give, "pipe")
     da_r = swap(after(da, half_0), "tensor")
@@ -1176,12 +1176,12 @@
     x_f = x_0.astype(F32)
     grad_0 = grad_h + norm_back(x_f, row_scale_of(x_f), attn_gains[0], da)
     got_g, input_grads = by_layer(grad_0, grad_1)
-    sum_0 = after(plane_copy(part, 0), far_z[0])
+    sum_0 = plane_copy(part, 0)
     core_v = core.astype(jnp.int32).reshape(1)
     over_0 = over(after(sum_0, got_g), 0)
     sizes = (width, model, experts)
     attn_g = attn_total(core_v, 0, sum_0, sum_1, (), *sizes)
-    over_1 = over(after(sum_1, far_z[1], attn_g[0]), 1)
+    over_1 = over(after(sum_1, far_z[0], attn_g[0]), 1)
     ff_g = ff_total(
         after(core_v, attn_g[0]), 0, (both_0, both_0r, far_z[0]), ff_grads_1, ()
     )

time: 525 us -> 526 us (level)
    ppermute x8, waiting for transfers between devices: 16.6 us -> 10.1 us  [across(): return lax.ppermute(value, ('pipe', 'tensor'), pairs)]
    unnamed x172 -> x174, local copies, waits for them, and re-layouts: 14.2 us -> 15.6 us
  transfers between devices with their start and end apart: 55 -> 55, of which waited for: 22 -> 21; matrix products, arithmetic and copies ran while one was open for 9% -> 9% of each run, Pallas kernels for 20% -> 21%
where the time goes in v5:
time: 526 us; the launch traced here: 516 us
  waiting for transfers between devices  159 us (30%)
  Pallas kernels  129 us (25%)
  starting transfers between devices  120 us (23%)
  other arithmetic  37.9 us (7%)
  blocking collectives  29.1 us (6%)
  local copies, waits for them, and re-layouts  19.3 us (4%)
  between operations  15.6 us (3%)
  matrix products  6.29 us (1%)
    pallas_call x21, Pallas kernels, call(): pl.pallas_call(body, out_shape=[jax.ShapeDtypeStruct(shape, kind) for sha...  129 us
    all_to_all x8, waiting for transfers between devices, expert_exchange(): lax.all_to_all(value, ('expert', 'tensor'), split_axis=0, concat_axis=0,...  65.4 us
    all_to_all x8, starting transfers between devices, expert_exchange(): lax.all_to_all(value, ('expert', 'tensor'), split_axis=0, concat_axis=0,...  52.6 us
    ppermute x24, waiting for transfers between devices, swap(): return lax.ppermute(value, axis, SWAP)  46.4 us
    all_to_all x2, blocking collectives, plane_exchange(): lax.all_to_all(value, ('pipe', 'expert'), split_axis=0, concat_axis=0, ax...  29.1 us
    all_to_all x2, waiting for transfers between devices, plane_exchange(): lax.all_to_all(value, ('pipe', 'expert'), split_axis=0, concat_axis=0, ax...  24.9 us
    ppermute x8, starting transfers between devices, across(): return lax.ppermute(value, ('pipe', 'tensor'), pairs)  22.3 us
    ppermute x9, starting transfers between devices, over(): return lax.ppermute(value, 'pipe', [(1 - layer, layer)])  22.2 us
  transfers between devices with their start and end apart: 55, of which 21 were waited for; matrix products, arithmetic and copies ran while one was open for 9% of the time, Pallas kernels for 21%

profile of v5, /device:TPU:0, one launch (start us, length us, event | category | flops | bytes accessed | tf_op | source)
XLA Modules:
  0.0 515.9 jit_solution(3075296037595036873)
XLA Ops:
  21.2 4.8 attend_forward.2
  33.6 5.1 collective-permute-done.7.b_ref
  47.4 9.7 %all-to-all-start = ((bf16[32,16,1536]{2,1,0:T(8,128)(2,1)}), bf16[32,16,1536]{2,1,0:T(8,128)(2,1)}, u32[]{:S(2)}, u32[]{:S(2)}) async-start(bf16[32,16,1536]{2,1,0:T(8,128)(2,1)} %bitcast.127), calls=%async_computation | async-start | bytes 3145728 | tf_op jit(solution)/shard_map/all_to_all | solution.py:26
  61.2 8.5 %collective-permute-done.14.refs_8_.refs_2_ = bf16[384,1536]{1,0:T(8,128)(2,1)} collective-permute-done((bf16[384,1536]{1,0:T(8,128)(2,1)S(1)}, bf16[384,1536]{1,0:T(8,128)(2,1)}, u32[]{:S(2)}, u32[]{:S(2)}) %collective-permute-start.14) | collective-permute-done | bytes 1179680 | tf_op jit(solution)/shard_map/ppermute | solution.py:1068
  78.0 8.2 %experts_forward.1 = bf16[512,1536]{1,0:T(8,128)(2,1)} custom-call(s32[1]{0:T(128)} %bitcast.8.own_ref, bf16[512,1536]{1,0:T(8,128)(2,1)} %bitcast.17.x_ref.x_in, bf16[1536,384]{1,0:T(8,128)(2,1)S(1)} %bitcast.90, bf16[1536,384]{1,0:T(8,128)(2,1)} %bitcast.18.refs_1_, bf16[384,1536]{1,0:T(8,128)(2,1)} %bitcast.79, bf16[1536,384]{1,0:T(8,128)(2,1)} %copy-done.65, ...), custom_call_target="tpu_custom_call" | custom-call | flops 1024 | bytes 1024 | tf_op jit(solution)/shard_map/experts_forward/pallas_call | solution.py:76
  86.3 9.6 %all-to-all-start.1 = ((bf16[32,16,1536]{2,1,0:T(8,128)(2,1)}), bf16[32,16,1536]{2,1,0:T(8,128)(2,1)}, u32[]{:S(2)}, u32[]{:S(2)}) async-start(bf16[32,16,1536]{2,1,0:T(8,128)(2,1)} %bitcast.114), calls=%async_computation.1 | async-start | bytes 3145728 | tf_op jit(solution)/shard_map/all_to_all | solution.py:26
  95.9 24.4 %all-to-all-done.1 = bf16[32,16,1536]{2,1,0:T(8,128)(2,1)} async-done(((bf16[32,16,1536]{2,1,0:T(8,128)(2,1)}), bf16[32,16,1536]{2,1,0:T(8,128)(2,1)}, u32[]{:S(2)}, u32[]{:S(2)}) %all-to-all-start.1) | async-done | bytes 1572896 | tf_op jit(solution)/shard_map/all_to_all | solution.py:26
  122.2 5.2 %all-to-all-start.2 = ((bf16[32,16,1536]{2,1,0:T(8,128)(2,1)}), bf16[32,16,1536]{2,1,0:T(8,128)(2,1)}, u32[]{:S(2)}, u32[]{:S(2)}) async-start(bf16[32,16,1536]{2,1,0:T(8,128)(2,1)} %bitcast.124), calls=%async_computation.2 | async-start | bytes 3145728 | tf_op jit(solution)/shard_map/all_to_all | solution.py:26
  132.1 6.7 %attend_forward.3 = (bf16[128,1536]{1,0:T(8,128)(2,1)S(1)}, bf16[128,768]{1,0:T(8,128)(2,1)S(1)}, bf16[128,256]{1,0:T(8,128)(2,1)S(1)}, bf16[128,768]{1,0:T(8,12...) custom-call(s32[1]{0:T(128)} %bitcast.own_ref, f32[128,1536]{1,0:T(8,128)} %get-tuple-element.121.refs_0_.refs_1_.h_ref, ...), custom_call_target="tpu_custom_call" | custom-call | flops 1024 | bytes 1024 | tf_op jit(solution)/shard_map/attend_forward/pallas_call | solution.py:76
  142.4 6.6 %collective-permute-done.18.b_ref = bf16[128,1536]{1,0:T(8,128)(2,1)S(1)} collective-permute-done((bf16[128,1536]{1,0:T(8,128)(2,1)S(1)}, bf16[128,1536]{1,0:T(8,128)(2,1)S(1)}, u32[]{:S(2)}, u32[]{:S(2)}) %collective-permute-start.18) | collective-permute-done | bytes 393248 | tf_op jit(solution)/shard_map/ppermute | solution.py:18
  153.7 6.5 %all-to-all-start.3 = ((bf16[32,16,1664]{2,1,0:T(8,128)(2,1)}), bf16[32,16,1664]{2,1,0:T(8,128)(2,1)}, u32[]{:S(2)}, u32[]{:S(2)}) async-start(bf16[32,16,1664]{2,1,0:T(8,128)(2,1)} %bitcast.122), calls=%async_computation.3 | async-start | bytes 3407872 | tf_op jit(solution)/shard_map/all_to_all | solution.py:26
  161.6 4.6 collective-permute-done.21.refs_9_.refs_3_
  166.2 19.1 %all-to-all-done.3 = bf16[32,16,1664]{2,1,0:T(8,128)(2,1)} async-done(((bf16[32,16,1664]{2,1,0:T(8,128)(2,1)}), bf16[32,16,1664]{2,1,0:T(8,128)(2,1)}, u32[]{:S(2)}, u32[]{:S(2)}) %all-to-all-start.3) | async-done | bytes 1703968 | tf_op jit(solution)/shard_map/all_to_all | solution.py:26
  185.3 12.5 %experts_backward.2 = (bf16[512,1664]{1,0:T(8,128)(2,1)}, bf16[512,768]{1,0:T(8,128)(2,1)S(1)}, bf16[512,1536]{1,0:T(8,128)(2,1)}) custom-call(s32[1]{0:T(128)} %bitcast.own_ref, bf16[512,1664]{1,0:T(8,128)(2,1)} %bitcast.25.x_ref.x_in, bf16[512,1536]{1,0:T(8,128)(2,1)} %bitcast.23.g_ref.g_in, bf16[1536,384]{1,0:T(8,128)(2,1)S(1)} %bitcast.91, ...), custom_call_target="tpu_custom_call" | custom-call | flops 1024 | bytes 1024 | tf_op jit(solution)/shard_map/experts_backward/pallas_call | solution.py:76
  198.7 4.8 all-to-all-start.4
  204.7 12.2 %experts_grads.2 = (bf16[2,1536,1152]{2,1,0:T(8,128)(2,1)}, bf16[512,1536]{1,0:T(8,128)(2,1)}) custom-call(s32[1]{0:T(128)} %bitcast.own_ref, bf16[512,1664]{1,0:T(8,128)(2,1)} %bitcast.25.x_ref.x_in, bf16[512,1536]{1,0:T(8,128)(2,1)} %bitcast.23.g_ref.g_in, bf16[512,768]{1,0:T(8,128)(2,1)S(1)} %copy-done.31, bf16[512,1536]{1,0:T(8,128)(2,1)} %get-tuple-element.143.dgu_in, ...), custom_call_target="tpu_custom_call" | custom-call | flops 1024 | bytes 1024 | tf_op jit(solution)/shard_map/experts_grads/pallas_call | solution.py:76
  216.9 10.5 %all-to-all-done.4 = bf16[32,16,1664]{2,1,0:T(8,128)(2,1)} async-done(((bf16[32,16,1664]{2,1,0:T(8,128)(2,1)}), bf16[32,16,1664]{2,1,0:T(8,128)(2,1)}, u32[]{:S(2)}, u32[]{:S(2)}) %all-to-all-start.4) | async-done | bytes 1703968 | tf_op jit(solution)/shard_map/all_to_all | solution.py:26
  229.4 4.3 collective-permute-start.23
  233.6 4.7 all-to-all-start.5
  243.5 8.2 %attend_backward.2 = (bf16[128,1024]{1,0:T(8,128)(2,1)S(1)}, bf16[128,1536]{1,0:T(8,128)(2,1)S(1)}, f32[128,1536]{1,0:T(8,128)}, bf16[32,128]{1,0:T(8,128)(2,1)S(1)}, bf16[16,1536]{1,0:T(8,128)(2,1)S(1)}) custom-call(s32[1]{0:T(128)} %bitcast.own_ref, f32[128,1536]{1,0:T(8,128)} %copy-done.10, f32[128,1536]{1,0:T(8,128)} %get-tuple-element.134.refs_1_.h_ref, ...), custom_call_target="tpu_custom_call" | custom-call | flops 1024 | bytes 1024 | tf_op jit(solution)/shard_map/attend_backward/pallas_call | solution.py:76
  253.8 4.4 fusion
  263.4 7.2 %all-to-all-start.6 = ((bf16[32,16,1536]{2,1,0:T(8,128)(2,1)}), bf16[32,16,1536]{2,1,0:T(8,128)(2,1)}, u32[]{:S(2)}, u32[]{:S(2)}) async-start(bf16[32,16,1536]{2,1,0:T(8,128)(2,1)} %bitcast.128), calls=%async_computation.6 | async-start | bytes 3145728 | tf_op jit(solution)/shard_map/all_to_all | solution.py:26
  273.2 7.0 %attend_grads.2 = (bf16[768,1920]{1,0:T(8,128)(2,1)}, bf16[768,1920]{1,0:T(8,128)(2,1)}) custom-call(s32[1]{0:T(128)} %bitcast.own_ref, bf16[128,1536]{1,0:T(8,128)(2,1)S(1)} %copy-done.15, f32[128,1536]{1,0:T(8,128)S(1)} %copy-done.11, f32[128,1536]{1,0:T(8,128)} %get-tuple-element.152.g_ref.gh_ref, bf16[128,768]{1,0:T(8,128)(2,1)S(1)} %copy-done.43, ...), custom_call_target="tpu_custom_call" | custom-call | flops 1024 | bytes 1024 | tf_op jit(solution)/shard_map/attend_grads/pallas_call | solution.py:76
  282.8 5.5 %all-to-all-done.6 = bf16[32,16,1536]{2,1,0:T(8,128)(2,1)} async-done(((bf16[32,16,1536]{2,1,0:T(8,128)(2,1)}), bf16[32,16,1536]{2,1,0:T(8,128)(2,1)}, u32[]{:S(2)}, u32[]{:S(2)}) %all-to-all-start.6) | async-done | bytes 1572896 | tf_op jit(solution)/shard_map/all_to_all | solution.py:26
  288.3 11.8 %experts_backward.3 = (bf16[512,1536]{1,0:T(8,128)(2,1)}, bf16[512,768]{1,0:T(8,128)(2,1)S(1)}, bf16[512,1536]{1,0:T(8,128)(2,1)}) custom-call(s32[1]{0:T(128)} %bitcast.8.own_ref, bf16[512,1536]{1,0:T(8,128)(2,1)} %bitcast.17.x_ref.x_in, bf16[512,1536]{1,0:T(8,128)(2,1)} %bitcast.32.g_ref.g_in, bf16[1536,384]{1,0:T(8,128)(2,1)S(1)} %bitcast.92, ...), custom_call_target="tpu_custom_call" | custom-call | flops 1024 | bytes 1024 | tf_op jit(solution)/shard_map/experts_backward/pallas_call | solution.py:76
  301.0 4.8 all-to-all-start.7
  310.9 10.3 %experts_grads.3.refs_0_ = bf16[2,1536,1152]{2,1,0:T(8,128)(2,1)} custom-call(s32[1]{0:T(128)} %bitcast.8.own_ref, bf16[512,1536]{1,0:T(8,128)(2,1)} %bitcast.17.x_ref.x_in, bf16[512,1536]{1,0:T(8,128)(2,1)} %bitcast.32.g_ref.g_in, bf16[512,768]{1,0:T(8,128)(2,1)S(1)} %copy-done.29, bf16[512,1536]{1,0:T(8,128)(2,1)} %get-tuple-element.169.dgu_in, ...), custom_call_target="tpu_custom_call" | custom-call | flops 1024 | bytes 1024 | tf_op jit(solution)/shard_map/experts_grads/pallas_call | solution.py:76
  321.2 4.3 add.80
  325.5 5.8 %all-to-all-done.7 = bf16[32,16,1536]{2,1,0:T(8,128)(2,1)} async-done(((bf16[32,16,1536]{2,1,0:T(8,128)(2,1)}), bf16[32,16,1536]{2,1,0:T(8,128)(2,1)}, u32[]{:S(2)}, u32[]{:S(2)}) %all-to-all-start.7) | async-done | bytes 1572896 | tf_op jit(solution)/shard_map/all_to_all | solution.py:26
  334.8 8.8 %collective-permute-done.30.refs_4_ = bf16[128,1536]{1,0:T(8,128)(2,1)S(1)} collective-permute-done((bf16[128,1536]{1,0:T(8,128)(2,1)S(1)}, bf16[128,1536]{1,0:T(8,128)(2,1)S(1)}, u32[]{:S(2)}, u32[]{:S(2)}) %collective-permute-start.30) | collective-permute-done | bytes 393248 | tf_op jit(solution)/shard_map/ppermute | solution.py:18
  344.5 7.8 %attend_backward.3 = (bf16[128,1024]{1,0:T(8,128)(2,1)S(1)}, bf16[128,1536]{1,0:T(8,128)(2,1)S(1)}, f32[128,1536]{1,0:T(8,128)}, bf16[32,128]{1,0:T(8,128)(2,1)S(1)}, bf16[16,1536]{1,0:T(8,128)(2,1)S(1)}) custom-call(s32[1]{0:T(128)} %bitcast.8.own_ref, bf16[128,1536]{1,0:T(8,128)(2,1)S(1)} %get-tuple-element.164.low_ref.refs_0_, ...), custom_call_target="tpu_custom_call" | custom-call | flops 1024 | bytes 1024 | tf_op jit(solution)/shard_map/attend_backward/pallas_call | solution.py:76
  352.5 3.9 collective-permute-done.31.rest_1_
  356.5 7.0 %attend_grads.3 = (bf16[768,1920]{1,0:T(8,128)(2,1)}, bf16[768,1920]{1,0:T(8,128)(2,1)}) custom-call(s32[1]{0:T(128)} %bitcast.8.own_ref, bf16[128,1536]{1,0:T(8,128)(2,1)S(1)} %copy-done.7, f32[128,1536]{1,0:T(8,128)S(1)} %copy-done.9, f32[128,1536]{1,0:T(8,128)} %get-tuple-element.177.gh_ref, bf16[128,768]{1,0:T(8,128)(2,1)S(1)} %copy-done.39, ...), custom_call_target="tpu_custom_call" | custom-call | flops 1024 | bytes 1024 | tf_op jit(solution)/shard_map/attend_grads/pallas_call | solution.py:76
  368.4 4.8 fusion.1
  375.5 4.6 all-to-all-start.8
  386.0 9.1 %collective-permute-done.35 = bf16[128,1536]{1,0:T(8,128)(2,1)S(1)} collective-permute-done((bf16[128,1536]{1,0:T(8,128)(2,1)S(1)}, bf16[128,1536]{1,0:T(8,128)(2,1)S(1)}, u32[]{:S(2)}, u32[]{:S(2)}) %collective-permute-start.35) | collective-permute-done | bytes 393248 | tf_op jit(solution)/shard_map/ppermute | solution.py:18
  395.1 8.9 %all-to-all-done.8 = bf16[4,192,1920]{2,1,0:T(8,128)(2,1)} async-done(((bf16[4,192,1920]{2,1,0:T(8,128)(2,1)}), bf16[4,192,1920]{2,1,0:T(8,128)(2,1)}, u32[]{:S(2)}, u32[]{:S(2)}) %all-to-all-start.8) | async-done | bytes 2949152 | tf_op jit(solution)/shard_map/all_to_all | solution.py:974
  407.0 7.0 %collective-permute-done.38 = bf16[48,1920]{1,0:T(8,128)(2,1)S(1)} collective-permute-done((bf16[48,1920]{1,0:T(8,128)(2,1)}, bf16[48,1920]{1,0:T(8,128)(2,1)S(1)}, u32[]{:S(2)}, u32[]{:S(2)}) %collective-permute-start.38) | collective-permute-done | bytes 184352 | tf_op jit(solution)/shard_map/ppermute | solution.py:1017
  415.7 14.6 %all_to_all.60 = bf16[8,24,1920]{2,1,0:T(8,128)(2,1)S(1)} all-to-all(bf16[8,24,1920]{2,1,0:T(8,128)(2,1)S(1)} %bitcast.118), channel_id=1, replica_groups={{0,2,4,6,8,10,12,14},{64,66,80,82,96,98,112,114},{16,18,20,22,24,26,28,..., dimensions={0} | all-to-all | bytes 1474560 | tf_op jit(solution)/shard_map/all_to_all | solution.py:974
  430.5 14.4 %all_to_all.61 = bf16[8,24,1920]{2,1,0:T(8,128)(2,1)S(1)} all-to-all(bf16[8,24,1920]{2,1,0:T(8,128)(2,1)S(1)} %broadcast_in_dim.20), channel_id=1, replica_groups={{0,2,4,6,8,10,12,14},{64,66,80,82,96,98,112,114},{16,18,20,22,24,26,28,..., dimensions={0} | all-to-all | bytes 1474560 | tf_op jit(solution)/shard_map/all_to_all | solution.py:974
  444.9 4.3 collective-permute-start.39
  451.1 4.7 all-to-all-start.11
  461.0 15.9 %all-to-all-done.11 = bf16[4,192,1920]{2,1,0:T(8,128)(2,1)} async-done(((bf16[4,192,1920]{2,1,0:T(8,128)(2,1)}), bf16[4,192,1920]{2,1,0:T(8,128)(2,1)}, u32[]{:S(2)}, u32[]{:S(2)}) %all-to-all-start.11) | async-done | bytes 2949152 | tf_op jit(solution)/shard_map/all_to_all | solution.py:974
  478.3 4.7 attn_total.2
  483.0 4.7 collective-permute-start.40
  493.6 4.6 ff_total.2
  499.8 4.5 attn_total.3
  504.4 4.5 ff_total.3
  (298 shorter events, 123.5 us)
Async XLA Ops:
  7.2 13.1 %collective-permute-start.2 = (bf16[1536,768]{1,0:T(8,128)(2,1)}, bf16[1536,768]{1,0:T(8,128)(2,1)}, u32[]{:S(2)}, u32[]{:S(2)}) collective-permute-start(bf16[1536,768]{1,0:T(8,128)(2,1)} %bitcast.98), channel_id=1, source_target_pairs={{0,64},{64,0},{1,65},{65,1},{2,66},{66,2},{3,67},{67,3},{4,68},{68... | collective-permute-start | bytes 7077896 | tf_op jit(solution)/shard_map/ppermute | solution.py:18
  7.3 13.0 %collective-permute-start.5 = (bf16[768,1536]{1,0:T(8,128)(2,1)}, bf16[768,1536]{1,0:T(8,128)(2,1)}, u32[]{:S(2)}, u32[]{:S(2)}) collective-permute-start(bf16[768,1536]{1,0:T(8,128)(2,1)} %bitcast.103), channel_id=1, source_target_pairs={{0,64},{64,0},{1,65},{65,1},{2,66},{66,2},{3,67},{67,3},{4,68},{68... | collective-permute-start | bytes 7077896 | tf_op jit(solution)/shard_map/ppermute | solution.py:18
  8.5 7.7 %collective-permute-start = (s32[128,4]{0,1:T(4,128)S(1)}, s32[128,4]{0,1:T(4,128)S(1)}, u32[]{:S(2)}, u32[]{:S(2)}) collective-permute-start(s32[128,4]{0,1:T(4,128)S(1)} %dynamic-slice_bitcast_fusion.2), channel_id=1, source_target_pairs={{0,64},{64,0},{1,65},{65,1},{2,66},{66,2},{3,67},{67,3},{4,68},{68... | collective-permute-start | bytes 6152 | tf_op jit(solution)/shard_map/ppermute | solution.py:18
  10.2 8.0 %collective-permute-start.1 = (bf16[34,1536]{1,0:T(8,128)(2,1)}, bf16[34,1536]{1,0:T(8,128)(2,1)}, u32[]{:S(2)}, u32[]{:S(2)}) collective-permute-start(bf16[34,1536]{1,0:T(8,128)(2,1)} %pad_maximum_fusion.1), channel_id=1, source_target_pairs={{0,64},{64,0},{1,65},{65,1},{2,66},{66,2},{3,67},{67,3},{4,68},{68... | collective-permute-start | bytes 313352 | tf_op jit(solution)/shard_map/ppermute | solution.py:18
  10.6 18.4 %collective-permute-start.6 = (bf16[1536,384]{1,0:T(8,128)(2,1)}, bf16[1536,384]{1,0:T(8,128)(2,1)}, u32[]{:S(2)}, u32[]{:S(2)}) collective-permute-start(bf16[1536,384]{1,0:T(8,128)(2,1)} %bitcast.87), channel_id=1, source_target_pairs={{0,1},{1,0},{2,3},{3,2},{4,5},{5,4},{6,7},{7,6},{8,9},{9,8},{10,11... | collective-permute-start | bytes 3538952 | tf_op jit(solution)/shard_map/ppermute | solution.py:1068
  29.0 9.7 %collective-permute-start.7 = (bf16[128,1536]{1,0:T(8,128)(2,1)S(1)}, bf16[128,1536]{1,0:T(8,128)(2,1)S(1)}, u32[]{:S(2)}, u32[]{:S(2)}) collective-permute-start(bf16[128,1536]{1,0:T(8,128)(2,1)S(1)} %get-tuple-element.120.a_ref), channel_id=1, source_target_pairs={{0,1},{1,0},{2,3},{3,2},{4,5},{5,4},{6,7},{7,6},{8,9},{9,8},{10,11... | collective-permute-start | bytes 1179656 | tf_op jit(solution)/shard_map/ppermute | solution.py:18
  31.3 26.5 %collective-permute-start.11 = (bf16[1536,384]{1,0:T(8,128)(2,1)}, bf16[1536,384]{1,0:T(8,128)(2,1)}, u32[]{:S(2)}, u32[]{:S(2)}) collective-permute-start(bf16[1536,384]{1,0:T(8,128)(2,1)} %collective-permute-done.6.refs_6_), channel_id=1, source_target_pairs={{0,64},{1,65},{2,66},{3,67},{4,68},{5,69},{6,70},{7,71},{8,72},{9,... | collective-permute-start | bytes 3538952 | tf_op jit(solution)/shard_map/ppermute | solution.py:1064
  38.7 19.2 %collective-permute-start.12 = (bf16[1536,384]{1,0:T(8,128)(2,1)}, bf16[1536,384]{1,0:T(8,128)(2,1)}, u32[]{:S(2)}, u32[]{:S(2)}) collective-permute-start(bf16[1536,384]{1,0:T(8,128)(2,1)} %bitcast.18.refs_1_), channel_id=1, source_target_pairs={{0,1},{1,0},{2,3},{3,2},{4,5},{5,4},{6,7},{7,6},{8,9},{9,8},{10,11... | collective-permute-start | bytes 3538952 | tf_op jit(solution)/shard_map/ppermute | solution.py:1068
  41.2 28.5 %collective-permute-start.14 = (bf16[384,1536]{1,0:T(8,128)(2,1)S(1)}, bf16[384,1536]{1,0:T(8,128)(2,1)}, u32[]{:S(2)}, u32[]{:S(2)}) collective-permute-start(bf16[384,1536]{1,0:T(8,128)(2,1)S(1)} %bitcast.82), channel_id=1, source_target_pairs={{0,1},{1,0},{2,3},{3,2},{4,5},{5,4},{6,7},{7,6},{8,9},{9,8},{10,11... | collective-permute-start | bytes 3538952 | tf_op jit(solution)/shard_map/ppermute | solution.py:1068
  47.4 28.5 %all-to-all-start = ((bf16[32,16,1536]{2,1,0:T(8,128)(2,1)}), bf16[32,16,1536]{2,1,0:T(8,128)(2,1)}, u32[]{:S(2)}, u32[]{:S(2)}) async-start(bf16[32,16,1536]{2,1,0:T(8,128)(2,1)} %bitcast.127), calls=%async_computation | async-start | bytes 3145728 | tf_op jit(solution)/shard_map/all_to_all | solution.py:26
  57.2 18.8 %collective-permute-start.9 = (bf16[1536,384]{1,0:T(8,128)(2,1)}, bf16[1536,384]{1,0:T(8,128)(2,1)}, u32[]{:S(2)}, u32[]{:S(2)}) collective-permute-start(bf16[1536,384]{1,0:T(8,128)(2,1)} %bitcast.18.refs_1_), channel_id=1, source_target_pairs={{0,64},{64,0},{1,65},{65,1},{2,66},{66,2},{3,67},{67,3},{4,68},{68... | collective-permute-start | bytes 3538952 | tf_op jit(solution)/shard_map/ppermute | solution.py:18
  57.3 17.6 %collective-permute-start.8 = (bf16[1536,384]{1,0:T(8,128)(2,1)S(1)}, bf16[1536,384]{1,0:T(8,128)(2,1)S(1)}, u32[]{:S(2)}, u32[]{:S(2)}) collective-permute-start(bf16[1536,384]{1,0:T(8,128)(2,1)S(1)} %bitcast.88), channel_id=1, source_target_pairs={{0,64},{64,0},{1,65},{65,1},{2,66},{66,2},{3,67},{67,3},{4,68},{68... | collective-permute-start | bytes 3538952 | tf_op jit(solution)/shard_map/ppermute | solution.py:18
  57.8 18.2 %collective-permute-start.10 = (bf16[384,1536]{1,0:T(8,128)(2,1)S(1)}, bf16[384,1536]{1,0:T(8,128)(2,1)}, u32[]{:S(2)}, u32[]{:S(2)}) collective-permute-start(bf16[384,1536]{1,0:T(8,128)(2,1)S(1)} %bitcast.83), channel_id=1, source_target_pairs={{0,64},{64,0},{1,65},{65,1},{2,66},{66,2},{3,67},{67,3},{4,68},{68... | collective-permute-start | bytes 3538952 | tf_op jit(solution)/shard_map/ppermute | solution.py:18
  57.9 18.1 %collective-permute-start.13 = (bf16[1536,384]{1,0:T(8,128)(2,1)}, bf16[1536,384]{1,0:T(8,128)(2,1)}, u32[]{:S(2)}, u32[]{:S(2)}) collective-permute-start(bf16[1536,384]{1,0:T(8,128)(2,1)} %collective-permute-done.12.refs_7_), channel_id=1, source_target_pairs={{0,64},{1,65},{2,66},{3,67},{4,68},{5,69},{6,70},{7,71},{8,72},{9,... | collective-permute-start | bytes 3538952 | tf_op jit(solution)/shard_map/ppermute | solution.py:1064
  75.9 46.2 %collective-permute-start.16 = (bf16[1536,768]{1,0:T(8,128)(2,1)}, bf16[1536,768]{1,0:T(8,128)(2,1)}, u32[]{:S(2)}, u32[]{:S(2)}) collective-permute-start(bf16[1536,768]{1,0:T(8,128)(2,1)} %pad_maximum_fusion), channel_id=1, source_target_pairs={{64,65},{65,64},{66,67},{67,66},{68,69},{69,68},{70,71},{71,70},{7... | collective-permute-start | bytes 7077896 | tf_op jit(solution)/shard_map/ppermute | solution.py:1068
  86.3 34.0 %all-to-all-start.1 = ((bf16[32,16,1536]{2,1,0:T(8,128)(2,1)}), bf16[32,16,1536]{2,1,0:T(8,128)(2,1)}, u32[]{:S(2)}, u32[]{:S(2)}) async-start(bf16[32,16,1536]{2,1,0:T(8,128)(2,1)} %bitcast.114), calls=%async_computation.1 | async-start | bytes 3145728 | tf_op jit(solution)/shard_map/all_to_all | solution.py:26
  122.2 9.2 %collective-permute-start.17 = (bf16[128,1536]{1,0:T(8,128)(2,1)S(1)}, bf16[128,1536]{1,0:T(8,128)(2,1)S(1)}, u32[]{:S(2)}, u32[]{:S(2)}) collective-permute-start(bf16[128,1536]{1,0:T(8,128)(2,1)S(1)} %convolution_convert_fusion.2.refs_1_), channel_id=1, source_target_pairs={{0,1},{1,0},{2,3},{3,2},{4,5},{5,4},{6,7},{7,6},{8,9},{9,8},{10,11... | collective-permute-start | bytes 1179656 | tf_op jit(solution)/shard_map/ppermute | solution.py:18
  122.2 30.8 %all-to-all-start.2 = ((bf16[32,16,1536]{2,1,0:T(8,128)(2,1)}), bf16[32,16,1536]{2,1,0:T(8,128)(2,1)}, u32[]{:S(2)}, u32[]{:S(2)}) async-start(bf16[32,16,1536]{2,1,0:T(8,128)(2,1)} %bitcast.124), calls=%async_computation.2 | async-start | bytes 3145728 | tf_op jit(solution)/shard_map/all_to_all | solution.py:26
  140.8 8.2 %collective-permute-start.18 = (bf16[128,1536]{1,0:T(8,128)(2,1)S(1)}, bf16[128,1536]{1,0:T(8,128)(2,1)S(1)}, u32[]{:S(2)}, u32[]{:S(2)}) collective-permute-start(bf16[128,1536]{1,0:T(8,128)(2,1)S(1)} %get-tuple-element.133.a_ref), channel_id=1, source_target_pairs={{0,1},{1,0},{2,3},{3,2},{4,5},{5,4},{6,7},{7,6},{8,9},{9,8},{10,11... | collective-permute-start | bytes 1179656 | tf_op jit(solution)/shard_map/ppermute | solution.py:18
  141.1 20.5 %collective-permute-start.20 = (bf16[1536,768]{1,0:T(8,128)(2,1)}, bf16[1536,768]{1,0:T(8,128)(2,1)}, u32[]{:S(2)}, u32[]{:S(2)}) collective-permute-start(bf16[1536,768]{1,0:T(8,128)(2,1)} %collective-permute-done.16.refs_6_), channel_id=1, source_target_pairs={{64,0},{65,1},{66,2},{67,3},{68,4},{69,5},{70,6},{71,7},{72,8},{73... | collective-permute-start | bytes 7077896 | tf_op jit(solution)/shard_map/ppermute | solution.py:1064
  149.0 11.3 %collective-permute-start.19 = (bf16[384,1536]{1,0:T(8,128)(2,1)S(1)}, bf16[384,1536]{1,0:T(8,128)(2,1)}, u32[]{:S(2)}, u32[]{:S(2)}) collective-permute-start(bf16[384,1536]{1,0:T(8,128)(2,1)S(1)} %bitcast.84), channel_id=1, source_target_pairs={{64,65},{65,64},{66,67},{67,66},{68,69},{69,68},{70,71},{71,70},{7... | collective-permute-start | bytes 3538952 | tf_op jit(solution)/shard_map/ppermute | solution.py:1068
  153.7 31.6 %all-to-all-start.3 = ((bf16[32,16,1664]{2,1,0:T(8,128)(2,1)}), bf16[32,16,1664]{2,1,0:T(8,128)(2,1)}, u32[]{:S(2)}, u32[]{:S(2)}) async-start(bf16[32,16,1664]{2,1,0:T(8,128)(2,1)} %bitcast.122), calls=%async_computation.3 | async-start | bytes 3407872 | tf_op jit(solution)/shard_map/all_to_all | solution.py:26
  198.7 28.7 %all-to-all-start.4 = ((bf16[32,16,1664]{2,1,0:T(8,128)(2,1)}), bf16[32,16,1664]{2,1,0:T(8,128)(2,1)}, u32[]{:S(2)}, u32[]{:S(2)}) async-start(bf16[32,16,1664]{2,1,0:T(8,128)(2,1)} %bitcast.123), calls=%async_computation.4 | async-start | bytes 3407872 | tf_op jit(solution)/shard_map/all_to_all | solution.py:26
  229.4 22.4 %collective-permute-start.23 = (bf16[2,1536,1152]{2,1,0:T(8,128)(2,1)}, bf16[2,1536,1152]{2,1,0:T(8,128)(2,1)}, u32[]{:S(2)}, u32[]{:S(2)}) collective-permute-start(bf16[2,1536,1152]{2,1,0:T(8,128)(2,1)} %get-tuple-element.154.refs_3_.refs_4_), channel_id=1, source_target_pairs={{0,64},{1,65},{2,66},{3,67},{4,68},{5,69},{6,70},{7,71},{8,72},{9,... | collective-permute-start | bytes 21233672 | tf_op jit(solution)/shard_map/ppermute | solution.py:1064
  233.6 8.1 %collective-permute-start.22 = (bf16[128,1664]{1,0:T(8,128)(2,1)S(1)}, bf16[128,1664]{1,0:T(8,128)(2,1)S(1)}, u32[]{:S(2)}, u32[]{:S(2)}) collective-permute-start(bf16[128,1664]{1,0:T(8,128)(2,1)S(1)} %collect.1.refs_3_), channel_id=1, source_target_pairs={{0,1},{1,0},{2,3},{3,2},{4,5},{5,4},{6,7},{7,6},{8,9},{9,8},{10,11... | collective-permute-start | bytes 1277960 | tf_op jit(solution)/shard_map/ppermute | solution.py:18
  233.6 25.2 %all-to-all-start.5 = ((bf16[32,16,1536]{2,1,0:T(8,128)(2,1)}), bf16[32,16,1536]{2,1,0:T(8,128)(2,1)}, u32[]{:S(2)}, u32[]{:S(2)}) async-start(bf16[32,16,1536]{2,1,0:T(8,128)(2,1)} %bitcast.125), calls=%async_computation.5 | async-start | bytes 3145728 | tf_op jit(solution)/shard_map/all_to_all | solution.py:26
  251.7 6.5 %collective-permute-start.25 = (bf16[16,1536]{1,0:T(8,128)(2,1)S(1)}, bf16[16,1536]{1,0:T(8,128)(2,1)S(1)}, u32[]{:S(2)}, u32[]{:S(2)}) collective-permute-start(bf16[16,1536]{1,0:T(8,128)(2,1)S(1)} %get-tuple-element.156.rest_0_), channel_id=1, source_target_pairs={{0,1},{1,0},{2,3},{3,2},{4,5},{5,4},{6,7},{7,6},{8,9},{9,8},{10,11... | collective-permute-start | bytes 147464 | tf_op jit(solution)/shard_map/ppermute | solution.py:18
  251.8 8.3 %collective-permute-start.24 = (bf16[128,1536]{1,0:T(8,128)(2,1)S(1)}, bf16[128,1536]{1,0:T(8,128)(2,1)S(1)}, u32[]{:S(2)}, u32[]{:S(2)}) collective-permute-start(bf16[128,1536]{1,0:T(8,128)(2,1)S(1)} %get-tuple-element.155.a_ref), channel_id=1, source_target_pairs={{0,1},{1,0},{2,3},{3,2},{4,5},{5,4},{6,7},{7,6},{8,9},{9,8},{10,11... | collective-permute-start | bytes 1179656 | tf_op jit(solution)/shard_map/ppermute | solution.py:18
  263.4 24.9 %all-to-all-start.6 = ((bf16[32,16,1536]{2,1,0:T(8,128)(2,1)}), bf16[32,16,1536]{2,1,0:T(8,128)(2,1)}, u32[]{:S(2)}, u32[]{:S(2)}) async-start(bf16[32,16,1536]{2,1,0:T(8,128)(2,1)} %bitcast.128), calls=%async_computation.6 | async-start | bytes 3145728 | tf_op jit(solution)/shard_map/all_to_all | solution.py:26
  270.6 60.8 %collective-permute-start.27 = (bf16[1536,1152]{1,0:T(8,128)(2,1)}, bf16[1536,1152]{1,0:T(8,128)(2,1)}, u32[]{:S(2)}, u32[]{:S(2)}) collective-permute-start(bf16[1536,1152]{1,0:T(8,128)(2,1)} %fusion), channel_id=1, source_target_pairs={{64,65},{65,64},{66,67},{67,66},{68,69},{69,68},{70,71},{71,70},{7... | collective-permute-start | bytes 10616840 | tf_op jit(solution)/shard_map/ppermute | solution.py:1068
  301.0 20.2 %collective-permute-start.28 = (bf16[768,1920]{1,0:T(8,128)(2,1)}, bf16[768,1920]{1,0:T(8,128)(2,1)}, u32[]{:S(2)}, u32[]{:S(2)}) collective-permute-start(bf16[768,1920]{1,0:T(8,128)(2,1)} %get-tuple-element.172), channel_id=1, source_target_pairs={{0,64},{64,0},{1,65},{65,1},{2,66},{66,2},{3,67},{67,3},{4,68},{68... | collective-permute-start | bytes 8847368 | tf_op jit(solution)/shard_map/ppermute | solution.py:18
  301.0 30.4 %all-to-all-start.7 = ((bf16[32,16,1536]{2,1,0:T(8,128)(2,1)}), bf16[32,16,1536]{2,1,0:T(8,128)(2,1)}, u32[]{:S(2)}, u32[]{:S(2)}) async-start(bf16[32,16,1536]{2,1,0:T(8,128)(2,1)} %bitcast.126), calls=%async_computation.7 | async-start | bytes 3145728 | tf_op jit(solution)/shard_map/all_to_all | solution.py:26
  305.9 74.3 %reduce-scatter.3.cloned.1.call-start = ((), (), s32[]{:S(2)}) async-start(), calls=%async_computation.14 | async-start | bytes 3686400 | tf_op jit(solution)/shard_map/reduce_scatter | solution.py:1007
  308.6 16.9 %collective-permute-start.26 = (bf16[128,1536]{1,0:T(8,128)(2,1)}, bf16[128,1536]{1,0:T(8,128)(2,1)}, u32[]{:S(2)}, u32[]{:S(2)}) collective-permute-start(bf16[128,1536]{1,0:T(8,128)(2,1)} %convolution_convert_fusion.1), channel_id=1, source_target_pairs={{0,1},{1,0},{2,3},{3,2},{4,5},{5,4},{6,7},{7,6},{8,9},{9,8},{10,11... | collective-permute-start | bytes 1179656 | tf_op jit(solution)/shard_map/ppermute | solution.py:18
  308.6 16.9 %collective-permute-start.29 = (f32[32,128]{1,0:T(8,128)S(1)}, f32[32,128]{1,0:T(8,128)S(1)}, u32[]{:S(2)}, u32[]{:S(2)}) collective-permute-start(f32[32,128]{1,0:T(8,128)S(1)} %copy-done.55), channel_id=1, source_target_pairs={{0,1},{1,0},{2,3},{3,2},{4,5},{5,4},{6,7},{7,6},{8,9},{9,8},{10,11... | collective-permute-start | bytes 49160 | tf_op jit(solution)/shard_map/ppermute | solution.py:18
  333.3 33.0 %collective-permute-start.33 = (bf16[2,1536,1152]{2,1,0:T(8,128)(2,1)}, bf16[2,1536,1152]{2,1,0:T(8,128)(2,1)}, u32[]{:S(2)}, u32[]{:S(2)}) collective-permute-start(bf16[2,1536,1152]{2,1,0:T(8,128)(2,1)} %experts_grads.3.refs_0_), channel_id=1, source_target_pairs={{64,0},{65,1},{66,2},{67,3},{68,4},{69,5},{70,6},{71,7},{72,8},{73... | collective-permute-start | bytes 21233672 | tf_op jit(solution)/shard_map/ppermute | solution.py:1064
  334.7 8.9 %collective-permute-start.30 = (bf16[128,1536]{1,0:T(8,128)(2,1)S(1)}, bf16[128,1536]{1,0:T(8,128)(2,1)S(1)}, u32[]{:S(2)}, u32[]{:S(2)}) collective-permute-start(bf16[128,1536]{1,0:T(8,128)(2,1)S(1)} %convolution_convert_fusion.refs_3_), channel_id=1, source_target_pairs={{0,1},{1,0},{2,3},{3,2},{4,5},{5,4},{6,7},{7,6},{8,9},{9,8},{10,11... | collective-permute-start | bytes 1179656 | tf_op jit(solution)/shard_map/ppermute | solution.py:18
  363.5 9.7 %collective-permute-start.34 = (bf16[768,1920]{1,0:T(8,128)(2,1)}, bf16[768,1920]{1,0:T(8,128)(2,1)S(1)}, u32[]{:S(2)}, u32[]{:S(2)}) collective-permute-start(bf16[768,1920]{1,0:T(8,128)(2,1)} %get-tuple-element.187), channel_id=1, source_target_pairs={{0,64},{64,0},{1,65},{65,1},{2,66},{66,2},{3,67},{67,3},{4,68},{68... | collective-permute-start | bytes 8847368 | tf_op jit(solution)/shard_map/ppermute | solution.py:18
  375.5 28.5 %all-to-all-start.8 = ((bf16[4,192,1920]{2,1,0:T(8,128)(2,1)}), bf16[4,192,1920]{2,1,0:T(8,128)(2,1)}, u32[]{:S(2)}, u32[]{:S(2)}) async-start(bf16[4,192,1920]{2,1,0:T(8,128)(2,1)} %bitcast.108), calls=%async_computation.8 | async-start | bytes 5898240 | tf_op jit(solution)/shard_map/all_to_all | solution.py:974
  380.2 26.5 %reduce-scatter.5.cloned.1.call-start = ((), (), s32[]{:S(2)}) async-start(), calls=%async_computation.15 | async-start | bytes 921600 | tf_op jit(solution)/shard_map/reduce_scatter | solution.py:1007
  380.9 97.3 %all-gather.2.cloned.1.call-start = ((), (), s32[]{:S(2)}) async-start(), calls=%async_computation.16 | async-start | bytes 3133440 | tf_op jit(solution)/shard_map/all_gather | solution.py:1001
  383.6 11.5 %collective-permute-start.35 = (bf16[128,1536]{1,0:T(8,128)(2,1)S(1)}, bf16[128,1536]{1,0:T(8,128)(2,1)S(1)}, u32[]{:S(2)}, u32[]{:S(2)}) collective-permute-start(bf16[128,1536]{1,0:T(8,128)(2,1)S(1)} %get-tuple-element.188), channel_id=1, source_target_pairs={{0,1},{1,0},{2,3},{3,2},{4,5},{5,4},{6,7},{7,6},{8,9},{9,8},{10,11... | collective-permute-start | bytes 1179656 | tf_op jit(solution)/shard_map/ppermute | solution.py:18
  406.7 7.3 %collective-permute-start.38 = (bf16[48,1920]{1,0:T(8,128)(2,1)}, bf16[48,1920]{1,0:T(8,128)(2,1)S(1)}, u32[]{:S(2)}, u32[]{:S(2)}) collective-permute-start(bf16[48,1920]{1,0:T(8,128)(2,1)} %reduce-scatter.5.cloned.1.call-done), channel_id=1, source_target_pairs={{0,2},{2,0},{4,6},{6,4},{8,10},{10,8},{12,14},{14,12},{16,18},{18,... | collective-permute-start | bytes 552968 | tf_op jit(solution)/shard_map/ppermute | solution.py:1017
  444.9 38.1 %collective-permute-start.39 = (bf16[1280,1152]{1,0:T(8,128)(2,1)}, bf16[1280,1152]{1,0:T(8,128)(2,1)}, u32[]{:S(2)}, u32[]{:S(2)}) collective-permute-start(bf16[1280,1152]{1,0:T(8,128)(2,1)} %fusion.1), channel_id=1, source_target_pairs={{0,1},{1,0},{2,3},{3,2},{4,5},{5,4},{6,7},{7,6},{8,9},{9,8},{10,11... | collective-permute-start | bytes 8847368 | tf_op jit(solution)/shard_map/ppermute | solution.py:1068
  451.1 25.9 %all-to-all-start.11 = ((bf16[4,192,1920]{2,1,0:T(8,128)(2,1)}), bf16[4,192,1920]{2,1,0:T(8,128)(2,1)}, u32[]{:S(2)}, u32[]{:S(2)}) async-start(bf16[4,192,1920]{2,1,0:T(8,128)(2,1)} %broadcast_in_dim.42), calls=%async_computation.11 | async-start | bytes 5898240 | tf_op jit(solution)/shard_map/all_to_all | solution.py:974
  476.9 21.3 %collective-permute-start.37 = (bf16[768,1920]{1,0:T(8,128)(2,1)}, bf16[768,1920]{1,0:T(8,128)(2,1)}, u32[]{:S(2)}, u32[]{:S(2)}) collective-permute-start(bf16[768,1920]{1,0:T(8,128)(2,1)} %bitcast.45.zero_ref), channel_id=1, source_target_pairs={{64,0},{65,1},{66,2},{67,3},{68,4},{69,5},{70,6},{71,7},{72,8},{73... | collective-permute-start | bytes 8847368 | tf_op jit(solution)/shard_map/ppermute | solution.py:1064
  483.0 15.2 %collective-permute-start.40 = (bf16[768,1920]{1,0:T(8,128)(2,1)S(1)}, bf16[768,1920]{1,0:T(8,128)(2,1)S(1)}, u32[]{:S(2)}, u32[]{:S(2)}) collective-permute-start(bf16[768,1920]{1,0:T(8,128)(2,1)S(1)} %copy-done.70), channel_id=1, source_target_pairs={{0,64},{1,65},{2,66},{3,67},{4,68},{5,69},{6,70},{7,71},{8,72},{9,... | collective-permute-start | bytes 8847368 | tf_op jit(solution)/shard_map/ppermute | solution.py:1064
  487.8 16.6 %collective-permute-start.41 = (bf16[256,1152]{1,0:T(8,128)(2,1)S(1)}, bf16[256,1152]{1,0:T(8,128)(2,1)S(1)}, u32[]{:S(2)}, u32[]{:S(2)}) collective-permute-start(bf16[256,1152]{1,0:T(8,128)(2,1)S(1)} %copy-done.77), channel_id=1, source_target_pairs={{0,1},{1,0},{2,3},{3,2},{4,5},{5,4},{6,7},{7,6},{8,9},{9,8},{10,11... | collective-permute-start | bytes 1769480 | tf_op jit(solution)/shard_map/ppermute | solution.py:1068
  (94 other events, 920.6 us)
Sparse Core Ops, SparseCore 0:
  334.9 26.1 reduce-scatter.2
  383.5 22.1 reduce-scatter.4
  415.8 47.3 all-gather.1
